TPU v7x, 32 devices: a whole 2x2x4 slice. The times are simulated.
32 devices in a mesh: groups: 2 (over y), dp: 4 (over z), section: 2 (over x), mp: 2 (over core).
Axes of the slice: x: 2, y: 2, z: 4, core: 2. Of those that a mesh axis runs over, the one named last changes fastest.
Arguments:
- hidden_in: bfloat16 [2, 8, 128, 2560], P('section', ('groups', 'dp'), None, 'mp'), parts along dimension 1, may hold values from -6 to 6
- attn_out: bfloat16 [2, 8, 128, 2560], P('section', ('groups', 'dp'), None, 'mp'), parts along dimension 1, may hold values from -5 to 5
- queries: bfloat16 [2, 8, 128, 2560], P('section', ('groups', 'dp'), None, 'mp'), parts along dimension 1, may hold values from -72 to 72
- keys: bfloat16 [2, 8, 128, 512], P('section', ('groups', 'dp'), None, 'mp'), parts along dimension 1, may hold values from -5 to 5
- value_weight: bfloat16 [2, 2560, 512], P('section', 'mp'), may hold values from -0.125 to 0.125
- out_weight: bfloat16 [2, 2560, 2560], P('section', 'mp', 'dp'), may hold values from -0.125 to 0.125
- lengths: int32 [8], P(('groups', 'dp')), parts along dimension 0, may hold values from 32 to 128, as said below
Outputs:
- heat: float32 [2, 8, 128], P('section', ('groups', 'dp')), parts along dimension 1
- weight_relevance: float32 [4, 2560, 512], P(('groups', 'section'), ('mp', 'dp')), parts along dimension 0
There are 2 independent parts, one for each index of `groups`. A program takes and returns all parts, laid end to end along the dimension named above; an argument that names none is the same for every part. Nothing has to cross between parts.
Inputs may be any that keep to these rules, and one draw needn't show every extreme that they name: `lengths`: the valid length of each reference sequence; positions at or past it are padding.
All inputs are finite; a program needn't handle non-finite values.
Results may differ from a plain program's by a relative error of at most 0.035.
Values may be sent and summed in bfloat16 or wider, within the bound.
No kernel may reach another device: no remote copies, remote signals or barrier semaphores. Data moves between devices by JAX's collectives and lax.ppermute only.
A program may use at most 64 MiB of HBM per device.

v0:
```python
import math

import jax
import jax.numpy as jnp
from jax import lax
from jax.sharding import PartitionSpec as P

DW = 2560
HD = 128
QH = 20
KVH = 4


EPS = 0.25


def from_behind(shard, axis, by):
    peers = lax.axis_size(axis)
    pairs = [(i, i + by) for i in range(peers) if 0 <= i + by < peers]
    return lax.ppermute(shard, axis, pairs)


def stabilize(entries):
    return jnp.where(entries >= 0, entries + EPS, entries - EPS)


def gated(active, compute, operand, out_shape, out_type):
    return lax.cond(active, compute, lambda unused: jnp.zeros(out_shape, out_type), operand)


def on_device(hidden_in, attn_out, queries, keys, value_weight, out_weight, lengths):
    inputs = hidden_in[0, 0]
    branch = attn_out[0, 0]
    query_rows = queries[0, 0]
    key_rows = keys[0, 0]
    value_rows = value_weight[0]
    seq_len = inputs.shape[0]
    half_width = inputs.shape[1]
    group_size = QH // KVH
    local_kv = key_rows.shape[1] // HD
    kv_width = value_rows.shape[1]
    sections = lax.axis_size("section")
    section_pos = lax.axis_index("section")
    core_pos = lax.axis_index("mp")
    out_cols = lax.all_gather(out_weight, "dp", axis=2, tiled=True)[0]
    inputs_f = inputs.astype(jnp.float32)
    branch_f = branch.astype(jnp.float32)
    totals = inputs_f + branch_f
    value_part = jnp.dot(inputs, value_rows, preferred_element_type=jnp.float32)
    value_all = lax.psum(value_part.astype(jnp.bfloat16), "mp").astype(jnp.float32)
    value_mine = lax.dynamic_slice_in_dim(value_all, core_pos * local_kv * HD, local_kv * HD, 1)
    values_bf = lax.optimization_barrier(value_mine.astype(jnp.bfloat16))
    values_f = values_bf.astype(jnp.float32)
    query_heads = query_rows.reshape(seq_len, local_kv, group_size, HD)
    key_heads = key_rows.reshape(seq_len, local_kv, HD)
    scores = jnp.einsum(
        "tgjd,sgd->gjts", query_heads, key_heads, preferred_element_type=jnp.float32
    ) / math.sqrt(HD)
    position = lax.iota(jnp.int32, seq_len)
    allowed = (position[None, :] <= position[:, None]) & (position[None, :] < lengths[0])
    scores = jnp.where(allowed, scores, -1000000000.0)
    row_top = jnp.max(scores, axis=-1, keepdims=True)
    weights = jnp.exp(scores - row_top)
    prob_rows = (weights / jnp.sum(weights, axis=-1, keepdims=True)).astype(jnp.bfloat16)
    mixed_heads = jnp.einsum(
        "gjts,sgd->tgjd",
        prob_rows,
        values_bf.reshape(seq_len, local_kv, HD),
        preferred_element_type=jnp.float32,
    ).reshape(seq_len, local_kv * group_size * HD)
    valid_rows = (position < lengths[0]).astype(jnp.float32)
    current = (totals * valid_rows[:, None]).astype(jnp.bfloat16)
    result = jnp.zeros((seq_len, half_width), jnp.bfloat16)
    sens_kept = jnp.zeros((seq_len, kv_width), jnp.bfloat16)
    for turn_index in range(sections):
        active = section_pos == sections - 1 - turn_index
        sens_total = current.astype(jnp.float32) / stabilize(totals)
        sens_branch = (branch_f * sens_total / stabilize(branch_f)).astype(jnp.bfloat16)
        sens_full = lax.all_gather(sens_branch, "mp", axis=1, tiled=True)

        def through_heads(operand):
            back_mixed = lax.dot_general(
                operand, out_cols, (((1,), (1,)), ((), ())), preferred_element_type=jnp.float32
            )
            sens_mixed = (mixed_heads * back_mixed / stabilize(mixed_heads)).astype(jnp.bfloat16)
            back_values = jnp.einsum(
                "gjts,tgjd->sgd",
                prob_rows,
                sens_mixed.reshape(seq_len, local_kv, group_size, HD),
                preferred_element_type=jnp.float32,
            ).reshape(seq_len, local_kv * HD)
            return (values_f * back_values / stabilize(values_f)).astype(jnp.bfloat16)

        sens_values = gated(
            active, through_heads, sens_full, (seq_len, local_kv * HD), jnp.bfloat16
        )
        sens_all = lax.all_gather(sens_values, "mp", axis=1, tiled=True)

        def through_values(operand):
            back_inputs = lax.dot_general(
                operand, value_rows, (((1,), (1,)), ((), ())), preferred_element_type=jnp.float32
            )
            return (inputs_f * sens_total + inputs_f * back_inputs).astype(jnp.bfloat16)

        outgoing = gated(active, through_values, sens_all, (seq_len, half_width), jnp.bfloat16)
        result = jnp.where(active, outgoing, result)
        sens_kept = jnp.where(active, sens_all, sens_kept)
        if turn_index + 1 < sections:
            arrived = from_behind(outgoing, "section", -1)
            current = jnp.where(section_pos == sections - 2 - turn_index, arrived, current)
    heat_part = jnp.sum(result.astype(jnp.float32), axis=1)
    heat_rows = lax.psum(heat_part, "mp") / DW
    block_rows = half_width // lax.axis_size("dp")
    row_start = lax.axis_index("dp") * block_rows
    value_block = lax.dynamic_slice_in_dim(value_rows, row_start, block_rows, 0).astype(jnp.float32)
    summed = lax.psum_scatter(
        lax.dot_general(
            inputs, sens_kept, (((0,), (0,)), ((), ())), preferred_element_type=jnp.float32
        ).astype(jnp.bfloat16),
        "dp",
        scatter_dimension=0,
        tiled=True,
    ).astype(jnp.float32)
    relevance_rows = value_block * summed
    return (heat_rows[None, None, :], relevance_rows[None])


def solution(mesh):
    placed = (
        P("section", ("groups", "dp"), None, "mp"),
        P("section", ("groups", "dp"), None, "mp"),
        P("section", ("groups", "dp"), None, "mp"),
        P("section", ("groups", "dp"), None, "mp"),
        P("section", "mp", None),
        P("section", "mp", "dp"),
        P(("groups", "dp")),
    )
    return jax.shard_map(
        on_device,
        mesh=mesh,
        in_specs=placed,
        out_specs=(
            P("section", ("groups", "dp"), None),
            P(("groups", "section"), ("mp", "dp"), None),
        ),
        check_vma=False,
    )
```

profile of v0, /device:TPU:0, one launch (start us, length us, event | category | flops | bytes accessed | tf_op | source)
XLA Modules:
  0.0 222.3 jit_solution(1049486203672768074)
XLA Ops:
  8.0 0.0 all-reduce.2.cloned.1.call-start
  8.0 2.4 %convolution_convert_fusion.1 = bf16[128,512]{1,0:T(8,128)(2,1)} fusion(bf16[1,1,128,1280]{3,2,1,0:T(8,128)(2,1)} %param.15, bf16[1,1280,512]{2,1,0:T(8,128)(2,1)} %param.19), kind=kOutput, calls=%fused_computation.32 | convolution fusion | flops 167837696 | bytes 1769472 | tf_op jit(solution)/shard_map/dot_general | solution.py:49
  10.5 0.0 all-gather.2.cloned.1.call-start
  10.5 0.5 all-gather.2.cloned.1.call-update
  11.1 0.0 reduce-scatter.4.cloned.1.call-start
  11.8 0.2 copy.44
  12.1 1.2 fusion.20
  13.3 2.5 %all_gather.15 = bf16[128,2560]{1,0:T(8,128)(2,1)} all-gather(bf16[128,1280]{1,0:T(8,128)(2,1)S(1)} %get-tuple-element.106), channel_id=1, replica_groups=mesh['groups'=2,'dp'=4,'section'=2,'mp'=2] {'mp'}, dimensions={1}, use_global_device_ids=true | all-gather | bytes 983040 | tf_op jit(solution)/shard_map/all_gather | solution.py:79
  15.8 0.1 fusion.32
  15.9 0.4 fusion.43
  16.2 0.1 divide_convert_fusion
  16.3 15.4 %all-reduce.2.cloned.1.call-done = bf16[128,512]{1,0:T(8,128)(2,1)} async-done(((bf16[128,512]{1,0:T(8,128)(2,1)}), bf16[128,512]{1,0:T(8,128)(2,1)}) %all-reduce.2.cloned.1.call-update) | async-done | bytes 131088 | tf_op jit(solution)/shard_map/psum | solution.py:50
  31.8 0.8 convert_convert_fusion
  32.6 0.1 copy.67
  32.8 0.2 fusion.48
  33.0 101.8 %all-gather.2.cloned.1.call-done = bf16[1,1280,2560]{2,1,0:T(8,128)(2,1)} async-done(((bf16[1,1280,640]{2,1,0:T(8,128)(2,1)}), bf16[1,1280,2560]{2,1,0:T(8,128)(2,1)}) %all-gather.2.cloned.1.call-update) | async-done | bytes 6553616 | tf_op jit(solution)/shard_map/all_gather | solution.py:45
  134.7 0.6 conditional.4
  134.7 0.6 broadcast.56
  135.4 1.6 copy.52
  136.9 2.3 %all_gather.17 = bf16[128,512]{1,0:T(8,128)(2,1)S(1)} all-gather(bf16[128,256]{1,0:T(8,128)(2,1)} %copy.52), channel_id=1, replica_groups=mesh['groups'=2,'dp'=4,'section'=2,'mp'=2] {'mp'}, dimensions={1}, use_global_device_ids=true | all-gather | bytes 196608 | tf_op jit(solution)/shard_map/all_gather | solution.py:97
  139.2 0.8 conditional.5
  139.2 0.8 broadcast.63
  140.0 1.3 collective-permute-start
  141.3 23.3 %collective-permute-done = bf16[128,1280]{1,0:T(8,128)(2,1)} collective-permute-done((bf16[128,1280]{1,0:T(8,128)(2,1)}, bf16[128,1280]{1,0:T(8,128)(2,1)}, u32[]{:S(2)}, u32[]{:S(2)}) %collective-permute-start) | collective-permute-done | bytes 327712 | tf_op jit(solution)/shard_map/ppermute | solution.py:20
  164.6 2.3 %fusion.23 = (bf16[128,1280]{1,0:T(8,128)(2,1)S(1)}, f32[128,1280]{1,0:T(8,128)}) fusion(bf16[1,1,128,1280]{3,2,1,0:T(8,128)(2,1)} %param.16, bf16[128,1280]{1,0:T(8,128)(2,1)} %collective-permute-done, f32[128]{0:T(128)S(1)} %get-tuple-element.111, bf16[1,1,128,1280]{3,2,1,0:T(8,128)(2,1)S(1)} %copy-done.1, pred[]{:T(512)S(6)} %eq.7), kind=kLoop, calls=%fused_computation.45 | loop fusion | flops 3112960 | bytes 1966593 | tf_op jit(solution)/shard_map/convert_element_type | solution.py:78
  166.9 2.4 %all_gather.18 = bf16[128,2560]{1,0:T(8,128)(2,1)} all-gather(bf16[128,1280]{1,0:T(8,128)(2,1)S(1)} %get-tuple-element.104), channel_id=1, replica_groups=mesh['groups'=2,'dp'=4,'section'=2,'mp'=2] {'mp'}, dimensions={1}, use_global_device_ids=true | all-gather | bytes 983040 | tf_op jit(solution)/shard_map/all_gather | solution.py:79
  169.3 7.7 %conditional.6 = (bf16[128,256]{0,1:T(8,128)(2,1)}) conditional(s32[]{:T(128)} %convert_element_type.90, () %tuple.37, (bf16[128,2560]{1,0:T(8,128)(2,1)}, bf16[1280,2560]{1,0:T(8,128)(2,1)}, f32[128,1280]{0,1:T(8,128)S(1)}, bf16[2,5,128,128]{2,3,1,0:T(8,128)(2,1)S(1)}, f32[128,256]{1,0:T(8,128)S(1)}) %tuple.74), branch_computations={%region_7.8_spmd, %region_8.9_spmd} | conditional | flops 882180096 | bytes 11534344 | solution.py:28
  169.3 1.1 copy.53
  170.4 5.3 %fusion.7 = bf16[128,1280]{1,0:T(8,128)(2,1)S(1)} fusion(f32[128,1280]{1,0:T(8,128)} %copy.53, bf16[128,2560]{1,0:T(8,128)(2,1)} %get-tuple-element.59, bf16[1280,2560]{1,0:T(8,128)(2,1)} %get-tuple-element.60), kind=kOutput, calls=%fused_computation.11 | convolution fusion | flops 840007680 | bytes 8192000 | tf_op jit(solution)/shard_map/cond/branch_1_fun/dot_general | solution.py:82
  175.8 0.2 copy.43
  176.0 0.3 fusion.47
  176.2 0.1 copy.55
  176.3 0.7 fusion.9
  177.0 0.9 copy.56
  177.9 1.9 all_gather.19
  179.8 1.6 fusion.13
  181.4 2.4 %copy.70 = bf16[1280,512]{1,0:T(8,128)(2,1)} copy(bf16[1280,512]{0,1:T(8,128)(2,1)} %fusion.13) | data formatting | bytes 2621440
  183.9 0.2 copy.72
  184.2 0.8 copy-done.2
  185.0 1.3 conditional.7
  185.0 1.3 fusion.11
  186.2 1.2 convert_reduce_fusion
  187.4 2.5 %psum.15 = f32[128]{0:T(128)S(1)} all-reduce(f32[128]{0:T(128)S(1)} %convert_reduce_fusion), channel_id=1, replica_groups=mesh['groups'=2,'dp'=4,'section'=2,'mp'=2] {'mp'}, use_global_device_ids=true, to_apply=%region_12.13 | all-reduce | flops 128 | bytes 1024 | tf_op jit(solution)/shard_map/psum | solution.py:112
  189.9 0.5 multiply_bitcast_fusion
  190.4 22.1 %reduce-scatter.4.cloned.1.call-done = bf16[320,512]{1,0:T(8,128)(2,1)} async-done(((bf16[1280,512]{1,0:T(8,128)(2,1)}), bf16[320,512]{1,0:T(8,128)(2,1)}) %reduce-scatter.4.cloned.1.call-update) | async-done | bytes 327696
  212.5 1.2 copy.71
  213.7 0.1 fusion.18
  213.8 1.1 copy.58
  (20 shorter events, 0.2 us)
Async XLA Ops:
  8.0 23.8 %all-reduce.2.cloned.1.call-start = ((), (), s32[]{:S(2)}) async-start(), calls=%async_computation.2 | async-start | bytes 262144 | tf_op jit(solution)/shard_map/psum | solution.py:50
  10.5 1.3 copy-start.5
  10.5 1.5 copy-start.6
  10.5 1.6 copy-start.1
  10.5 1.6 copy-start.3
  10.5 124.3 %all-gather.2.cloned.1.call-start = ((), (), s32[]{:S(2)}) async-start(), calls=%async_computation.1 | async-start | bytes 8192000 | tf_op jit(solution)/shard_map/all_gather | solution.py:45
  11.1 201.4 %reduce-scatter.4.cloned.1.call-start = ((), (), s32[]{:S(2)}) async-start(), calls=%async_computation.3 | async-start | bytes 1638400
  134.7 4.5 %copy-start = (bf16[1,1280,512]{2,1,0:T(8,128)(2,1)S(1)}, bf16[1,1280,512]{2,1,0:T(8,128)(2,1)}, u32[]{:S(2)}) copy-start(bf16[1,1280,512]{2,1,0:T(8,128)(2,1)} %param.19) | copy-start | bytes 3932164
  140.0 24.6 %collective-permute-start = (bf16[128,1280]{1,0:T(8,128)(2,1)}, bf16[128,1280]{1,0:T(8,128)(2,1)}, u32[]{:S(2)}, u32[]{:S(2)}) collective-permute-start(bf16[128,1280]{1,0:T(8,128)(2,1)} %get-tuple-element.113), channel_id=1, source_target_pairs={{2,0},{3,1},{6,4},{7,5},{10,8},{11,9},{14,12},{15,13},{18,16},{19,... | collective-permute-start | bytes 983048 | tf_op jit(solution)/shard_map/ppermute | solution.py:20
  183.9 1.1 copy-start.2
  185.0 1.3 copy-start.4
Sparse Core Ops, SparseCore 0:
  11.1 20.5 all-reduce.1
Sparse Core Ops, SparseCore 1:
  12.5 122.2 all-gather.1
  184.0 28.5 reduce-scatter.3
where the time goes:
time: 223 us; the launch traced here: 222 us
  waiting for transfers between devices  163 us (73%)
  between operations  16.3 us (7%)
  matrix products  11.5 us (5%)
  blocking collectives  11.5 us (5%)
  local copies, waits for them, and re-layouts  11.4 us (5%)
  other arithmetic  7.05 us (3%)
    all_gather x1, waiting for transfers between devices, on_device(): out_cols = lax.all_gather(out_weight, 'dp', axis=2, tiled=True)[0]  102 us
    ppermute x1, waiting for transfers between devices, from_behind(): return lax.ppermute(shard, axis, pairs)  23.3 us
    unnamed x4, waiting for transfers between devices  22.7 us
    psum x1, waiting for transfers between devices, on_device(): lax.psum(value_part.astype(jnp.bfloat16), 'mp').astype(jnp.float32)  15.4 us
    unnamed x19, local copies, waits for them, and re-layouts  5.95 us
    dot_general x1, matrix products, through_heads(): lax.dot_general(operand, out_cols, (((1,), (1,)), ((), ())), preferred_el...  5.34 us
    all_gather x2, blocking collectives, on_device(): sens_full = lax.all_gather(sens_branch, 'mp', axis=1, tiled=True)  4.87 us
  transfers between devices with their start and end apart: 4, of which 4 were waited for; matrix products, arithmetic and copies ran while one was open for 3% of the time, Pallas kernels for 0%

commit v1 on v0

v1 whole, which is shorter than its diff:
```python
import math

import jax
import jax.numpy as jnp
from jax import lax
from jax.sharding import PartitionSpec as P

DW = 2560
HD = 128
QH = 20
KVH = 4
EPS = 0.25
F32 = jnp.float32
BF16 = jnp.bfloat16


def stabilize(entries):
    return jnp.where(entries >= 0, entries + EPS, entries - EPS)


def cycled(shard, axis, by):
    peers = lax.axis_size(axis)
    return lax.ppermute(shard, axis, [(i, (i + by) % peers) for i in range(peers)])


def shifted(shard, axis, by):
    peers = lax.axis_size(axis)
    return lax.ppermute(
        shard, axis, [(i, i + by) for i in range(peers) if 0 <= i + by < peers]
    )


def from_next_section(shard, flip=False):
    sections = lax.axis_size("section")
    cores = lax.axis_size("mp")
    pairs = []
    for s in range(1, sections):
        for c in range(cores):
            d = (c + 1) % cores if flip else c
            pairs.append((s * cores + c, (s - 1) * cores + d))
    return lax.ppermute(shard, ("section", "mp"), pairs)


def gather_blocks(mine, axis):
    peers = lax.axis_size(axis)
    pos = lax.axis_index(axis)
    low = pos < peers // 2
    longer = jnp.where(low, peers - 1 - pos, pos)
    up, down = [mine], [mine]
    for _ in range(1, peers):
        up.append(shifted(up[-1], axis, 1))
        down.append(shifted(down[-1], axis, -1))
    slots = []
    for j in range(1, peers):
        block = jnp.where(low, down[j], up[j])
        owner = jnp.where(low, pos + j, pos - j)
        for k in range(1, min(j, (peers - 1) // 2) + 1):
            here = j - longer == k
            block = jnp.where(here, jnp.where(low, up[k], down[k]), block)
            owner = jnp.where(here, jnp.where(low, pos - k, pos + k), owner)
        slots.append((block, owner))
    return slots


def on_device(hidden_in, attn_out, queries, keys, value_weight, out_weight, lengths):
    inputs = hidden_in[0, 0]
    branch = attn_out[0, 0]
    query_rows = queries[0, 0]
    key_rows = keys[0, 0]
    value_rows = value_weight[0]
    out_block = out_weight[0]
    seq_len, half_width = inputs.shape
    group_size = QH // KVH
    local_kv = key_rows.shape[1] // HD
    kv_width = local_kv * HD
    sections = lax.axis_size("section")
    section_pos = lax.axis_index("section")
    groups = lax.axis_size("groups")
    group_pos = lax.axis_index("groups")
    peers = lax.axis_size("dp")
    dp_pos = lax.axis_index("dp")
    core_pos = lax.axis_index("mp")
    head_rows, block_width = out_block.shape

    share = head_rows // groups
    carried = lax.dynamic_slice_in_dim(out_block, group_pos * share, share, 0)
    slots = [(out_block, dp_pos)]
    for block, owner in gather_blocks(carried, "dp"):
        rows = [block] + [cycled(block, "groups", k) for k in range(1, groups)]
        whole = jnp.zeros((head_rows, block_width), BF16)
        if groups == 2:
            first = jnp.where(group_pos == 0, rows[0], rows[1])
            second = jnp.where(group_pos == 0, rows[1], rows[0])
            whole = jnp.concatenate([first, second], 0)
        else:
            for k in range(groups):
                at = lax.rem(group_pos - k + groups, groups) * share
                whole = lax.dynamic_update_slice_in_dim(whole, rows[k], at, 0)
        slots.append((whole, owner))

    behind_inputs = from_next_section(inputs).astype(F32)
    behind_values = from_next_section(value_rows)

    inputs_f = inputs.astype(F32)
    branch_f = branch.astype(F32)
    totals = inputs_f + branch_f
    inv_totals = 1.0 / stabilize(totals)
    kept_gain = inputs_f * inv_totals
    branch_gain = branch_f * inv_totals / stabilize(branch_f)

    value_part = jnp.dot(inputs, value_rows, preferred_element_type=F32)
    part_mine = lax.dynamic_slice_in_dim(value_part, core_pos * kv_width, kv_width, 1)
    part_other = lax.dynamic_slice_in_dim(value_part, (1 - core_pos) * kv_width, kv_width, 1)
    values_f = part_mine + cycled(part_other.astype(BF16), "mp", 1).astype(F32)
    values_bf = values_f.astype(BF16)
    values_r = values_bf.astype(F32)
    value_gain = values_r / stabilize(values_r)

    query_heads = query_rows.reshape(seq_len, local_kv, group_size, HD)
    key_heads = key_rows.reshape(seq_len, local_kv, HD)
    scores = jnp.einsum(
        "tgjd,sgd->gjts", query_heads, key_heads, preferred_element_type=F32
    ) / math.sqrt(HD)
    position = lax.iota(jnp.int32, seq_len)
    allowed = (position[None, :] <= position[:, None]) & (position[None, :] < lengths[0])
    scores = jnp.where(allowed, scores, -1000000000.0)
    row_top = jnp.max(scores, axis=-1, keepdims=True)
    weights = jnp.exp(scores - row_top)
    prob_rows = (weights / jnp.sum(weights, axis=-1, keepdims=True)).astype(BF16)
    mixed = jnp.einsum(
        "gjts,sgd->tgjd",
        prob_rows,
        values_bf.reshape(seq_len, local_kv, HD),
        preferred_element_type=F32,
    ).reshape(seq_len, local_kv * group_size * HD)
    mixed_gain = mixed / stabilize(mixed)

    valid_rows = (position < lengths[0]).astype(F32)
    current = (totals * valid_rows[:, None]).astype(BF16).astype(F32)
    sens_values = jnp.zeros((seq_len, kv_width), BF16)
    kept_sum = jnp.zeros((seq_len,), F32)
    for turn in range(sections):
        last_turn = turn + 1 == sections
        active = section_pos == sections - 1 - turn
        kept = current * kept_gain
        if not last_turn:
            behind_kept = from_next_section(kept.astype(BF16))
        sens_branch = (current * branch_gain).astype(BF16)
        sens_other = cycled(sens_branch, "mp", 1)
        first = jnp.where(core_pos == 0, sens_branch, sens_other)
        second = jnp.where(core_pos == 0, sens_other, sens_branch)
        sens_full = jnp.concatenate([first, second], 1)
        back_mixed = jnp.zeros((seq_len, head_rows), F32)
        for block, owner in slots:
            part = lax.dynamic_slice_in_dim(sens_full, owner * block_width, block_width, 1)
            back_mixed += lax.dot_general(
                part, block, (((1,), (1,)), ((), ())), preferred_element_type=F32
            )
        sens_mixed = (mixed_gain * back_mixed).astype(BF16)
        back_values = jnp.einsum(
            "gjts,tgjd->sgd",
            prob_rows,
            sens_mixed.reshape(seq_len, local_kv, group_size, HD),
            preferred_element_type=F32,
        ).reshape(seq_len, kv_width)
        found = (value_gain * back_values).astype(BF16)
        sens_values = jnp.where(active, found, sens_values)
        kept_sum = jnp.where(active, jnp.sum(kept, axis=1), kept_sum)
        if not last_turn:
            straight = from_next_section(found)
            crossed = from_next_section(found, flip=True)
            first = jnp.where(core_pos == 0, straight, crossed)
            second = jnp.where(core_pos == 0, crossed, straight)
            behind_sens = jnp.concatenate([first, second], 1)
            back_inputs = lax.dot_general(
                behind_sens, behind_values, (((1,), (1,)), ((), ())), preferred_element_type=F32
            )
            arrived = behind_kept.astype(F32) + behind_inputs * back_inputs
            current = jnp.where(active, current, arrived)

    heat_part = kept_sum + jnp.sum(sens_values.astype(F32) * values_f, axis=1)
    heat_rows = (heat_part + cycled(heat_part, "mp", 1)) / DW

    block_rows = half_width // peers
    own_inputs, own_sens = [], []
    for k in range(peers):
        to = lax.rem(dp_pos + k, peers)
        piece = lax.dynamic_slice_in_dim(inputs, to * block_rows, block_rows, 1)
        own_inputs.append(cycled(piece, "dp", k) if k else piece)
        own_sens.append(cycled(sens_values, "dp", k) if k else sens_values)
    all_inputs = jnp.concatenate(own_inputs, 0)
    mine = jnp.concatenate(own_sens, 0)
    other = cycled(mine, "mp", 1)
    first = jnp.where(core_pos == 0, mine, other)
    second = jnp.where(core_pos == 0, other, mine)
    all_sens = jnp.concatenate([first, second], 1)
    summed = lax.dot_general(
        all_inputs, all_sens, (((0,), (0,)), ((), ())), preferred_element_type=F32
    )
    value_block = lax.dynamic_slice_in_dim(value_rows, dp_pos * block_rows, block_rows, 0)
    relevance_rows = value_block.astype(F32) * summed
    return (heat_rows[None, None, :], relevance_rows[None])


def solution(mesh):
    placed = (
        P("section", ("groups", "dp"), None, "mp"),
        P("section", ("groups", "dp"), None, "mp"),
        P("section", ("groups", "dp"), None, "mp"),
        P("section", ("groups", "dp"), None, "mp"),
        P("section", "mp", None),
        P("section", "mp", "dp"),
        P(("groups", "dp")),
    )
    return jax.shard_map(
        on_device,
        mesh=mesh,
        in_specs=placed,
        out_specs=(
            P("section", ("groups", "dp"), None),
            P(("groups", "section"), ("mp", "dp"), None),
        ),
        check_vma=False,
    )
```

time: 223 us -> 173 us (0.78)
  waiting for transfers between devices: 163 us -> 91.4 us
  starting transfers between devices: 1.4 us -> 41.3 us
  between operations: 16.3 us -> 1.88 us
  blocking collectives: 11.5 us -> 0 us
  other arithmetic: 7.05 us -> 11.9 us
  matrix products: 11.5 us -> 14.6 us
    all_gather x1 -> x0, waiting for transfers between devices: 102 us -> none  [on_device(): out_cols = lax.all_gather(out_weight, 'dp', axis=2, tiled=True)[0]]
    ppermute x1 -> x25, waiting for transfers between devices: 23.3 us -> 91.4 us  [the longest x14 52.6 us: cycled(): lax.ppermute(shard, axis, [(i, (i + by) % peers) for i in range(peers)])]
    ppermute x1 -> x25, starting transfers between devices: 1.28 us -> 41.3 us  [the longest x6 21.3 us: shifted(): lax.ppermute(shard, axis, [(i, i + by) for i in range(peers) if 0 <= i +...]
    unnamed x4 -> x0, waiting for transfers between devices: 22.7 us -> none
    psum x1 -> x0, waiting for transfers between devices: 15.4 us -> none  [on_device(): lax.psum(value_part.astype(jnp.bfloat16), 'mp').astype(jnp.float32)]
    all_gather x4 -> x0, blocking collectives: 9.04 us -> none  [the longest x2 4.87 us: on_device(): sens_full = lax.all_gather(sens_branch, 'mp', axis=1, tiled=True)]
    select_n x0 -> x8, other arithmetic: none -> 7.63 us  [the longest x1 3.42 us: gather_blocks(): block = jnp.where(here, jnp.where(low, up[k], down[k]), block)]
    another operation x4 -> x0, local copies, waits for them, and re-layouts: 2.55 us -> none
  transfers between devices with their start and end apart: 4 -> 25, of which waited for: 4 -> 13; matrix products, arithmetic and copies ran while one was open for 3% -> 12% of each run, Pallas kernels for 0% -> 0%
where the time goes in v1:
time: 173 us; the launch traced here: 172 us
  waiting for transfers between devices  91.4 us (53%)
  starting transfers between devices  41.3 us (24%)
  matrix products  14.6 us (8%)
  other arithmetic  11.9 us (7%)
  local copies, waits for them, and re-layouts  10.8 us (6%)
  between operations  1.88 us (1%)
    ppermute x14, waiting for transfers between devices, cycled(): lax.ppermute(shard, axis, [(i, (i + by) % peers) for i in range(peers)])  52.6 us
    ppermute x6, waiting for transfers between devices, shifted(): lax.ppermute(shard, axis, [(i, i + by) for i in range(peers) if 0 <= i +...  33.9 us
    ppermute x6, starting transfers between devices, shifted(): lax.ppermute(shard, axis, [(i, i + by) for i in range(peers) if 0 <= i +...  21.3 us
    ppermute x14, starting transfers between devices, cycled(): lax.ppermute(shard, axis, [(i, (i + by) % peers) for i in range(peers)])  13.6 us
    ppermute x5, starting transfers between devices, from_next_section(): return lax.ppermute(shard, ('section', 'mp'), pairs)  6.43 us
    unnamed x41, local copies, waits for them, and re-layouts  6.08 us
    dot_general x8, matrix products, on_device(): lax.dot_general(part, block, (((1,), (1,)), ((), ())), preferred_element_...  6.07 us
    ppermute x5, waiting for transfers between devices, from_next_section(): return lax.ppermute(shard, ('section', 'mp'), pairs)  4.99 us
  transfers between devices with their start and end apart: 25, of which 13 were waited for; matrix products, arithmetic and copies ran while one was open for 12% of the time, Pallas kernels for 0%

profile of v1, /device:TPU:0, one launch (start us, length us, event | category | flops | bytes accessed | tf_op | source)
XLA Modules:
  0.0 171.9 jit_solution(7991651635532877557)
XLA Ops:
  0.7 1.4 copy-done
  2.1 1.3 collective-permute-start.5
  3.4 6.5 %collective-permute-start.4 = (bf16[640,640]{1,0:T(8,128)(2,1)S(1)}, bf16[640,640]{1,0:T(8,128)(2,1)}, u32[]{:S(2)}, u32[]{:S(2)}) collective-permute-start(bf16[640,640]{1,0:T(8,128)(2,1)S(1)} %dynamic-slice_bitcast_fusion), channel_id=1, source_target_pairs={{0,4},{4,8},{8,12},{1,5},{5,9},{9,13},{2,6},{6,10},{10,14},{3,7},{... | collective-permute-start | bytes 2457608 | tf_op jit(solution)/shard_map/ppermute | solution.py:28
  10.6 14.8 %collective-permute-done.5 = bf16[640,640]{1,0:T(8,128)(2,1)} collective-permute-done((bf16[640,640]{1,0:T(8,128)(2,1)S(1)}, bf16[640,640]{1,0:T(8,128)(2,1)}, u32[]{:S(2)}, u32[]{:S(2)}) %collective-permute-start.5) | collective-permute-done | bytes 819232 | tf_op jit(solution)/shard_map/ppermute | solution.py:28
  25.4 1.3 collective-permute-start.7
  26.7 5.5 %collective-permute-start.8 = (bf16[640,640]{1,0:T(8,128)(2,1)}, bf16[640,640]{1,0:T(8,128)(2,1)}, u32[]{:S(2)}, u32[]{:S(2)}) collective-permute-start(bf16[640,640]{1,0:T(8,128)(2,1)} %collective-permute-done.4), channel_id=1, source_target_pairs={{0,4},{4,8},{8,12},{1,5},{5,9},{9,13},{2,6},{6,10},{10,14},{3,7},{... | collective-permute-start | bytes 2457608 | tf_op jit(solution)/shard_map/ppermute | solution.py:28
  32.2 2.3 %fusion.32 = (bf16[128,1280]{1,0:T(8,128)(2,1)}, bf16[128,1280]{1,0:T(8,128)(2,1)}) fusion(bf16[1,1,128,1280]{3,2,1,0:T(8,128)(2,1)S(1)} %copy-done.1, f32[128]{0:T(128)S(1)} %fusion.89, bf16[1,1,128,1280]{3,2,1,0:T(8,128)(2,1)} %param.8), kind=kLoop, calls=%fused_computation.90 | loop fusion | flops 3604480 | bytes 1311232 | tf_op jit(solution)/shard_map/convert_element_type | solution.py:147
  34.8 0.6 dynamic-slice_convert_fusion
  35.9 1.3 collective-permute-start
  37.3 1.2 copy.23
  38.5 0.9 reshape_squeeze.6
  39.4 7.7 %collective-permute-done.7 = bf16[640,640]{1,0:T(8,128)(2,1)} collective-permute-done((bf16[640,640]{1,0:T(8,128)(2,1)}, bf16[640,640]{1,0:T(8,128)(2,1)}, u32[]{:S(2)}, u32[]{:S(2)}) %collective-permute-start.7) | collective-permute-done | bytes 819232 | tf_op jit(solution)/shard_map/ppermute | solution.py:28
  47.0 1.3 collective-permute-start.10
  48.3 5.5 %collective-permute-start.11 = (bf16[640,640]{1,0:T(8,128)(2,1)}, bf16[640,640]{1,0:T(8,128)(2,1)}, u32[]{:S(2)}, u32[]{:S(2)}) collective-permute-start(bf16[640,640]{1,0:T(8,128)(2,1)} %collective-permute-done.8), channel_id=1, source_target_pairs={{0,4},{4,8},{8,12},{1,5},{5,9},{9,13},{2,6},{6,10},{10,14},{3,7},{... | collective-permute-start | bytes 2457608 | tf_op jit(solution)/shard_map/ppermute | solution.py:28
  53.9 1.2 fusion.91
  55.1 1.1 divide_convert_fusion
  56.3 11.4 %collective-permute-done.10 = bf16[640,640]{1,0:T(8,128)(2,1)S(1)} collective-permute-done((bf16[640,640]{1,0:T(8,128)(2,1)}, bf16[640,640]{1,0:T(8,128)(2,1)S(1)}, u32[]{:S(2)}, u32[]{:S(2)}) %collective-permute-start.10) | collective-permute-done | bytes 819232 | tf_op jit(solution)/shard_map/ppermute | solution.py:28
  67.6 1.3 collective-permute-start.15
  69.0 3.4 %select_select_fusion.1 = (bf16[640,640]{1,0:T(8,128)(2,1)}, bf16[640,640]{1,0:T(8,128)(2,1)S(1)}, bf16[640,640]{1,0:T(8,128)(2,1)}) fusion(bf16[640,640]{1,0:T(8,128)(2,1)} %collective-permute-done.7, bf16[640,640]{1,0:T(8,128)(2,1)} %collective-permute-done.8, pred[]{:T(512)S(6)} %eq.38, pred[]{:T(512)S(6)} %lt.65, ...), kind=kLoop, calls=%fused_computation.52 | loop fusion | flops 2867200 | bytes 7372804 | tf_op jit(solution)/shard_map/jit(_where)/select_n | solution.py:59
  72.4 1.0 collective-permute-start.6
  74.2 1.1 fusion.94
  75.3 2.2 %copy.31 = f32[128,1280]{1,0:T(8,128)} copy(f32[128,1280]{0,1:T(8,128)} %bitcast.126) | data formatting | bytes 1310720 | tf_op jit(solution)/shard_map/reshape | solution.py:135
  77.4 1.0 collective-permute-start.9
  78.4 1.0 collective-permute-start.12
  79.5 1.1 broadcast_select_fusion.9
  80.6 13.3 %collective-permute-done.6 = bf16[640,640]{1,0:T(8,128)(2,1)} collective-permute-done((bf16[640,640]{1,0:T(8,128)(2,1)}, bf16[640,640]{1,0:T(8,128)(2,1)}, u32[]{:S(2)}, u32[]{:S(2)}) %collective-permute-start.6) | collective-permute-done | bytes 819232 | tf_op jit(solution)/shard_map/ppermute | solution.py:23
  93.9 1.3 collective-permute-start.1
  95.2 1.5 broadcast_select_fusion.6
  97.9 13.4 %collective-permute-done.9 = bf16[640,640]{1,0:T(8,128)(2,1)S(1)} collective-permute-done((bf16[640,640]{1,0:T(8,128)(2,1)}, bf16[640,640]{1,0:T(8,128)(2,1)S(1)}, u32[]{:S(2)}, u32[]{:S(2)}) %collective-permute-start.9) | collective-permute-done | bytes 819232 | tf_op jit(solution)/shard_map/ppermute | solution.py:23
  111.5 13.8 %collective-permute-done.12 = bf16[640,640]{1,0:T(8,128)(2,1)S(1)} collective-permute-done((bf16[640,640]{1,0:T(8,128)(2,1)S(1)}, bf16[640,640]{1,0:T(8,128)(2,1)S(1)}, u32[]{:S(2)}, u32[]{:S(2)}) %collective-permute-start.12) | collective-permute-done | bytes 819232 | tf_op jit(solution)/shard_map/ppermute | solution.py:23
  129.0 1.3 collective-permute-start.13
  130.3 1.3 collective-permute-start.14
  131.6 5.0 %collective-permute-done.13 = bf16[128,256]{1,0:T(8,128)(2,1)S(1)} collective-permute-done((bf16[128,256]{1,0:T(8,128)(2,1)S(1)}, bf16[128,256]{1,0:T(8,128)(2,1)S(1)}, u32[]{:S(2)}, u32[]{:S(2)}) %collective-permute-start.13) | collective-permute-done | bytes 65568 | tf_op jit(solution)/shard_map/ppermute | solution.py:41
  136.7 3.2 %fusion.31 = (f32[128]{0:T(128)S(1)}, f32[128]{0:T(128)S(1)}, bf16[128,1280]{1,0:T(8,128)(2,1)}) fusion(bf16[1,1,128,1280]{3,2,1,0:T(8,128)(2,1)S(1)} %copy-done.1, f32[128]{0:T(128)S(1)} %fusion.89, bf16[1,1,128,1280]{3,2,1,0:T(8,128)(2,1)} %param.8, bf16[1280,512]{1,0:T(8,128)(2,1)} %collective-permute-done.15, ...), kind=kOutput, calls=%fused_computation.89 | convolution fusion | flops 172785408 | bytes 3081729 | tf_op jit(solution)/shard_map/dot_general | solution.py:175
  140.4 1.6 collective-permute-done.16
  142.0 1.1 broadcast_select_fusion.7
  143.2 1.9 %fusion.16 = f32[128,1280]{1,0:T(8,128)S(1)} fusion(bf16[640,640]{1,0:T(8,128)(2,1)} %copy-done.10, bf16[640,640]{1,0:T(8,128)(2,1)S(1)} %copy-done.9, s32[]{:T(128)S(6)} %select_n.249, bf16[128,1280]{1,0:T(8,128)(2,1)S(1)} %get-tuple-element.19, bf16[128,1280]{1,0:T(8,128)(2,1)S(1)} %get-tuple-element.18), kind=kOutput, calls=%fused_computation.30 | convolution fusion | flops 213319680 | bytes 2949124 | tf_op jit(solution)/shard_map/dot_general | solution.py:156
  148.8 1.6 collective-permute-start.21
  150.4 2.4 %collective-permute-start.22 = (bf16[128,256]{1,0:T(8,128)(2,1)S(1)}, bf16[128,256]{1,0:T(8,128)(2,1)S(1)}, u32[]{:S(2)}, u32[]{:S(2)}) collective-permute-start(bf16[128,256]{1,0:T(8,128)(2,1)S(1)} %get-tuple-element.5), channel_id=1, source_target_pairs={{0,8},{4,12},{8,0},{12,4},{1,9},{5,13},{9,1},{13,5},{2,10},{6,14},... | collective-permute-start | bytes 196616 | tf_op jit(solution)/shard_map/ppermute | solution.py:23
  152.8 1.0 collective-permute-start.23
  154.0 1.7 collective-permute-done.21
  155.7 2.3 %collective-permute-done.22 = bf16[128,256]{1,0:T(8,128)(2,1)S(1)} collective-permute-done((bf16[128,256]{1,0:T(8,128)(2,1)S(1)}, bf16[128,256]{1,0:T(8,128)(2,1)S(1)}, u32[]{:S(2)}, u32[]{:S(2)}) %collective-permute-start.22) | collective-permute-done | bytes 65568 | tf_op jit(solution)/shard_map/ppermute | solution.py:23
  158.8 1.6 collective-permute-start.18
  160.4 1.4 collective-permute-start.19
  161.9 0.9 collective-permute-start.20
  163.4 2.9 %collective-permute-done.18 = bf16[128,320]{1,0:T(8,128)(2,1)S(1)} collective-permute-done((bf16[128,320]{1,0:T(8,128)(2,1)S(1)}, bf16[128,320]{1,0:T(8,128)(2,1)S(1)}, u32[]{:S(2)}, u32[]{:S(2)}) %collective-permute-start.18) | collective-permute-done | bytes 81952 | tf_op jit(solution)/shard_map/ppermute | solution.py:23
  166.4 3.3 %collective-permute-done.19 = bf16[128,320]{1,0:T(8,128)(2,1)S(1)} collective-permute-done((bf16[128,320]{1,0:T(8,128)(2,1)S(1)}, bf16[128,320]{1,0:T(8,128)(2,1)S(1)}, u32[]{:S(2)}, u32[]{:S(2)}) %collective-permute-start.19) | collective-permute-done | bytes 81952 | tf_op jit(solution)/shard_map/ppermute | solution.py:23
  169.7 2.2 %fusion.10 = f32[1,320,512]{2,1,0:T(8,128)} fusion(bf16[512,256]{1,0:T(8,128)(2,1)S(1)} %get-tuple-element.23, bf16[512,256]{1,0:T(8,128)(2,1)S(1)} %get-tuple-element.22, bf16[128,320]{1,0:T(8,128)(2,1)S(1)} %collective-permute-done.20, bf16[128,320]{1,0:T(8,128)(2,1)S(1)} %collective-permute-done.19, bf16[128,320]{1,0:T(8,128)(2,1)S(1)} %collective-permute-done.18, ...), kind=kOutput, calls=%fused_computation.23 | convolution fusion | flops 170459136 | bytes 1835012 | tf_op jit(solution)/shard_map/dot_general | solution.py:197
  (87 shorter events, 12.7 us)
Async XLA Ops:
  0.6 1.4 copy-start
  0.6 31.5 %copy-start.1 = (bf16[1,1,128,1280]{3,2,1,0:T(8,128)(2,1)S(1)}, bf16[1,1,128,1280]{3,2,1,0:T(8,128)(2,1)}, u32[]{:S(2)}) copy-start(bf16[1,1,128,1280]{3,2,1,0:T(8,128)(2,1)} %param.7) | copy-start | bytes 983044
  0.7 33.8 %copy-start.3 = (bf16[1,1280,512]{2,1,0:T(8,128)(2,1)S(1)}, bf16[1,1280,512]{2,1,0:T(8,128)(2,1)}, u32[]{:S(2)}) copy-start(bf16[1,1280,512]{2,1,0:T(8,128)(2,1)} %param.11) | copy-start | bytes 3932164
  2.1 23.3 %collective-permute-start.5 = (bf16[640,640]{1,0:T(8,128)(2,1)S(1)}, bf16[640,640]{1,0:T(8,128)(2,1)}, u32[]{:S(2)}, u32[]{:S(2)}) collective-permute-start(bf16[640,640]{1,0:T(8,128)(2,1)S(1)} %dynamic-slice_bitcast_fusion), channel_id=1, source_target_pairs={{4,0},{8,4},{12,8},{5,1},{9,5},{13,9},{6,2},{10,6},{14,10},{7,3},{... | collective-permute-start | bytes 2457608 | tf_op jit(solution)/shard_map/ppermute | solution.py:28
  3.4 23.3 %collective-permute-start.4 = (bf16[640,640]{1,0:T(8,128)(2,1)S(1)}, bf16[640,640]{1,0:T(8,128)(2,1)}, u32[]{:S(2)}, u32[]{:S(2)}) collective-permute-start(bf16[640,640]{1,0:T(8,128)(2,1)S(1)} %dynamic-slice_bitcast_fusion), channel_id=1, source_target_pairs={{0,4},{4,8},{8,12},{1,5},{5,9},{9,13},{2,6},{6,10},{10,14},{3,7},{... | collective-permute-start | bytes 2457608 | tf_op jit(solution)/shard_map/ppermute | solution.py:28
  25.4 21.6 %collective-permute-start.7 = (bf16[640,640]{1,0:T(8,128)(2,1)}, bf16[640,640]{1,0:T(8,128)(2,1)}, u32[]{:S(2)}, u32[]{:S(2)}) collective-permute-start(bf16[640,640]{1,0:T(8,128)(2,1)} %collective-permute-done.5), channel_id=1, source_target_pairs={{4,0},{8,4},{12,8},{5,1},{9,5},{13,9},{6,2},{10,6},{14,10},{7,3},{... | collective-permute-start | bytes 2457608 | tf_op jit(solution)/shard_map/ppermute | solution.py:28
  26.7 21.6 %collective-permute-start.8 = (bf16[640,640]{1,0:T(8,128)(2,1)}, bf16[640,640]{1,0:T(8,128)(2,1)}, u32[]{:S(2)}, u32[]{:S(2)}) collective-permute-start(bf16[640,640]{1,0:T(8,128)(2,1)} %collective-permute-done.4), channel_id=1, source_target_pairs={{0,4},{4,8},{8,12},{1,5},{5,9},{9,13},{2,6},{6,10},{10,14},{3,7},{... | collective-permute-start | bytes 2457608 | tf_op jit(solution)/shard_map/ppermute | solution.py:28
  34.5 44.0 %collective-permute-start.3 = (bf16[128,1280]{1,0:T(8,128)(2,1)}, bf16[128,1280]{1,0:T(8,128)(2,1)}, u32[]{:S(2)}, u32[]{:S(2)}) collective-permute-start(bf16[128,1280]{1,0:T(8,128)(2,1)} %get-tuple-element.17), channel_id=1, source_target_pairs={{0,1},{1,0},{2,3},{3,2},{4,5},{5,4},{6,7},{7,6},{8,9},{9,8},{10,11... | collective-permute-start | bytes 983048 | tf_op jit(solution)/shard_map/ppermute | solution.py:23
  35.4 38.0 %collective-permute-start.2 = (bf16[128,256]{1,0:T(8,128)(2,1)}, bf16[128,256]{1,0:T(8,128)(2,1)S(1)}, u32[]{:S(2)}, u32[]{:S(2)}) collective-permute-start(bf16[128,256]{1,0:T(8,128)(2,1)} %dynamic-slice_convert_fusion), channel_id=1, source_target_pairs={{0,1},{1,0},{2,3},{3,2},{4,5},{5,4},{6,7},{7,6},{8,9},{9,8},{10,11... | collective-permute-start | bytes 196616 | tf_op jit(solution)/shard_map/ppermute | solution.py:23
  35.9 100.7 %collective-permute-start = (bf16[128,1280]{1,0:T(8,128)(2,1)}, bf16[128,1280]{1,0:T(8,128)(2,1)}, u32[]{:S(2)}, u32[]{:S(2)}) collective-permute-start(bf16[128,1280]{1,0:T(8,128)(2,1)} %get-tuple-element.16), channel_id=1, source_target_pairs={{2,0},{3,1},{6,4},{7,5},{10,8},{11,9},{14,12},{15,13},{18,16},{19,... | collective-permute-start | bytes 983048 | tf_op jit(solution)/shard_map/ppermute | solution.py:41
  47.0 20.6 %collective-permute-start.10 = (bf16[640,640]{1,0:T(8,128)(2,1)}, bf16[640,640]{1,0:T(8,128)(2,1)S(1)}, u32[]{:S(2)}, u32[]{:S(2)}) collective-permute-start(bf16[640,640]{1,0:T(8,128)(2,1)} %collective-permute-done.7), channel_id=1, source_target_pairs={{4,0},{8,4},{12,8},{5,1},{9,5},{13,9},{6,2},{10,6},{14,10},{7,3},{... | collective-permute-start | bytes 2457608 | tf_op jit(solution)/shard_map/ppermute | solution.py:28
  48.3 20.6 %collective-permute-start.11 = (bf16[640,640]{1,0:T(8,128)(2,1)}, bf16[640,640]{1,0:T(8,128)(2,1)}, u32[]{:S(2)}, u32[]{:S(2)}) collective-permute-start(bf16[640,640]{1,0:T(8,128)(2,1)} %collective-permute-done.8), channel_id=1, source_target_pairs={{0,4},{4,8},{8,12},{1,5},{5,9},{9,13},{2,6},{6,10},{10,14},{3,7},{... | collective-permute-start | bytes 2457608 | tf_op jit(solution)/shard_map/ppermute | solution.py:28
  67.6 1.3 copy-start.15
  67.6 69.0 %collective-permute-start.15 = (bf16[1280,512]{1,0:T(8,128)(2,1)}, bf16[1280,512]{1,0:T(8,128)(2,1)}, u32[]{:S(2)}, u32[]{:S(2)}) collective-permute-start(bf16[1280,512]{1,0:T(8,128)(2,1)} %bitcast.129), channel_id=1, source_target_pairs={{2,0},{3,1},{6,4},{7,5},{10,8},{11,9},{14,12},{15,13},{18,16},{19,... | collective-permute-start | bytes 3932168 | tf_op jit(solution)/shard_map/ppermute | solution.py:41
  72.4 21.5 %collective-permute-start.6 = (bf16[640,640]{1,0:T(8,128)(2,1)}, bf16[640,640]{1,0:T(8,128)(2,1)}, u32[]{:S(2)}, u32[]{:S(2)}) collective-permute-start(bf16[640,640]{1,0:T(8,128)(2,1)} %get-tuple-element.10), channel_id=1, source_target_pairs={{0,16},{16,0},{1,17},{17,1},{2,18},{18,2},{3,19},{19,3},{4,20},{20... | collective-permute-start | bytes 2457608 | tf_op jit(solution)/shard_map/ppermute | solution.py:23
  73.4 0.6 copy-start.18
  77.4 33.9 %collective-permute-start.9 = (bf16[640,640]{1,0:T(8,128)(2,1)}, bf16[640,640]{1,0:T(8,128)(2,1)S(1)}, u32[]{:S(2)}, u32[]{:S(2)}) collective-permute-start(bf16[640,640]{1,0:T(8,128)(2,1)} %get-tuple-element.8), channel_id=1, source_target_pairs={{0,16},{16,0},{1,17},{17,1},{2,18},{18,2},{3,19},{19,3},{4,20},{20... | collective-permute-start | bytes 2457608 | tf_op jit(solution)/shard_map/ppermute | solution.py:23
  78.4 46.9 %collective-permute-start.12 = (bf16[640,640]{1,0:T(8,128)(2,1)S(1)}, bf16[640,640]{1,0:T(8,128)(2,1)S(1)}, u32[]{:S(2)}, u32[]{:S(2)}) collective-permute-start(bf16[640,640]{1,0:T(8,128)(2,1)S(1)} %get-tuple-element.9), channel_id=1, source_target_pairs={{0,16},{16,0},{1,17},{17,1},{2,18},{18,2},{3,19},{19,3},{4,20},{20... | collective-permute-start | bytes 2457608 | tf_op jit(solution)/shard_map/ppermute | solution.py:23
  93.9 42.8 %collective-permute-start.1 = (bf16[128,1280]{1,0:T(8,128)(2,1)S(1)}, bf16[128,1280]{1,0:T(8,128)(2,1)}, u32[]{:S(2)}, u32[]{:S(2)}) collective-permute-start(bf16[128,1280]{1,0:T(8,128)(2,1)S(1)} %bitcast.125), channel_id=1, source_target_pairs={{2,0},{3,1},{6,4},{7,5},{10,8},{11,9},{14,12},{15,13},{18,16},{19,... | collective-permute-start | bytes 983048 | tf_op jit(solution)/shard_map/ppermute | solution.py:41
  96.7 0.9 copy-start.8
  96.7 1.2 copy-start.10
  96.7 14.6 %copy-start.2 = (bf16[640,640]{1,0:T(8,128)(2,1)S(1)}, bf16[640,640]{1,0:T(8,128)(2,1)}, u32[]{:S(2)}) copy-start(bf16[640,640]{1,0:T(8,128)(2,1)} %get-tuple-element.8) | copy-start | bytes 2457604
  111.5 15.8 %copy-start.4 = (bf16[640,640]{1,0:T(8,128)(2,1)}, bf16[640,640]{1,0:T(8,128)(2,1)S(1)}, u32[]{:S(2)}) copy-start(bf16[640,640]{1,0:T(8,128)(2,1)S(1)} %get-tuple-element.6) | copy-start | bytes 2457604
  111.5 15.8 %copy-start.6 = (bf16[640,640]{1,0:T(8,128)(2,1)}, bf16[640,640]{1,0:T(8,128)(2,1)S(1)}, u32[]{:S(2)}) copy-start(bf16[640,640]{1,0:T(8,128)(2,1)S(1)} %get-tuple-element.7) | copy-start | bytes 2457604
  125.5 0.9 copy-start.11
  125.5 1.2 copy-start.13
  126.7 1.1 copy-start.16
  129.0 7.6 %collective-permute-start.13 = (bf16[128,256]{1,0:T(8,128)(2,1)S(1)}, bf16[128,256]{1,0:T(8,128)(2,1)S(1)}, u32[]{:S(2)}, u32[]{:S(2)}) collective-permute-start(bf16[128,256]{1,0:T(8,128)(2,1)S(1)} %multiply_convert_fusion.3), channel_id=1, source_target_pairs={{2,0},{3,1},{6,4},{7,5},{10,8},{11,9},{14,12},{15,13},{18,16},{19,... | collective-permute-start | bytes 196616 | tf_op jit(solution)/shard_map/ppermute | solution.py:41
  130.3 6.3 %collective-permute-start.14 = (bf16[128,256]{1,0:T(8,128)(2,1)S(1)}, bf16[128,256]{1,0:T(8,128)(2,1)S(1)}, u32[]{:S(2)}, u32[]{:S(2)}) collective-permute-start(bf16[128,256]{1,0:T(8,128)(2,1)S(1)} %multiply_convert_fusion.3), channel_id=1, source_target_pairs={{2,1},{3,0},{6,5},{7,4},{10,9},{11,8},{14,13},{15,12},{18,17},{19,... | collective-permute-start | bytes 196616 | tf_op jit(solution)/shard_map/ppermute | solution.py:41
  136.7 6.5 %copy-start.9 = (bf16[640,640]{1,0:T(8,128)(2,1)S(1)}, bf16[640,640]{1,0:T(8,128)(2,1)}, u32[]{:S(2)}) copy-start(bf16[640,640]{1,0:T(8,128)(2,1)} %copy-done.8) | copy-start | bytes 2457604
  139.9 2.1 %collective-permute-start.16 = (bf16[128,1280]{1,0:T(8,128)(2,1)}, bf16[128,1280]{1,0:T(8,128)(2,1)}, u32[]{:S(2)}, u32[]{:S(2)}) collective-permute-start(bf16[128,1280]{1,0:T(8,128)(2,1)} %get-tuple-element.15), channel_id=1, source_target_pairs={{0,1},{1,0},{2,3},{3,2},{4,5},{5,4},{6,7},{7,6},{8,9},{9,8},{10,11... | collective-permute-start | bytes 983048 | tf_op jit(solution)/shard_map/ppermute | solution.py:23
  143.2 1.9 %copy-start.12 = (bf16[640,640]{1,0:T(8,128)(2,1)S(1)}, bf16[640,640]{1,0:T(8,128)(2,1)}, u32[]{:S(2)}) copy-start(bf16[640,640]{1,0:T(8,128)(2,1)} %copy-done.11) | copy-start | bytes 2457604
  143.2 1.9 %copy-start.14 = (bf16[640,640]{1,0:T(8,128)(2,1)S(1)}, bf16[640,640]{1,0:T(8,128)(2,1)}, u32[]{:S(2)}) copy-start(bf16[640,640]{1,0:T(8,128)(2,1)} %copy-done.13) | copy-start | bytes 2457604
  145.7 1.1 copy-start.5
  145.7 1.4 copy-start.7
  145.7 1.6 copy-start.17
  147.9 0.8 copy-start.19
  148.8 6.9 %collective-permute-start.21 = (bf16[128,256]{1,0:T(8,128)(2,1)S(1)}, bf16[128,256]{1,0:T(8,128)(2,1)S(1)}, u32[]{:S(2)}, u32[]{:S(2)}) collective-permute-start(bf16[128,256]{1,0:T(8,128)(2,1)S(1)} %get-tuple-element.5), channel_id=1, source_target_pairs={{0,4},{4,8},{8,12},{12,0},{1,5},{5,9},{9,13},{13,1},{2,6},{6,10},{... | collective-permute-start | bytes 196616 | tf_op jit(solution)/shard_map/ppermute | solution.py:23
  150.4 7.6 %collective-permute-start.22 = (bf16[128,256]{1,0:T(8,128)(2,1)S(1)}, bf16[128,256]{1,0:T(8,128)(2,1)S(1)}, u32[]{:S(2)}, u32[]{:S(2)}) collective-permute-start(bf16[128,256]{1,0:T(8,128)(2,1)S(1)} %get-tuple-element.5), channel_id=1, source_target_pairs={{0,8},{4,12},{8,0},{12,4},{1,9},{5,13},{9,1},{13,5},{2,10},{6,14},... | collective-permute-start | bytes 196616 | tf_op jit(solution)/shard_map/ppermute | solution.py:23
  152.8 5.4 %collective-permute-start.23 = (bf16[128,256]{1,0:T(8,128)(2,1)S(1)}, bf16[128,256]{1,0:T(8,128)(2,1)S(1)}, u32[]{:S(2)}, u32[]{:S(2)}) collective-permute-start(bf16[128,256]{1,0:T(8,128)(2,1)S(1)} %get-tuple-element.5), channel_id=1, source_target_pairs={{0,12},{4,0},{8,4},{12,8},{1,13},{5,1},{9,5},{13,9},{2,14},{6,2},{... | collective-permute-start | bytes 196616 | tf_op jit(solution)/shard_map/ppermute | solution.py:23
  158.2 5.1 %collective-permute-start.24 = (bf16[512,256]{1,0:T(8,128)(2,1)S(1)}, bf16[512,256]{1,0:T(8,128)(2,1)S(1)}, u32[]{:S(2)}, u32[]{:S(2)}) collective-permute-start(bf16[512,256]{1,0:T(8,128)(2,1)S(1)} %pad_maximum_fusion.9), channel_id=1, source_target_pairs={{0,1},{1,0},{2,3},{3,2},{4,5},{5,4},{6,7},{7,6},{8,9},{9,8},{10,11... | collective-permute-start | bytes 786440 | tf_op jit(solution)/shard_map/ppermute | solution.py:23
  158.3 4.5 %collective-permute-start.17 = (f32[128]{0:T(128)S(1)}, f32[128]{0:T(128)S(1)}, u32[]{:S(2)}, u32[]{:S(2)}) collective-permute-start(f32[128]{0:T(128)S(1)} %fusion.70), channel_id=1, source_target_pairs={{0,1},{1,0},{2,3},{3,2},{4,5},{5,4},{6,7},{7,6},{8,9},{9,8},{10,11... | collective-permute-start | bytes 1544 | tf_op jit(solution)/shard_map/ppermute | solution.py:23
  158.8 7.5 %collective-permute-start.18 = (bf16[128,320]{1,0:T(8,128)(2,1)S(1)}, bf16[128,320]{1,0:T(8,128)(2,1)S(1)}, u32[]{:S(2)}, u32[]{:S(2)}) collective-permute-start(bf16[128,320]{1,0:T(8,128)(2,1)S(1)} %get-tuple-element.25), channel_id=1, source_target_pairs={{0,4},{4,8},{8,12},{12,0},{1,5},{5,9},{9,13},{13,1},{2,6},{6,10},{... | collective-permute-start | bytes 245768 | tf_op jit(solution)/shard_map/ppermute | solution.py:23
  160.4 9.3 %collective-permute-start.19 = (bf16[128,320]{1,0:T(8,128)(2,1)S(1)}, bf16[128,320]{1,0:T(8,128)(2,1)S(1)}, u32[]{:S(2)}, u32[]{:S(2)}) collective-permute-start(bf16[128,320]{1,0:T(8,128)(2,1)S(1)} %get-tuple-element.27), channel_id=1, source_target_pairs={{0,8},{4,12},{8,0},{12,4},{1,9},{5,13},{9,1},{13,5},{2,10},{6,14},... | collective-permute-start | bytes 245768 | tf_op jit(solution)/shard_map/ppermute | solution.py:23
  161.9 7.8 %collective-permute-start.20 = (bf16[128,320]{1,0:T(8,128)(2,1)S(1)}, bf16[128,320]{1,0:T(8,128)(2,1)S(1)}, u32[]{:S(2)}, u32[]{:S(2)}) collective-permute-start(bf16[128,320]{1,0:T(8,128)(2,1)S(1)} %get-tuple-element.26), channel_id=1, source_target_pairs={{0,12},{4,0},{8,4},{12,8},{1,13},{5,1},{9,5},{13,9},{2,14},{6,2},{... | collective-permute-start | bytes 245768 | tf_op jit(solution)/shard_map/ppermute | solution.py:23

commit v2 on v1

--- a/solution.py
+++ b/solution.py
@@ -1,3 +1,4 @@
+import itertools
 import math
 
 import jax
@@ -30,36 +31,111 @@
     )
 
 
+def moved(shard, axes, target):
+    sizes = [lax.axis_size(axis) for axis in axes]
+    places = list(itertools.product(*[range(size) for size in sizes]))
+    index = {place: i for i, place in enumerate(places)}
+    pairs = [(index[place], index[target(*place)]) for place in places if target(*place) is not None]
+    return lax.ppermute(shard, axes, pairs)
+
+
 def from_next_section(shard, flip=False):
-    sections = lax.axis_size("section")
     cores = lax.axis_size("mp")
-    pairs = []
-    for s in range(1, sections):
-        for c in range(cores):
-            d = (c + 1) % cores if flip else c
-            pairs.append((s * cores + c, (s - 1) * cores + d))
-    return lax.ppermute(shard, ("section", "mp"), pairs)
-
-
-def gather_blocks(mine, axis):
-    peers = lax.axis_size(axis)
-    pos = lax.axis_index(axis)
+    return moved(
+        shard, ("section", "mp"), lambda s, c: (s - 1, (c + flip) % cores) if s > 0 else None
+    )
+
+
+def chain_hop(shard, by, step):
+    sections, peers = lax.axis_size("section"), lax.axis_size("dp")
+
+    def target(i, s):
+        inside = 0 <= i + by < peers and 0 <= i - by * (step - 1) < peers
+        return (i + by, s) if inside and s < sections - 1 else None
+
+    return moved(shard, ("dp", "section"), target)
+
+
+def swapped_groups(shard):
+    sections, groups = lax.axis_size("section"), lax.axis_size("groups")
+    return moved(
+        shard,
+        ("groups", "section"),
+        lambda g, s: ((g + 1) % groups, s) if s < sections - 1 else None,
+    )
+
+
+def gather_blocks(mine, chunks):
+    peers = lax.axis_size("dp")
+    pos = lax.axis_index("dp")
     low = pos < peers // 2
     longer = jnp.where(low, peers - 1 - pos, pos)
-    up, down = [mine], [mine]
-    for _ in range(1, peers):
-        up.append(shifted(up[-1], axis, 1))
-        down.append(shifted(down[-1], axis, -1))
+    pieces = jnp.split(mine, chunks, axis=0)
+    up = [[piece] for piece in pieces]
+    down = [[piece] for piece in pieces]
+    swaps = [[] for _ in pieces]
     slots = []
     for j in range(1, peers):
-        block = jnp.where(low, down[j], up[j])
+        own_rows, other_rows = [], []
+        for q in range(chunks):
+            send_up, send_down = up[q][-1], down[q][-1]
+            if len(swaps[q]) > 1:
+                send_up, send_down, swaps[q][-2] = lax.optimization_barrier(
+                    (send_up, send_down, swaps[q][-2])
+                )
+            up[q].append(chain_hop(send_up, 1, j))
+            down[q].append(chain_hop(send_down, -1, j))
+            block = jnp.where(low, down[q][j], up[q][j])
+            for k in range(1, min(j, (peers - 1) // 2) + 1):
+                block = jnp.where(j - longer == k, jnp.where(low, up[q][k], down[q][k]), block)
+            own_rows.append(block)
+            swaps[q].append(swapped_groups(block))
         owner = jnp.where(low, pos + j, pos - j)
         for k in range(1, min(j, (peers - 1) // 2) + 1):
-            here = j - longer == k
-            block = jnp.where(here, jnp.where(low, up[k], down[k]), block)
-            owner = jnp.where(here, jnp.where(low, pos - k, pos + k), owner)
-        slots.append((block, owner))
+            owner = jnp.where(j - longer == k, jnp.where(low, pos - k, pos + k), owner)
+        slots.append([own_rows, None, owner])
+    for j in range(peers - 1):
+        slots[j][1] = [swaps[q][j] for q in range(chunks)]
     return slots
+
+
+def spread_product(sens_branch, out_block):
+    axes = ("dp", "section", "mp")
+    peers, cores = lax.axis_size("dp"), lax.axis_size("mp")
+    last = lax.axis_size("section") - 1
+    pos, core = lax.axis_index("dp"), lax.axis_index("mp")
+    seq_len = sens_branch.shape[0]
+    width = out_block.shape[1]
+    per_core = peers // cores
+    arrived = []
+    for k in range(peers):
+        to = lax.rem(pos + k, peers)
+        part = lax.dynamic_slice_in_dim(sens_branch, lax.rem(to, per_core) * width, width, 1)
+        if k:
+            part = moved(
+                part,
+                axes,
+                lambda i, s, c: ((i + k) % peers, s, c)
+                if s == last and c == (i + k) % peers // per_core
+                else None,
+            )
+        arrived.append(part)
+    mine = jnp.concatenate(arrived, 0)
+    theirs = moved(
+        mine,
+        axes,
+        lambda i, s, c: (i, s, 1 - c) if s == last and c == i // per_core else None,
+    )
+    operand = jnp.where(core == pos // per_core, mine, theirs)
+    product = lax.dot_general(
+        operand, out_block, (((1,), (1,)), ((), ())), preferred_element_type=F32
+    )
+    total = product[:seq_len]
+    for k in range(1, peers):
+        back = product[k * seq_len : (k + 1) * seq_len].astype(BF16)
+        back = moved(back, axes, lambda i, s, c: ((i - k) % peers, s, c) if s == last else None)
+        total = total + back.astype(F32)
+    return total
 
 
 def on_device(hidden_in, attn_out, queries, keys, value_weight, out_weight, lengths):
@@ -83,20 +159,9 @@
     head_rows, block_width = out_block.shape
 
     share = head_rows // groups
-    carried = lax.dynamic_slice_in_dim(out_block, group_pos * share, share, 0)
-    slots = [(out_block, dp_pos)]
-    for block, owner in gather_blocks(carried, "dp"):
-        rows = [block] + [cycled(block, "groups", k) for k in range(1, groups)]
-        whole = jnp.zeros((head_rows, block_width), BF16)
-        if groups == 2:
-            first = jnp.where(group_pos == 0, rows[0], rows[1])
-            second = jnp.where(group_pos == 0, rows[1], rows[0])
-            whole = jnp.concatenate([first, second], 0)
-        else:
-            for k in range(groups):
-                at = lax.rem(group_pos - k + groups, groups) * share
-                whole = lax.dynamic_update_slice_in_dim(whole, rows[k], at, 0)
-        slots.append((whole, owner))
+    own_rows = lax.dynamic_slice_in_dim(out_block, group_pos * share, share, 0)
+    other_rows = lax.dynamic_slice_in_dim(out_block, (1 - group_pos) * share, share, 0)
+    slots = [[[own_rows], [other_rows], dp_pos]] + gather_blocks(own_rows, 2)
 
     behind_inputs = from_next_section(inputs).astype(F32)
     behind_values = from_next_section(value_rows)
@@ -146,16 +211,26 @@
         if not last_turn:
             behind_kept = from_next_section(kept.astype(BF16))
         sens_branch = (current * branch_gain).astype(BF16)
-        sens_other = cycled(sens_branch, "mp", 1)
-        first = jnp.where(core_pos == 0, sens_branch, sens_other)
-        second = jnp.where(core_pos == 0, sens_other, sens_branch)
-        sens_full = jnp.concatenate([first, second], 1)
-        back_mixed = jnp.zeros((seq_len, head_rows), F32)
-        for block, owner in slots:
-            part = lax.dynamic_slice_in_dim(sens_full, owner * block_width, block_width, 1)
-            back_mixed += lax.dot_general(
-                part, block, (((1,), (1,)), ((), ())), preferred_element_type=F32
-            )
+        if turn == 0:
+            back_mixed = spread_product(sens_branch, out_block)
+        else:
+            sens_other = cycled(sens_branch, "mp", 1)
+            first = jnp.where(core_pos == 0, sens_branch, sens_other)
+            second = jnp.where(core_pos == 0, sens_other, sens_branch)
+            sens_full = jnp.concatenate([first, second], 1)
+            halves = [jnp.zeros((seq_len, share), F32) for _ in range(2)]
+            for *blocks, owner in slots:
+                part = lax.dynamic_slice_in_dim(sens_full, owner * block_width, block_width, 1)
+                for side in range(2):
+                    halves[side] += lax.dot_general(
+                        part,
+                        jnp.concatenate(blocks[side], 0),
+                        (((1,), (1,)), ((), ())),
+                        preferred_element_type=F32,
+                    )
+            first = jnp.where(group_pos == 0, halves[0], halves[1])
+            second = jnp.where(group_pos == 0, halves[1], halves[0])
+            back_mixed = jnp.concatenate([first, second], 1)
         sens_mixed = (mixed_gain * back_mixed).astype(BF16)
         back_values = jnp.einsum(
             "gjts,tgjd->sgd",

time: 173 us -> 169 us (0.977)
  waiting for transfers between devices: 91.4 us -> 68.4 us
  starting transfers between devices: 41.3 us -> 63.8 us
  local copies, waits for them, and re-layouts: 10.8 us -> 7.38 us
  other arithmetic: 11.9 us -> 9.51 us
  matrix products: 14.6 us -> 16.8 us
    ppermute x14 -> x10, waiting for transfers between devices: 52.6 us -> 12.8 us  [cycled(): lax.ppermute(shard, axis, [(i, (i + by) % peers) for i in range(peers)])]
    ppermute x11 -> x30, starting transfers between devices: 27.7 us -> 52.9 us  [moved(): return lax.ppermute(shard, axes, pairs)]
    ppermute x11 -> x30, waiting for transfers between devices: 38.9 us -> 55.6 us  [moved(): return lax.ppermute(shard, axes, pairs)]
    unnamed x41 -> x39, local copies, waits for them, and re-layouts: 6.08 us -> 1.66 us
    ppermute x14 -> x10, starting transfers between devices: 13.6 us -> 10.9 us  [cycled(): lax.ppermute(shard, axis, [(i, (i + by) % peers) for i in range(peers)])]
    dot_general x8 -> x9, matrix products: 6.07 us -> 8.54 us  [the longest x8 6.21 us: on_device(): lax.dot_general(part, jnp.concatenate(blocks[side], 0), (((1,), (1,)), ((...]
    split x0 -> x1, local copies, waits for them, and re-layouts: none -> 2.17 us  [gather_blocks(): pieces = jnp.split(mine, chunks, axis=0)]
    select_n x2 -> x1, other arithmetic: 2.24 us -> 0.08 us  [on_device(): second = jnp.where(core_pos == 0, sens_other, sens_branch)]
  transfers between devices with their start and end apart: 25 -> 40, of which waited for: 13 -> 12; matrix products, arithmetic and copies ran while one was open for 12% -> 16% of each run, Pallas kernels for 0% -> 0%
where the time goes in v2:
time: 169 us; the launch traced here: 168 us
  waiting for transfers between devices  68.4 us (40%)
  starting transfers between devices  63.8 us (38%)
  matrix products  16.8 us (10%)
  other arithmetic  9.51 us (6%)
  local copies, waits for them, and re-layouts  7.38 us (4%)
  between operations  2.3 us (1%)
    ppermute x30, waiting for transfers between devices, moved(): return lax.ppermute(shard, axes, pairs)  55.6 us
    ppermute x30, starting transfers between devices, moved(): return lax.ppermute(shard, axes, pairs)  52.9 us
    ppermute x10, waiting for transfers between devices, cycled(): lax.ppermute(shard, axis, [(i, (i + by) % peers) for i in range(peers)])  12.8 us
    ppermute x10, starting transfers between devices, cycled(): lax.ppermute(shard, axis, [(i, (i + by) % peers) for i in range(peers)])  10.9 us
    dot_general x8, matrix products, on_device(): lax.dot_general(part, jnp.concatenate(blocks[side], 0), (((1,), (1,)), ((...  6.21 us
    select_n x4, other arithmetic, gather_blocks(): jnp.where(j - longer == k, jnp.where(low, up[q][k], down[q][k]), block)  5.32 us
  transfers between devices with their start and end apart: 40, of which 12 were waited for; matrix products, arithmetic and copies ran while one was open for 16% of the time, Pallas kernels for 0%

profile of v2, /device:TPU:0, one launch (start us, length us, event | category | flops | bytes accessed | tf_op | source)
XLA Modules:
  0.0 168.2 jit_solution(2184327869382431542)
XLA Ops:
  0.7 2.2 %dynamic-slice_bitcast_fusion.1 = (bf16[320,640]{1,0:T(8,128)(2,1)}, bf16[320,640]{1,0:T(8,128)(2,1)}) fusion(bf16[1,1280,640]{2,1,0:T(8,128)(2,1)} %param.12, s32[]{:T(128)S(6)} %select_n.297, s32[]{:T(128)S(6)} %add.174), kind=kLoop, calls=%fused_computation.85 | loop fusion | bytes 1638408 | tf_op jit(solution)/shard_map/split | solution.py:73
  2.8 4.9 %collective-permute-start.16 = (bf16[320,640]{1,0:T(8,128)(2,1)}, bf16[320,640]{1,0:T(8,128)(2,1)S(1)}, u32[]{:S(2)}, u32[]{:S(2)}) collective-permute-start(bf16[320,640]{1,0:T(8,128)(2,1)} %get-tuple-element.19), channel_id=1, source_target_pairs={{0,4},{4,8},{8,12},{1,5},{5,9},{9,13},{16,20},{20,24},{24,28},{17,... | collective-permute-start | bytes 1228808 | tf_op jit(solution)/shard_map/ppermute | solution.py:39
  7.8 1.3 collective-permute-start.17
  13.7 1.7 fusion.88
  16.2 1.3 collective-permute-start.15
  18.4 1.5 collective-permute-start.6
  20.1 6.1 %collective-permute-start.14 = (bf16[320,640]{1,0:T(8,128)(2,1)}, bf16[320,640]{1,0:T(8,128)(2,1)}, u32[]{:S(2)}, u32[]{:S(2)}) collective-permute-start(bf16[320,640]{1,0:T(8,128)(2,1)} %get-tuple-element.18), channel_id=1, source_target_pairs={{0,4},{4,8},{8,12},{1,5},{5,9},{9,13},{16,20},{20,24},{24,28},{17,... | collective-permute-start | bytes 1228808 | tf_op jit(solution)/shard_map/ppermute | solution.py:39
  27.4 1.3 copy.32
  29.5 1.3 collective-permute-start.20
  30.8 2.3 %fusion.110 = (bf16[512,1280]{1,0:T(8,128)(2,1)S(1)}, f32[512,1280]{1,0:T(8,128)S(1)}) fusion(bf16[1,1280,640]{2,1,0:T(8,128)(2,1)S(1)} %copy-done, bf16[512,640]{1,0:T(8,128)(2,1)} %collective-permute-done.6, pred[]{:T(512)S(6)} %eq.19, bf16[128,640]{1,0:T(8,128)(2,1)} %copy-done.7, bf16[128,640]{1,0:T(8,128)(2,1)} %copy-done.8, ...), kind=kOutput, calls=%fused_computation.171 | convolution fusion | flops 842465280 | bytes 6881281 | tf_op jit(solution)/shard_map/dot_general | solution.py:130
  35.7 2.0 %select_select_fusion.5 = bf16[320,640]{1,0:T(8,128)(2,1)} fusion(bf16[320,640]{1,0:T(8,128)(2,1)} %collective-permute-done.15, bf16[320,640]{1,0:T(8,128)(2,1)} %collective-permute-done.14, pred[]{:T(512)S(6)} %lt.81, pred[]{:T(512)S(6)} %eq.41), kind=kLoop, calls=%fused_computation.91 | loop fusion | flops 614400 | bytes 1228802 | tf_op jit(solution)/shard_map/jit(_where)/select_n | solution.py:90
  37.7 1.3 collective-permute-start.12
  39.0 6.7 %collective-permute-done.20 = bf16[320,640]{1,0:T(8,128)(2,1)S(1)} collective-permute-done((bf16[320,640]{1,0:T(8,128)(2,1)}, bf16[320,640]{1,0:T(8,128)(2,1)S(1)}, u32[]{:S(2)}, u32[]{:S(2)}) %collective-permute-start.20) | collective-permute-done | bytes 409632 | tf_op jit(solution)/shard_map/ppermute | solution.py:39
  45.6 3.4 %collective-permute-start.22 = (bf16[320,640]{1,0:T(8,128)(2,1)}, bf16[320,640]{1,0:T(8,128)(2,1)}, u32[]{:S(2)}, u32[]{:S(2)}) collective-permute-start(bf16[320,640]{1,0:T(8,128)(2,1)} %select_select_fusion.5), channel_id=1, source_target_pairs={{0,16},{16,0},{1,17},{17,1},{4,20},{20,4},{5,21},{21,5},{8,24},{24... | collective-permute-start | bytes 1228808 | tf_op jit(solution)/shard_map/ppermute | solution.py:39
  49.1 2.0 %select_select_fusion.2 = (bf16[320,640]{1,0:T(8,128)(2,1)}, bf16[320,640]{1,0:T(8,128)(2,1)}) fusion(bf16[320,640]{1,0:T(8,128)(2,1)S(1)} %collective-permute-done.20, bf16[320,640]{1,0:T(8,128)(2,1)S(1)} %collective-permute-done.21, pred[]{:T(512)S(6)} %eq.42, pred[]{:T(512)S(6)} %lt.81, bf16[320,640]{1,0:T(8,128)(2,1)S(1)} %collective-permute-done.16, ...), kind=kLoop, calls=%fused_computation.88 | loop fusion | flops 1024000 | bytes 2457603 | tf_op jit(solution)/shard_map/jit(_where)/select_n | solution.py:90
  51.1 1.3 collective-permute-start.18
  52.4 1.4 collective-permute-start.19
  53.8 2.4 %collective-permute-start.25 = (bf16[320,640]{1,0:T(8,128)(2,1)}, bf16[320,640]{1,0:T(8,128)(2,1)}, u32[]{:S(2)}, u32[]{:S(2)}) collective-permute-start(bf16[320,640]{1,0:T(8,128)(2,1)} %get-tuple-element.27), channel_id=1, source_target_pairs={{0,16},{16,0},{1,17},{17,1},{4,20},{20,4},{5,21},{21,5},{8,24},{24... | collective-permute-start | bytes 1228808 | tf_op jit(solution)/shard_map/ppermute | solution.py:39
  57.3 1.2 copy.33
  59.0 4.5 %collective-permute-done.18 = bf16[320,640]{1,0:T(8,128)(2,1)} collective-permute-done((bf16[320,640]{1,0:T(8,128)(2,1)}, bf16[320,640]{1,0:T(8,128)(2,1)}, u32[]{:S(2)}, u32[]{:S(2)}) %collective-permute-start.18) | collective-permute-done | bytes 409632 | tf_op jit(solution)/shard_map/ppermute | solution.py:39
  63.4 1.3 collective-permute-start.10
  64.7 1.3 collective-permute-start.1
  66.0 1.3 collective-permute-start
  67.3 13.3 %collective-permute-done.10 = bf16[128,256]{1,0:T(8,128)(2,1)S(1)} collective-permute-done((bf16[128,256]{1,0:T(8,128)(2,1)S(1)}, bf16[128,256]{1,0:T(8,128)(2,1)S(1)}, u32[]{:S(2)}, u32[]{:S(2)}) %collective-permute-start.10) | collective-permute-done | bytes 65568 | tf_op jit(solution)/shard_map/ppermute | solution.py:39
  80.6 1.3 collective-permute-start.11
  82.0 10.5 %collective-permute-done.11 = bf16[128,256]{1,0:T(8,128)(2,1)S(1)} collective-permute-done((bf16[128,256]{1,0:T(8,128)(2,1)S(1)}, bf16[128,256]{1,0:T(8,128)(2,1)S(1)}, u32[]{:S(2)}, u32[]{:S(2)}) %collective-permute-start.11) | collective-permute-done | bytes 65568 | tf_op jit(solution)/shard_map/ppermute | solution.py:39
  92.6 1.3 collective-permute-start.23
  94.6 3.4 %collective-permute-start.29 = (bf16[320,640]{1,0:T(8,128)(2,1)}, bf16[320,640]{1,0:T(8,128)(2,1)S(1)}, u32[]{:S(2)}, u32[]{:S(2)}) collective-permute-start(bf16[320,640]{1,0:T(8,128)(2,1)} %get-tuple-element.26), channel_id=1, source_target_pairs={{0,16},{16,0},{1,17},{17,1},{4,20},{20,4},{5,21},{21,5},{8,24},{24... | collective-permute-start | bytes 1228808 | tf_op jit(solution)/shard_map/ppermute | solution.py:39
  98.0 1.3 collective-permute-start.26
  100.1 2.4 %fusion.57 = (f32[128]{0:T(128)S(1)}, f32[128]{0:T(128)S(1)}, bf16[128,1280]{1,0:T(8,128)(2,1)S(1)}) fusion(bf16[1,1,128,1280]{3,2,1,0:T(8,128)(2,1)S(1)} %copy-done.1, f32[128]{0:T(128)} %copy-done.18, bf16[1,1,128,1280]{3,2,1,0:T(8,128)(2,1)S(1)} %copy-done.14, bf16[1280,512]{1,0:T(8,128)(2,1)} %collective-permute-done.12, ...), kind=kOutput, calls=%fused_computation.107 | convolution fusion | flops 172785408 | bytes 3081729 | tf_op jit(solution)/shard_map/dot_general | solution.py:250
  102.5 4.0 %collective-permute-done.23 = bf16[320,640]{1,0:T(8,128)(2,1)S(1)} collective-permute-done((bf16[320,640]{1,0:T(8,128)(2,1)}, bf16[320,640]{1,0:T(8,128)(2,1)S(1)}, u32[]{:S(2)}, u32[]{:S(2)}) %collective-permute-start.23) | collective-permute-done | bytes 409632 | tf_op jit(solution)/shard_map/ppermute | solution.py:39
  106.4 1.2 collective-permute-start.13
  107.7 1.3 select_select_fusion.3
  108.9 3.4 %collective-permute-start.30 = (bf16[320,640]{1,0:T(8,128)(2,1)S(1)}, bf16[320,640]{1,0:T(8,128)(2,1)S(1)}, u32[]{:S(2)}, u32[]{:S(2)}) collective-permute-start(bf16[320,640]{1,0:T(8,128)(2,1)S(1)} %get-tuple-element.25), channel_id=1, source_target_pairs={{0,16},{16,0},{1,17},{17,1},{4,20},{20,4},{5,21},{21,5},{8,24},{24... | collective-permute-start | bytes 1228808 | tf_op jit(solution)/shard_map/ppermute | solution.py:39
  112.4 2.8 %collective-permute-done.26 = bf16[320,640]{1,0:T(8,128)(2,1)S(1)} collective-permute-done((bf16[320,640]{1,0:T(8,128)(2,1)}, bf16[320,640]{1,0:T(8,128)(2,1)S(1)}, u32[]{:S(2)}, u32[]{:S(2)}) %collective-permute-start.26) | collective-permute-done | bytes 409632 | tf_op jit(solution)/shard_map/ppermute | solution.py:39
  115.2 3.4 %collective-permute-start.28 = (bf16[320,640]{1,0:T(8,128)(2,1)S(1)}, bf16[320,640]{1,0:T(8,128)(2,1)S(1)}, u32[]{:S(2)}, u32[]{:S(2)}) collective-permute-start(bf16[320,640]{1,0:T(8,128)(2,1)S(1)} %get-tuple-element.24), channel_id=1, source_target_pairs={{0,16},{16,0},{1,17},{17,1},{4,20},{20,4},{5,21},{21,5},{8,24},{24... | collective-permute-start | bytes 1228808 | tf_op jit(solution)/shard_map/ppermute | solution.py:39
  118.8 2.4 %collective-permute-start.31 = (bf16[320,640]{1,0:T(8,128)(2,1)S(1)}, bf16[320,640]{1,0:T(8,128)(2,1)S(1)}, u32[]{:S(2)}, u32[]{:S(2)}) collective-permute-start(bf16[320,640]{1,0:T(8,128)(2,1)S(1)} %select_select_fusion), channel_id=1, source_target_pairs={{0,16},{16,0},{1,17},{17,1},{4,20},{20,4},{5,21},{21,5},{8,24},{24... | collective-permute-start | bytes 1228808 | tf_op jit(solution)/shard_map/ppermute | solution.py:39
  121.3 1.5 fusion.9
  122.8 1.5 fusion.19
  125.0 1.4 convolution_add_fusion.3
  126.4 13.3 %collective-permute-done.31 = bf16[320,640]{1,0:T(8,128)(2,1)S(1)} collective-permute-done((bf16[320,640]{1,0:T(8,128)(2,1)S(1)}, bf16[320,640]{1,0:T(8,128)(2,1)S(1)}, u32[]{:S(2)}, u32[]{:S(2)}) %collective-permute-start.31) | collective-permute-done | bytes 409632 | tf_op jit(solution)/shard_map/ppermute | solution.py:39
  142.7 4.4 %collective-permute-start.38 = (bf16[128,256]{1,0:T(8,128)(2,1)S(1)}, bf16[128,256]{1,0:T(8,128)(2,1)S(1)}, u32[]{:S(2)}, u32[]{:S(2)}) collective-permute-start(bf16[128,256]{1,0:T(8,128)(2,1)S(1)} %get-tuple-element.17), channel_id=1, source_target_pairs={{0,12},{4,0},{8,4},{12,8},{1,13},{5,1},{9,5},{13,9},{2,14},{6,2},{... | collective-permute-start | bytes 196616 | tf_op jit(solution)/shard_map/ppermute | solution.py:24
  148.0 1.6 collective-permute-done.38
  149.7 4.1 %collective-permute-done.37 = bf16[128,256]{1,0:T(8,128)(2,1)S(1)} collective-permute-done((bf16[128,256]{1,0:T(8,128)(2,1)S(1)}, bf16[128,256]{1,0:T(8,128)(2,1)S(1)}, u32[]{:S(2)}, u32[]{:S(2)}) %collective-permute-start.37) | collective-permute-done | bytes 65568 | tf_op jit(solution)/shard_map/ppermute | solution.py:24
  154.3 2.0 %collective-permute-start.35 = (bf16[128,320]{1,0:T(8,128)(2,1)S(1)}, bf16[128,320]{1,0:T(8,128)(2,1)S(1)}, u32[]{:S(2)}, u32[]{:S(2)}) collective-permute-start(bf16[128,320]{1,0:T(8,128)(2,1)S(1)} %get-tuple-element.38), channel_id=1, source_target_pairs={{0,12},{4,0},{8,4},{12,8},{1,13},{5,1},{9,5},{13,9},{2,14},{6,2},{... | collective-permute-start | bytes 245768 | tf_op jit(solution)/shard_map/ppermute | solution.py:24
  156.4 1.9 %collective-permute-start.33 = (bf16[128,320]{1,0:T(8,128)(2,1)S(1)}, bf16[128,320]{1,0:T(8,128)(2,1)S(1)}, u32[]{:S(2)}, u32[]{:S(2)}) collective-permute-start(bf16[128,320]{1,0:T(8,128)(2,1)S(1)} %get-tuple-element.37), channel_id=1, source_target_pairs={{0,4},{4,8},{8,12},{12,0},{1,5},{5,9},{9,13},{13,1},{2,6},{6,10},{... | collective-permute-start | bytes 245768 | tf_op jit(solution)/shard_map/ppermute | solution.py:24
  159.6 6.4 %collective-permute-done.34 = bf16[128,320]{1,0:T(8,128)(2,1)S(1)} collective-permute-done((bf16[128,320]{1,0:T(8,128)(2,1)S(1)}, bf16[128,320]{1,0:T(8,128)(2,1)S(1)}, u32[]{:S(2)}, u32[]{:S(2)}) %collective-permute-start.34) | collective-permute-done | bytes 81952 | tf_op jit(solution)/shard_map/ppermute | solution.py:24
  166.0 2.2 %fusion.4 = f32[1,320,512]{2,1,0:T(8,128)} fusion(bf16[512,256]{1,0:T(8,128)(2,1)S(1)} %get-tuple-element.35, bf16[512,256]{1,0:T(8,128)(2,1)S(1)} %get-tuple-element.34, bf16[128,320]{1,0:T(8,128)(2,1)S(1)} %collective-permute-done.35, bf16[128,320]{1,0:T(8,128)(2,1)S(1)} %collective-permute-done.34, bf16[128,320]{1,0:T(8,128)(2,1)S(1)} %collective-permute-done.33, ...), kind=kOutput, calls=%fused_computation.10 | convolution fusion | flops 170459136 | bytes 1835012 | tf_op jit(solution)/shard_map/dot_general | solution.py:272
  (120 shorter events, 19.5 us)
Async XLA Ops:
  0.6 9.7 %copy-start.1 = (bf16[1,1,128,1280]{3,2,1,0:T(8,128)(2,1)S(1)}, bf16[1,1,128,1280]{3,2,1,0:T(8,128)(2,1)}, u32[]{:S(2)}) copy-start(bf16[1,1,128,1280]{3,2,1,0:T(8,128)(2,1)} %param.7) | copy-start | bytes 983044
  0.6 9.7 %copy-start.13 = (bf16[1,1,128,1280]{3,2,1,0:T(8,128)(2,1)S(1)}, bf16[1,1,128,1280]{3,2,1,0:T(8,128)(2,1)}, u32[]{:S(2)}) copy-start(bf16[1,1,128,1280]{3,2,1,0:T(8,128)(2,1)} %param.8) | copy-start | bytes 983044
  2.8 25.9 %collective-permute-start.16 = (bf16[320,640]{1,0:T(8,128)(2,1)}, bf16[320,640]{1,0:T(8,128)(2,1)S(1)}, u32[]{:S(2)}, u32[]{:S(2)}) collective-permute-start(bf16[320,640]{1,0:T(8,128)(2,1)} %get-tuple-element.19), channel_id=1, source_target_pairs={{0,4},{4,8},{8,12},{1,5},{5,9},{9,13},{16,20},{20,24},{24,28},{17,... | collective-permute-start | bytes 1228808 | tf_op jit(solution)/shard_map/ppermute | solution.py:39
  7.8 21.7 %collective-permute-start.17 = (bf16[320,640]{1,0:T(8,128)(2,1)}, bf16[320,640]{1,0:T(8,128)(2,1)}, u32[]{:S(2)}, u32[]{:S(2)}) collective-permute-start(bf16[320,640]{1,0:T(8,128)(2,1)} %get-tuple-element.19), channel_id=1, source_target_pairs={{4,0},{8,4},{12,8},{5,1},{9,5},{13,9},{20,16},{24,20},{28,24},{21,... | collective-permute-start | bytes 1228808 | tf_op jit(solution)/shard_map/ppermute | solution.py:39
  11.5 4.6 %collective-permute-start.5 = (bf16[128,640]{1,0:T(8,128)(2,1)S(1)}, bf16[128,640]{1,0:T(8,128)(2,1)S(1)}, u32[]{:S(2)}, u32[]{:S(2)}) collective-permute-start(bf16[128,640]{1,0:T(8,128)(2,1)S(1)} %get-tuple-element.41), channel_id=1, source_target_pairs={{3,15},{6,2},{10,6},{15,11},{19,31},{22,18},{26,22},{31,27}} | collective-permute-start | bytes 491528 | tf_op jit(solution)/shard_map/ppermute | solution.py:39
  12.3 3.9 %collective-permute-start.4 = (bf16[128,640]{1,0:T(8,128)(2,1)S(1)}, bf16[128,640]{1,0:T(8,128)(2,1)S(1)}, u32[]{:S(2)}, u32[]{:S(2)}) collective-permute-start(bf16[128,640]{1,0:T(8,128)(2,1)S(1)} %get-tuple-element.42), channel_id=1, source_target_pairs={{3,11},{7,15},{10,2},{14,6},{19,27},{23,31},{26,18},{30,22}} | collective-permute-start | bytes 491528 | tf_op jit(solution)/shard_map/ppermute | solution.py:39
  13.0 4.5 %collective-permute-start.3 = (bf16[128,640]{1,0:T(8,128)(2,1)S(1)}, bf16[128,640]{1,0:T(8,128)(2,1)S(1)}, u32[]{:S(2)}, u32[]{:S(2)}) collective-permute-start(bf16[128,640]{1,0:T(8,128)(2,1)S(1)} %get-tuple-element.43), channel_id=1, source_target_pairs={{2,6},{7,11},{11,15},{14,2},{18,22},{23,27},{27,31},{30,18}} | collective-permute-start | bytes 491528 | tf_op jit(solution)/shard_map/ppermute | solution.py:39
  15.4 10.8 %copy-start.3 = (f32[128,512]{1,0:T(8,128)}, f32[128,512]{1,0:T(8,128)S(1)}, u32[]{:S(2)}) copy-start(f32[128,512]{1,0:T(8,128)S(1)} %fusion.88) | copy-start | bytes 786436
  16.1 3.9 %collective-permute-start.2 = (bf16[128,256]{1,0:T(8,128)(2,1)S(1)}, bf16[128,256]{1,0:T(8,128)(2,1)S(1)}, u32[]{:S(2)}, u32[]{:S(2)}) collective-permute-start(bf16[128,256]{1,0:T(8,128)(2,1)S(1)} %dynamic-slice_convert_fusion), channel_id=1, source_target_pairs={{0,1},{1,0},{2,3},{3,2},{4,5},{5,4},{6,7},{7,6},{8,9},{9,8},{10,11... | collective-permute-start | bytes 196616 | tf_op jit(solution)/shard_map/ppermute | solution.py:24
  16.2 17.7 %collective-permute-start.15 = (bf16[320,640]{1,0:T(8,128)(2,1)}, bf16[320,640]{1,0:T(8,128)(2,1)}, u32[]{:S(2)}, u32[]{:S(2)}) collective-permute-start(bf16[320,640]{1,0:T(8,128)(2,1)} %get-tuple-element.18), channel_id=1, source_target_pairs={{4,0},{8,4},{12,8},{5,1},{9,5},{13,9},{20,16},{24,20},{28,24},{21,... | collective-permute-start | bytes 1228808 | tf_op jit(solution)/shard_map/ppermute | solution.py:39
  18.4 12.3 %collective-permute-start.6 = (bf16[512,640]{1,0:T(8,128)(2,1)}, bf16[512,640]{1,0:T(8,128)(2,1)}, u32[]{:S(2)}, u32[]{:S(2)}) collective-permute-start(bf16[512,640]{1,0:T(8,128)(2,1)} %pad_maximum_fusion), channel_id=1, source_target_pairs={{2,3},{6,7},{11,10},{15,14},{18,19},{22,23},{27,26},{31,30}} | collective-permute-start | bytes 1966088 | tf_op jit(solution)/shard_map/ppermute | solution.py:39
  20.0 10.7 %copy-start = (bf16[1,1280,640]{2,1,0:T(8,128)(2,1)S(1)}, bf16[1,1280,640]{2,1,0:T(8,128)(2,1)}, u32[]{:S(2)}) copy-start(bf16[1,1280,640]{2,1,0:T(8,128)(2,1)} %param.12) | copy-start | bytes 4915204
  20.1 7.3 %copy-start.15 = (bf16[128,256]{1,0:T(8,128)(2,1)}, bf16[128,256]{1,0:T(8,128)(2,1)S(1)}, u32[]{:S(2)}) copy-start(bf16[128,256]{1,0:T(8,128)(2,1)S(1)} %collective-permute-done.2) | copy-start | bytes 196612
  20.1 15.0 %collective-permute-start.14 = (bf16[320,640]{1,0:T(8,128)(2,1)}, bf16[320,640]{1,0:T(8,128)(2,1)}, u32[]{:S(2)}, u32[]{:S(2)}) collective-permute-start(bf16[320,640]{1,0:T(8,128)(2,1)} %get-tuple-element.18), channel_id=1, source_target_pairs={{0,4},{4,8},{8,12},{1,5},{5,9},{9,13},{16,20},{20,24},{24,28},{17,... | collective-permute-start | bytes 1228808 | tf_op jit(solution)/shard_map/ppermute | solution.py:39
  28.8 8.9 %collective-permute-start.21 = (bf16[320,640]{1,0:T(8,128)(2,1)S(1)}, bf16[320,640]{1,0:T(8,128)(2,1)S(1)}, u32[]{:S(2)}, u32[]{:S(2)}) collective-permute-start(bf16[320,640]{1,0:T(8,128)(2,1)S(1)} %collective-permute-done.16), channel_id=1, source_target_pairs={{4,8},{8,12},{5,9},{9,13},{20,24},{24,28},{21,25},{25,29}} | collective-permute-start | bytes 1228808 | tf_op jit(solution)/shard_map/ppermute | solution.py:39
  29.5 16.2 %collective-permute-start.20 = (bf16[320,640]{1,0:T(8,128)(2,1)}, bf16[320,640]{1,0:T(8,128)(2,1)S(1)}, u32[]{:S(2)}, u32[]{:S(2)}) collective-permute-start(bf16[320,640]{1,0:T(8,128)(2,1)} %collective-permute-done.17), channel_id=1, source_target_pairs={{4,0},{8,4},{5,1},{9,5},{20,16},{24,20},{21,17},{25,21}} | collective-permute-start | bytes 1228808 | tf_op jit(solution)/shard_map/ppermute | solution.py:39
  33.2 17.9 %collective-permute-start.9 = (bf16[128,1280]{1,0:T(8,128)(2,1)S(1)}, bf16[128,1280]{1,0:T(8,128)(2,1)S(1)}, u32[]{:S(2)}, u32[]{:S(2)}) collective-permute-start(bf16[128,1280]{1,0:T(8,128)(2,1)S(1)} %get-tuple-element.22), channel_id=1, source_target_pairs={{2,6},{3,7},{6,10},{7,11},{10,14},{11,15},{14,2},{15,3},{18,22},{1... | collective-permute-start | bytes 983048 | tf_op jit(solution)/shard_map/ppermute | solution.py:39
  33.9 18.5 %collective-permute-start.8 = (bf16[128,1280]{1,0:T(8,128)(2,1)S(1)}, bf16[128,1280]{1,0:T(8,128)(2,1)S(1)}, u32[]{:S(2)}, u32[]{:S(2)}) collective-permute-start(bf16[128,1280]{1,0:T(8,128)(2,1)S(1)} %get-tuple-element.23), channel_id=1, source_target_pairs={{2,10},{3,11},{6,14},{7,15},{10,2},{11,3},{14,6},{15,7},{18,26},{1... | collective-permute-start | bytes 983048 | tf_op jit(solution)/shard_map/ppermute | solution.py:39
  35.1 18.8 %collective-permute-start.7 = (bf16[128,1280]{1,0:T(8,128)(2,1)S(1)}, bf16[128,1280]{1,0:T(8,128)(2,1)S(1)}, u32[]{:S(2)}, u32[]{:S(2)}) collective-permute-start(bf16[128,1280]{1,0:T(8,128)(2,1)S(1)} %get-tuple-element.21), channel_id=1, source_target_pairs={{2,14},{3,15},{6,2},{7,3},{10,6},{11,7},{14,10},{15,11},{18,30},{1... | collective-permute-start | bytes 983048 | tf_op jit(solution)/shard_map/ppermute | solution.py:39
  37.7 18.5 %copy-start.10 = (bf16[320,640]{1,0:T(8,128)(2,1)}, bf16[320,640]{1,0:T(8,128)(2,1)S(1)}, u32[]{:S(2)}) copy-start(bf16[320,640]{1,0:T(8,128)(2,1)S(1)} %collective-permute-done.21) | copy-start | bytes 1228804
  37.7 61.7 %collective-permute-start.12 = (bf16[1280,512]{1,0:T(8,128)(2,1)}, bf16[1280,512]{1,0:T(8,128)(2,1)}, u32[]{:S(2)}, u32[]{:S(2)}) collective-permute-start(bf16[1280,512]{1,0:T(8,128)(2,1)} %bitcast.3), channel_id=1, source_target_pairs={{2,0},{3,1},{6,4},{7,5},{10,8},{11,9},{14,12},{15,13},{18,16},{19,... | collective-permute-start | bytes 3932168 | tf_op jit(solution)/shard_map/ppermute | solution.py:39
  45.6 10.6 %copy-start.11 = (bf16[320,640]{1,0:T(8,128)(2,1)}, bf16[320,640]{1,0:T(8,128)(2,1)S(1)}, u32[]{:S(2)}) copy-start(bf16[320,640]{1,0:T(8,128)(2,1)S(1)} %collective-permute-done.20) | copy-start | bytes 1228804
  45.6 20.4 %collective-permute-start.22 = (bf16[320,640]{1,0:T(8,128)(2,1)}, bf16[320,640]{1,0:T(8,128)(2,1)}, u32[]{:S(2)}, u32[]{:S(2)}) collective-permute-start(bf16[320,640]{1,0:T(8,128)(2,1)} %select_select_fusion.5), channel_id=1, source_target_pairs={{0,16},{16,0},{1,17},{17,1},{4,20},{20,4},{5,21},{21,5},{8,24},{24... | collective-permute-start | bytes 1228808 | tf_op jit(solution)/shard_map/ppermute | solution.py:39
  51.1 12.3 %collective-permute-start.18 = (bf16[320,640]{1,0:T(8,128)(2,1)}, bf16[320,640]{1,0:T(8,128)(2,1)}, u32[]{:S(2)}, u32[]{:S(2)}) collective-permute-start(bf16[320,640]{1,0:T(8,128)(2,1)} %collective-permute-done.15), channel_id=1, source_target_pairs={{4,0},{8,4},{5,1},{9,5},{20,16},{24,20},{21,17},{25,21}} | collective-permute-start | bytes 1228808 | tf_op jit(solution)/shard_map/ppermute | solution.py:39
  52.4 12.3 %collective-permute-start.19 = (bf16[320,640]{1,0:T(8,128)(2,1)}, bf16[320,640]{1,0:T(8,128)(2,1)}, u32[]{:S(2)}, u32[]{:S(2)}) collective-permute-start(bf16[320,640]{1,0:T(8,128)(2,1)} %collective-permute-done.14), channel_id=1, source_target_pairs={{4,8},{8,12},{5,9},{9,13},{20,24},{24,28},{21,25},{25,29}} | collective-permute-start | bytes 1228808 | tf_op jit(solution)/shard_map/ppermute | solution.py:39
  53.8 40.1 %collective-permute-start.25 = (bf16[320,640]{1,0:T(8,128)(2,1)}, bf16[320,640]{1,0:T(8,128)(2,1)}, u32[]{:S(2)}, u32[]{:S(2)}) collective-permute-start(bf16[320,640]{1,0:T(8,128)(2,1)} %get-tuple-element.27), channel_id=1, source_target_pairs={{0,16},{16,0},{1,17},{17,1},{4,20},{20,4},{5,21},{21,5},{8,24},{24... | collective-permute-start | bytes 1228808 | tf_op jit(solution)/shard_map/ppermute | solution.py:39
  57.3 42.8 %copy-start.14 = (bf16[1,1,128,1280]{3,2,1,0:T(8,128)(2,1)S(1)}, bf16[1,1,128,1280]{3,2,1,0:T(8,128)(2,1)}, u32[]{:S(2)}) copy-start(bf16[1,1,128,1280]{3,2,1,0:T(8,128)(2,1)} %param.8) | copy-start | bytes 983044
  63.4 17.2 %collective-permute-start.10 = (bf16[128,256]{1,0:T(8,128)(2,1)S(1)}, bf16[128,256]{1,0:T(8,128)(2,1)S(1)}, u32[]{:S(2)}, u32[]{:S(2)}) collective-permute-start(bf16[128,256]{1,0:T(8,128)(2,1)S(1)} %multiply_convert_fusion.3), channel_id=1, source_target_pairs={{2,0},{3,1},{6,4},{7,5},{10,8},{11,9},{14,12},{15,13},{18,16},{19,... | collective-permute-start | bytes 196616 | tf_op jit(solution)/shard_map/ppermute | solution.py:39
  64.7 29.9 %collective-permute-start.1 = (bf16[128,1280]{1,0:T(8,128)(2,1)S(1)}, bf16[128,1280]{1,0:T(8,128)(2,1)}, u32[]{:S(2)}, u32[]{:S(2)}) collective-permute-start(bf16[128,1280]{1,0:T(8,128)(2,1)S(1)} %bitcast.148), channel_id=1, source_target_pairs={{2,0},{3,1},{6,4},{7,5},{10,8},{11,9},{14,12},{15,13},{18,16},{19,... | collective-permute-start | bytes 983048 | tf_op jit(solution)/shard_map/ppermute | solution.py:39
  66.0 32.0 %collective-permute-start = (bf16[128,1280]{1,0:T(8,128)(2,1)}, bf16[128,1280]{1,0:T(8,128)(2,1)}, u32[]{:S(2)}, u32[]{:S(2)}) collective-permute-start(bf16[128,1280]{1,0:T(8,128)(2,1)} %get-tuple-element.28), channel_id=1, source_target_pairs={{2,0},{3,1},{6,4},{7,5},{10,8},{11,9},{14,12},{15,13},{18,16},{19,... | collective-permute-start | bytes 983048 | tf_op jit(solution)/shard_map/ppermute | solution.py:39
  80.6 11.9 %collective-permute-start.11 = (bf16[128,256]{1,0:T(8,128)(2,1)S(1)}, bf16[128,256]{1,0:T(8,128)(2,1)S(1)}, u32[]{:S(2)}, u32[]{:S(2)}) collective-permute-start(bf16[128,256]{1,0:T(8,128)(2,1)S(1)} %multiply_convert_fusion.3), channel_id=1, source_target_pairs={{2,1},{3,0},{6,5},{7,4},{10,9},{11,8},{14,13},{15,12},{18,17},{19,... | collective-permute-start | bytes 196616 | tf_op jit(solution)/shard_map/ppermute | solution.py:39
  92.6 13.9 %collective-permute-start.23 = (bf16[320,640]{1,0:T(8,128)(2,1)}, bf16[320,640]{1,0:T(8,128)(2,1)S(1)}, u32[]{:S(2)}, u32[]{:S(2)}) collective-permute-start(bf16[320,640]{1,0:T(8,128)(2,1)} %collective-permute-done.18), channel_id=1, source_target_pairs={{4,0},{5,1},{20,16},{21,17}} | collective-permute-start | bytes 1228808 | tf_op jit(solution)/shard_map/ppermute | solution.py:39
  93.9 13.8 %collective-permute-start.24 = (bf16[320,640]{1,0:T(8,128)(2,1)}, bf16[320,640]{1,0:T(8,128)(2,1)S(1)}, u32[]{:S(2)}, u32[]{:S(2)}) collective-permute-start(bf16[320,640]{1,0:T(8,128)(2,1)} %collective-permute-done.19), channel_id=1, source_target_pairs={{8,12},{9,13},{24,28},{25,29}} | collective-permute-start | bytes 1228808 | tf_op jit(solution)/shard_map/ppermute | solution.py:39
  94.6 45.5 %collective-permute-start.29 = (bf16[320,640]{1,0:T(8,128)(2,1)}, bf16[320,640]{1,0:T(8,128)(2,1)S(1)}, u32[]{:S(2)}, u32[]{:S(2)}) collective-permute-start(bf16[320,640]{1,0:T(8,128)(2,1)} %get-tuple-element.26), channel_id=1, source_target_pairs={{0,16},{16,0},{1,17},{17,1},{4,20},{20,4},{5,21},{21,5},{8,24},{24... | collective-permute-start | bytes 1228808 | tf_op jit(solution)/shard_map/ppermute | solution.py:39
  98.0 17.2 %collective-permute-start.26 = (bf16[320,640]{1,0:T(8,128)(2,1)}, bf16[320,640]{1,0:T(8,128)(2,1)S(1)}, u32[]{:S(2)}, u32[]{:S(2)}) collective-permute-start(bf16[320,640]{1,0:T(8,128)(2,1)} %copy-done.11), channel_id=1, source_target_pairs={{4,0},{5,1},{20,16},{21,17}} | collective-permute-start | bytes 1228808 | tf_op jit(solution)/shard_map/ppermute | solution.py:39
  99.4 19.3 %collective-permute-start.27 = (bf16[320,640]{1,0:T(8,128)(2,1)}, bf16[320,640]{1,0:T(8,128)(2,1)S(1)}, u32[]{:S(2)}, u32[]{:S(2)}) collective-permute-start(bf16[320,640]{1,0:T(8,128)(2,1)} %copy-done.10), channel_id=1, source_target_pairs={{8,12},{9,13},{24,28},{25,29}} | collective-permute-start | bytes 1228808 | tf_op jit(solution)/shard_map/ppermute | solution.py:39
  106.4 14.7 %collective-permute-start.13 = (bf16[128,1280]{1,0:T(8,128)(2,1)S(1)}, bf16[128,1280]{1,0:T(8,128)(2,1)S(1)}, u32[]{:S(2)}, u32[]{:S(2)}) collective-permute-start(bf16[128,1280]{1,0:T(8,128)(2,1)S(1)} %get-tuple-element.20), channel_id=1, source_target_pairs={{0,1},{1,0},{2,3},{3,2},{4,5},{5,4},{6,7},{7,6},{8,9},{9,8},{10,11... | collective-permute-start | bytes 983048 | tf_op jit(solution)/shard_map/ppermute | solution.py:24
  108.9 17.5 %collective-permute-start.30 = (bf16[320,640]{1,0:T(8,128)(2,1)S(1)}, bf16[320,640]{1,0:T(8,128)(2,1)S(1)}, u32[]{:S(2)}, u32[]{:S(2)}) collective-permute-start(bf16[320,640]{1,0:T(8,128)(2,1)S(1)} %get-tuple-element.25), channel_id=1, source_target_pairs={{0,16},{16,0},{1,17},{17,1},{4,20},{20,4},{5,21},{21,5},{8,24},{24... | collective-permute-start | bytes 1228808 | tf_op jit(solution)/shard_map/ppermute | solution.py:39
  115.2 24.9 %collective-permute-start.28 = (bf16[320,640]{1,0:T(8,128)(2,1)S(1)}, bf16[320,640]{1,0:T(8,128)(2,1)S(1)}, u32[]{:S(2)}, u32[]{:S(2)}) collective-permute-start(bf16[320,640]{1,0:T(8,128)(2,1)S(1)} %get-tuple-element.24), channel_id=1, source_target_pairs={{0,16},{16,0},{1,17},{17,1},{4,20},{20,4},{5,21},{21,5},{8,24},{24... | collective-permute-start | bytes 1228808 | tf_op jit(solution)/shard_map/ppermute | solution.py:39
  118.8 21.0 %collective-permute-start.31 = (bf16[320,640]{1,0:T(8,128)(2,1)S(1)}, bf16[320,640]{1,0:T(8,128)(2,1)S(1)}, u32[]{:S(2)}, u32[]{:S(2)}) collective-permute-start(bf16[320,640]{1,0:T(8,128)(2,1)S(1)} %select_select_fusion), channel_id=1, source_target_pairs={{0,16},{16,0},{1,17},{17,1},{4,20},{20,4},{5,21},{21,5},{8,24},{24... | collective-permute-start | bytes 1228808 | tf_op jit(solution)/shard_map/ppermute | solution.py:39
  142.7 6.9 %collective-permute-start.38 = (bf16[128,256]{1,0:T(8,128)(2,1)S(1)}, bf16[128,256]{1,0:T(8,128)(2,1)S(1)}, u32[]{:S(2)}, u32[]{:S(2)}) collective-permute-start(bf16[128,256]{1,0:T(8,128)(2,1)S(1)} %get-tuple-element.17), channel_id=1, source_target_pairs={{0,12},{4,0},{8,4},{12,8},{1,13},{5,1},{9,5},{13,9},{2,14},{6,2},{... | collective-permute-start | bytes 196616 | tf_op jit(solution)/shard_map/ppermute | solution.py:24
  147.2 6.6 %collective-permute-start.37 = (bf16[128,256]{1,0:T(8,128)(2,1)S(1)}, bf16[128,256]{1,0:T(8,128)(2,1)S(1)}, u32[]{:S(2)}, u32[]{:S(2)}) collective-permute-start(bf16[128,256]{1,0:T(8,128)(2,1)S(1)} %get-tuple-element.17), channel_id=1, source_target_pairs={{0,8},{4,12},{8,0},{12,4},{1,9},{5,13},{9,1},{13,5},{2,10},{6,14},... | collective-permute-start | bytes 196616 | tf_op jit(solution)/shard_map/ppermute | solution.py:24
  147.2 6.6 %collective-permute-start.36 = (bf16[128,256]{1,0:T(8,128)(2,1)S(1)}, bf16[128,256]{1,0:T(8,128)(2,1)S(1)}, u32[]{:S(2)}, u32[]{:S(2)}) collective-permute-start(bf16[128,256]{1,0:T(8,128)(2,1)S(1)} %get-tuple-element.17), channel_id=1, source_target_pairs={{0,4},{4,8},{8,12},{12,0},{1,5},{5,9},{9,13},{13,1},{2,6},{6,10},{... | collective-permute-start | bytes 196616 | tf_op jit(solution)/shard_map/ppermute | solution.py:24
  153.8 5.1 %collective-permute-start.39 = (bf16[512,256]{1,0:T(8,128)(2,1)S(1)}, bf16[512,256]{1,0:T(8,128)(2,1)S(1)}, u32[]{:S(2)}, u32[]{:S(2)}) collective-permute-start(bf16[512,256]{1,0:T(8,128)(2,1)S(1)} %pad_maximum_fusion.1), channel_id=1, source_target_pairs={{0,1},{1,0},{2,3},{3,2},{4,5},{5,4},{6,7},{7,6},{8,9},{9,8},{10,11... | collective-permute-start | bytes 786440 | tf_op jit(solution)/shard_map/ppermute | solution.py:24
  153.9 4.5 %collective-permute-start.32 = (f32[128]{0:T(128)S(1)}, f32[128]{0:T(128)S(1)}, u32[]{:S(2)}, u32[]{:S(2)}) collective-permute-start(f32[128]{0:T(128)S(1)} %fusion.78), channel_id=1, source_target_pairs={{0,1},{1,0},{2,3},{3,2},{4,5},{5,4},{6,7},{7,6},{8,9},{9,8},{10,11... | collective-permute-start | bytes 1544 | tf_op jit(solution)/shard_map/ppermute | solution.py:24
  154.3 5.2 %collective-permute-start.35 = (bf16[128,320]{1,0:T(8,128)(2,1)S(1)}, bf16[128,320]{1,0:T(8,128)(2,1)S(1)}, u32[]{:S(2)}, u32[]{:S(2)}) collective-permute-start(bf16[128,320]{1,0:T(8,128)(2,1)S(1)} %get-tuple-element.38), channel_id=1, source_target_pairs={{0,12},{4,0},{8,4},{12,8},{1,13},{5,1},{9,5},{13,9},{2,14},{6,2},{... | collective-permute-start | bytes 245768 | tf_op jit(solution)/shard_map/ppermute | solution.py:24
  156.4 9.6 %collective-permute-start.34 = (bf16[128,320]{1,0:T(8,128)(2,1)S(1)}, bf16[128,320]{1,0:T(8,128)(2,1)S(1)}, u32[]{:S(2)}, u32[]{:S(2)}) collective-permute-start(bf16[128,320]{1,0:T(8,128)(2,1)S(1)} %get-tuple-element.39), channel_id=1, source_target_pairs={{0,8},{4,12},{8,0},{12,4},{1,9},{5,13},{9,1},{13,5},{2,10},{6,14},... | collective-permute-start | bytes 245768 | tf_op jit(solution)/shard_map/ppermute | solution.py:24
  156.4 9.6 %collective-permute-start.33 = (bf16[128,320]{1,0:T(8,128)(2,1)S(1)}, bf16[128,320]{1,0:T(8,128)(2,1)S(1)}, u32[]{:S(2)}, u32[]{:S(2)}) collective-permute-start(bf16[128,320]{1,0:T(8,128)(2,1)S(1)} %get-tuple-element.37), channel_id=1, source_target_pairs={{0,4},{4,8},{8,12},{12,0},{1,5},{5,9},{9,13},{13,1},{2,6},{6,10},{... | collective-permute-start | bytes 245768 | tf_op jit(solution)/shard_map/ppermute | solution.py:24
  (11 other events, 24.4 us)

commit v3 on v1

v3 whole, which is shorter than its diff:
```python
import itertools
import math

import jax
import jax.numpy as jnp
from jax import lax
from jax.sharding import PartitionSpec as P

DW = 2560
HD = 128
QH = 20
KVH = 4
EPS = 0.25
F32 = jnp.float32
BF16 = jnp.bfloat16


def stabilize(entries):
    return jnp.where(entries >= 0, entries + EPS, entries - EPS)


def moved(shard, axes, target):
    sizes = [lax.axis_size(axis) for axis in axes]
    places = list(itertools.product(*[range(size) for size in sizes]))
    index = {place: i for i, place in enumerate(places)}
    pairs = [(index[place], index[target(*place)]) for place in places if target(*place) is not None]
    return lax.ppermute(shard, axes, pairs)


def along_dp(shard, by):
    peers = lax.axis_size("dp")
    return moved(shard, ("dp",), lambda i: ((i + by) % peers,)) if by else shard


def other_core(shard):
    return moved(shard, ("mp",), lambda c: (1 - c,))


def other_group(shard):
    return moved(shard, ("groups",), lambda g: (1 - g,))


def pair_partner(shard):
    return moved(shard, ("dp",), lambda i: (i ^ 1,))


def from_next_section(shard, flip_pair=0, flip_core=0):
    return moved(
        shard,
        ("dp", "section", "mp"),
        lambda i, s, c: (i ^ flip_pair, s - 1, c ^ flip_core) if s > 0 else None,
    )


def ordered(first_is_mine, mine, theirs, axis):
    return jnp.concatenate(
        [jnp.where(first_is_mine, mine, theirs), jnp.where(first_is_mine, theirs, mine)], axis
    )


def part_of(array, index, width, axis):
    return lax.dynamic_slice_in_dim(array, index * width, width, axis)


def on_device(hidden_in, attn_out, queries, keys, value_weight, out_weight, lengths):
    inputs = hidden_in[0, 0]
    branch = attn_out[0, 0]
    query_rows = queries[0, 0]
    key_rows = keys[0, 0]
    value_rows = value_weight[0]
    out_block = out_weight[0]
    seq_len, half_width = inputs.shape
    group_size = QH // KVH
    kv_width = key_rows.shape[1]
    head_width = group_size * HD
    sections = lax.axis_size("section")
    section_pos = lax.axis_index("section")
    group_pos = lax.axis_index("groups")
    peers = lax.axis_size("dp")
    dp_pos = lax.axis_index("dp")
    core_pos = lax.axis_index("mp")
    block_width = out_block.shape[1]
    side = dp_pos % 2
    even = side == 0
    quarter = head_width // 2

    own_quarters = [part_of(out_block, 2 * side + group_pos, quarter, 0)]
    other_quarters = [part_of(out_block, 2 * side + 1 - group_pos, quarter, 0)]
    sent = [
        part_of(out_block, 2 * ((dp_pos + k) % 2) + group_pos, quarter, 0) for k in range(1, peers)
    ]
    for k in range(1, peers):
        own_quarters.append(along_dp(sent[k - 1], k))
        other_quarters.append(other_group(own_quarters[k]))
    own_rows = jnp.concatenate(own_quarters, 1)
    other_rows = jnp.concatenate(other_quarters, 1)

    inputs_f = inputs.astype(F32)
    branch_f = branch.astype(F32)
    totals = inputs_f + branch_f
    inv_totals = 1.0 / stabilize(totals)
    kept_gain = inputs_f * inv_totals
    branch_gain = branch_f * inv_totals / stabilize(branch_f)
    position = lax.iota(jnp.int32, seq_len)
    valid_rows = (position < lengths[0]).astype(F32)
    current = (totals * valid_rows[:, None]).astype(BF16).astype(F32)
    sens_branch = (current * branch_gain).astype(BF16)

    def both_cores(mine):
        return ordered(core_pos == 0, mine, other_core(mine), 1)

    def both_sequences(mine):
        return ordered(even, mine, pair_partner(mine), 0)

    sens_full = both_cores(both_sequences(sens_branch))

    behind_inputs = from_next_section(inputs).astype(F32)
    behind_values = from_next_section(value_rows)
    behind_values = ordered(core_pos == 0, behind_values, other_core(behind_values), 0)
    bent_full = both_cores(both_sequences((branch_gain * behind_inputs).astype(BF16)))

    value_part = jnp.dot(inputs, value_rows, preferred_element_type=F32)
    part_mine = part_of(value_part, core_pos, kv_width, 1)
    part_other = part_of(value_part, 1 - core_pos, kv_width, 1)
    values_own = part_mine + other_core(part_other.astype(BF16)).astype(F32)
    own_len = jnp.broadcast_to(lengths[0].astype(BF16), (8, HD))
    sent_values = jnp.concatenate(
        [part_of(values_own, 1 - side, HD, 1).astype(BF16), own_len], 0
    )
    got_values = pair_partner(sent_values)
    kept_values = jnp.concatenate([part_of(values_own, side, HD, 1).astype(BF16), own_len], 0)
    pair_values = jnp.stack(
        [jnp.where(even, kept_values, got_values), jnp.where(even, got_values, kept_values)]
    )
    pair_lengths = pair_values[:, seq_len, 0].astype(jnp.int32)
    pair_values = pair_values[:, :seq_len]
    values_r = pair_values.astype(F32)
    value_gain = values_r / stabilize(values_r)

    sent_heads = jnp.concatenate(
        [part_of(query_rows, 1 - side, head_width, 1), part_of(key_rows, 1 - side, HD, 1)], 1
    )
    kept_heads = jnp.concatenate(
        [part_of(query_rows, side, head_width, 1), part_of(key_rows, side, HD, 1)], 1
    )
    got_heads = pair_partner(sent_heads)
    heads = jnp.stack(
        [jnp.where(even, kept_heads, got_heads), jnp.where(even, got_heads, kept_heads)]
    )
    query_heads = heads[:, :, :head_width].reshape(2, seq_len, group_size, HD)
    key_heads = heads[:, :, head_width:]
    scores = jnp.einsum(
        "btjd,bsd->bjts", query_heads, key_heads, preferred_element_type=F32
    ) / math.sqrt(HD)
    allowed = (position[None, None, :] <= position[None, :, None]) & (
        position[None, None, :] < pair_lengths[:, None, None]
    )
    scores = jnp.where(allowed[:, None], scores, -1000000000.0)
    row_top = jnp.max(scores, axis=-1, keepdims=True)
    weights = jnp.exp(scores - row_top)
    prob_rows = (weights / jnp.sum(weights, axis=-1, keepdims=True)).astype(BF16)
    mixed = jnp.einsum(
        "bjts,bsd->btjd", prob_rows, pair_values, preferred_element_type=F32
    ).reshape(2 * seq_len, head_width)
    mixed_gain = mixed / stabilize(mixed)

    sens_values = jnp.zeros((2 * seq_len, HD), BF16)
    kept_sum = jnp.zeros((seq_len,), F32)
    for turn in range(sections):
        active = section_pos == sections - 1 - turn
        kept = current * kept_gain
        if turn + 1 < sections:
            behind_kept = from_next_section(kept.astype(BF16)).astype(F32)
            flat_full = both_cores(both_sequences((branch_gain * behind_kept).astype(BF16)))
        halves = [jnp.zeros((2 * seq_len, quarter), F32) for _ in range(2)]
        turned = jnp.concatenate(
            [part_of(sens_full, (dp_pos - k) % peers, block_width, 1) for k in range(peers)], 1
        )
        for half, rows in enumerate((own_rows, other_rows)):
            halves[half] = lax.dot_general(
                turned, rows, (((1,), (1,)), ((), ())), preferred_element_type=F32
            )
        back_mixed = ordered(group_pos == 0, halves[0], halves[1], 1)
        sens_mixed = (mixed_gain * back_mixed).astype(BF16)
        back_values = jnp.einsum(
            "bjts,btjd->bsd",
            prob_rows,
            sens_mixed.reshape(2, seq_len, group_size, HD),
            preferred_element_type=F32,
        )
        found = (value_gain * back_values).astype(BF16).reshape(2 * seq_len, HD)
        sens_values = jnp.where(active, found, sens_values)
        kept_sum = jnp.where(active, jnp.sum(kept, axis=1), kept_sum)
        if turn + 1 < sections:
            pieces = [[from_next_section(found, i, j) for j in range(2)] for i in range(2)]
            columns = [ordered(even, pieces[0][j], pieces[1][j], 1) for j in range(2)]
            behind_sens = ordered(core_pos == 0, columns[0], columns[1], 1)
            back_inputs = lax.dot_general(
                behind_sens, behind_values, (((1,), (1,)), ((), ())), preferred_element_type=F32
            )
            sens_full = (flat_full.astype(F32) + bent_full.astype(F32) * back_inputs).astype(BF16)
            mine = part_of(part_of(back_inputs, side, seq_len, 0), core_pos, half_width, 1)
            current = jnp.where(active, current, behind_kept + behind_inputs * mine)

    from_values = jnp.sum(
        (sens_values.astype(F32) * values_r.reshape(2 * seq_len, HD)).reshape(2, seq_len, HD), axis=2
    )
    kept_part = jnp.where(even, from_values[0], from_values[1])
    sent_part = jnp.where(even, from_values[1], from_values[0])
    heat_part = kept_sum + kept_part + pair_partner(sent_part)
    heat_rows = (heat_part + other_core(heat_part)) / DW

    block_rows = half_width // peers
    got_inputs = [
        along_dp(part_of(inputs, (dp_pos + k) % peers, block_rows, 1), k) for k in range(peers)
    ]
    all_inputs = []
    for j in range(0, peers, 2):
        after, before = got_inputs[j + 1], got_inputs[(j - 1) % peers]
        all_inputs.append(jnp.where(even, got_inputs[j], after))
        all_inputs.append(jnp.where(even, before, got_inputs[j]))
    all_inputs = jnp.concatenate(all_inputs, 0)
    got_sens = [along_dp(sens_values, k) for k in range(peers)]
    same_side = jnp.concatenate([got_sens[j] for j in range(0, peers, 2)], 0)
    other_side = jnp.concatenate(
        [jnp.where(even, got_sens[(j - 1) % peers], got_sens[j + 1]) for j in range(0, peers, 2)], 0
    )
    core_sens = ordered(even, same_side, other_side, 1)
    all_sens = both_cores(core_sens)
    summed = lax.dot_general(
        all_inputs, all_sens, (((0,), (0,)), ((), ())), preferred_element_type=F32
    )
    value_block = part_of(value_rows, dp_pos, block_rows, 0)
    relevance_rows = value_block.astype(F32) * summed
    return (heat_rows[None, None, :], relevance_rows[None])


def solution(mesh):
    placed = (
        P("section", ("groups", "dp"), None, "mp"),
        P("section", ("groups", "dp"), None, "mp"),
        P("section", ("groups", "dp"), None, "mp"),
        P("section", ("groups", "dp"), None, "mp"),
        P("section", "mp", None),
        P("section", "mp", "dp"),
        P(("groups", "dp")),
    )
    return jax.shard_map(
        on_device,
        mesh=mesh,
        in_specs=placed,
        out_specs=(
            P("section", ("groups", "dp"), None),
            P(("groups", "section"), ("mp", "dp"), None),
        ),
        check_vma=False,
    )
```

time: 173 us -> 169 us (0.977)
  other arithmetic: 11.9 us -> 19 us
  starting transfers between devices: 41.3 us -> 37.7 us
  matrix products: 14.6 us -> 11.7 us
  waiting for transfers between devices: 91.4 us -> 89.1 us
  local copies, waits for them, and re-layouts: 10.8 us -> 8.59 us
    dynamic_slice x2 -> x5, local copies, waits for them, and re-layouts: 0.29 us -> 4.04 us  [part_of(): return lax.dynamic_slice_in_dim(array, index * width, width, axis)]
    ppermute x25 -> x32, starting transfers between devices: 41.3 us -> 37.7 us  [moved(): return lax.ppermute(shard, axes, pairs)]
    concatenate x1 -> x8, other arithmetic: 0.02 us -> 3.44 us  [the longest x7 3.42 us: ordered(): jnp.concatenate([jnp.where(first_is_mine, mine, theirs), jnp.where(first_...]
    unnamed x41 -> x46, local copies, waits for them, and re-layouts: 6.08 us -> 2.93 us
    reshape x4 -> x0, local copies, waits for them, and re-layouts: 2.48 us -> none  [the longest x1 2.17 us: on_device(): mixed = jnp.einsum('gjts,sgd->tgjd', prob_rows, values_bf.reshape(seq_len...]
    dot_general x1, matrix products: 3.24 us -> 0.87 us  [on_device(): lax.dot_general(behind_sens, behind_values, (((1,), (1,)), ((), ())), pre...]
    ppermute x25 -> x32, waiting for transfers between devices: 91.4 us -> 89.1 us  [moved(): return lax.ppermute(shard, axes, pairs)]
    reduce_sum x1, other arithmetic: 0.15 us -> 2.04 us  [on_device(): kept_sum = jnp.where(active, jnp.sum(kept, axis=1), kept_sum)]
  transfers between devices with their start and end apart: 25 -> 32, of which waited for: 13 -> 14; matrix products, arithmetic and copies ran while one was open for 12% -> 18% of each run, Pallas kernels for 0% -> 0%
where the time goes in v3:
time: 169 us; the launch traced here: 168 us
  waiting for transfers between devices  89.1 us (53%)
  starting transfers between devices  37.7 us (22%)
  other arithmetic  19 us (11%)
  matrix products  11.7 us (7%)
  local copies, waits for them, and re-layouts  8.59 us (5%)
  between operations  2.11 us (1%)
    ppermute x32, waiting for transfers between devices, moved(): return lax.ppermute(shard, axes, pairs)  89.1 us
    ppermute x32, starting transfers between devices, moved(): return lax.ppermute(shard, axes, pairs)  37.7 us
    select_n x11, other arithmetic, ordered(): jnp.where(first_is_mine, mine, theirs)  6.14 us
    dot_general x4, matrix products, on_device(): lax.dot_general(turned, rows, (((1,), (1,)), ((), ())), preferred_element...  5.16 us
    dynamic_slice x5, local copies, waits for them, and re-layouts, part_of(): return lax.dynamic_slice_in_dim(array, index * width, width, axis)  4.04 us
    concatenate x7, other arithmetic, ordered(): jnp.concatenate([jnp.where(first_is_mine, mine, theirs), jnp.where(first_...  3.42 us
  transfers between devices with their start and end apart: 32, of which 14 were waited for; matrix products, arithmetic and copies ran while one was open for 18% of the time, Pallas kernels for 0%

profile of v3, /device:TPU:0, one launch (start us, length us, event | category | flops | bytes accessed | tf_op | source)
XLA Modules:
  0.0 168.2 jit_solution(14058446910031326004)
XLA Ops:
  1.3 2.3 %fusion.47 = (bf16[128,1280]{1,0:T(8,128)(2,1)}, bf16[128,1280]{1,0:T(8,128)(2,1)S(1)}) fusion(bf16[1,1,128,1280]{3,2,1,0:T(8,128)(2,1)} %param.7, f32[128]{0:T(128)S(1)} %compare_convert_fusion, bf16[1,1,128,1280]{3,2,1,0:T(8,128)(2,1)} %param.8), kind=kLoop, calls=%fused_computation.115 | loop fusion | flops 3604480 | bytes 1311232 | tf_op jit(solution)/shard_map/convert_element_type | solution.py:173
  3.5 3.0 %collective-permute-start.5 = (bf16[128,1280]{1,0:T(8,128)(2,1)S(1)}, bf16[128,1280]{1,0:T(8,128)(2,1)}, u32[]{:S(2)}, u32[]{:S(2)}) collective-permute-start(bf16[128,1280]{1,0:T(8,128)(2,1)S(1)} %get-tuple-element.28), channel_id=1, source_target_pairs={{0,4},{4,0},{8,12},{12,8},{1,5},{5,1},{9,13},{13,9},{2,6},{6,2},{1... | collective-permute-start | bytes 983048 | tf_op jit(solution)/shard_map/ppermute | solution.py:27
  6.6 3.0 %dynamic-slice_bitcast_fusion.4 = (bf16[320,640]{1,0:T(8,128)(2,1)}, bf16[320,640]{1,0:T(8,128)(2,1)}, bf16[320,640]{1,0:T(8,128)(2,1)}, bf16[320,640]{1,0:T(8,128)(2,1)}, bf16[320,640]{1,0:T(8,128)(2,1)}) fusion(bf16[1,1280,640]{2,1,0:T(8,128)(2,1)} %param.12, s32[]{:T(128)S(6)} %select_n.445, s32[]{:T(128)S(6)} %select_n.449, s32[]{:T(128)S(6)} %select_n.447, ...), kind=kLoop, calls=%fused_computation.80 | loop fusion | bytes 4096020 | tf_op jit(solution)/shard_map/dynamic_slice | solution.py:62
  9.6 3.0 %collective-permute-start.8 = (bf16[320,640]{1,0:T(8,128)(2,1)}, bf16[320,640]{1,0:T(8,128)(2,1)}, u32[]{:S(2)}, u32[]{:S(2)}) collective-permute-start(bf16[320,640]{1,0:T(8,128)(2,1)} %get-tuple-element.7), channel_id=1, source_target_pairs={{0,8},{4,12},{8,0},{12,4},{1,9},{5,13},{9,1},{13,5},{2,10},{6,14},... | collective-permute-start | bytes 1228808 | tf_op jit(solution)/shard_map/ppermute | solution.py:27
  12.6 2.5 %collective-permute-start.9 = (bf16[320,640]{1,0:T(8,128)(2,1)}, bf16[320,640]{1,0:T(8,128)(2,1)}, u32[]{:S(2)}, u32[]{:S(2)}) collective-permute-start(bf16[320,640]{1,0:T(8,128)(2,1)} %get-tuple-element.10), channel_id=1, source_target_pairs={{0,12},{4,0},{8,4},{12,8},{1,13},{5,1},{9,5},{13,9},{2,14},{6,2},{... | collective-permute-start | bytes 1228808 | tf_op jit(solution)/shard_map/ppermute | solution.py:27
  15.6 1.1 collective-permute-done.2
  17.0 24.4 %collective-permute-done.3 = bf16[136,128]{1,0:T(8,128)(2,1)S(1)} collective-permute-done((bf16[136,128]{1,0:T(8,128)(2,1)S(1)}, bf16[136,128]{1,0:T(8,128)(2,1)S(1)}, u32[]{:S(2)}, u32[]{:S(2)}) %collective-permute-start.3) | collective-permute-done | bytes 34848 | tf_op jit(solution)/shard_map/ppermute | solution.py:27
  41.3 1.8 %collective-permute-start.4 = (bf16[128,768]{1,0:T(8,128)(2,1)S(1)}, bf16[128,768]{1,0:T(8,128)(2,1)S(1)}, u32[]{:S(2)}, u32[]{:S(2)}) collective-permute-start(bf16[128,768]{1,0:T(8,128)(2,1)S(1)} %pad_maximum_fusion.20), channel_id=1, source_target_pairs={{0,4},{4,0},{8,12},{12,8},{1,5},{5,1},{9,13},{13,9},{2,6},{6,2},{1... | collective-permute-start | bytes 589832 | tf_op jit(solution)/shard_map/ppermute | solution.py:27
  43.5 3.8 %collective-permute-done.4 = bf16[128,768]{1,0:T(8,128)(2,1)S(1)} collective-permute-done((bf16[128,768]{1,0:T(8,128)(2,1)S(1)}, bf16[128,768]{1,0:T(8,128)(2,1)S(1)}, u32[]{:S(2)}, u32[]{:S(2)}) %collective-permute-start.4) | collective-permute-done | bytes 196640 | tf_op jit(solution)/shard_map/ppermute | solution.py:27
  47.3 1.3 collective-permute-start.17
  48.7 0.9 copy.13
  49.6 1.0 broadcast_select_fusion.13
  50.6 0.9 pad_maximum_fusion.4
  51.5 2.2 %fusion.75 = (f32[2,5,128]{2,1,0:T(8,128)S(1)}, f32[2,5,128,128]{2,3,1,0:T(8,128)}) fusion(bf16[2,128,5,128]{1,3,2,0:T(8,128)(2,1)} %bitcast.174, pred[2,128,128]{1,2,0:T(8,128)(4,1)S(1)} %broadcast_and_fusion, bf16[1,128,768]{2,1,0:T(8,128)(2,1)S(1)} %get-tuple-element.42, bf16[1,128,768]{2,1,0:T(8,128)(2,1)S(1)} %get-tuple-element.41), kind=kOutput, calls=%fused_computation.199 | convolution fusion | flops 42729600 | bytes 1414144 | tf_op jit(solution)/shard_map/sub | solution.py:160
  53.7 1.1 divide_convert_fusion
  55.2 1.6 collective-permute-start.10
  57.3 1.5 collective-permute-start.12
  58.8 1.3 broadcast_select_fusion.6
  61.1 1.9 %fusion.42 = f32[256,320]{0,1:T(8,128)S(1)} fusion(bf16[320,640]{1,0:T(8,128)(2,1)} %collective-permute-done.9, bf16[320,640]{1,0:T(8,128)(2,1)} %collective-permute-done.8, bf16[320,640]{1,0:T(8,128)(2,1)} %collective-permute-done.7, bf16[320,640]{1,0:T(8,128)(2,1)S(1)} %copy-done.13, bf16[256,640]{1,0:T(8,128)(2,1)S(1)} %get-tuple-element.22, ...), kind=kOutput, calls=%fused_computation.102 | convolution fusion | flops 431226880 | bytes 3276800 | tf_op jit(solution)/shard_map/dot_general | solution.py:180
  63.1 15.1 %collective-permute-done.17 = bf16[1280,512]{1,0:T(8,128)(2,1)} collective-permute-done((bf16[1280,512]{1,0:T(8,128)(2,1)S(1)}, bf16[1280,512]{1,0:T(8,128)(2,1)}, u32[]{:S(2)}, u32[]{:S(2)}) %collective-permute-start.17) | collective-permute-done | bytes 1310752 | tf_op jit(solution)/shard_map/ppermute | solution.py:27
  78.2 6.7 %collective-permute-done.12 = bf16[320,640]{1,0:T(8,128)(2,1)S(1)} collective-permute-done((bf16[320,640]{1,0:T(8,128)(2,1)}, bf16[320,640]{1,0:T(8,128)(2,1)S(1)}, u32[]{:S(2)}, u32[]{:S(2)}) %collective-permute-start.12) | collective-permute-done | bytes 409632 | tf_op jit(solution)/shard_map/ppermute | solution.py:27
  86.4 1.3 collective-permute-start.13
  87.7 1.3 collective-permute-start.14
  89.0 1.3 collective-permute-start
  90.3 1.3 collective-permute-start.1
  91.6 2.0 %collective-permute-done.13 = bf16[256,128]{1,0:T(8,128)(2,1)S(1)} collective-permute-done((bf16[256,128]{1,0:T(8,128)(2,1)S(1)}, bf16[256,128]{1,0:T(8,128)(2,1)S(1)}, u32[]{:S(2)}, u32[]{:S(2)}) %collective-permute-start.13) | collective-permute-done | bytes 65568 | tf_op jit(solution)/shard_map/ppermute | solution.py:27
  93.6 1.3 collective-permute-start.15
  94.9 1.2 collective-permute-done.14
  96.1 1.3 collective-permute-start.16
  97.4 14.9 %collective-permute-done.15 = bf16[256,128]{1,0:T(8,128)(2,1)S(1)} collective-permute-done((bf16[256,128]{1,0:T(8,128)(2,1)S(1)}, bf16[256,128]{1,0:T(8,128)(2,1)S(1)}, u32[]{:S(2)}, u32[]{:S(2)}) %collective-permute-start.15) | collective-permute-done | bytes 65568 | tf_op jit(solution)/shard_map/ppermute | solution.py:27
  112.5 1.9 %broadcast_select_fusion.1 = (bf16[1280,512]{1,0:T(8,128)(2,1)S(1)}, bf16[1280,512]{1,0:T(8,128)(2,1)S(1)}) fusion(bf16[1280,512]{1,0:T(8,128)(2,1)} %collective-permute-done.17, bf16[1280,512]{1,0:T(8,128)(2,1)} %collective-permute-done.18, pred[]{:T(512)S(6)} %eq.40), kind=kLoop, calls=%fused_computation.25 | loop fusion | flops 1310720 | bytes 5242881 | tf_op jit(solution)/shard_map/jit(_where)/select_n | solution.py:57
  115.3 2.0 %fusion.46 = (f32[128]{0:T(128)S(1)}, f32[128]{0:T(128)S(1)}, bf16[128,1280]{1,0:T(8,128)(2,1)S(1)}, bf16[128,1280]{1,0:T(8,128)(2,1)S(1)}) fusion(bf16[1,1,128,1280]{3,2,1,0:T(8,128)(2,1)S(1)} %copy-done, f32[128]{0:T(128)S(1)} %compare_convert_fusion, bf16[1,1,128,1280]{3,2,1,0:T(8,128)(2,1)S(1)} %copy-done.10, f32[256,2560]{1,0:T(8,128)S(1)} %fusion.1, ...), kind=kLoop, calls=%fused_computation.114 | loop fusion | flops 5078784 | bytes 2622985 | tf_op jit(solution)/shard_map/reduce_sum | solution.py:193
  118.0 1.5 collective-permute-start.19
  119.5 8.5 %collective-permute-done.21 = bf16[128,1280]{1,0:T(8,128)(2,1)S(1)} collective-permute-done((bf16[128,1280]{1,0:T(8,128)(2,1)S(1)}, bf16[128,1280]{1,0:T(8,128)(2,1)S(1)}, u32[]{:S(2)}, u32[]{:S(2)}) %collective-permute-start.21) | collective-permute-done | bytes 327712 | tf_op jit(solution)/shard_map/ppermute | solution.py:27
  128.1 1.0 pad_maximum_fusion.7
  129.0 5.1 %collective-permute-done.19 = bf16[128,1280]{1,0:T(8,128)(2,1)S(1)} collective-permute-done((bf16[128,1280]{1,0:T(8,128)(2,1)S(1)}, bf16[128,1280]{1,0:T(8,128)(2,1)S(1)}, u32[]{:S(2)}, u32[]{:S(2)}) %collective-permute-start.19) | collective-permute-done | bytes 327712 | tf_op jit(solution)/shard_map/ppermute | solution.py:27
  134.9 0.9 pad_maximum_fusion.6
  136.0 0.9 dynamic-slice_bitcast_fusion.8
  136.9 0.9 collective-permute-start.25
  137.8 5.5 %collective-permute-start.26 = (bf16[128,320]{1,0:T(8,128)(2,1)}, bf16[128,320]{1,0:T(8,128)(2,1)}, u32[]{:S(2)}, u32[]{:S(2)}) collective-permute-start(bf16[128,320]{1,0:T(8,128)(2,1)} %get-tuple-element.45), channel_id=1, source_target_pairs={{0,12},{4,0},{8,4},{12,8},{1,13},{5,1},{9,5},{13,9},{2,14},{6,2},{... | collective-permute-start | bytes 245768 | tf_op jit(solution)/shard_map/ppermute | solution.py:27
  143.3 1.8 %collective-permute-start.27 = (bf16[128,320]{1,0:T(8,128)(2,1)}, bf16[128,320]{1,0:T(8,128)(2,1)}, u32[]{:S(2)}, u32[]{:S(2)}) collective-permute-start(bf16[128,320]{1,0:T(8,128)(2,1)} %get-tuple-element.47), channel_id=1, source_target_pairs={{0,8},{4,12},{8,0},{12,4},{1,9},{5,13},{9,1},{13,5},{2,10},{6,14},... | collective-permute-start | bytes 245768 | tf_op jit(solution)/shard_map/ppermute | solution.py:27
  145.2 1.5 broadcast_select_fusion.3
  146.7 1.3 broadcast_select_fusion.5
  149.6 2.0 %fusion.41 = f32[256,320]{0,1:T(8,128)S(1)} fusion(bf16[320,640]{1,0:T(8,128)(2,1)} %collective-permute-done.9, bf16[320,640]{1,0:T(8,128)(2,1)} %collective-permute-done.8, bf16[320,640]{1,0:T(8,128)(2,1)} %collective-permute-done.7, bf16[320,640]{1,0:T(8,128)(2,1)S(1)} %copy-done.14, bf16[256,640]{1,0:T(8,128)(2,1)S(1)} %get-tuple-element.12, ...), kind=kOutput, calls=%fused_computation.101 | convolution fusion | flops 431226880 | bytes 3276800 | tf_op jit(solution)/shard_map/dot_general | solution.py:180
  154.6 1.9 %collective-permute-start.29 = (bf16[256,128]{1,0:T(8,128)(2,1)S(1)}, bf16[256,128]{1,0:T(8,128)(2,1)S(1)}, u32[]{:S(2)}, u32[]{:S(2)}) collective-permute-start(bf16[256,128]{1,0:T(8,128)(2,1)S(1)} %bitcast_select_fusion.2), channel_id=1, source_target_pairs={{0,12},{4,0},{8,4},{12,8},{1,13},{5,1},{9,5},{13,9},{2,14},{6,2},{... | collective-permute-start | bytes 196616 | tf_op jit(solution)/shard_map/ppermute | solution.py:27
  159.6 3.8 %collective-permute-done.30 = bf16[256,128]{1,0:T(8,128)(2,1)S(1)} collective-permute-done((bf16[256,128]{1,0:T(8,128)(2,1)S(1)}, bf16[256,128]{1,0:T(8,128)(2,1)S(1)}, u32[]{:S(2)}, u32[]{:S(2)}) %collective-permute-start.30) | collective-permute-done | bytes 65568 | tf_op jit(solution)/shard_map/ppermute | solution.py:27
  164.3 1.1 bitcast_select_fusion.1
  166.0 2.2 %fusion.6 = f32[1,320,512]{2,1,0:T(8,128)} fusion(bf16[512,256]{1,0:T(8,128)(2,1)S(1)} %get-tuple-element.40, bf16[512,256]{1,0:T(8,128)(2,1)S(1)} %get-tuple-element.39, bf16[128,320]{1,0:T(8,128)(2,1)S(1)} %get-tuple-element.61, bf16[128,320]{1,0:T(8,128)(2,1)S(1)} %get-tuple-element.60, bf16[128,320]{1,0:T(8,128)(2,1)S(1)} %get-tuple-element.44, ...), kind=kOutput, calls=%fused_computation.27 | convolution fusion | flops 170459136 | bytes 1835012 | tf_op jit(solution)/shard_map/dot_general | solution.py:230
  (123 shorter events, 16.0 us)
Async XLA Ops:
  3.5 46.1 %collective-permute-start.5 = (bf16[128,1280]{1,0:T(8,128)(2,1)S(1)}, bf16[128,1280]{1,0:T(8,128)(2,1)}, u32[]{:S(2)}, u32[]{:S(2)}) collective-permute-start(bf16[128,1280]{1,0:T(8,128)(2,1)S(1)} %get-tuple-element.28), channel_id=1, source_target_pairs={{0,4},{4,0},{8,12},{12,8},{1,5},{5,1},{9,13},{13,9},{2,6},{6,2},{1... | collective-permute-start | bytes 983048 | tf_op jit(solution)/shard_map/ppermute | solution.py:27
  6.6 8.5 %copy-start = (bf16[1,1,128,1280]{3,2,1,0:T(8,128)(2,1)S(1)}, bf16[1,1,128,1280]{3,2,1,0:T(8,128)(2,1)}, u32[]{:S(2)}) copy-start(bf16[1,1,128,1280]{3,2,1,0:T(8,128)(2,1)} %param.7) | copy-start | bytes 983044
  6.6 8.5 %copy-start.9 = (bf16[1,1280,512]{2,1,0:T(8,128)(2,1)S(1)}, bf16[1,1280,512]{2,1,0:T(8,128)(2,1)}, u32[]{:S(2)}) copy-start(bf16[1,1280,512]{2,1,0:T(8,128)(2,1)} %param.11) | copy-start | bytes 3932164
  9.5 6.0 %copy-start.15 = (bf16[1,1,128,1280]{3,2,1,0:T(8,128)(2,1)S(1)}, bf16[1,1,128,1280]{3,2,1,0:T(8,128)(2,1)}, u32[]{:S(2)}) copy-start(bf16[1,1,128,1280]{3,2,1,0:T(8,128)(2,1)} %param.9) | copy-start | bytes 983044
  9.5 6.1 %copy-start.16 = (bf16[1,1,128,256]{3,2,1,0:T(8,128)(2,1)S(1)}, bf16[1,1,128,256]{3,2,1,0:T(8,128)(2,1)}, u32[]{:S(2)}) copy-start(bf16[1,1,128,256]{3,2,1,0:T(8,128)(2,1)} %param.10) | copy-start | bytes 196612
  9.5 45.7 %collective-permute-start.7 = (bf16[320,640]{1,0:T(8,128)(2,1)}, bf16[320,640]{1,0:T(8,128)(2,1)}, u32[]{:S(2)}, u32[]{:S(2)}) collective-permute-start(bf16[320,640]{1,0:T(8,128)(2,1)} %get-tuple-element.8), channel_id=1, source_target_pairs={{0,4},{4,8},{8,12},{12,0},{1,5},{5,9},{9,13},{13,1},{2,6},{6,10},{... | collective-permute-start | bytes 1228808 | tf_op jit(solution)/shard_map/ppermute | solution.py:27
  9.6 47.2 %collective-permute-start.8 = (bf16[320,640]{1,0:T(8,128)(2,1)}, bf16[320,640]{1,0:T(8,128)(2,1)}, u32[]{:S(2)}, u32[]{:S(2)}) collective-permute-start(bf16[320,640]{1,0:T(8,128)(2,1)} %get-tuple-element.7), channel_id=1, source_target_pairs={{0,8},{4,12},{8,0},{12,4},{1,9},{5,13},{9,1},{13,5},{2,10},{6,14},... | collective-permute-start | bytes 1228808 | tf_op jit(solution)/shard_map/ppermute | solution.py:27
  12.6 44.7 %collective-permute-start.9 = (bf16[320,640]{1,0:T(8,128)(2,1)}, bf16[320,640]{1,0:T(8,128)(2,1)}, u32[]{:S(2)}, u32[]{:S(2)}) collective-permute-start(bf16[320,640]{1,0:T(8,128)(2,1)} %get-tuple-element.10), channel_id=1, source_target_pairs={{0,12},{4,0},{8,4},{12,8},{1,13},{5,1},{9,5},{13,9},{2,14},{6,2},{... | collective-permute-start | bytes 1228808 | tf_op jit(solution)/shard_map/ppermute | solution.py:27
  15.4 1.3 collective-permute-start.2
  16.8 24.6 %collective-permute-start.3 = (bf16[136,128]{1,0:T(8,128)(2,1)S(1)}, bf16[136,128]{1,0:T(8,128)(2,1)S(1)}, u32[]{:S(2)}, u32[]{:S(2)}) collective-permute-start(bf16[136,128]{1,0:T(8,128)(2,1)S(1)} %concatenate.80), channel_id=1, source_target_pairs={{0,4},{4,0},{8,12},{12,8},{1,5},{5,1},{9,13},{13,9},{2,6},{6,2},{1... | collective-permute-start | bytes 104456 | tf_op jit(solution)/shard_map/ppermute | solution.py:27
  41.3 5.9 %collective-permute-start.4 = (bf16[128,768]{1,0:T(8,128)(2,1)S(1)}, bf16[128,768]{1,0:T(8,128)(2,1)S(1)}, u32[]{:S(2)}, u32[]{:S(2)}) collective-permute-start(bf16[128,768]{1,0:T(8,128)(2,1)S(1)} %pad_maximum_fusion.20), channel_id=1, source_target_pairs={{0,4},{4,0},{8,12},{12,8},{1,5},{5,1},{9,13},{13,9},{2,6},{6,2},{1... | collective-permute-start | bytes 589832 | tf_op jit(solution)/shard_map/ppermute | solution.py:27
  47.3 30.9 %collective-permute-start.17 = (bf16[1280,512]{1,0:T(8,128)(2,1)S(1)}, bf16[1280,512]{1,0:T(8,128)(2,1)}, u32[]{:S(2)}, u32[]{:S(2)}) collective-permute-start(bf16[1280,512]{1,0:T(8,128)(2,1)S(1)} %bitcast.169), channel_id=1, source_target_pairs={{2,0},{3,1},{6,4},{7,5},{10,8},{11,9},{14,12},{15,13},{18,16},{19,... | collective-permute-start | bytes 3932168 | tf_op jit(solution)/shard_map/ppermute | solution.py:27
  51.5 7.3 %collective-permute-start.6 = (bf16[256,1280]{1,0:T(8,128)(2,1)}, bf16[256,1280]{1,0:T(8,128)(2,1)}, u32[]{:S(2)}, u32[]{:S(2)}) collective-permute-start(bf16[256,1280]{1,0:T(8,128)(2,1)} %pad_maximum_fusion.4), channel_id=1, source_target_pairs={{0,1},{1,0},{2,3},{3,2},{4,5},{5,4},{6,7},{7,6},{8,9},{9,8},{10,11... | collective-permute-start | bytes 1966088 | tf_op jit(solution)/shard_map/ppermute | solution.py:27
  55.2 30.9 %copy-start.7 = (f32[2,128,5,128]{1,3,2,0:T(8,128)}, f32[2,128,5,128]{1,3,2,0:T(8,128)S(1)}, u32[]{:S(2)}) copy-start(f32[2,128,5,128]{1,3,2,0:T(8,128)S(1)} %select_divide_fusion) | copy-start | bytes 1966084
  55.2 23.0 %collective-permute-start.10 = (bf16[320,640]{1,0:T(8,128)(2,1)}, bf16[320,640]{1,0:T(8,128)(2,1)S(1)}, u32[]{:S(2)}, u32[]{:S(2)}) collective-permute-start(bf16[320,640]{1,0:T(8,128)(2,1)} %collective-permute-done.7), channel_id=1, source_target_pairs={{0,16},{16,0},{1,17},{17,1},{2,18},{18,2},{3,19},{19,3},{4,20},{20... | collective-permute-start | bytes 1228808 | tf_op jit(solution)/shard_map/ppermute | solution.py:27
  56.8 21.4 %collective-permute-start.11 = (bf16[320,640]{1,0:T(8,128)(2,1)}, bf16[320,640]{1,0:T(8,128)(2,1)S(1)}, u32[]{:S(2)}, u32[]{:S(2)}) collective-permute-start(bf16[320,640]{1,0:T(8,128)(2,1)} %collective-permute-done.8), channel_id=1, source_target_pairs={{0,16},{16,0},{1,17},{17,1},{2,18},{18,2},{3,19},{19,3},{4,20},{20... | collective-permute-start | bytes 1228808 | tf_op jit(solution)/shard_map/ppermute | solution.py:27
  57.3 27.6 %collective-permute-start.12 = (bf16[320,640]{1,0:T(8,128)(2,1)}, bf16[320,640]{1,0:T(8,128)(2,1)S(1)}, u32[]{:S(2)}, u32[]{:S(2)}) collective-permute-start(bf16[320,640]{1,0:T(8,128)(2,1)} %collective-permute-done.9), channel_id=1, source_target_pairs={{0,16},{16,0},{1,17},{17,1},{2,18},{18,2},{3,19},{19,3},{4,20},{20... | collective-permute-start | bytes 1228808 | tf_op jit(solution)/shard_map/ppermute | solution.py:27
  61.1 23.8 %copy-start.11 = (bf16[320,640]{1,0:T(8,128)(2,1)S(1)}, bf16[320,640]{1,0:T(8,128)(2,1)}, u32[]{:S(2)}) copy-start(bf16[320,640]{1,0:T(8,128)(2,1)} %get-tuple-element.9) | copy-start | bytes 1228804
  78.2 34.3 %collective-permute-start.18 = (bf16[1280,512]{1,0:T(8,128)(2,1)}, bf16[1280,512]{1,0:T(8,128)(2,1)}, u32[]{:S(2)}, u32[]{:S(2)}) collective-permute-start(bf16[1280,512]{1,0:T(8,128)(2,1)} %collective-permute-done.17), channel_id=1, source_target_pairs={{0,1},{1,0},{2,3},{3,2},{4,5},{5,4},{6,7},{7,6},{8,9},{9,8},{10,11... | collective-permute-start | bytes 3932168 | tf_op jit(solution)/shard_map/ppermute | solution.py:27
  78.2 7.4 %copy-start.17 = (bf16[320,640]{1,0:T(8,128)(2,1)}, bf16[320,640]{1,0:T(8,128)(2,1)S(1)}, u32[]{:S(2)}) copy-start(bf16[320,640]{1,0:T(8,128)(2,1)S(1)} %collective-permute-done.10) | copy-start | bytes 1228804
  78.2 7.4 %copy-start.19 = (bf16[320,640]{1,0:T(8,128)(2,1)}, bf16[320,640]{1,0:T(8,128)(2,1)S(1)}, u32[]{:S(2)}) copy-start(bf16[320,640]{1,0:T(8,128)(2,1)S(1)} %collective-permute-done.11) | copy-start | bytes 1228804
  86.4 7.2 %collective-permute-start.13 = (bf16[256,128]{1,0:T(8,128)(2,1)S(1)}, bf16[256,128]{1,0:T(8,128)(2,1)S(1)}, u32[]{:S(2)}, u32[]{:S(2)}) collective-permute-start(bf16[256,128]{1,0:T(8,128)(2,1)S(1)} %bitcast.170), channel_id=1, source_target_pairs={{2,0},{3,1},{6,4},{7,5},{10,8},{11,9},{14,12},{15,13},{18,16},{19,... | collective-permute-start | bytes 196616 | tf_op jit(solution)/shard_map/ppermute | solution.py:27
  87.7 8.5 %collective-permute-start.14 = (bf16[256,128]{1,0:T(8,128)(2,1)S(1)}, bf16[256,128]{1,0:T(8,128)(2,1)S(1)}, u32[]{:S(2)}, u32[]{:S(2)}) collective-permute-start(bf16[256,128]{1,0:T(8,128)(2,1)S(1)} %bitcast.171), channel_id=1, source_target_pairs={{2,4},{3,5},{6,0},{7,1},{10,12},{11,13},{14,8},{15,9},{18,20},{19,... | collective-permute-start | bytes 196616 | tf_op jit(solution)/shard_map/ppermute | solution.py:27
  89.0 26.3 %collective-permute-start = (bf16[128,1280]{1,0:T(8,128)(2,1)}, bf16[128,1280]{1,0:T(8,128)(2,1)}, u32[]{:S(2)}, u32[]{:S(2)}) collective-permute-start(bf16[128,1280]{1,0:T(8,128)(2,1)} %get-tuple-element.27), channel_id=1, source_target_pairs={{2,0},{3,1},{6,4},{7,5},{10,8},{11,9},{14,12},{15,13},{18,16},{19,... | collective-permute-start | bytes 983048 | tf_op jit(solution)/shard_map/ppermute | solution.py:27
  90.3 25.0 %collective-permute-start.1 = (bf16[128,1280]{1,0:T(8,128)(2,1)S(1)}, bf16[128,1280]{1,0:T(8,128)(2,1)}, u32[]{:S(2)}, u32[]{:S(2)}) collective-permute-start(bf16[128,1280]{1,0:T(8,128)(2,1)S(1)} %bitcast.168), channel_id=1, source_target_pairs={{2,0},{3,1},{6,4},{7,5},{10,8},{11,9},{14,12},{15,13},{18,16},{19,... | collective-permute-start | bytes 983048 | tf_op jit(solution)/shard_map/ppermute | solution.py:27
  93.6 18.7 %collective-permute-start.15 = (bf16[256,128]{1,0:T(8,128)(2,1)S(1)}, bf16[256,128]{1,0:T(8,128)(2,1)S(1)}, u32[]{:S(2)}, u32[]{:S(2)}) collective-permute-start(bf16[256,128]{1,0:T(8,128)(2,1)S(1)} %bitcast.172), channel_id=1, source_target_pairs={{2,1},{3,0},{6,5},{7,4},{10,9},{11,8},{14,13},{15,12},{18,17},{19,... | collective-permute-start | bytes 196616 | tf_op jit(solution)/shard_map/ppermute | solution.py:27
  96.1 16.2 %collective-permute-start.16 = (bf16[256,128]{1,0:T(8,128)(2,1)S(1)}, bf16[256,128]{1,0:T(8,128)(2,1)S(1)}, u32[]{:S(2)}, u32[]{:S(2)}) collective-permute-start(bf16[256,128]{1,0:T(8,128)(2,1)S(1)} %bitcast.173), channel_id=1, source_target_pairs={{2,5},{3,4},{6,1},{7,0},{10,13},{11,12},{14,9},{15,8},{18,21},{19,... | collective-permute-start | bytes 196616 | tf_op jit(solution)/shard_map/ppermute | solution.py:27
  117.4 10.6 %collective-permute-start.21 = (bf16[128,1280]{1,0:T(8,128)(2,1)S(1)}, bf16[128,1280]{1,0:T(8,128)(2,1)S(1)}, u32[]{:S(2)}, u32[]{:S(2)}) collective-permute-start(bf16[128,1280]{1,0:T(8,128)(2,1)S(1)} %get-tuple-element.26), channel_id=1, source_target_pairs={{0,4},{4,0},{8,12},{12,8},{1,5},{5,1},{9,13},{13,9},{2,6},{6,2},{1... | collective-permute-start | bytes 983048 | tf_op jit(solution)/shard_map/ppermute | solution.py:27
  118.0 16.2 %collective-permute-start.19 = (bf16[128,1280]{1,0:T(8,128)(2,1)S(1)}, bf16[128,1280]{1,0:T(8,128)(2,1)S(1)}, u32[]{:S(2)}, u32[]{:S(2)}) collective-permute-start(bf16[128,1280]{1,0:T(8,128)(2,1)S(1)} %get-tuple-element.25), channel_id=1, source_target_pairs={{0,4},{4,0},{8,12},{12,8},{1,5},{5,1},{9,13},{13,9},{2,6},{6,2},{1... | collective-permute-start | bytes 983048 | tf_op jit(solution)/shard_map/ppermute | solution.py:27
  128.0 7.8 %copy-start.1 = (bf16[128,1280]{1,0:T(8,128)(2,1)}, bf16[128,1280]{1,0:T(8,128)(2,1)S(1)}, u32[]{:S(2)}) copy-start(bf16[128,1280]{1,0:T(8,128)(2,1)S(1)} %get-tuple-element.31) | copy-start | bytes 983044
  128.0 7.8 %copy-start.2 = (bf16[128,1280]{1,0:T(8,128)(2,1)}, bf16[128,1280]{1,0:T(8,128)(2,1)S(1)}, u32[]{:S(2)}) copy-start(bf16[128,1280]{1,0:T(8,128)(2,1)S(1)} %get-tuple-element.32) | copy-start | bytes 983044
  129.0 16.1 %collective-permute-start.22 = (bf16[256,1280]{1,0:T(8,128)(2,1)}, bf16[256,1280]{1,0:T(8,128)(2,1)}, u32[]{:S(2)}, u32[]{:S(2)}) collective-permute-start(bf16[256,1280]{1,0:T(8,128)(2,1)} %pad_maximum_fusion.7), channel_id=1, source_target_pairs={{0,1},{1,0},{2,3},{3,2},{4,5},{5,4},{6,7},{7,6},{8,9},{9,8},{10,11... | collective-permute-start | bytes 1966088 | tf_op jit(solution)/shard_map/ppermute | solution.py:27
  134.2 1.6 copy-start.5
  135.8 10.9 %collective-permute-start.20 = (bf16[256,1280]{1,0:T(8,128)(2,1)}, bf16[256,1280]{1,0:T(8,128)(2,1)}, u32[]{:S(2)}, u32[]{:S(2)}) collective-permute-start(bf16[256,1280]{1,0:T(8,128)(2,1)} %pad_maximum_fusion.6), channel_id=1, source_target_pairs={{0,1},{1,0},{2,3},{3,2},{4,5},{5,4},{6,7},{7,6},{8,9},{9,8},{10,11... | collective-permute-start | bytes 1966088 | tf_op jit(solution)/shard_map/ppermute | solution.py:27
  136.9 27.4 %collective-permute-start.25 = (bf16[128,320]{1,0:T(8,128)(2,1)}, bf16[128,320]{1,0:T(8,128)(2,1)S(1)}, u32[]{:S(2)}, u32[]{:S(2)}) collective-permute-start(bf16[128,320]{1,0:T(8,128)(2,1)} %get-tuple-element.46), channel_id=1, source_target_pairs={{0,4},{4,8},{8,12},{12,0},{1,5},{5,9},{9,13},{13,1},{2,6},{6,10},{... | collective-permute-start | bytes 245768 | tf_op jit(solution)/shard_map/ppermute | solution.py:27
  137.8 26.5 %collective-permute-start.26 = (bf16[128,320]{1,0:T(8,128)(2,1)}, bf16[128,320]{1,0:T(8,128)(2,1)}, u32[]{:S(2)}, u32[]{:S(2)}) collective-permute-start(bf16[128,320]{1,0:T(8,128)(2,1)} %get-tuple-element.45), channel_id=1, source_target_pairs={{0,12},{4,0},{8,4},{12,8},{1,13},{5,1},{9,5},{13,9},{2,14},{6,2},{... | collective-permute-start | bytes 245768 | tf_op jit(solution)/shard_map/ppermute | solution.py:27
  143.3 21.0 %collective-permute-start.27 = (bf16[128,320]{1,0:T(8,128)(2,1)}, bf16[128,320]{1,0:T(8,128)(2,1)}, u32[]{:S(2)}, u32[]{:S(2)}) collective-permute-start(bf16[128,320]{1,0:T(8,128)(2,1)} %get-tuple-element.47), channel_id=1, source_target_pairs={{0,8},{4,12},{8,0},{12,4},{1,9},{5,13},{9,1},{13,5},{2,10},{6,14},... | collective-permute-start | bytes 245768 | tf_op jit(solution)/shard_map/ppermute | solution.py:27
  145.1 1.6 copy-start.6
  149.6 2.0 %copy-start.12 = (bf16[320,640]{1,0:T(8,128)(2,1)S(1)}, bf16[320,640]{1,0:T(8,128)(2,1)}, u32[]{:S(2)}) copy-start(bf16[320,640]{1,0:T(8,128)(2,1)} %get-tuple-element.9) | copy-start | bytes 1228804
  149.6 2.0 %copy-start.18 = (bf16[320,640]{1,0:T(8,128)(2,1)S(1)}, bf16[320,640]{1,0:T(8,128)(2,1)}, u32[]{:S(2)}) copy-start(bf16[320,640]{1,0:T(8,128)(2,1)} %copy-done.17) | copy-start | bytes 1228804
  149.6 2.0 %copy-start.20 = (bf16[320,640]{1,0:T(8,128)(2,1)S(1)}, bf16[320,640]{1,0:T(8,128)(2,1)}, u32[]{:S(2)}) copy-start(bf16[320,640]{1,0:T(8,128)(2,1)} %copy-done.19) | copy-start | bytes 1228804
  149.6 2.0 %copy-start.22 = (bf16[320,640]{1,0:T(8,128)(2,1)S(1)}, bf16[320,640]{1,0:T(8,128)(2,1)}, u32[]{:S(2)}) copy-start(bf16[320,640]{1,0:T(8,128)(2,1)} %copy-done.21) | copy-start | bytes 1228804
  153.8 3.6 %collective-permute-start.23 = (f32[128]{0:T(128)S(1)}, f32[128]{0:T(128)S(1)}, u32[]{:S(2)}, u32[]{:S(2)}) collective-permute-start(f32[128]{0:T(128)S(1)} %fusion.59), channel_id=1, source_target_pairs={{0,4},{4,0},{8,12},{12,8},{1,5},{5,1},{9,13},{13,9},{2,6},{6,2},{1... | collective-permute-start | bytes 1544 | tf_op jit(solution)/shard_map/ppermute | solution.py:27
  154.6 4.3 %collective-permute-start.29 = (bf16[256,128]{1,0:T(8,128)(2,1)S(1)}, bf16[256,128]{1,0:T(8,128)(2,1)S(1)}, u32[]{:S(2)}, u32[]{:S(2)}) collective-permute-start(bf16[256,128]{1,0:T(8,128)(2,1)S(1)} %bitcast_select_fusion.2), channel_id=1, source_target_pairs={{0,12},{4,0},{8,4},{12,8},{1,13},{5,1},{9,5},{13,9},{2,14},{6,2},{... | collective-permute-start | bytes 196616 | tf_op jit(solution)/shard_map/ppermute | solution.py:27
  157.4 6.1 %collective-permute-start.30 = (bf16[256,128]{1,0:T(8,128)(2,1)S(1)}, bf16[256,128]{1,0:T(8,128)(2,1)S(1)}, u32[]{:S(2)}, u32[]{:S(2)}) collective-permute-start(bf16[256,128]{1,0:T(8,128)(2,1)S(1)} %bitcast_select_fusion.2), channel_id=1, source_target_pairs={{0,4},{4,8},{8,12},{12,0},{1,5},{5,9},{9,13},{13,1},{2,6},{6,10},{... | collective-permute-start | bytes 196616 | tf_op jit(solution)/shard_map/ppermute | solution.py:27
  158.9 5.2 %collective-permute-start.28 = (bf16[256,128]{1,0:T(8,128)(2,1)S(1)}, bf16[256,128]{1,0:T(8,128)(2,1)S(1)}, u32[]{:S(2)}, u32[]{:S(2)}) collective-permute-start(bf16[256,128]{1,0:T(8,128)(2,1)S(1)} %bitcast_select_fusion.2), channel_id=1, source_target_pairs={{0,8},{4,12},{8,0},{12,4},{1,9},{5,13},{9,1},{13,5},{2,10},{6,14},... | collective-permute-start | bytes 196616 | tf_op jit(solution)/shard_map/ppermute | solution.py:27
  163.4 2.0 %collective-permute-start.24 = (f32[128]{0:T(128)S(1)}, f32[128]{0:T(128)S(1)}, u32[]{:S(2)}, u32[]{:S(2)}) collective-permute-start(f32[128]{0:T(128)S(1)} %fusion.57), channel_id=1, source_target_pairs={{0,1},{1,0},{2,3},{3,2},{4,5},{5,4},{6,7},{7,6},{8,9},{9,8},{10,11... | collective-permute-start | bytes 1544 | tf_op jit(solution)/shard_map/ppermute | solution.py:27
  164.2 1.7 %collective-permute-start.31 = (bf16[512,256]{1,0:T(8,128)(2,1)S(1)}, bf16[512,256]{1,0:T(8,128)(2,1)S(1)}, u32[]{:S(2)}, u32[]{:S(2)}) collective-permute-start(bf16[512,256]{1,0:T(8,128)(2,1)S(1)} %pad_maximum_fusion.14), channel_id=1, source_target_pairs={{0,1},{1,0},{2,3},{3,2},{4,5},{5,4},{6,7},{7,6},{8,9},{9,8},{10,11... | collective-permute-start | bytes 786440 | tf_op jit(solution)/shard_map/ppermute | solution.py:27
  (7 other events, 7.1 us)

commit v4 on v0

v4 whole, which is shorter than its diff:
```python
import functools
import itertools
import math

import jax
import jax.numpy as jnp
from jax import lax
from jax.experimental import pallas as pl
from jax.experimental.pallas import tpu as pltpu
from jax.sharding import PartitionSpec as P

DW = 2560
HD = 128
QH = 20
KVH = 4
EPS = 0.25
F32 = jnp.float32
BF16 = jnp.bfloat16


def stabilize(entries):
    return jnp.where(entries >= 0, entries + EPS, entries - EPS)


VMEM = pl.BlockSpec(memory_space=pltpu.VMEM)
SMEM = pl.BlockSpec(memory_space=pltpu.SMEM)
ANY = pl.BlockSpec(memory_space=pl.ANY)


def by_columns(left, right):
    return lax.dot_general(left, right, (((1,), (1,)), ((), ())), preferred_element_type=F32)


def kernel_call(body, shapes, in_specs, scratch=(), flops=0, nbytes=0, limit=24):
    return pl.pallas_call(
        body,
        out_shape=shapes,
        in_specs=in_specs,
        out_specs=jax.tree.map(lambda _: VMEM, shapes),
        scratch_shapes=scratch,
        compiler_params=pltpu.CompilerParams(vmem_limit_bytes=limit * 2**20),
        cost_estimate=pl.CostEstimate(flops=flops, bytes_accessed=nbytes, transcendentals=0),
    )


def attention_kernel(length, queries, keys, values, probs_t, mixed_gain, value_gain):
    seq_len = queries.shape[0]
    kv_heads = keys.shape[1] // HD
    group_size = queries.shape[1] // HD // kv_heads
    row = lax.broadcasted_iota(jnp.int32, (seq_len, seq_len), 0)
    column = lax.broadcasted_iota(jnp.int32, (seq_len, seq_len), 1)
    allowed = (column <= row) & (column < length[0])
    values_bf = values[...].astype(BF16)
    values_r = values_bf.astype(F32)
    value_gain[...] = values_r / stabilize(values_r)
    for g in range(kv_heads):
        key_head = keys[:, g * HD : (g + 1) * HD]
        value_head = values_bf[:, g * HD : (g + 1) * HD]
        for h in range(g * group_size, (g + 1) * group_size):
            scores = by_columns(queries[:, h * HD : (h + 1) * HD], key_head) / math.sqrt(HD)
            scores = jnp.where(allowed, scores, -1000000000.0)
            weights = jnp.exp(scores - jnp.max(scores, axis=1, keepdims=True))
            probs = weights / jnp.sum(weights, axis=1, keepdims=True)
            probs_t[h] = probs.T.astype(BF16)
            mixed = jnp.dot(probs.astype(BF16), value_head, preferred_element_type=F32)
            mixed_gain[:, h * HD : (h + 1) * HD] = mixed / stabilize(mixed)


def attend(length, queries, keys, values):
    seq_len, width = queries.shape
    shapes = (
        jax.ShapeDtypeStruct((width // HD, seq_len, seq_len), BF16),
        jax.ShapeDtypeStruct((seq_len, width), F32),
        jax.ShapeDtypeStruct(values.shape, F32),
    )
    call = kernel_call(
        attention_kernel, shapes, [SMEM, VMEM, VMEM, VMEM], flops=10**8, nbytes=3 * 10**6
    )
    return call(length, queries, keys, values)


def head_step(back_mixed, probs_t, mixed_gain, value_gain, found):
    heads = probs_t.shape[0]
    kv_heads = value_gain.shape[1] // HD
    group_size = heads // kv_heads
    for g in range(kv_heads):
        total = jnp.zeros((probs_t.shape[1], HD), F32)
        for h in range(g * group_size, (g + 1) * group_size):
            at = slice(h * HD, (h + 1) * HD)
            sens_mixed = (mixed_gain[:, at] * back_mixed[:, at]).astype(BF16)
            total += jnp.dot(probs_t[h], sens_mixed, preferred_element_type=F32)
        at = slice(g * HD, (g + 1) * HD)
        found[:, at] = (value_gain[:, at] * total).astype(BF16)


def sum_heads_kernel(count, product, *refs):
    backs, (probs_t, mixed_gain, value_gain, found, total) = refs[:count], refs[count:]
    back_mixed = product[...]
    for back in backs:
        back_mixed += back[...].astype(F32)
    total[...] = back_mixed
    head_step(total, probs_t, mixed_gain, value_gain, found)


def sum_heads(product, backs, probs_t, mixed_gain, value_gain):
    call = kernel_call(
        functools.partial(sum_heads_kernel, len(backs)),
        jax.ShapeDtypeStruct(value_gain.shape, BF16),
        [VMEM] * (4 + len(backs)),
        [pltpu.VMEM(product.shape, F32)],
        flops=5 * 10**7,
        nbytes=3 * 10**6,
    )
    return call(product, *backs, probs_t, mixed_gain, value_gain)


def sensitivity_kernel(length, inputs, branch, *refs):
    current, sens = refs if len(refs) == 2 else (None, refs[0])
    inputs_f = inputs[...].astype(F32)
    branch_f = branch[...].astype(F32)
    totals = inputs_f + branch_f
    if current is None:
        row = lax.broadcasted_iota(jnp.int32, totals.shape, 0)
        entering = jnp.where(row < length[0], totals, 0.0).astype(BF16).astype(F32)
    else:
        entering = current[...].astype(F32)
    sens[...] = (branch_f * (entering / stabilize(totals)) / stabilize(branch_f)).astype(BF16)


def sensitivity(length, inputs, branch, *current):
    call = kernel_call(
        sensitivity_kernel,
        jax.ShapeDtypeStruct(inputs.shape, BF16),
        [SMEM] + [VMEM] * (2 + len(current)),
        flops=10**7,
        nbytes=10**6,
    )
    return call(length, inputs, branch, *current)


def outgoing_kernel(place, inputs, branch, sens_own, sens_other, value_rows, outgoing):
    core, length = place[0], place[1]
    width = sens_own.shape[1]
    inputs_f = inputs[...].astype(F32)
    totals = inputs_f + branch[...].astype(F32)
    row = lax.broadcasted_iota(jnp.int32, totals.shape, 0)
    entering = jnp.where(row < length, totals, 0.0).astype(BF16).astype(F32)
    own = value_rows[:, pl.ds(pl.multiple_of(core * width, 128), width)]
    other = value_rows[:, pl.ds(pl.multiple_of((1 - core) * width, 128), width)]
    back_inputs = by_columns(sens_own[...], own) + by_columns(sens_other[...], other)
    kept = inputs_f * (entering / stabilize(totals))
    outgoing[...] = (kept + inputs_f * back_inputs).astype(BF16)


def last_outgoing(place, inputs, branch, sens_own, sens_other, value_rows):
    call = kernel_call(
        outgoing_kernel,
        jax.ShapeDtypeStruct(inputs.shape, BF16),
        [SMEM] + [VMEM] * 5,
        flops=2 * 10**8,
        nbytes=2 * 10**6,
    )
    return call(place, inputs, branch, sens_own, sens_other, value_rows)


def product_kernel(use_mine, mine, theirs, block, own, *backs):
    seq_len = own.shape[0]

    def multiply(operand):
        product = by_columns(operand[...], block[...])
        own[...] = product[:seq_len]
        for k, back in enumerate(backs):
            back[...] = product[(k + 1) * seq_len : (k + 2) * seq_len].astype(BF16)

    @pl.when(use_mine[0] == 1)
    def _():
        multiply(mine)

    @pl.when(use_mine[0] == 0)
    def _():
        multiply(theirs)


def spread_products(use_mine, mine, theirs, block, seq_len):
    count = mine.shape[0] // seq_len
    width = block.shape[0]
    shapes = (jax.ShapeDtypeStruct((seq_len, width), F32),) + tuple(
        jax.ShapeDtypeStruct((seq_len, width), BF16) for _ in range(count - 1)
    )
    call = kernel_call(
        product_kernel, shapes, [SMEM, VMEM, VMEM, VMEM], flops=10**9, nbytes=5 * 10**6, limit=32
    )
    return call(use_mine, mine, theirs, block)


def main_kernel(layout, place, sens_own, sens_other, out_block, *refs):
    count = len(layout)
    pieces = refs[:count]
    probs_t, mixed_gain, value_gain, found, halves, total, block, sem = refs[count : count + 8]
    held, sems = refs[count + 8 :][:count], refs[count + 8 + count]
    pos, core, group = place[0], place[1], place[2]
    width = out_block.shape[1]
    per_core = sens_own.shape[1] // width
    copies = [pltpu.make_async_copy(out_block, block, sem)]
    copies += [pltpu.make_async_copy(pieces[i], held[i], sems.at[i]) for i in range(count)]
    for copy in copies:
        copy.start()
    halves[core] = sens_own[...]
    halves[1 - core] = sens_other[...]

    def part(slot):
        owner = pos ^ slot
        start = pl.multiple_of(lax.rem(owner, per_core) * width, 128)
        return halves[owner // per_core, :, pl.ds(start, width)]

    copies[0].wait()
    total[...] = by_columns(part(0), block[...])
    for i, (slot, side, start) in enumerate(layout):
        copies[i + 1].wait()
        rows = held[i].shape[0]
        at = (group if side == 0 else 1 - group) * (total.shape[1] // 2) + start
        total[:, pl.ds(pl.multiple_of(at, 128), rows)] += by_columns(part(slot), held[i][...])
    head_step(total, probs_t, mixed_gain, value_gain, found)


def main_step(place, sens_own, sens_other, out_block, slots, probs_t, mixed_gain, value_gain):
    layout, pieces = [], []
    for k, sides in enumerate(slots):
        for side in range(2):
            start = 0
            for piece in sides[side]:
                layout.append((k + 1, side, start))
                pieces.append(piece)
                start += piece.shape[0]
    seq_len, half_width = sens_own.shape
    call = kernel_call(
        functools.partial(main_kernel, tuple(layout)),
        jax.ShapeDtypeStruct(value_gain.shape, BF16),
        [SMEM, VMEM, VMEM, ANY] + [ANY] * len(pieces) + [VMEM] * 3,
        [
            pltpu.VMEM((2, seq_len, half_width), BF16),
            pltpu.VMEM(mixed_gain.shape, F32),
            pltpu.VMEM(out_block.shape, BF16),
            pltpu.SemaphoreType.DMA,
        ]
        + [pltpu.VMEM(piece.shape, BF16) for piece in pieces]
        + [pltpu.SemaphoreType.DMA((len(pieces),))],
        flops=10**9,
        nbytes=8 * 10**6,
        limit=32,
    )
    return call(place, sens_own, sens_other, out_block, *pieces, probs_t, mixed_gain, value_gain)


def moved(shard, axes, target):
    sizes = [lax.axis_size(axis) for axis in axes]
    places = list(itertools.product(*[range(size) for size in sizes]))
    index = {place: i for i, place in enumerate(places)}
    pairs = [(index[place], index[target(*place)]) for place in places if target(*place) is not None]
    return lax.ppermute(shard, axes, pairs)


def along_dp(shard, by):
    peers = lax.axis_size("dp")
    return moved(shard, ("dp",), lambda i: ((i + by) % peers,)) if by else shard


def other_core(shard):
    return moved(shard, ("mp",), lambda c: (1 - c,))


def from_next_section(shard):
    return moved(shard, ("section",), lambda s: (s - 1,) if s > 0 else None)


def ordered(first_is_mine, mine, theirs, axis):
    return jnp.concatenate(
        [jnp.where(first_is_mine, mine, theirs), jnp.where(first_is_mine, theirs, mine)], axis
    )


def part_of(array, index, width, axis):
    return lax.dynamic_slice_in_dim(array, index * width, width, axis)


def once(array, *others):
    return lax.optimization_barrier((array,) + others)[0]


def early_move(shard, axes, target):
    last = lax.axis_size("section") - 1
    at = axes.index("section")
    return moved(shard, axes, lambda *place: target(*place) if place[at] < last else None)


def between(shard, pairs):
    return early_move(shard, ("dp", "section"), lambda i, s: (pairs[i], s) if i in pairs else None)


def swap_groups(shard):
    return early_move(shard, ("groups", "section"), lambda g, s: (1 - g, s))


MIDDLE = {1: 2, 2: 1}
OUTWARD = {1: 0, 2: 3}


def start_gather(mine, *others):
    peers = lax.axis_size("dp")
    pos = lax.axis_index("dp")
    if peers != 4:
        return [between(mine, {i: i ^ k for i in range(peers)}) for k in range(1, peers)]
    pair = between(mine, {i: i ^ 1 for i in range(peers)})
    near = between(mine, MIDDLE)
    pair, near, *_ = lax.optimization_barrier((pair, near, *others))
    crossed = between(pair, MIDDLE)
    relayed = between(near, OUTWARD)
    pair_swapped = swap_groups(pair)
    second = jnp.where((pos == 1) | (pos == 2), crossed, relayed)
    return [pair, pair_swapped, second, near]


def finish_gather(started):
    peers = lax.axis_size("dp")
    pos = lax.axis_index("dp")
    if peers != 4:
        return [([block], [swap_groups(block)]) for block in started]
    pair, pair_swapped, second, near = started
    cut = [second.shape[0] * 3 // 5]
    third = [
        jnp.where((pos == 1) | (pos == 2), direct, between(far, OUTWARD))
        for direct, far in zip(jnp.split(near, cut), jnp.split(second, cut))
    ]
    return [
        ([pair], [pair_swapped]),
        ([second], [swap_groups(second)]),
        (third, [swap_groups(piece) for piece in third]),
    ]


def spread_product(sens_branch, out_block):
    axes = ("dp", "section", "mp")
    peers, cores = lax.axis_size("dp"), lax.axis_size("mp")
    last = lax.axis_size("section") - 1
    pos, core = lax.axis_index("dp"), lax.axis_index("mp")
    seq_len = sens_branch.shape[0]
    width = out_block.shape[1]
    per_core = peers // cores
    arrived = []
    for k in range(peers):
        to = lax.rem(pos + k, peers)
        part = part_of(sens_branch, lax.rem(to, per_core), width, 1)
        if k:
            part = moved(
                part,
                axes,
                lambda i, s, c: ((i + k) % peers, s, c)
                if s == last and c == (i + k) % peers // per_core
                else None,
            )
        arrived.append(part)
    mine = jnp.concatenate(arrived, 0)
    theirs = moved(
        mine,
        axes,
        lambda i, s, c: (i, s, 1 - c) if s == last and c == i // per_core else None,
    )
    if width % 128 == 0:
        use_mine = (core == pos // per_core).astype(jnp.int32)[None]
        own, *sent = spread_products(use_mine, mine, theirs, out_block, seq_len)
    else:
        product = by_columns(jnp.where(core == pos // per_core, mine, theirs), out_block)
        own, *sent = jnp.split(product, peers, axis=0)
    backs = [
        moved(
            sent[k - 1].astype(BF16),
            axes,
            lambda i, s, c: ((i - k) % peers, s, c) if s == last else None,
        )
        for k in range(1, peers)
    ]
    return own, backs


def on_device(hidden_in, attn_out, queries, keys, value_weight, out_weight, lengths):
    inputs = hidden_in[0, 0]
    branch = attn_out[0, 0]
    query_rows = queries[0, 0]
    key_rows = keys[0, 0]
    value_rows = value_weight[0]
    out_block = out_weight[0]
    seq_len, half_width = inputs.shape
    kv_width = key_rows.shape[1]
    sections = lax.axis_size("section")
    section_pos = lax.axis_index("section")
    group_pos = lax.axis_index("groups")
    peers = lax.axis_size("dp")
    dp_pos = lax.axis_index("dp")
    core_pos = lax.axis_index("mp")
    head_rows, block_width = out_block.shape
    is_last = section_pos == sections - 1

    totals = inputs.astype(F32) + branch.astype(F32)
    valid_rows = (lax.iota(jnp.int32, seq_len) < lengths[0]).astype(F32)
    current = (totals * valid_rows[:, None]).astype(BF16)

    def kept_of(entering):
        return inputs.astype(F32) * (entering.astype(F32) / stabilize(totals))

    def core_exchange(mine, take):
        return moved(
            mine, ("section", "mp"), lambda s, c: (s, 1 - c) if take(s == sections - 1) else None
        )

    def attention(take):
        value_part = jnp.dot(inputs, value_rows, preferred_element_type=F32)
        part_mine = part_of(value_part, core_pos, kv_width, 1)
        part_other = part_of(value_part, 1 - core_pos, kv_width, 1)
        values_f = part_mine + core_exchange(part_other.astype(BF16), take).astype(F32)
        return values_f, attend(lengths, query_rows, key_rows, values_f)

    block_rows = half_width // peers

    def inputs_of_all(rows, take):
        pieces = []
        for k in range(peers):
            piece = part_of(rows, lax.rem(dp_pos + k, peers), block_rows, 1)
            if k:
                piece = moved(
                    piece,
                    ("dp", "section"),
                    lambda i, s: ((i + k) % peers, s) if take(s == sections - 1) else None,
                )
            pieces.append(piece)
        return jnp.concatenate(pieces, 0)

    def last_section():
        values_f, rest = attention(lambda last: last)
        sens_branch = sensitivity(lengths, inputs, branch)
        own, backs = spread_product(sens_branch, out_block)
        all_inputs = inputs_of_all(inputs, lambda last: last)
        started = [jnp.zeros(leaf.shape, leaf.dtype) for leaf in early_shapes[-1]]
        own, all_inputs, *started = lax.optimization_barrier((own, all_inputs, *started))
        if peers > 4:
            for back in backs:
                own = own + back.astype(F32)
            backs = []
        found = sum_heads(own, backs, *rest)
        other = core_exchange(found, lambda last: last)
        place = jnp.stack([core_pos, lengths[0]])
        outgoing = last_outgoing(place, inputs, branch, found, other, value_rows)
        return values_f, rest, found, outgoing, all_inputs, started

    def early_section():
        mine = part_of(out_block, group_pos, head_rows // 2, 0)
        all_inputs = inputs_of_all(inputs, lambda last: not last)
        values_f, rest = attention(lambda last: not last)
        started = start_gather(mine, values_f, *rest, all_inputs)
        found = jnp.zeros((seq_len, kv_width), BF16)
        outgoing = jnp.zeros((seq_len, half_width), BF16)
        return values_f, rest, found, outgoing, all_inputs, started

    early_shapes = jax.eval_shape(early_section)
    values_f, rest, sens_values, outgoing, all_inputs, started = lax.cond(
        is_last, last_section, early_section
    )
    arrived = from_next_section(outgoing)
    slots = finish_gather(started)

    for turn in range(1, sections):
        active = section_pos == sections - 1 - turn
        current = jnp.where(active, arrived, current)
        sens_branch = sensitivity(lengths, inputs, branch, current)
        sens_other = core_exchange(sens_branch, lambda last: not last)
        if block_width % 128 == 0:
            place = jnp.stack([dp_pos, core_pos, group_pos])
            found = main_step(place, sens_branch, sens_other, out_block, slots, *rest)
        else:
            share = head_rows // 2
            own_rows = part_of(out_block, group_pos, share, 0)
            other_rows = part_of(out_block, 1 - group_pos, share, 0)
            sens_full = ordered(core_pos == 0, sens_branch, sens_other, 1)
            halves = [jnp.zeros((seq_len, share), F32) for _ in range(2)]
            for k, blocks in enumerate([([own_rows], [other_rows])] + slots):
                part = part_of(sens_full, dp_pos ^ k, block_width, 1)
                for side in range(2):
                    halves[side] += jnp.concatenate(
                        [by_columns(part, piece) for piece in blocks[side]], 1
                    )
            found = sum_heads(ordered(group_pos == 0, halves[0], halves[1], 1), [], *rest)
        sens_values = jnp.where(active, found, sens_values)
        if turn + 1 < sections:
            sens_all = ordered(
                core_pos == 0, found, core_exchange(found, lambda last: not last), 1
            )
            back_inputs = by_columns(sens_all, value_rows)
            outgoing = kept_of(current) + inputs.astype(F32) * back_inputs
            arrived = from_next_section(outgoing.astype(BF16))

    heat_part = jnp.sum(kept_of(current), axis=1)
    heat_part += jnp.sum(sens_values.astype(F32) * values_f, axis=1)
    heat_rows = (heat_part + other_core(heat_part)) / DW

    mine = jnp.concatenate([along_dp(sens_values, k) for k in range(peers)], 0)
    all_sens = ordered(core_pos == 0, mine, other_core(mine), 1)
    summed = lax.dot_general(
        all_inputs, all_sens, (((0,), (0,)), ((), ())), preferred_element_type=F32
    )
    value_block = part_of(value_rows, dp_pos, block_rows, 0)
    relevance_rows = value_block.astype(F32) * summed
    return (heat_rows[None, None, :], relevance_rows[None])


def solution(mesh):
    placed = (
        P("section", ("groups", "dp"), None, "mp"),
        P("section", ("groups", "dp"), None, "mp"),
        P("section", ("groups", "dp"), None, "mp"),
        P("section", ("groups", "dp"), None, "mp"),
        P("section", "mp", None),
        P("section", "mp", "dp"),
        P(("groups", "dp")),
    )
    return jax.shard_map(
        on_device,
        mesh=mesh,
        in_specs=placed,
        out_specs=(
            P("section", ("groups", "dp"), None),
            P(("groups", "section"), ("mp", "dp"), None),
        ),
        check_vma=False,
    )
```

time: 223 us -> 128 us (0.57)
  waiting for transfers between devices: 163 us -> 47.4 us
  starting transfers between devices: 1.4 us -> 50.3 us
  between operations: 16.3 us -> 1.46 us
  Pallas kernels: 0 us -> 11.9 us
  blocking collectives: 11.5 us -> 0 us
  matrix products: 11.5 us -> 2.52 us
  local copies, waits for them, and re-layouts: 11.4 us -> 6.68 us
    all_gather x1 -> x0, waiting for transfers between devices: 102 us -> none  [on_device(): out_cols = lax.all_gather(out_weight, 'dp', axis=2, tiled=True)[0]]
    ppermute x1 -> x21, starting transfers between devices: 1.28 us -> 50.3 us  [moved(): return lax.ppermute(shard, axes, pairs)]
    ppermute x1 -> x21, waiting for transfers between devices: 23.3 us -> 47.4 us  [moved(): return lax.ppermute(shard, axes, pairs)]
    unnamed x4 -> x0, waiting for transfers between devices: 22.7 us -> none
    psum x1 -> x0, waiting for transfers between devices: 15.4 us -> none  [on_device(): lax.psum(value_part.astype(jnp.bfloat16), 'mp').astype(jnp.float32)]
    pallas_call x0 -> x3, Pallas kernels: none -> 11.9 us  [the longest x1 6.58 us: main_step(): call(place, sens_own, sens_other, out_block, *pieces, probs_t, mixed_gain...]
    all_gather x4 -> x0, blocking collectives: 9.04 us -> none  [the longest x2 4.87 us: on_device(): sens_full = lax.all_gather(sens_branch, 'mp', axis=1, tiled=True)]
    dot_general x6 -> x2, matrix products: 11.1 us -> 2.52 us  [the longest x1 2.18 us: on_device(): lax.dot_general(all_inputs, all_sens, (((0,), (0,)), ((), ())), preferred...]
  transfers between devices with their start and end apart: 4 -> 21, of which waited for: 4 -> 11; matrix products, arithmetic and copies ran while one was open for 3% -> 6% of each run, Pallas kernels for 0% -> 4%
where the time goes in v4:
time: 128 us; the launch traced here: 127 us
  starting transfers between devices  50.3 us (39%)
  waiting for transfers between devices  47.4 us (37%)
  Pallas kernels  11.9 us (9%)
  local copies, waits for them, and re-layouts  6.68 us (5%)
  other arithmetic  6.29 us (5%)
  matrix products  2.52 us (2%)
  between operations  1.46 us (1%)
    ppermute x21, starting transfers between devices, moved(): return lax.ppermute(shard, axes, pairs)  50.3 us
    ppermute x21, waiting for transfers between devices, moved(): return lax.ppermute(shard, axes, pairs)  47.4 us
    pallas_call x1, Pallas kernels, main_step(): call(place, sens_own, sens_other, out_block, *pieces, probs_t, mixed_gain...  6.58 us
    pallas_call x1, Pallas kernels, attend(): return call(length, queries, keys, values)  4.93 us
    split x2, local copies, waits for them, and re-layouts, finish_gather(): jnp.split(second, cut)  2.8 us
  transfers between devices with their start and end apart: 21, of which 11 were waited for; matrix products, arithmetic and copies ran while one was open for 6% of the time, Pallas kernels for 4%

profile of v4, /device:TPU:0, one launch (start us, length us, event | category | flops | bytes accessed | tf_op | source)
XLA Modules:
  0.0 126.8 jit_solution(12353429862166225955)
XLA Ops:
  0.6 62.5 %conditional.1 = (f32[128,256]{1,0:T(8,128)S(1)}, bf16[10,128,128]{2,1,0:T(8,128)(2,1)}, f32[128,1280]{1,0:T(8,128)}, f32[128,256]{1,0:T(8,128)S(1)}, bf16[128,2...) conditional(s32[]{:T(128)} %convert_element_type.46, ...), branch_computations={%region_0.1_spmd, %region_1.2_spmd} | conditional | flops 1531769856 | bytes 59386080 | solution.py:464
  0.7 2.2 %constant_dynamic-slice_fusion = bf16[640,640]{1,0:T(8,128)(2,1)} fusion(bf16[1280,640]{1,0:T(8,128)(2,1)} %get-tuple-element.46, s32[]{:T(128)S(6)} %select_n.88), kind=kLoop, calls=%fused_computation.4 | loop fusion | bytes 1638404 | tf_op jit(solution)/shard_map/cond/branch_0_fun/dynamic_slice | solution.py:283
  2.9 4.9 %collective-permute-start.4 = (bf16[640,640]{1,0:T(8,128)(2,1)}, bf16[640,640]{1,0:T(8,128)(2,1)S(1)}, u32[]{:S(2)}, u32[]{:S(2)}) collective-permute-start(bf16[640,640]{1,0:T(8,128)(2,1)} %constant_dynamic-slice_fusion), channel_id=1, source_target_pairs={{0,4},{4,0},{8,12},{12,8},{1,5},{5,1},{9,13},{13,9},{16,20},{20,16... | collective-permute-start | bytes 2457608 | tf_op jit(solution)/shard_map/cond/branch_0_fun/ppermute | solution.py:260
  7.8 1.6 %collective-permute-start.5 = (bf16[640,640]{1,0:T(8,128)(2,1)}, bf16[640,640]{1,0:T(8,128)(2,1)}, u32[]{:S(2)}, u32[]{:S(2)}) collective-permute-start(bf16[640,640]{1,0:T(8,128)(2,1)} %constant_dynamic-slice_fusion), channel_id=1, source_target_pairs={{4,8},{8,4},{5,9},{9,5},{20,24},{24,20},{21,25},{25,21}} | collective-permute-start | bytes 2457608 | tf_op jit(solution)/shard_map/cond/branch_0_fun/ppermute | solution.py:260
  9.4 0.3 fusion.9
  9.8 1.9 %collective-permute-start = (bf16[128,256]{1,0:T(8,128)(2,1)S(1)}, bf16[128,256]{1,0:T(8,128)(2,1)S(1)}, u32[]{:S(2)}, u32[]{:S(2)}) collective-permute-start(bf16[128,256]{1,0:T(8,128)(2,1)S(1)} %dynamic-slice_convert_fusion), channel_id=1, source_target_pairs={{0,1},{1,0},{4,5},{5,4},{8,9},{9,8},{12,13},{13,12},{16,17},{17,16... | collective-permute-start | bytes 196616 | tf_op jit(solution)/shard_map/cond/branch_0_fun/ppermute | solution.py:260
  12.0 5.4 %collective-permute-start.1 = (bf16[128,320]{1,0:T(8,128)(2,1)S(1)}, bf16[128,320]{1,0:T(8,128)(2,1)S(1)}, u32[]{:S(2)}, u32[]{:S(2)}) collective-permute-start(bf16[128,320]{1,0:T(8,128)(2,1)S(1)} %get-tuple-element.103), channel_id=1, source_target_pairs={{0,4},{4,8},{8,12},{12,0},{1,5},{5,9},{9,13},{13,1},{16,20},{20,24... | collective-permute-start | bytes 245768 | tf_op jit(solution)/shard_map/cond/branch_0_fun/ppermute | solution.py:260
  17.4 1.9 %collective-permute-start.2 = (bf16[128,320]{1,0:T(8,128)(2,1)S(1)}, bf16[128,320]{1,0:T(8,128)(2,1)S(1)}, u32[]{:S(2)}, u32[]{:S(2)}) collective-permute-start(bf16[128,320]{1,0:T(8,128)(2,1)S(1)} %get-tuple-element.102), channel_id=1, source_target_pairs={{0,8},{4,12},{8,0},{12,4},{1,9},{5,13},{9,1},{13,5},{16,24},{20,28... | collective-permute-start | bytes 245768 | tf_op jit(solution)/shard_map/cond/branch_0_fun/ppermute | solution.py:260
  19.4 4.3 %collective-permute-start.3 = (bf16[128,320]{1,0:T(8,128)(2,1)S(1)}, bf16[128,320]{1,0:T(8,128)(2,1)S(1)}, u32[]{:S(2)}, u32[]{:S(2)}) collective-permute-start(bf16[128,320]{1,0:T(8,128)(2,1)S(1)} %get-tuple-element.101), channel_id=1, source_target_pairs={{0,12},{4,0},{8,4},{12,8},{1,13},{5,1},{9,5},{13,9},{16,28},{20,16... | collective-permute-start | bytes 245768 | tf_op jit(solution)/shard_map/cond/branch_0_fun/ppermute | solution.py:260
  23.7 4.9 %branch_0_fun.1 = (bf16[10,128,128]{2,1,0:T(8,128)(2,1)}, f32[128,1280]{1,0:T(8,128)}, f32[128,256]{1,0:T(8,128)S(1)}) custom-call(s32[1]{0:T(128)} %get-tuple-element.39.length, bf16[128,1280]{1,0:T(8,128)(2,1)S(1)} %copy-done.13, bf16[128,256]{1,0:T(8,128)(2,1)S(1)} %copy-done.18, f32[128,256]{1,0:T(8,128)S(1)} %convert_add_fusion.values), custom_call_target="tpu_custom_call" | custom-call | flops 100000000 | bytes 3000000 | tf_op jit(solution)/shard_map/cond/branch_0_fun/pallas_call | solution.py:79
  28.6 3.1 %collective-permute-done.1 = bf16[128,320]{1,0:T(8,128)(2,1)S(1)} collective-permute-done((bf16[128,320]{1,0:T(8,128)(2,1)S(1)}, bf16[128,320]{1,0:T(8,128)(2,1)S(1)}, u32[]{:S(2)}, u32[]{:S(2)}) %collective-permute-start.1) | collective-permute-done | bytes 81952 | tf_op jit(solution)/shard_map/cond/branch_0_fun/ppermute | solution.py:260
  31.8 6.1 %collective-permute-done.2 = bf16[128,320]{1,0:T(8,128)(2,1)S(1)} collective-permute-done((bf16[128,320]{1,0:T(8,128)(2,1)S(1)}, bf16[128,320]{1,0:T(8,128)(2,1)S(1)}, u32[]{:S(2)}, u32[]{:S(2)}) %collective-permute-start.2) | collective-permute-done | bytes 81952 | tf_op jit(solution)/shard_map/cond/branch_0_fun/ppermute | solution.py:260
  37.9 0.8 pad_maximum_fusion
  38.7 0.7 collective-permute-start.7
  39.4 1.3 %collective-permute-start.8 = (bf16[640,640]{1,0:T(8,128)(2,1)}, bf16[640,640]{1,0:T(8,128)(2,1)S(1)}, u32[]{:S(2)}, u32[]{:S(2)}) collective-permute-start(bf16[640,640]{1,0:T(8,128)(2,1)} %collective-permute-done.5), channel_id=1, source_target_pairs={{4,0},{8,12},{5,1},{9,13},{20,16},{24,28},{21,17},{25,29}} | collective-permute-start | bytes 2457608 | tf_op jit(solution)/shard_map/cond/branch_0_fun/ppermute | solution.py:260
  40.7 3.4 %collective-permute-start.6 = (bf16[640,640]{1,0:T(8,128)(2,1)S(1)}, bf16[640,640]{1,0:T(8,128)(2,1)}, u32[]{:S(2)}, u32[]{:S(2)}) collective-permute-start(bf16[640,640]{1,0:T(8,128)(2,1)S(1)} %collective-permute-done.4), channel_id=1, source_target_pairs={{0,16},{16,0},{1,17},{17,1},{4,20},{20,4},{5,21},{21,5},{8,24},{24... | collective-permute-start | bytes 2457608 | tf_op jit(solution)/shard_map/cond/branch_0_fun/ppermute | solution.py:260
  44.1 16.6 %collective-permute-done.8 = bf16[640,640]{1,0:T(8,128)(2,1)S(1)} collective-permute-done((bf16[640,640]{1,0:T(8,128)(2,1)}, bf16[640,640]{1,0:T(8,128)(2,1)S(1)}, u32[]{:S(2)}, u32[]{:S(2)}) %collective-permute-start.8) | collective-permute-done | bytes 819232 | tf_op jit(solution)/shard_map/cond/branch_0_fun/ppermute | solution.py:260
  60.8 1.0 broadcast_select_fusion
  61.8 0.8 broadcast.33
  62.5 0.6 broadcast.32
  63.1 1.7 %split.15 = bf16[256,640]{1,0:T(8,128)(2,1)} slice(bf16[640,640]{1,0:T(8,128)(2,1)} %get-tuple-element.88.refs_2_), slice={[384:640], [0:640]} | slice | bytes 655360 | tf_op jit(solution)/shard_map/split | solution.py:332
  64.9 1.3 %collective-permute-start.25 = (bf16[256,640]{1,0:T(8,128)(2,1)}, bf16[256,640]{1,0:T(8,128)(2,1)S(1)}, u32[]{:S(2)}, u32[]{:S(2)}) collective-permute-start(bf16[256,640]{1,0:T(8,128)(2,1)} %split.15), channel_id=1, source_target_pairs={{4,0},{8,12},{5,1},{9,13},{20,16},{24,28},{21,17},{25,29}} | collective-permute-start | bytes 983048 | tf_op jit(solution)/shard_map/ppermute | solution.py:260
  66.1 1.1 split.13
  67.2 1.4 %collective-permute-start.24 = (bf16[384,640]{1,0:T(8,128)(2,1)S(1)}, bf16[384,640]{1,0:T(8,128)(2,1)}, u32[]{:S(2)}, u32[]{:S(2)}) collective-permute-start(bf16[384,640]{1,0:T(8,128)(2,1)S(1)} %split.13), channel_id=1, source_target_pairs={{4,0},{8,12},{5,1},{9,13},{20,16},{24,28},{21,17},{25,29}} | collective-permute-start | bytes 1474568 | tf_op jit(solution)/shard_map/ppermute | solution.py:260
  68.7 3.4 %collective-permute-start.23 = (bf16[640,640]{1,0:T(8,128)(2,1)}, bf16[640,640]{1,0:T(8,128)(2,1)S(1)}, u32[]{:S(2)}, u32[]{:S(2)}) collective-permute-start(bf16[640,640]{1,0:T(8,128)(2,1)} %get-tuple-element.88.refs_2_), channel_id=1, source_target_pairs={{0,16},{16,0},{1,17},{17,1},{4,20},{20,4},{5,21},{21,5},{8,24},{24... | collective-permute-start | bytes 2457608 | tf_op jit(solution)/shard_map/ppermute | solution.py:260
  72.1 1.3 %collective-permute-start.21 = (bf16[128,1280]{1,0:T(8,128)(2,1)}, bf16[128,1280]{1,0:T(8,128)(2,1)}, u32[]{:S(2)}, u32[]{:S(2)}) collective-permute-start(bf16[128,1280]{1,0:T(8,128)(2,1)} %get-tuple-element.85), channel_id=1, source_target_pairs={{2,0},{3,1},{6,4},{7,5},{10,8},{11,9},{14,12},{15,13},{18,16},{19,... | collective-permute-start | bytes 983048 | tf_op jit(solution)/shard_map/ppermute | solution.py:260
  74.1 3.5 %collective-permute-done.25 = bf16[256,640]{1,0:T(8,128)(2,1)S(1)} collective-permute-done((bf16[256,640]{1,0:T(8,128)(2,1)}, bf16[256,640]{1,0:T(8,128)(2,1)S(1)}, u32[]{:S(2)}, u32[]{:S(2)}) %collective-permute-start.25) | collective-permute-done | bytes 327712 | tf_op jit(solution)/shard_map/ppermute | solution.py:260
  77.6 1.0 slice_select_fusion.1.refs_5_
  78.6 3.4 %collective-permute-start.27 = (bf16[256,640]{1,0:T(8,128)(2,1)S(1)}, bf16[256,640]{1,0:T(8,128)(2,1)S(1)}, u32[]{:S(2)}, u32[]{:S(2)}) collective-permute-start(bf16[256,640]{1,0:T(8,128)(2,1)S(1)} %slice_select_fusion.1.refs_5_), channel_id=1, source_target_pairs={{0,16},{16,0},{1,17},{17,1},{4,20},{20,4},{5,21},{21,5},{8,24},{24... | collective-permute-start | bytes 983048 | tf_op jit(solution)/shard_map/ppermute | solution.py:260
  82.0 2.6 %collective-permute-done.24 = bf16[384,640]{1,0:T(8,128)(2,1)} collective-permute-done((bf16[384,640]{1,0:T(8,128)(2,1)S(1)}, bf16[384,640]{1,0:T(8,128)(2,1)}, u32[]{:S(2)}, u32[]{:S(2)}) %collective-permute-start.24) | collective-permute-done | bytes 491552 | tf_op jit(solution)/shard_map/ppermute | solution.py:260
  84.7 1.2 slice_select_fusion.refs_4_
  85.9 3.6 %collective-permute-start.26 = (bf16[384,640]{1,0:T(8,128)(2,1)S(1)}, bf16[384,640]{1,0:T(8,128)(2,1)S(1)}, u32[]{:S(2)}, u32[]{:S(2)}) collective-permute-start(bf16[384,640]{1,0:T(8,128)(2,1)S(1)} %slice_select_fusion.refs_4_), channel_id=1, source_target_pairs={{0,16},{16,0},{1,17},{17,1},{4,20},{20,4},{5,21},{21,5},{8,24},{24... | collective-permute-start | bytes 1474568 | tf_op jit(solution)/shard_map/ppermute | solution.py:260
  89.5 6.4 %collective-permute-done.21 = bf16[128,1280]{1,0:T(8,128)(2,1)} collective-permute-done((bf16[128,1280]{1,0:T(8,128)(2,1)}, bf16[128,1280]{1,0:T(8,128)(2,1)}, u32[]{:S(2)}, u32[]{:S(2)}) %collective-permute-start.21) | collective-permute-done | bytes 327712 | tf_op jit(solution)/shard_map/ppermute | solution.py:260
  95.9 1.4 %fusion.1 = (f32[128]{0:T(128)S(1)}, bf16[128,1280]{1,0:T(8,128)(2,1)S(1)}) fusion(bf16[1,1,128,1280]{3,2,1,0:T(8,128)(2,1)S(1)} %copy-done.8, bf16[1,1,128,1280]{3,2,1,0:T(8,128)(2,1)S(1)} %copy-done, bf16[128,1280]{1,0:T(8,128)(2,1)} %collective-permute-done.21, f32[128]{0:T(128)S(1)} %compare_convert_fusion, pred[]{:T(512)S(6)} %eq.26), kind=kLoop, calls=%fused_computation.26 | loop fusion | flops 2293632 | bytes 1311745 | tf_op jit(solution)/shard_map/reduce_sum | solution.py:500
  97.3 0.4 shard_map.86.sens_own
  97.7 2.1 %collective-permute-start.22 = (bf16[128,1280]{1,0:T(8,128)(2,1)S(1)}, bf16[128,1280]{1,0:T(8,128)(2,1)S(1)}, u32[]{:S(2)}, u32[]{:S(2)}) collective-permute-start(bf16[128,1280]{1,0:T(8,128)(2,1)S(1)} %shard_map.86.sens_own), channel_id=1, source_target_pairs={{0,1},{1,0},{4,5},{5,4},{8,9},{9,8},{12,13},{13,12},{16,17},{17,16... | collective-permute-start | bytes 983048 | tf_op jit(solution)/shard_map/ppermute | solution.py:260
  99.8 1.3 %collective-permute-done.22.sens_other = bf16[128,1280]{1,0:T(8,128)(2,1)S(1)} collective-permute-done((bf16[128,1280]{1,0:T(8,128)(2,1)S(1)}, bf16[128,1280]{1,0:T(8,128)(2,1)S(1)}, u32[]{:S(2)}, u32[]{:S(2)}) %collective-permute-start.22) | collective-permute-done | bytes 327712 | tf_op jit(solution)/shard_map/ppermute | solution.py:260
  101.2 4.8 %collective-permute-done.26.refs_6_ = bf16[384,640]{1,0:T(8,128)(2,1)S(1)} collective-permute-done((bf16[384,640]{1,0:T(8,128)(2,1)S(1)}, bf16[384,640]{1,0:T(8,128)(2,1)S(1)}, u32[]{:S(2)}, u32[]{:S(2)}) %collective-permute-start.26) | collective-permute-done | bytes 491552 | tf_op jit(solution)/shard_map/ppermute | solution.py:260
  105.9 6.6 %shard_map.87 = bf16[128,256]{1,0:T(8,128)(2,1)S(1)} custom-call(s32[3]{0:T(128)S(1)} %pad_add_fusion.1.place, bf16[128,1280]{1,0:T(8,128)(2,1)S(1)} %shard_map.86.sens_own, bf16[128,1280]{1,0:T(8,128)(2,1)S(1)} %collective-permute-done.22.sens_other, bf16[1280,640]{1,0:T(8,128)(2,1)S(1)} %bitcast.40, bf16[640,640]{1,0:T(8,128)(2,1)S(1)} %get-tuple-element.86.refs_0_, ...), custom_call_target="tpu_custom_call" | custom-call | flops 1000000000 | bytes 8000000 | tf_op jit(solution)/shard_map/pallas_call | solution.py:252
  112.7 3.2 %collective-permute-start.29 = (bf16[128,256]{1,0:T(8,128)(2,1)S(1)}, bf16[128,256]{1,0:T(8,128)(2,1)S(1)}, u32[]{:S(2)}, u32[]{:S(2)}) collective-permute-start(bf16[128,256]{1,0:T(8,128)(2,1)S(1)} %get-tuple-element.97), channel_id=1, source_target_pairs={{0,4},{4,8},{8,12},{12,0},{1,5},{5,9},{9,13},{13,1},{2,6},{6,10},{... | collective-permute-start | bytes 196616 | tf_op jit(solution)/shard_map/ppermute | solution.py:260
  115.9 1.7 %collective-permute-start.30 = (bf16[128,256]{1,0:T(8,128)(2,1)S(1)}, bf16[128,256]{1,0:T(8,128)(2,1)S(1)}, u32[]{:S(2)}, u32[]{:S(2)}) collective-permute-start(bf16[128,256]{1,0:T(8,128)(2,1)S(1)} %get-tuple-element.97), channel_id=1, source_target_pairs={{0,8},{4,12},{8,0},{12,4},{1,9},{5,13},{9,1},{13,5},{2,10},{6,14},... | collective-permute-start | bytes 196616 | tf_op jit(solution)/shard_map/ppermute | solution.py:260
  117.6 2.8 %collective-permute-start.31 = (bf16[128,256]{1,0:T(8,128)(2,1)S(1)}, bf16[128,256]{1,0:T(8,128)(2,1)S(1)}, u32[]{:S(2)}, u32[]{:S(2)}) collective-permute-start(bf16[128,256]{1,0:T(8,128)(2,1)S(1)} %get-tuple-element.97), channel_id=1, source_target_pairs={{0,12},{4,0},{8,4},{12,8},{1,13},{5,1},{9,5},{13,9},{2,14},{6,2},{... | collective-permute-start | bytes 196616 | tf_op jit(solution)/shard_map/ppermute | solution.py:260
  120.4 0.6 collective-permute-done.30
  121.1 1.3 %collective-permute-done.31 = bf16[128,256]{1,0:T(8,128)(2,1)S(1)} collective-permute-done((bf16[128,256]{1,0:T(8,128)(2,1)S(1)}, bf16[128,256]{1,0:T(8,128)(2,1)S(1)}, u32[]{:S(2)}, u32[]{:S(2)}) %collective-permute-start.31) | collective-permute-done | bytes 65568 | tf_op jit(solution)/shard_map/ppermute | solution.py:260
  122.4 0.5 collective-permute-start.28
  122.9 1.0 collective-permute-done.28
  124.0 0.5 multiply_bitcast_fusion
  124.6 2.2 %fusion = f32[1,320,512]{2,1,0:T(8,128)} fusion(bf16[512,320]{1,0:T(8,128)(2,1)S(1)} %copy-done.17, bf16[512,256]{1,0:T(8,128)(2,1)S(1)} %get-tuple-element.113, bf16[512,256]{1,0:T(8,128)(2,1)S(1)} %get-tuple-element.112, bf16[1,1280,512]{2,1,0:T(8,128)(2,1)} %param.13, s32[]{:T(128)S(6)} %select_n.124), kind=kOutput, calls=%fused_computation.23 | convolution fusion | flops 169148416 | bytes 1835012 | tf_op jit(solution)/shard_map/dot_general | solution.py:506
  (36 shorter events, 0.7 us)
Async XLA Ops:
  0.6 8.8 %copy-start.1 = (bf16[128,1280]{1,0:T(8,128)(2,1)S(1)}, bf16[128,1280]{1,0:T(8,128)(2,1)}, u32[]{:S(2)}) copy-start(bf16[128,1280]{1,0:T(8,128)(2,1)} %get-tuple-element.36) | copy-start | bytes 983044 | tf_op jit(solution)/shard_map/cond
  0.7 8.8 %copy-start.5 = (bf16[1280,512]{1,0:T(8,128)(2,1)S(1)}, bf16[1280,512]{1,0:T(8,128)(2,1)}, u32[]{:S(2)}) copy-start(bf16[1280,512]{1,0:T(8,128)(2,1)} %get-tuple-element.37) | copy-start | bytes 3932164 | tf_op jit(solution)/shard_map/cond
  2.9 35.8 %collective-permute-start.4 = (bf16[640,640]{1,0:T(8,128)(2,1)}, bf16[640,640]{1,0:T(8,128)(2,1)S(1)}, u32[]{:S(2)}, u32[]{:S(2)}) collective-permute-start(bf16[640,640]{1,0:T(8,128)(2,1)} %constant_dynamic-slice_fusion), channel_id=1, source_target_pairs={{0,4},{4,0},{8,12},{12,8},{1,5},{5,1},{9,13},{13,9},{16,20},{20,16... | collective-permute-start | bytes 2457608 | tf_op jit(solution)/shard_map/cond/branch_0_fun/ppermute | solution.py:260
  7.8 30.8 %collective-permute-start.5 = (bf16[640,640]{1,0:T(8,128)(2,1)}, bf16[640,640]{1,0:T(8,128)(2,1)}, u32[]{:S(2)}, u32[]{:S(2)}) collective-permute-start(bf16[640,640]{1,0:T(8,128)(2,1)} %constant_dynamic-slice_fusion), channel_id=1, source_target_pairs={{4,8},{8,4},{5,9},{9,5},{20,24},{24,20},{21,25},{25,21}} | collective-permute-start | bytes 2457608 | tf_op jit(solution)/shard_map/cond/branch_0_fun/ppermute | solution.py:260
  9.4 14.2 %copy-start.13 = (bf16[128,1280]{1,0:T(8,128)(2,1)S(1)}, bf16[128,1280]{1,0:T(8,128)(2,1)}, u32[]{:S(2)}) copy-start(bf16[128,1280]{1,0:T(8,128)(2,1)} %get-tuple-element.40.queries) | copy-start | bytes 983044 | tf_op jit(solution)/shard_map/cond
  9.4 14.2 %copy-start.18 = (bf16[128,256]{1,0:T(8,128)(2,1)S(1)}, bf16[128,256]{1,0:T(8,128)(2,1)}, u32[]{:S(2)}) copy-start(bf16[128,256]{1,0:T(8,128)(2,1)} %get-tuple-element.41.keys) | copy-start | bytes 196612 | tf_op jit(solution)/shard_map/cond
  9.8 9.5 %collective-permute-start = (bf16[128,256]{1,0:T(8,128)(2,1)S(1)}, bf16[128,256]{1,0:T(8,128)(2,1)S(1)}, u32[]{:S(2)}, u32[]{:S(2)}) collective-permute-start(bf16[128,256]{1,0:T(8,128)(2,1)S(1)} %dynamic-slice_convert_fusion), channel_id=1, source_target_pairs={{0,1},{1,0},{4,5},{5,4},{8,9},{9,8},{12,13},{13,12},{16,17},{17,16... | collective-permute-start | bytes 196616 | tf_op jit(solution)/shard_map/cond/branch_0_fun/ppermute | solution.py:260
  12.0 19.8 %collective-permute-start.1 = (bf16[128,320]{1,0:T(8,128)(2,1)S(1)}, bf16[128,320]{1,0:T(8,128)(2,1)S(1)}, u32[]{:S(2)}, u32[]{:S(2)}) collective-permute-start(bf16[128,320]{1,0:T(8,128)(2,1)S(1)} %get-tuple-element.103), channel_id=1, source_target_pairs={{0,4},{4,8},{8,12},{12,0},{1,5},{5,9},{9,13},{13,1},{16,20},{20,24... | collective-permute-start | bytes 245768 | tf_op jit(solution)/shard_map/cond/branch_0_fun/ppermute | solution.py:260
  17.4 20.5 %collective-permute-start.2 = (bf16[128,320]{1,0:T(8,128)(2,1)S(1)}, bf16[128,320]{1,0:T(8,128)(2,1)S(1)}, u32[]{:S(2)}, u32[]{:S(2)}) collective-permute-start(bf16[128,320]{1,0:T(8,128)(2,1)S(1)} %get-tuple-element.102), channel_id=1, source_target_pairs={{0,8},{4,12},{8,0},{12,4},{1,9},{5,13},{9,1},{13,5},{16,24},{20,28... | collective-permute-start | bytes 245768 | tf_op jit(solution)/shard_map/cond/branch_0_fun/ppermute | solution.py:260
  19.4 18.5 %collective-permute-start.3 = (bf16[128,320]{1,0:T(8,128)(2,1)S(1)}, bf16[128,320]{1,0:T(8,128)(2,1)S(1)}, u32[]{:S(2)}, u32[]{:S(2)}) collective-permute-start(bf16[128,320]{1,0:T(8,128)(2,1)S(1)} %get-tuple-element.101), channel_id=1, source_target_pairs={{0,12},{4,0},{8,4},{12,8},{1,13},{5,1},{9,5},{13,9},{16,28},{20,16... | collective-permute-start | bytes 245768 | tf_op jit(solution)/shard_map/cond/branch_0_fun/ppermute | solution.py:260
  38.7 5.5 %collective-permute-start.7 = (bf16[640,640]{1,0:T(8,128)(2,1)S(1)}, bf16[640,640]{1,0:T(8,128)(2,1)S(1)}, u32[]{:S(2)}, u32[]{:S(2)}) collective-permute-start(bf16[640,640]{1,0:T(8,128)(2,1)S(1)} %collective-permute-done.4), channel_id=1, source_target_pairs={{4,8},{8,4},{5,9},{9,5},{20,24},{24,20},{21,25},{25,21}} | collective-permute-start | bytes 2457608 | tf_op jit(solution)/shard_map/cond/branch_0_fun/ppermute | solution.py:260
  39.4 21.4 %collective-permute-start.8 = (bf16[640,640]{1,0:T(8,128)(2,1)}, bf16[640,640]{1,0:T(8,128)(2,1)S(1)}, u32[]{:S(2)}, u32[]{:S(2)}) collective-permute-start(bf16[640,640]{1,0:T(8,128)(2,1)} %collective-permute-done.5), channel_id=1, source_target_pairs={{4,0},{8,12},{5,1},{9,13},{20,16},{24,28},{21,17},{25,29}} | collective-permute-start | bytes 2457608 | tf_op jit(solution)/shard_map/cond/branch_0_fun/ppermute | solution.py:260
  40.7 21.1 %collective-permute-start.6 = (bf16[640,640]{1,0:T(8,128)(2,1)S(1)}, bf16[640,640]{1,0:T(8,128)(2,1)}, u32[]{:S(2)}, u32[]{:S(2)}) collective-permute-start(bf16[640,640]{1,0:T(8,128)(2,1)S(1)} %collective-permute-done.4), channel_id=1, source_target_pairs={{0,16},{16,0},{1,17},{17,1},{4,20},{20,4},{5,21},{21,5},{8,24},{24... | collective-permute-start | bytes 2457608 | tf_op jit(solution)/shard_map/cond/branch_0_fun/ppermute | solution.py:260
  64.9 12.7 %collective-permute-start.25 = (bf16[256,640]{1,0:T(8,128)(2,1)}, bf16[256,640]{1,0:T(8,128)(2,1)S(1)}, u32[]{:S(2)}, u32[]{:S(2)}) collective-permute-start(bf16[256,640]{1,0:T(8,128)(2,1)} %split.15), channel_id=1, source_target_pairs={{4,0},{8,12},{5,1},{9,13},{20,16},{24,28},{21,17},{25,29}} | collective-permute-start | bytes 983048 | tf_op jit(solution)/shard_map/ppermute | solution.py:260
  67.2 28.6 %copy-start = (bf16[1,1,128,1280]{3,2,1,0:T(8,128)(2,1)S(1)}, bf16[1,1,128,1280]{3,2,1,0:T(8,128)(2,1)}, u32[]{:S(2)}) copy-start(bf16[1,1,128,1280]{3,2,1,0:T(8,128)(2,1)} %param.9) | copy-start | bytes 983044
  67.2 28.6 %copy-start.8 = (bf16[1,1,128,1280]{3,2,1,0:T(8,128)(2,1)S(1)}, bf16[1,1,128,1280]{3,2,1,0:T(8,128)(2,1)}, u32[]{:S(2)}) copy-start(bf16[1,1,128,1280]{3,2,1,0:T(8,128)(2,1)} %param.10) | copy-start | bytes 983044
  67.2 17.4 %collective-permute-start.24 = (bf16[384,640]{1,0:T(8,128)(2,1)S(1)}, bf16[384,640]{1,0:T(8,128)(2,1)}, u32[]{:S(2)}, u32[]{:S(2)}) collective-permute-start(bf16[384,640]{1,0:T(8,128)(2,1)S(1)} %split.13), channel_id=1, source_target_pairs={{4,0},{8,12},{5,1},{9,13},{20,16},{24,28},{21,17},{25,29}} | collective-permute-start | bytes 1474568 | tf_op jit(solution)/shard_map/ppermute | solution.py:260
  68.7 32.5 %collective-permute-start.23 = (bf16[640,640]{1,0:T(8,128)(2,1)}, bf16[640,640]{1,0:T(8,128)(2,1)S(1)}, u32[]{:S(2)}, u32[]{:S(2)}) collective-permute-start(bf16[640,640]{1,0:T(8,128)(2,1)} %get-tuple-element.88.refs_2_), channel_id=1, source_target_pairs={{0,16},{16,0},{1,17},{17,1},{4,20},{20,4},{5,21},{21,5},{8,24},{24... | collective-permute-start | bytes 2457608 | tf_op jit(solution)/shard_map/ppermute | solution.py:260
  72.1 23.7 %collective-permute-start.21 = (bf16[128,1280]{1,0:T(8,128)(2,1)}, bf16[128,1280]{1,0:T(8,128)(2,1)}, u32[]{:S(2)}, u32[]{:S(2)}) collective-permute-start(bf16[128,1280]{1,0:T(8,128)(2,1)} %get-tuple-element.85), channel_id=1, source_target_pairs={{2,0},{3,1},{6,4},{7,5},{10,8},{11,9},{14,12},{15,13},{18,16},{19,... | collective-permute-start | bytes 983048 | tf_op jit(solution)/shard_map/ppermute | solution.py:260
  78.6 21.2 %collective-permute-start.27 = (bf16[256,640]{1,0:T(8,128)(2,1)S(1)}, bf16[256,640]{1,0:T(8,128)(2,1)S(1)}, u32[]{:S(2)}, u32[]{:S(2)}) collective-permute-start(bf16[256,640]{1,0:T(8,128)(2,1)S(1)} %slice_select_fusion.1.refs_5_), channel_id=1, source_target_pairs={{0,16},{16,0},{1,17},{17,1},{4,20},{20,4},{5,21},{21,5},{8,24},{24... | collective-permute-start | bytes 983048 | tf_op jit(solution)/shard_map/ppermute | solution.py:260
  85.9 20.0 %copy-start.10 = (bf16[1,1280,640]{2,1,0:T(8,128)(2,1)S(1)}, bf16[1,1280,640]{2,1,0:T(8,128)(2,1)}, u32[]{:S(2)}) copy-start(bf16[1,1280,640]{2,1,0:T(8,128)(2,1)} %param.14) | copy-start | bytes 4915204
  85.9 20.0 %collective-permute-start.26 = (bf16[384,640]{1,0:T(8,128)(2,1)S(1)}, bf16[384,640]{1,0:T(8,128)(2,1)S(1)}, u32[]{:S(2)}, u32[]{:S(2)}) collective-permute-start(bf16[384,640]{1,0:T(8,128)(2,1)S(1)} %slice_select_fusion.refs_4_), channel_id=1, source_target_pairs={{0,16},{16,0},{1,17},{17,1},{4,20},{20,4},{5,21},{21,5},{8,24},{24... | collective-permute-start | bytes 1474568 | tf_op jit(solution)/shard_map/ppermute | solution.py:260
  97.7 3.5 %collective-permute-start.22 = (bf16[128,1280]{1,0:T(8,128)(2,1)S(1)}, bf16[128,1280]{1,0:T(8,128)(2,1)S(1)}, u32[]{:S(2)}, u32[]{:S(2)}) collective-permute-start(bf16[128,1280]{1,0:T(8,128)(2,1)S(1)} %shard_map.86.sens_own), channel_id=1, source_target_pairs={{0,1},{1,0},{4,5},{5,4},{8,9},{9,8},{12,13},{13,12},{16,17},{17,16... | collective-permute-start | bytes 983048 | tf_op jit(solution)/shard_map/ppermute | solution.py:260
  112.5 12.0 %copy-start.17 = (bf16[512,320]{1,0:T(8,128)(2,1)S(1)}, bf16[512,320]{1,0:T(8,128)(2,1)}, u32[]{:S(2)}) copy-start(bf16[512,320]{1,0:T(8,128)(2,1)} %get-tuple-element.95) | copy-start | bytes 983044
  112.7 7.8 %collective-permute-start.29 = (bf16[128,256]{1,0:T(8,128)(2,1)S(1)}, bf16[128,256]{1,0:T(8,128)(2,1)S(1)}, u32[]{:S(2)}, u32[]{:S(2)}) collective-permute-start(bf16[128,256]{1,0:T(8,128)(2,1)S(1)} %get-tuple-element.97), channel_id=1, source_target_pairs={{0,4},{4,8},{8,12},{12,0},{1,5},{5,9},{9,13},{13,1},{2,6},{6,10},{... | collective-permute-start | bytes 196616 | tf_op jit(solution)/shard_map/ppermute | solution.py:260
  115.9 5.2 %collective-permute-start.30 = (bf16[128,256]{1,0:T(8,128)(2,1)S(1)}, bf16[128,256]{1,0:T(8,128)(2,1)S(1)}, u32[]{:S(2)}, u32[]{:S(2)}) collective-permute-start(bf16[128,256]{1,0:T(8,128)(2,1)S(1)} %get-tuple-element.97), channel_id=1, source_target_pairs={{0,8},{4,12},{8,0},{12,4},{1,9},{5,13},{9,1},{13,5},{2,10},{6,14},... | collective-permute-start | bytes 196616 | tf_op jit(solution)/shard_map/ppermute | solution.py:260
  117.6 4.8 %collective-permute-start.31 = (bf16[128,256]{1,0:T(8,128)(2,1)S(1)}, bf16[128,256]{1,0:T(8,128)(2,1)S(1)}, u32[]{:S(2)}, u32[]{:S(2)}) collective-permute-start(bf16[128,256]{1,0:T(8,128)(2,1)S(1)} %get-tuple-element.97), channel_id=1, source_target_pairs={{0,12},{4,0},{8,4},{12,8},{1,13},{5,1},{9,5},{13,9},{2,14},{6,2},{... | collective-permute-start | bytes 196616 | tf_op jit(solution)/shard_map/ppermute | solution.py:260
  122.4 2.1 %collective-permute-start.32 = (bf16[512,256]{1,0:T(8,128)(2,1)S(1)}, bf16[512,256]{1,0:T(8,128)(2,1)S(1)}, u32[]{:S(2)}, u32[]{:S(2)}) collective-permute-start(bf16[512,256]{1,0:T(8,128)(2,1)S(1)} %pad_maximum_fusion.3), channel_id=1, source_target_pairs={{0,1},{1,0},{2,3},{3,2},{4,5},{5,4},{6,7},{7,6},{8,9},{9,8},{10,11... | collective-permute-start | bytes 786440 | tf_op jit(solution)/shard_map/ppermute | solution.py:260
  122.4 1.5 %collective-permute-start.28 = (f32[128]{0:T(128)S(1)}, f32[128]{0:T(128)S(1)}, u32[]{:S(2)}, u32[]{:S(2)}) collective-permute-start(f32[128]{0:T(128)S(1)} %add.103), channel_id=1, source_target_pairs={{0,1},{1,0},{2,3},{3,2},{4,5},{5,4},{6,7},{7,6},{8,9},{9,8},{10,11... | collective-permute-start | bytes 1544 | tf_op jit(solution)/shard_map/ppermute | solution.py:260

commit v5 on v4

--- a/solution.py
+++ b/solution.py
@@ -24,7 +24,6 @@
 
 VMEM = pl.BlockSpec(memory_space=pltpu.VMEM)
 SMEM = pl.BlockSpec(memory_space=pltpu.SMEM)
-ANY = pl.BlockSpec(memory_space=pl.ANY)
 
 
 def by_columns(left, right):
@@ -196,15 +195,10 @@
 def main_kernel(layout, place, sens_own, sens_other, out_block, *refs):
     count = len(layout)
     pieces = refs[:count]
-    probs_t, mixed_gain, value_gain, found, halves, total, block, sem = refs[count : count + 8]
-    held, sems = refs[count + 8 :][:count], refs[count + 8 + count]
-    pos, core, group = place[0], place[1], place[2]
+    before, probs_t, mixed_gain, value_gain, found, halves, total = refs[count:]
+    pos, core, group, active = place[0], place[1], place[2], place[3]
     width = out_block.shape[1]
     per_core = sens_own.shape[1] // width
-    copies = [pltpu.make_async_copy(out_block, block, sem)]
-    copies += [pltpu.make_async_copy(pieces[i], held[i], sems.at[i]) for i in range(count)]
-    for copy in copies:
-        copy.start()
     halves[core] = sens_own[...]
     halves[1 - core] = sens_other[...]
 
@@ -213,17 +207,19 @@
         start = pl.multiple_of(lax.rem(owner, per_core) * width, 128)
         return halves[owner // per_core, :, pl.ds(start, width)]
 
-    copies[0].wait()
-    total[...] = by_columns(part(0), block[...])
-    for i, (slot, side, start) in enumerate(layout):
-        copies[i + 1].wait()
-        rows = held[i].shape[0]
+    total[...] = by_columns(part(0), out_block[...])
+    for piece, (slot, side, start) in zip(pieces, layout):
         at = (group if side == 0 else 1 - group) * (total.shape[1] // 2) + start
-        total[:, pl.ds(pl.multiple_of(at, 128), rows)] += by_columns(part(slot), held[i][...])
+        at = pl.ds(pl.multiple_of(at, 128), piece.shape[0])
+        total[:, at] += by_columns(part(slot), piece[...])
     head_step(total, probs_t, mixed_gain, value_gain, found)
 
-
-def main_step(place, sens_own, sens_other, out_block, slots, probs_t, mixed_gain, value_gain):
+    @pl.when(active == 0)
+    def _():
+        found[...] = before[...]
+
+
+def main_step(place, sens_own, sens_other, out_block, slots, before, probs_t, mixed_gain, value_gain):
     layout, pieces = [], []
     for k, sides in enumerate(slots):
         for side in range(2):
@@ -236,20 +232,53 @@
     call = kernel_call(
         functools.partial(main_kernel, tuple(layout)),
         jax.ShapeDtypeStruct(value_gain.shape, BF16),
-        [SMEM, VMEM, VMEM, ANY] + [ANY] * len(pieces) + [VMEM] * 3,
-        [
-            pltpu.VMEM((2, seq_len, half_width), BF16),
-            pltpu.VMEM(mixed_gain.shape, F32),
-            pltpu.VMEM(out_block.shape, BF16),
-            pltpu.SemaphoreType.DMA,
-        ]
-        + [pltpu.VMEM(piece.shape, BF16) for piece in pieces]
-        + [pltpu.SemaphoreType.DMA((len(pieces),))],
+        [SMEM] + [VMEM] * (7 + len(pieces)),
+        [pltpu.VMEM((2, seq_len, half_width), BF16), pltpu.VMEM(mixed_gain.shape, F32)],
         flops=10**9,
         nbytes=8 * 10**6,
         limit=32,
     )
-    return call(place, sens_own, sens_other, out_block, *pieces, probs_t, mixed_gain, value_gain)
+    return call(
+        place, sens_own, sens_other, out_block, *pieces, before, probs_t, mixed_gain, value_gain
+    )
+
+
+def turn_kernel(*refs):
+    *pieces, turned = refs
+    for k, piece in enumerate(pieces):
+        rows = piece.shape[0]
+        turned[:, k * rows : (k + 1) * rows] = piece[...].astype(F32).T.astype(BF16)
+
+
+def turned_side_by_side(pieces):
+    rows, width = pieces[0].shape
+    shape = jax.ShapeDtypeStruct((width, rows * len(pieces)), BF16)
+    return kernel_call(turn_kernel, shape, [VMEM] * len(pieces), nbytes=10**6)(*pieces)
+
+
+def relevance_kernel(count, core, inputs_t, value_block, *refs):
+    own, (other, relevance) = refs[:count], refs[count:]
+    seq_len, width = own[0].shape
+    mine = jnp.zeros((inputs_t.shape[0], width), F32)
+    for k in range(count):
+        tokens = inputs_t[:, k * seq_len : (k + 1) * seq_len]
+        mine += jnp.dot(tokens, own[k][...], preferred_element_type=F32)
+    theirs = jnp.dot(inputs_t[...], other[...], preferred_element_type=F32)
+    at = pl.ds(pl.multiple_of(core[0] * width, 128), width)
+    relevance[:, at] = value_block[:, at].astype(F32) * mine
+    at = pl.ds(pl.multiple_of((1 - core[0]) * width, 128), width)
+    relevance[:, at] = value_block[:, at].astype(F32) * theirs
+
+
+def relevance_step(core, inputs_t, value_block, own, other):
+    call = kernel_call(
+        functools.partial(relevance_kernel, len(own)),
+        jax.ShapeDtypeStruct(value_block.shape, F32),
+        [SMEM] + [VMEM] * (3 + len(own)),
+        flops=2 * 10**8,
+        nbytes=2 * 10**6,
+    )
+    return call(core, inputs_t, value_block, *own, other)
 
 
 def moved(shard, axes, target):
@@ -309,15 +338,20 @@
     peers = lax.axis_size("dp")
     pos = lax.axis_index("dp")
     if peers != 4:
-        return [between(mine, {i: i ^ k for i in range(peers)}) for k in range(1, peers)]
+        return [between(mine, {i: i ^ k for i in range(peers)}) for k in range(1, peers)], *others[-2:]
+    cut = [mine.shape[0] * 3 // 5]
     pair = between(mine, {i: i ^ 1 for i in range(peers)})
     near = between(mine, MIDDLE)
-    pair, near, *_ = lax.optimization_barrier((pair, near, *others))
+    pair, near, *others = lax.optimization_barrier((pair, near, *others))
     crossed = between(pair, MIDDLE)
     relayed = between(near, OUTWARD)
     pair_swapped = swap_groups(pair)
-    second = jnp.where((pos == 1) | (pos == 2), crossed, relayed)
-    return [pair, pair_swapped, second, near]
+    crossed, relayed, pair_swapped = lax.optimization_barrier((crossed, relayed, pair_swapped))
+    second = [
+        jnp.where((pos == 1) | (pos == 2), *both)
+        for both in zip(jnp.split(crossed, cut), jnp.split(relayed, cut))
+    ]
+    return [pair, pair_swapped, second, jnp.split(near, cut)], *others[-2:]
 
 
 def finish_gather(started):
@@ -326,14 +360,13 @@
     if peers != 4:
         return [([block], [swap_groups(block)]) for block in started]
     pair, pair_swapped, second, near = started
-    cut = [second.shape[0] * 3 // 5]
     third = [
         jnp.where((pos == 1) | (pos == 2), direct, between(far, OUTWARD))
-        for direct, far in zip(jnp.split(near, cut), jnp.split(second, cut))
+        for direct, far in zip(near, second)
     ]
     return [
         ([pair], [pair_swapped]),
-        ([second], [swap_groups(second)]),
+        (second, [swap_groups(piece) for piece in second]),
         (third, [swap_groups(piece) for piece in third]),
     ]
 
@@ -412,35 +445,21 @@
             mine, ("section", "mp"), lambda s, c: (s, 1 - c) if take(s == sections - 1) else None
         )
 
-    def attention(take):
+    def values_of(take):
         value_part = jnp.dot(inputs, value_rows, preferred_element_type=F32)
         part_mine = part_of(value_part, core_pos, kv_width, 1)
         part_other = part_of(value_part, 1 - core_pos, kv_width, 1)
-        values_f = part_mine + core_exchange(part_other.astype(BF16), take).astype(F32)
-        return values_f, attend(lengths, query_rows, key_rows, values_f)
-
-    block_rows = half_width // peers
-
-    def inputs_of_all(rows, take):
-        pieces = []
-        for k in range(peers):
-            piece = part_of(rows, lax.rem(dp_pos + k, peers), block_rows, 1)
-            if k:
-                piece = moved(
-                    piece,
-                    ("dp", "section"),
-                    lambda i, s: ((i + k) % peers, s) if take(s == sections - 1) else None,
-                )
-            pieces.append(piece)
-        return jnp.concatenate(pieces, 0)
+        return part_mine + core_exchange(part_other.astype(BF16), take).astype(F32)
 
     def last_section():
-        values_f, rest = attention(lambda last: last)
+        values_f = values_of(lambda last: last)
+        rest = attend(lengths, query_rows, key_rows, values_f)
         sens_branch = sensitivity(lengths, inputs, branch)
         own, backs = spread_product(sens_branch, out_block)
-        all_inputs = inputs_of_all(inputs, lambda last: last)
-        started = [jnp.zeros(leaf.shape, leaf.dtype) for leaf in early_shapes[-1]]
-        own, all_inputs, *started = lax.optimization_barrier((own, all_inputs, *started))
+        leaves, tree = jax.tree.flatten(early_shapes[-1])
+        filler = lengths[0].astype(BF16)
+        unused = [jnp.full(leaf.shape, filler + k, BF16) for k, leaf in enumerate(leaves)]
+        own, *unused = lax.optimization_barrier((own, *unused))
         if peers > 4:
             for back in backs:
                 own = own + back.astype(F32)
@@ -449,33 +468,53 @@
         other = core_exchange(found, lambda last: last)
         place = jnp.stack([core_pos, lengths[0]])
         outgoing = last_outgoing(place, inputs, branch, found, other, value_rows)
-        return values_f, rest, found, outgoing, all_inputs, started
+        return values_f, found, outgoing, jax.tree.unflatten(tree, unused)
 
     def early_section():
         mine = part_of(out_block, group_pos, head_rows // 2, 0)
-        all_inputs = inputs_of_all(inputs, lambda last: not last)
-        values_f, rest = attention(lambda last: not last)
-        started = start_gather(mine, values_f, *rest, all_inputs)
-        found = jnp.zeros((seq_len, kv_width), BF16)
-        outgoing = jnp.zeros((seq_len, half_width), BF16)
-        return values_f, rest, found, outgoing, all_inputs, started
+        values_f = values_of(lambda last: not last)
+        found = jnp.full((seq_len, kv_width), lengths[0].astype(BF16))
+        outgoing = jnp.full((seq_len, half_width), lengths[0].astype(BF16))
+        started, found, outgoing = start_gather(mine, values_f, found, outgoing)
+        return values_f, found, outgoing, started
 
     early_shapes = jax.eval_shape(early_section)
-    values_f, rest, sens_values, outgoing, all_inputs, started = lax.cond(
-        is_last, last_section, early_section
-    )
+    values_f, sens_values, outgoing, started = lax.cond(is_last, last_section, early_section)
     arrived = from_next_section(outgoing)
     slots = finish_gather(started)
-
+    rest = attend(lengths, query_rows, key_rows, values_f)
+
+    def inputs_of_all(*others):
+        rows = once(inputs, *others)
+        pieces = [
+            along_dp(part_of(rows, lax.rem(dp_pos + k, peers), block_rows, 1), k)
+            for k in range(peers)
+        ]
+        if block_rows % 8 == 0 and peers <= 8:
+            return turned_side_by_side(pieces)
+        return jnp.concatenate(pieces, 0).T
+
+    block_rows = half_width // peers
+    value_block = part_of(value_rows, dp_pos, block_rows, 0)
     for turn in range(1, sections):
         active = section_pos == sections - 1 - turn
         current = jnp.where(active, arrived, current)
-        sens_branch = sensitivity(lengths, inputs, branch, current)
+        sens_branch = sensitivity(lengths, inputs, branch, arrived)
         sens_other = core_exchange(sens_branch, lambda last: not last)
         if block_width % 128 == 0:
-            place = jnp.stack([dp_pos, core_pos, group_pos])
-            found = main_step(place, sens_branch, sens_other, out_block, slots, *rest)
+            place = jnp.stack([dp_pos, core_pos, group_pos, active.astype(jnp.int32)])
+            if turn == 1:
+                behind = [slots[-2][1], slots[-1][0], slots[-1][1][1:]]
+                inputs_t = inputs_of_all(sens_other, *jax.tree.leaves(behind))
+                sens_other, inputs_t, value_block, *_ = lax.optimization_barrier(
+                    (sens_other, inputs_t, value_block)
+                )
+            found = main_step(
+                place, sens_branch, sens_other, out_block, slots, sens_values, *rest
+            )
         else:
+            if turn == 1:
+                inputs_t = inputs_of_all(sens_other)
             share = head_rows // 2
             own_rows = part_of(out_block, group_pos, share, 0)
             other_rows = part_of(out_block, 1 - group_pos, share, 0)
@@ -488,7 +527,8 @@
                         [by_columns(part, piece) for piece in blocks[side]], 1
                     )
             found = sum_heads(ordered(group_pos == 0, halves[0], halves[1], 1), [], *rest)
-        sens_values = jnp.where(active, found, sens_values)
+            found = jnp.where(active, found, sens_values)
+        sens_values = found
         if turn + 1 < sections:
             sens_all = ordered(
                 core_pos == 0, found, core_exchange(found, lambda last: not last), 1
@@ -501,13 +541,18 @@
     heat_part += jnp.sum(sens_values.astype(F32) * values_f, axis=1)
     heat_rows = (heat_part + other_core(heat_part)) / DW
 
-    mine = jnp.concatenate([along_dp(sens_values, k) for k in range(peers)], 0)
-    all_sens = ordered(core_pos == 0, mine, other_core(mine), 1)
-    summed = lax.dot_general(
-        all_inputs, all_sens, (((0,), (0,)), ((), ())), preferred_element_type=F32
-    )
-    value_block = part_of(value_rows, dp_pos, block_rows, 0)
-    relevance_rows = value_block.astype(F32) * summed
+    own_sens = [along_dp(sens_values, k) for k in range(peers)]
+    *own_sens, heat_rows = lax.optimization_barrier((*own_sens, heat_rows))
+    other_sens = other_core(jnp.concatenate(own_sens, 0))
+    if block_rows % 8 == 0 and peers <= 8:
+        relevance_rows = relevance_step(
+            core_pos[None], inputs_t, value_block, own_sens, other_sens
+        )
+    else:
+        all_sens = ordered(core_pos == 0, jnp.concatenate(own_sens, 0), other_sens, 1)
+        relevance_rows = value_block.astype(F32) * jnp.dot(
+            inputs_t, all_sens, preferred_element_type=F32
+        )
     return (heat_rows[None, None, :], relevance_rows[None])
 
 

time: 128 us -> 119 us (0.930)
  waiting for transfers between devices: 47.4 us -> 42.1 us
  starting transfers between devices: 50.3 us -> 45.6 us
  other arithmetic: 6.29 us -> 8.64 us
  matrix products: 2.52 us -> 0.33 us
  local copies, waits for them, and re-layouts: 6.68 us -> 8.78 us
  Pallas kernels: 11.9 us -> 10.6 us
    ppermute x21 -> x22, waiting for transfers between devices: 47.4 us -> 42.1 us  [moved(): return lax.ppermute(shard, axes, pairs)]
    ppermute x21 -> x22, starting transfers between devices: 50.3 us -> 45.6 us  [moved(): return lax.ppermute(shard, axes, pairs)]
    select_n x2, other arithmetic: 1.07 us -> 3.83 us  [start_gather(): jnp.where((pos == 1) | (pos == 2), *both)]
    dot_general x2 -> x1, matrix products: 2.52 us -> 0.33 us  [values_of(): value_part = jnp.dot(inputs, value_rows, preferred_element_type=F32)]
    add x1, other arithmetic: 0.02 us -> 1.58 us  [values_of(): return part_mine + core_exchange(part_other.astype(BF16), take).astype(F32)]
    another operation x2 -> x0, local copies, waits for them, and re-layouts: 1.37 us -> none
    dynamic_slice x2 -> x3, local copies, waits for them, and re-layouts: 2.45 us -> 3.68 us  [part_of(): return lax.dynamic_slice_in_dim(array, index * width, width, axis)]
    pallas_call x1 -> x3, Pallas kernels: 6.58 us -> 5.79 us  [the longest x1 4.34 us: main_step(): call(place, sens_own, sens_other, out_block, *pieces, before, probs_t, mi...]
  transfers between devices with their start and end apart: 21 -> 22, of which waited for: 11 -> 10; matrix products, arithmetic and copies ran while one was open for 6% -> 8% of each run, Pallas kernels for 4% -> 4%
where the time goes in v5:
time: 119 us; the launch traced here: 118 us
  starting transfers between devices  45.6 us (38%)
  waiting for transfers between devices  42.1 us (35%)
  Pallas kernels  10.6 us (9%)
  local copies, waits for them, and re-layouts  8.78 us (7%)
  other arithmetic  8.64 us (7%)
  between operations  1.65 us (1%)
    ppermute x22, starting transfers between devices, moved(): return lax.ppermute(shard, axes, pairs)  45.6 us
    ppermute x22, waiting for transfers between devices, moved(): return lax.ppermute(shard, axes, pairs)  42.1 us
    pallas_call x1, Pallas kernels, attend(): return call(length, queries, keys, values)  4.4 us
    pallas_call x1, Pallas kernels, main_step(): call(place, sens_own, sens_other, out_block, *pieces, before, probs_t, mi...  4.34 us
    select_n x2, other arithmetic, start_gather(): jnp.where((pos == 1) | (pos == 2), *both)  3.83 us
    dynamic_slice x3, local copies, waits for them, and re-layouts, part_of(): return lax.dynamic_slice_in_dim(array, index * width, width, axis)  3.68 us
    split x2, local copies, waits for them, and re-layouts, start_gather(): return ([pair, pair_swapped, second, jnp.split(near, cut)], *others[-2:])  3.59 us
  transfers between devices with their start and end apart: 22, of which 10 were waited for; matrix products, arithmetic and copies ran while one was open for 8% of the time, Pallas kernels for 4%

profile of v5, /device:TPU:0, one launch (start us, length us, event | category | flops | bytes accessed | tf_op | source)
XLA Modules:
  0.0 118.5 jit_solution(1592821061105418215)
XLA Ops:
  0.6 55.9 %conditional.1 = (f32[128,256]{1,0:T(8,128)}, bf16[128,256]{1,0:T(8,128)(2,1)}, bf16[128,1280]{1,0:T(8,128)(2,1)S(1)}, bf16[640,640]{1,0:T(8,128)(2,1)}, bf16[64...) conditional(s32[]{:T(128)} %convert_element_type.53, ...), branch_computations={%region_0.1_spmd, %region_1.2_spmd} | conditional | flops 1530459136 | bytes 52274720 | solution.py:482
  0.7 1.3 %constant_dynamic-slice_fusion = bf16[640,640]{1,0:T(8,128)(2,1)S(1)} fusion(bf16[1280,640]{1,0:T(8,128)(2,1)} %get-tuple-element.31, s32[]{:T(128)S(6)} %select_n.63), kind=kLoop, calls=%fused_computation.4 | loop fusion | bytes 1638404 | tf_op jit(solution)/shard_map/cond/branch_0_fun/dynamic_slice | solution.py:312
  2.0 4.9 %collective-permute-start.1 = (bf16[640,640]{1,0:T(8,128)(2,1)S(1)}, bf16[640,640]{1,0:T(8,128)(2,1)S(1)}, u32[]{:S(2)}, u32[]{:S(2)}) collective-permute-start(bf16[640,640]{1,0:T(8,128)(2,1)S(1)} %constant_dynamic-slice_fusion), channel_id=1, source_target_pairs={{0,4},{4,0},{8,12},{12,8},{1,5},{5,1},{9,13},{13,9},{16,20},{20,16... | collective-permute-start | bytes 2457608 | tf_op jit(solution)/shard_map/cond/branch_0_fun/ppermute | solution.py:289
  7.0 1.6 %collective-permute-start.2 = (bf16[640,640]{1,0:T(8,128)(2,1)S(1)}, bf16[640,640]{1,0:T(8,128)(2,1)}, u32[]{:S(2)}, u32[]{:S(2)}) collective-permute-start(bf16[640,640]{1,0:T(8,128)(2,1)S(1)} %constant_dynamic-slice_fusion), channel_id=1, source_target_pairs={{4,8},{8,4},{5,9},{9,5},{20,24},{24,20},{21,25},{25,21}} | collective-permute-start | bytes 2457608 | tf_op jit(solution)/shard_map/cond/branch_0_fun/ppermute | solution.py:289
  8.5 0.3 fusion.3
  8.9 0.7 copy-done.19
  9.6 1.9 %collective-permute-start = (bf16[128,256]{1,0:T(8,128)(2,1)S(1)}, bf16[128,256]{1,0:T(8,128)(2,1)S(1)}, u32[]{:S(2)}, u32[]{:S(2)}) collective-permute-start(bf16[128,256]{1,0:T(8,128)(2,1)S(1)} %dynamic-slice_convert_fusion), channel_id=1, source_target_pairs={{0,1},{1,0},{4,5},{5,4},{8,9},{9,8},{12,13},{13,12},{16,17},{17,16... | collective-permute-start | bytes 196616 | tf_op jit(solution)/shard_map/cond/branch_0_fun/ppermute | solution.py:289
  12.2 0.6 collective-permute-done
  12.7 1.6 %convert_add_fusion = f32[128,256]{1,0:T(8,128)} fusion(bf16[128,256]{1,0:T(8,128)(2,1)S(1)} %collective-permute-done, f32[128,512]{1,0:T(8,128)} %copy-done.19, s32[]{:T(128)S(6)} %select_n.61), kind=kLoop, calls=%fused_computation.2 | loop fusion | flops 65536 | bytes 327684 | tf_op jit(solution)/shard_map/cond/branch_0_fun/add | solution.py:452
  14.3 10.9 %collective-permute-done.1 = bf16[640,640]{1,0:T(8,128)(2,1)S(1)} collective-permute-done((bf16[640,640]{1,0:T(8,128)(2,1)S(1)}, bf16[640,640]{1,0:T(8,128)(2,1)S(1)}, u32[]{:S(2)}, u32[]{:S(2)}) %collective-permute-start.1) | collective-permute-done | bytes 819232 | tf_op jit(solution)/shard_map/cond/branch_0_fun/ppermute | solution.py:289
  25.2 0.7 broadcast_in_dim.21
  25.9 0.7 collective-permute-start.3
  26.6 1.3 %collective-permute-start.4 = (bf16[640,640]{1,0:T(8,128)(2,1)}, bf16[640,640]{1,0:T(8,128)(2,1)}, u32[]{:S(2)}, u32[]{:S(2)}) collective-permute-start(bf16[640,640]{1,0:T(8,128)(2,1)} %collective-permute-done.2), channel_id=1, source_target_pairs={{4,0},{8,12},{5,1},{9,13},{20,16},{24,28},{21,17},{25,29}} | collective-permute-start | bytes 2457608 | tf_op jit(solution)/shard_map/cond/branch_0_fun/ppermute | solution.py:289
  27.9 3.6 %collective-permute-start.5 = (bf16[640,640]{1,0:T(8,128)(2,1)S(1)}, bf16[640,640]{1,0:T(8,128)(2,1)S(1)}, u32[]{:S(2)}, u32[]{:S(2)}) collective-permute-start(bf16[640,640]{1,0:T(8,128)(2,1)S(1)} %collective-permute-done.1), channel_id=1, source_target_pairs={{0,16},{16,0},{1,17},{17,1},{4,20},{20,4},{5,21},{21,5},{8,24},{24... | collective-permute-start | bytes 2457608 | tf_op jit(solution)/shard_map/cond/branch_0_fun/ppermute | solution.py:289
  31.5 1.9 %split.16 = bf16[384,640]{1,0:T(8,128)(2,1)} slice(bf16[640,640]{1,0:T(8,128)(2,1)} %collective-permute-done.2), slice={[0:384], [0:640]} | slice | bytes 983040 | tf_op jit(solution)/shard_map/cond/branch_0_fun/split | solution.py:354
  33.4 1.7 %split.17 = bf16[256,640]{1,0:T(8,128)(2,1)} slice(bf16[640,640]{1,0:T(8,128)(2,1)} %collective-permute-done.2), slice={[384:640], [0:640]} | slice | bytes 655360 | tf_op jit(solution)/shard_map/cond/branch_0_fun/split | solution.py:354
  35.1 17.6 %collective-permute-done.4 = bf16[640,640]{1,0:T(8,128)(2,1)} collective-permute-done((bf16[640,640]{1,0:T(8,128)(2,1)}, bf16[640,640]{1,0:T(8,128)(2,1)}, u32[]{:S(2)}, u32[]{:S(2)}) %collective-permute-start.4) | collective-permute-done | bytes 819232 | tf_op jit(solution)/shard_map/cond/branch_0_fun/ppermute | solution.py:289
  52.7 2.0 %slice_select_fusion.1 = bf16[256,640]{1,0:T(8,128)(2,1)} fusion(bf16[640,640]{1,0:T(8,128)(2,1)} %collective-permute-done.4, bf16[640,640]{1,0:T(8,128)(2,1)S(1)} %collective-permute-done.3, pred[]{:T(512)S(6)} %or.4), kind=kLoop, calls=%fused_computation.1 | loop fusion | flops 163840 | bytes 983041 | tf_op jit(solution)/shard_map/cond/branch_0_fun/jit(_where)/select_n | solution.py:351
  54.7 1.9 %slice_select_fusion = bf16[384,640]{1,0:T(8,128)(2,1)} fusion(bf16[640,640]{1,0:T(8,128)(2,1)} %collective-permute-done.4, bf16[640,640]{1,0:T(8,128)(2,1)S(1)} %collective-permute-done.3, pred[]{:T(512)S(6)} %or.4), kind=kLoop, calls=%fused_computation | loop fusion | flops 245760 | bytes 1474561 | tf_op jit(solution)/shard_map/cond/branch_0_fun/jit(_where)/select_n | solution.py:351
  56.6 1.4 %collective-permute-start.20 = (bf16[256,640]{1,0:T(8,128)(2,1)}, bf16[256,640]{1,0:T(8,128)(2,1)S(1)}, u32[]{:S(2)}, u32[]{:S(2)}) collective-permute-start(bf16[256,640]{1,0:T(8,128)(2,1)} %get-tuple-element.88.refs_3_), channel_id=1, source_target_pairs={{4,0},{8,12},{5,1},{9,13},{20,16},{24,28},{21,17},{25,29}} | collective-permute-start | bytes 983048 | tf_op jit(solution)/shard_map/ppermute | solution.py:289
  58.0 1.3 %collective-permute-start.19 = (bf16[384,640]{1,0:T(8,128)(2,1)}, bf16[384,640]{1,0:T(8,128)(2,1)}, u32[]{:S(2)}, u32[]{:S(2)}) collective-permute-start(bf16[384,640]{1,0:T(8,128)(2,1)} %get-tuple-element.87.refs_2_), channel_id=1, source_target_pairs={{4,0},{8,12},{5,1},{9,13},{20,16},{24,28},{21,17},{25,29}} | collective-permute-start | bytes 1474568 | tf_op jit(solution)/shard_map/ppermute | solution.py:289
  59.3 3.4 %collective-permute-start.17 = (bf16[384,640]{1,0:T(8,128)(2,1)}, bf16[384,640]{1,0:T(8,128)(2,1)S(1)}, u32[]{:S(2)}, u32[]{:S(2)}) collective-permute-start(bf16[384,640]{1,0:T(8,128)(2,1)} %get-tuple-element.87.refs_2_), channel_id=1, source_target_pairs={{0,16},{16,0},{1,17},{17,1},{4,20},{20,4},{5,21},{21,5},{8,24},{24... | collective-permute-start | bytes 1474568 | tf_op jit(solution)/shard_map/ppermute | solution.py:289
  62.8 2.4 %collective-permute-start.18 = (bf16[256,640]{1,0:T(8,128)(2,1)}, bf16[256,640]{1,0:T(8,128)(2,1)S(1)}, u32[]{:S(2)}, u32[]{:S(2)}) collective-permute-start(bf16[256,640]{1,0:T(8,128)(2,1)} %get-tuple-element.88.refs_3_), channel_id=1, source_target_pairs={{0,16},{16,0},{1,17},{17,1},{4,20},{20,4},{5,21},{21,5},{8,24},{24... | collective-permute-start | bytes 983048 | tf_op jit(solution)/shard_map/ppermute | solution.py:289
  65.2 1.3 %collective-permute-start.15 = (bf16[128,1280]{1,0:T(8,128)(2,1)}, bf16[128,1280]{1,0:T(8,128)(2,1)S(1)}, u32[]{:S(2)}, u32[]{:S(2)}) collective-permute-start(bf16[128,1280]{1,0:T(8,128)(2,1)} %copy-done.20), channel_id=1, source_target_pairs={{2,0},{3,1},{6,4},{7,5},{10,8},{11,9},{14,12},{15,13},{18,16},{19,... | collective-permute-start | bytes 983048 | tf_op jit(solution)/shard_map/ppermute | solution.py:289
  67.2 4.4 %shard_map.88 = (bf16[10,128,128]{2,1,0:T(8,128)(2,1)S(1)}, f32[128,1280]{1,0:T(8,128)S(1)}, f32[128,256]{1,0:T(8,128)S(1)}) custom-call(s32[1]{0:T(128)} %copy.27.length, bf16[128,1280]{1,0:T(8,128)(2,1)} %bitcast.38, bf16[128,256]{1,0:T(8,128)(2,1)} %bitcast.41, f32[128,256]{1,0:T(8,128)} %get-tuple-element.96.values), custom_call_target="tpu_custom_call" | custom-call | flops 100000000 | bytes 3000000 | tf_op jit(solution)/shard_map/pallas_call | solution.py:78
  71.8 3.4 %collective-permute-start.21 = (bf16[256,640]{1,0:T(8,128)(2,1)S(1)}, bf16[256,640]{1,0:T(8,128)(2,1)}, u32[]{:S(2)}, u32[]{:S(2)}) collective-permute-start(bf16[256,640]{1,0:T(8,128)(2,1)S(1)} %broadcast_select_fusion.1.refs_7_), channel_id=1, source_target_pairs={{0,16},{16,0},{1,17},{17,1},{4,20},{20,4},{5,21},{21,5},{8,24},{24... | collective-permute-start | bytes 983048 | tf_op jit(solution)/shard_map/ppermute | solution.py:289
  75.2 1.5 %collective-permute-done.15.refs_0_ = bf16[128,1280]{1,0:T(8,128)(2,1)S(1)} collective-permute-done((bf16[128,1280]{1,0:T(8,128)(2,1)}, bf16[128,1280]{1,0:T(8,128)(2,1)S(1)}, u32[]{:S(2)}, u32[]{:S(2)}) %collective-permute-start.15) | collective-permute-done | bytes 327712 | tf_op jit(solution)/shard_map/ppermute | solution.py:289
  76.7 0.4 shard_map.86.sens_own
  77.0 1.9 %collective-permute-start.16 = (bf16[128,1280]{1,0:T(8,128)(2,1)S(1)}, bf16[128,1280]{1,0:T(8,128)(2,1)}, u32[]{:S(2)}, u32[]{:S(2)}) collective-permute-start(bf16[128,1280]{1,0:T(8,128)(2,1)S(1)} %shard_map.86.sens_own), channel_id=1, source_target_pairs={{0,1},{1,0},{4,5},{5,4},{8,9},{9,8},{12,13},{13,12},{16,17},{17,16... | collective-permute-start | bytes 983048 | tf_op jit(solution)/shard_map/ppermute | solution.py:289
  79.0 1.1 broadcast_select_fusion.refs_6_
  80.1 3.4 %collective-permute-start.25 = (bf16[384,640]{1,0:T(8,128)(2,1)S(1)}, bf16[384,640]{1,0:T(8,128)(2,1)S(1)}, u32[]{:S(2)}, u32[]{:S(2)}) collective-permute-start(bf16[384,640]{1,0:T(8,128)(2,1)S(1)} %broadcast_select_fusion.refs_6_), channel_id=1, source_target_pairs={{0,16},{16,0},{1,17},{17,1},{4,20},{20,4},{5,21},{21,5},{8,24},{24... | collective-permute-start | bytes 1474568 | tf_op jit(solution)/shard_map/ppermute | solution.py:289
  83.6 1.1 dynamic-slice_bitcast_fusion.value_block
  84.7 2.9 %collective-permute-done.21.refs_9_ = bf16[256,640]{1,0:T(8,128)(2,1)} collective-permute-done((bf16[256,640]{1,0:T(8,128)(2,1)S(1)}, bf16[256,640]{1,0:T(8,128)(2,1)}, u32[]{:S(2)}, u32[]{:S(2)}) %collective-permute-start.21) | collective-permute-done | bytes 327712 | tf_op jit(solution)/shard_map/ppermute | solution.py:289
  87.6 1.3 %constant_dynamic-slice_fusion.5 = (bf16[128,320]{1,0:T(8,128)(2,1)S(1)}, bf16[128,320]{1,0:T(8,128)(2,1)S(1)}, bf16[128,320]{1,0:T(8,128)(2,1)S(1)}, bf16[128,320]{1,0:T(8,128)(2,1)S(1)}) fusion(bf16[128,1280]{1,0:T(8,128)(2,1)} %bitcast.28, s32[]{:T(128)S(6)} %select_n.94, s32[]{:T(128)S(6)} %select_n.93, s32[]{:T(128)S(6)} %select_n.92, s32[]{:T(128)S(6)} %select_n.91), kind=kLoop, calls=%fused_computation.25 | loop fusion | bytes 655376 | tf_op jit(solution)/shard_map/dynamic_slice | solution.py:312
  88.9 4.9 %collective-permute-start.22 = (bf16[128,320]{1,0:T(8,128)(2,1)S(1)}, bf16[128,320]{1,0:T(8,128)(2,1)S(1)}, u32[]{:S(2)}, u32[]{:S(2)}) collective-permute-start(bf16[128,320]{1,0:T(8,128)(2,1)S(1)} %get-tuple-element.113), channel_id=1, source_target_pairs={{0,4},{4,8},{8,12},{12,0},{1,5},{5,9},{9,13},{13,1},{2,6},{6,10},{... | collective-permute-start | bytes 245768 | tf_op jit(solution)/shard_map/ppermute | solution.py:289
  93.8 0.8 collective-permute-start.23
  94.6 2.8 %collective-permute-start.24 = (bf16[128,320]{1,0:T(8,128)(2,1)S(1)}, bf16[128,320]{1,0:T(8,128)(2,1)S(1)}, u32[]{:S(2)}, u32[]{:S(2)}) collective-permute-start(bf16[128,320]{1,0:T(8,128)(2,1)S(1)} %get-tuple-element.111), channel_id=1, source_target_pairs={{0,12},{4,0},{8,4},{12,8},{1,13},{5,1},{9,5},{13,9},{2,14},{6,2},{... | collective-permute-start | bytes 245768 | tf_op jit(solution)/shard_map/ppermute | solution.py:289
  97.4 0.4 fusion
  97.9 2.5 %collective-permute-done.23.refs_2_ = bf16[128,320]{1,0:T(8,128)(2,1)S(1)} collective-permute-done((bf16[128,320]{1,0:T(8,128)(2,1)S(1)}, bf16[128,320]{1,0:T(8,128)(2,1)S(1)}, u32[]{:S(2)}, u32[]{:S(2)}) %collective-permute-start.23) | collective-permute-done | bytes 81952 | tf_op jit(solution)/shard_map/ppermute | solution.py:289
  100.6 4.3 %shard_map.89.refs_0_ = bf16[128,256]{1,0:T(8,128)(2,1)S(1)} custom-call(s32[4]{0:T(128)S(1)} %pad_add_fusion.1.place, bf16[128,1280]{1,0:T(8,128)(2,1)S(1)} %shard_map.86.sens_own, bf16[128,1280]{1,0:T(8,128)(2,1)} %collective-permute-done.16.sens_other, bf16[1280,640]{1,0:T(8,128)(2,1)S(1)} %bitcast.36, bf16[640,640]{1,0:T(8,128)(2,1)} %get-tuple-element.93.refs_0_, ...), custom_call_target="tpu_custom_call" | custom-call | flops 1000000000 | bytes 8000000 | tf_op jit(solution)/shard_map/pallas_call | solution.py:241
  105.0 1.0 multiply_reduce_fusion
  106.1 1.7 %collective-permute-start.26 = (bf16[128,256]{1,0:T(8,128)(2,1)S(1)}, bf16[128,256]{1,0:T(8,128)(2,1)S(1)}, u32[]{:S(2)}, u32[]{:S(2)}) collective-permute-start(bf16[128,256]{1,0:T(8,128)(2,1)S(1)} %shard_map.89.refs_0_), channel_id=1, source_target_pairs={{0,4},{4,8},{8,12},{12,0},{1,5},{5,9},{9,13},{13,1},{2,6},{6,10},{... | collective-permute-start | bytes 196616 | tf_op jit(solution)/shard_map/ppermute | solution.py:289
  107.7 2.4 %collective-permute-start.27 = (bf16[128,256]{1,0:T(8,128)(2,1)S(1)}, bf16[128,256]{1,0:T(8,128)(2,1)S(1)}, u32[]{:S(2)}, u32[]{:S(2)}) collective-permute-start(bf16[128,256]{1,0:T(8,128)(2,1)S(1)} %shard_map.89.refs_0_), channel_id=1, source_target_pairs={{0,8},{4,12},{8,0},{12,4},{1,9},{5,13},{9,1},{13,5},{2,10},{6,14},... | collective-permute-start | bytes 196616 | tf_op jit(solution)/shard_map/ppermute | solution.py:289
  110.4 0.5 add_multiply_fusion
  110.9 2.0 %collective-permute-done.26.refs_1_ = bf16[128,256]{1,0:T(8,128)(2,1)S(1)} collective-permute-done((bf16[128,256]{1,0:T(8,128)(2,1)S(1)}, bf16[128,256]{1,0:T(8,128)(2,1)S(1)}, u32[]{:S(2)}, u32[]{:S(2)}) %collective-permute-start.26) | collective-permute-done | bytes 65568 | tf_op jit(solution)/shard_map/ppermute | solution.py:289
  112.9 2.4 %collective-permute-done.27.refs_2_ = bf16[128,256]{1,0:T(8,128)(2,1)S(1)} collective-permute-done((bf16[128,256]{1,0:T(8,128)(2,1)S(1)}, bf16[128,256]{1,0:T(8,128)(2,1)S(1)}, u32[]{:S(2)}, u32[]{:S(2)}) %collective-permute-start.27) | collective-permute-done | bytes 65568 | tf_op jit(solution)/shard_map/ppermute | solution.py:289
  115.7 1.5 %collective-permute-done.30.refs_4_ = bf16[512,256]{1,0:T(8,128)(2,1)S(1)} collective-permute-done((bf16[512,256]{1,0:T(8,128)(2,1)S(1)}, bf16[512,256]{1,0:T(8,128)(2,1)S(1)}, u32[]{:S(2)}, u32[]{:S(2)}) %collective-permute-start.30) | collective-permute-done | bytes 262176 | tf_op jit(solution)/shard_map/ppermute | solution.py:289
  117.2 1.3 %shard_map.90 = f32[320,512]{1,0:T(8,128)} custom-call(s32[1]{0:T(128)} %bitcast.5.core, bf16[320,512]{1,0:T(8,128)(2,1)S(1)} %shard_map.87.inputs_t, bf16[320,512]{1,0:T(8,128)(2,1)S(1)} %dynamic-slice_bitcast_fusion.value_block, bf16[128,256]{1,0:T(8,128)(2,1)S(1)} %shard_map.89.refs_0_, bf16[128,256]{1,0:T(8,128)(2,1)S(1)} %collective-permute-done.26.refs_1_, ...), custom_call_target="tpu_custom_call" | custom-call | flops 200000000 | bytes 2000000 | tf_op jit(solution)/shard_map/pallas_call | solution.py:281
  (53 shorter events, 1.2 us)
Async XLA Ops:
  0.6 7.9 %copy-start.6 = (bf16[128,1280]{1,0:T(8,128)(2,1)S(1)}, bf16[128,1280]{1,0:T(8,128)(2,1)}, u32[]{:S(2)}) copy-start(bf16[128,1280]{1,0:T(8,128)(2,1)} %get-tuple-element.28) | copy-start | bytes 983044 | tf_op jit(solution)/shard_map/cond
  0.7 7.9 %copy-start.9 = (bf16[1280,512]{1,0:T(8,128)(2,1)S(1)}, bf16[1280,512]{1,0:T(8,128)(2,1)}, u32[]{:S(2)}) copy-start(bf16[1280,512]{1,0:T(8,128)(2,1)} %get-tuple-element.29) | copy-start | bytes 3932164 | tf_op jit(solution)/shard_map/cond
  2.0 23.2 %collective-permute-start.1 = (bf16[640,640]{1,0:T(8,128)(2,1)S(1)}, bf16[640,640]{1,0:T(8,128)(2,1)S(1)}, u32[]{:S(2)}, u32[]{:S(2)}) collective-permute-start(bf16[640,640]{1,0:T(8,128)(2,1)S(1)} %constant_dynamic-slice_fusion), channel_id=1, source_target_pairs={{0,4},{4,0},{8,12},{12,8},{1,5},{5,1},{9,13},{13,9},{16,20},{20,16... | collective-permute-start | bytes 2457608 | tf_op jit(solution)/shard_map/cond/branch_0_fun/ppermute | solution.py:289
  7.0 18.2 %collective-permute-start.2 = (bf16[640,640]{1,0:T(8,128)(2,1)S(1)}, bf16[640,640]{1,0:T(8,128)(2,1)}, u32[]{:S(2)}, u32[]{:S(2)}) collective-permute-start(bf16[640,640]{1,0:T(8,128)(2,1)S(1)} %constant_dynamic-slice_fusion), channel_id=1, source_target_pairs={{4,8},{8,4},{5,9},{9,5},{20,24},{24,20},{21,25},{25,21}} | collective-permute-start | bytes 2457608 | tf_op jit(solution)/shard_map/cond/branch_0_fun/ppermute | solution.py:289
  8.9 0.7 copy-start.19
  9.6 3.1 %collective-permute-start = (bf16[128,256]{1,0:T(8,128)(2,1)S(1)}, bf16[128,256]{1,0:T(8,128)(2,1)S(1)}, u32[]{:S(2)}, u32[]{:S(2)}) collective-permute-start(bf16[128,256]{1,0:T(8,128)(2,1)S(1)} %dynamic-slice_convert_fusion), channel_id=1, source_target_pairs={{0,1},{1,0},{4,5},{5,4},{8,9},{9,8},{12,13},{13,12},{16,17},{17,16... | collective-permute-start | bytes 196616 | tf_op jit(solution)/shard_map/cond/branch_0_fun/ppermute | solution.py:289
  25.2 31.4 %copy-start.17 = (bf16[640,640]{1,0:T(8,128)(2,1)}, bf16[640,640]{1,0:T(8,128)(2,1)S(1)}, u32[]{:S(2)}) copy-start(bf16[640,640]{1,0:T(8,128)(2,1)S(1)} %collective-permute-done.1) | copy-start | bytes 2457604 | tf_op jit(solution)/shard_map/cond
  25.9 9.2 %collective-permute-start.3 = (bf16[640,640]{1,0:T(8,128)(2,1)S(1)}, bf16[640,640]{1,0:T(8,128)(2,1)S(1)}, u32[]{:S(2)}, u32[]{:S(2)}) collective-permute-start(bf16[640,640]{1,0:T(8,128)(2,1)S(1)} %collective-permute-done.1), channel_id=1, source_target_pairs={{4,8},{8,4},{5,9},{9,5},{20,24},{24,20},{21,25},{25,21}} | collective-permute-start | bytes 2457608 | tf_op jit(solution)/shard_map/cond/branch_0_fun/ppermute | solution.py:289
  26.6 26.1 %collective-permute-start.4 = (bf16[640,640]{1,0:T(8,128)(2,1)}, bf16[640,640]{1,0:T(8,128)(2,1)}, u32[]{:S(2)}, u32[]{:S(2)}) collective-permute-start(bf16[640,640]{1,0:T(8,128)(2,1)} %collective-permute-done.2), channel_id=1, source_target_pairs={{4,0},{8,12},{5,1},{9,13},{20,16},{24,28},{21,17},{25,29}} | collective-permute-start | bytes 2457608 | tf_op jit(solution)/shard_map/cond/branch_0_fun/ppermute | solution.py:289
  27.9 24.8 %collective-permute-start.5 = (bf16[640,640]{1,0:T(8,128)(2,1)S(1)}, bf16[640,640]{1,0:T(8,128)(2,1)S(1)}, u32[]{:S(2)}, u32[]{:S(2)}) collective-permute-start(bf16[640,640]{1,0:T(8,128)(2,1)S(1)} %collective-permute-done.1), channel_id=1, source_target_pairs={{0,16},{16,0},{1,17},{17,1},{4,20},{20,4},{5,21},{21,5},{8,24},{24... | collective-permute-start | bytes 2457608 | tf_op jit(solution)/shard_map/cond/branch_0_fun/ppermute | solution.py:289
  52.7 3.8 %copy-start.18 = (bf16[640,640]{1,0:T(8,128)(2,1)}, bf16[640,640]{1,0:T(8,128)(2,1)S(1)}, u32[]{:S(2)}) copy-start(bf16[640,640]{1,0:T(8,128)(2,1)S(1)} %collective-permute-done.5) | copy-start | bytes 2457604 | tf_op jit(solution)/shard_map/cond
  56.6 1.5 %copy-start.20 = (bf16[128,1280]{1,0:T(8,128)(2,1)}, bf16[128,1280]{1,0:T(8,128)(2,1)S(1)}, u32[]{:S(2)}) copy-start(bf16[128,1280]{1,0:T(8,128)(2,1)S(1)} %get-tuple-element.86) | copy-start | bytes 983044
  56.6 20.1 %copy-start.4 = (bf16[1,1,128,1280]{3,2,1,0:T(8,128)(2,1)S(1)}, bf16[1,1,128,1280]{3,2,1,0:T(8,128)(2,1)}, u32[]{:S(2)}) copy-start(bf16[1,1,128,1280]{3,2,1,0:T(8,128)(2,1)} %param.9) | copy-start | bytes 983044
  56.6 20.1 %copy-start.12 = (bf16[1,1,128,1280]{3,2,1,0:T(8,128)(2,1)S(1)}, bf16[1,1,128,1280]{3,2,1,0:T(8,128)(2,1)}, u32[]{:S(2)}) copy-start(bf16[1,1,128,1280]{3,2,1,0:T(8,128)(2,1)} %param.10) | copy-start | bytes 983044
  56.6 15.1 %collective-permute-start.20 = (bf16[256,640]{1,0:T(8,128)(2,1)}, bf16[256,640]{1,0:T(8,128)(2,1)S(1)}, u32[]{:S(2)}, u32[]{:S(2)}) collective-permute-start(bf16[256,640]{1,0:T(8,128)(2,1)} %get-tuple-element.88.refs_3_), channel_id=1, source_target_pairs={{4,0},{8,12},{5,1},{9,13},{20,16},{24,28},{21,17},{25,29}} | collective-permute-start | bytes 983048 | tf_op jit(solution)/shard_map/ppermute | solution.py:289
  58.0 20.9 %collective-permute-start.19 = (bf16[384,640]{1,0:T(8,128)(2,1)}, bf16[384,640]{1,0:T(8,128)(2,1)}, u32[]{:S(2)}, u32[]{:S(2)}) collective-permute-start(bf16[384,640]{1,0:T(8,128)(2,1)} %get-tuple-element.87.refs_2_), channel_id=1, source_target_pairs={{4,0},{8,12},{5,1},{9,13},{20,16},{24,28},{21,17},{25,29}} | collective-permute-start | bytes 1474568 | tf_op jit(solution)/shard_map/ppermute | solution.py:289
  59.3 25.4 %collective-permute-start.17 = (bf16[384,640]{1,0:T(8,128)(2,1)}, bf16[384,640]{1,0:T(8,128)(2,1)S(1)}, u32[]{:S(2)}, u32[]{:S(2)}) collective-permute-start(bf16[384,640]{1,0:T(8,128)(2,1)} %get-tuple-element.87.refs_2_), channel_id=1, source_target_pairs={{0,16},{16,0},{1,17},{17,1},{4,20},{20,4},{5,21},{21,5},{8,24},{24... | collective-permute-start | bytes 1474568 | tf_op jit(solution)/shard_map/ppermute | solution.py:289
  62.8 21.9 %collective-permute-start.18 = (bf16[256,640]{1,0:T(8,128)(2,1)}, bf16[256,640]{1,0:T(8,128)(2,1)S(1)}, u32[]{:S(2)}, u32[]{:S(2)}) collective-permute-start(bf16[256,640]{1,0:T(8,128)(2,1)} %get-tuple-element.88.refs_3_), channel_id=1, source_target_pairs={{0,16},{16,0},{1,17},{17,1},{4,20},{20,4},{5,21},{21,5},{8,24},{24... | collective-permute-start | bytes 983048 | tf_op jit(solution)/shard_map/ppermute | solution.py:289
  65.2 11.5 %collective-permute-start.15 = (bf16[128,1280]{1,0:T(8,128)(2,1)}, bf16[128,1280]{1,0:T(8,128)(2,1)S(1)}, u32[]{:S(2)}, u32[]{:S(2)}) collective-permute-start(bf16[128,1280]{1,0:T(8,128)(2,1)} %copy-done.20), channel_id=1, source_target_pairs={{2,0},{3,1},{6,4},{7,5},{10,8},{11,9},{14,12},{15,13},{18,16},{19,... | collective-permute-start | bytes 983048 | tf_op jit(solution)/shard_map/ppermute | solution.py:289
  71.6 7.4 %copy-start = (bf16[10,128,128]{2,1,0:T(8,128)(2,1)}, bf16[10,128,128]{2,1,0:T(8,128)(2,1)S(1)}, u32[]{:S(2)}) copy-start(bf16[10,128,128]{2,1,0:T(8,128)(2,1)S(1)} %get-tuple-element.97.refs_11_) | copy-start | bytes 983044
  71.6 7.4 %copy-start.2 = (f32[128,256]{1,0:T(8,128)}, f32[128,256]{1,0:T(8,128)S(1)}, u32[]{:S(2)}) copy-start(f32[128,256]{1,0:T(8,128)S(1)} %get-tuple-element.99.refs_13_) | copy-start | bytes 393220
  71.8 15.9 %collective-permute-start.21 = (bf16[256,640]{1,0:T(8,128)(2,1)S(1)}, bf16[256,640]{1,0:T(8,128)(2,1)}, u32[]{:S(2)}, u32[]{:S(2)}) collective-permute-start(bf16[256,640]{1,0:T(8,128)(2,1)S(1)} %broadcast_select_fusion.1.refs_7_), channel_id=1, source_target_pairs={{0,16},{16,0},{1,17},{17,1},{4,20},{20,4},{5,21},{21,5},{8,24},{24... | collective-permute-start | bytes 983048 | tf_op jit(solution)/shard_map/ppermute | solution.py:289
  77.0 10.6 %collective-permute-start.16 = (bf16[128,1280]{1,0:T(8,128)(2,1)S(1)}, bf16[128,1280]{1,0:T(8,128)(2,1)}, u32[]{:S(2)}, u32[]{:S(2)}) collective-permute-start(bf16[128,1280]{1,0:T(8,128)(2,1)S(1)} %shard_map.86.sens_own), channel_id=1, source_target_pairs={{0,1},{1,0},{4,5},{5,4},{8,9},{9,8},{12,13},{13,12},{16,17},{17,16... | collective-permute-start | bytes 983048 | tf_op jit(solution)/shard_map/ppermute | solution.py:289
  80.1 20.5 %collective-permute-start.25 = (bf16[384,640]{1,0:T(8,128)(2,1)S(1)}, bf16[384,640]{1,0:T(8,128)(2,1)S(1)}, u32[]{:S(2)}, u32[]{:S(2)}) collective-permute-start(bf16[384,640]{1,0:T(8,128)(2,1)S(1)} %broadcast_select_fusion.refs_6_), channel_id=1, source_target_pairs={{0,16},{16,0},{1,17},{17,1},{4,20},{20,4},{5,21},{21,5},{8,24},{24... | collective-permute-start | bytes 1474568 | tf_op jit(solution)/shard_map/ppermute | solution.py:289
  83.6 13.9 %copy-start.5 = (bf16[1,1,128,1280]{3,2,1,0:T(8,128)(2,1)S(1)}, bf16[1,1,128,1280]{3,2,1,0:T(8,128)(2,1)}, u32[]{:S(2)}) copy-start(bf16[1,1,128,1280]{3,2,1,0:T(8,128)(2,1)} %param.9) | copy-start | bytes 983044
  83.6 13.9 %copy-start.13 = (bf16[1,1,128,1280]{3,2,1,0:T(8,128)(2,1)S(1)}, bf16[1,1,128,1280]{3,2,1,0:T(8,128)(2,1)}, u32[]{:S(2)}) copy-start(bf16[1,1,128,1280]{3,2,1,0:T(8,128)(2,1)} %param.10) | copy-start | bytes 983044
  84.7 15.9 %copy-start.1 = (bf16[10,128,128]{2,1,0:T(8,128)(2,1)S(1)}, bf16[10,128,128]{2,1,0:T(8,128)(2,1)}, u32[]{:S(2)}) copy-start(bf16[10,128,128]{2,1,0:T(8,128)(2,1)} %copy-done) | copy-start | bytes 983044
  84.7 15.9 %copy-start.3 = (f32[128,256]{1,0:T(8,128)S(1)}, f32[128,256]{1,0:T(8,128)}, u32[]{:S(2)}) copy-start(f32[128,256]{1,0:T(8,128)} %copy-done.2) | copy-start | bytes 393220
  84.7 15.9 %copy-start.15 = (bf16[1,1280,640]{2,1,0:T(8,128)(2,1)S(1)}, bf16[1,1280,640]{2,1,0:T(8,128)(2,1)}, u32[]{:S(2)}) copy-start(bf16[1,1280,640]{2,1,0:T(8,128)(2,1)} %param.14) | copy-start | bytes 4915204
  88.9 9.0 %collective-permute-start.22 = (bf16[128,320]{1,0:T(8,128)(2,1)S(1)}, bf16[128,320]{1,0:T(8,128)(2,1)S(1)}, u32[]{:S(2)}, u32[]{:S(2)}) collective-permute-start(bf16[128,320]{1,0:T(8,128)(2,1)S(1)} %get-tuple-element.113), channel_id=1, source_target_pairs={{0,4},{4,8},{8,12},{12,0},{1,5},{5,9},{9,13},{13,1},{2,6},{6,10},{... | collective-permute-start | bytes 245768 | tf_op jit(solution)/shard_map/ppermute | solution.py:289
  93.8 6.6 %collective-permute-start.23 = (bf16[128,320]{1,0:T(8,128)(2,1)S(1)}, bf16[128,320]{1,0:T(8,128)(2,1)S(1)}, u32[]{:S(2)}, u32[]{:S(2)}) collective-permute-start(bf16[128,320]{1,0:T(8,128)(2,1)S(1)} %get-tuple-element.112), channel_id=1, source_target_pairs={{0,8},{4,12},{8,0},{12,4},{1,9},{5,13},{9,1},{13,5},{2,10},{6,14},... | collective-permute-start | bytes 245768 | tf_op jit(solution)/shard_map/ppermute | solution.py:289
  94.6 5.8 %collective-permute-start.24 = (bf16[128,320]{1,0:T(8,128)(2,1)S(1)}, bf16[128,320]{1,0:T(8,128)(2,1)S(1)}, u32[]{:S(2)}, u32[]{:S(2)}) collective-permute-start(bf16[128,320]{1,0:T(8,128)(2,1)S(1)} %get-tuple-element.111), channel_id=1, source_target_pairs={{0,12},{4,0},{8,4},{12,8},{1,13},{5,1},{9,5},{13,9},{2,14},{6,2},{... | collective-permute-start | bytes 245768 | tf_op jit(solution)/shard_map/ppermute | solution.py:289
  106.0 4.4 %collective-permute-start.29 = (f32[128]{0:T(128)S(1)}, f32[128]{0:T(128)S(1)}, u32[]{:S(2)}, u32[]{:S(2)}) collective-permute-start(f32[128]{0:T(128)S(1)} %add.105), channel_id=1, source_target_pairs={{0,1},{1,0},{2,3},{3,2},{4,5},{5,4},{6,7},{7,6},{8,9},{9,8},{10,11... | collective-permute-start | bytes 1544 | tf_op jit(solution)/shard_map/ppermute | solution.py:289
  106.1 6.8 %collective-permute-start.26 = (bf16[128,256]{1,0:T(8,128)(2,1)S(1)}, bf16[128,256]{1,0:T(8,128)(2,1)S(1)}, u32[]{:S(2)}, u32[]{:S(2)}) collective-permute-start(bf16[128,256]{1,0:T(8,128)(2,1)S(1)} %shard_map.89.refs_0_), channel_id=1, source_target_pairs={{0,4},{4,8},{8,12},{12,0},{1,5},{5,9},{9,13},{13,1},{2,6},{6,10},{... | collective-permute-start | bytes 196616 | tf_op jit(solution)/shard_map/ppermute | solution.py:289
  107.7 7.5 %collective-permute-start.27 = (bf16[128,256]{1,0:T(8,128)(2,1)S(1)}, bf16[128,256]{1,0:T(8,128)(2,1)S(1)}, u32[]{:S(2)}, u32[]{:S(2)}) collective-permute-start(bf16[128,256]{1,0:T(8,128)(2,1)S(1)} %shard_map.89.refs_0_), channel_id=1, source_target_pairs={{0,8},{4,12},{8,0},{12,4},{1,9},{5,13},{9,1},{13,5},{2,10},{6,14},... | collective-permute-start | bytes 196616 | tf_op jit(solution)/shard_map/ppermute | solution.py:289
  110.1 5.5 %collective-permute-start.28 = (bf16[128,256]{1,0:T(8,128)(2,1)S(1)}, bf16[128,256]{1,0:T(8,128)(2,1)S(1)}, u32[]{:S(2)}, u32[]{:S(2)}) collective-permute-start(bf16[128,256]{1,0:T(8,128)(2,1)S(1)} %shard_map.89.refs_0_), channel_id=1, source_target_pairs={{0,12},{4,0},{8,4},{12,8},{1,13},{5,1},{9,5},{13,9},{2,14},{6,2},{... | collective-permute-start | bytes 196616 | tf_op jit(solution)/shard_map/ppermute | solution.py:289
  115.6 1.6 %collective-permute-start.30 = (bf16[512,256]{1,0:T(8,128)(2,1)S(1)}, bf16[512,256]{1,0:T(8,128)(2,1)S(1)}, u32[]{:S(2)}, u32[]{:S(2)}) collective-permute-start(bf16[512,256]{1,0:T(8,128)(2,1)S(1)} %pad_maximum_fusion.1), channel_id=1, source_target_pairs={{0,1},{1,0},{2,3},{3,2},{4,5},{5,4},{6,7},{7,6},{8,9},{9,8},{10,11... | collective-permute-start | bytes 786440 | tf_op jit(solution)/shard_map/ppermute | solution.py:289

commit v6 on v5

v6 whole, which is shorter than its diff:
```python
import functools
import itertools
import math

import jax
import jax.numpy as jnp
from jax import lax
from jax.experimental import pallas as pl
from jax.experimental.pallas import tpu as pltpu
from jax.sharding import PartitionSpec as P

DW = 2560
HD = 128
QH = 20
KVH = 4
EPS = 0.25
F32 = jnp.float32
BF16 = jnp.bfloat16


def stabilize(entries):
    return jnp.where(entries >= 0, entries + EPS, entries - EPS)


VMEM = pl.BlockSpec(memory_space=pltpu.VMEM)
SMEM = pl.BlockSpec(memory_space=pltpu.SMEM)


def by_columns(left, right):
    return lax.dot_general(left, right, (((1,), (1,)), ((), ())), preferred_element_type=F32)


def kernel_call(body, shapes, in_specs, scratch=(), flops=0, nbytes=0, limit=24):
    return pl.pallas_call(
        body,
        out_shape=shapes,
        in_specs=in_specs,
        out_specs=jax.tree.map(lambda _: VMEM, shapes),
        scratch_shapes=scratch,
        compiler_params=pltpu.CompilerParams(vmem_limit_bytes=limit * 2**20),
        cost_estimate=pl.CostEstimate(flops=flops, bytes_accessed=nbytes, transcendentals=0),
    )


def attention_kernel(length, queries, keys, values, probs_t, mixed_gain, value_gain):
    seq_len = queries.shape[0]
    kv_heads = keys.shape[1] // HD
    group_size = queries.shape[1] // HD // kv_heads
    row = lax.broadcasted_iota(jnp.int32, (seq_len, seq_len), 0)
    column = lax.broadcasted_iota(jnp.int32, (seq_len, seq_len), 1)
    allowed = (column <= row) & (column < length[0])
    values_bf = values[...].astype(BF16)
    values_r = values_bf.astype(F32)
    value_gain[...] = values_r / stabilize(values_r)
    for g in range(kv_heads):
        key_head = keys[:, g * HD : (g + 1) * HD]
        value_head = values_bf[:, g * HD : (g + 1) * HD]
        for h in range(g * group_size, (g + 1) * group_size):
            scores = by_columns(queries[:, h * HD : (h + 1) * HD], key_head) / math.sqrt(HD)
            scores = jnp.where(allowed, scores, -1000000000.0)
            weights = jnp.exp(scores - jnp.max(scores, axis=1, keepdims=True))
            probs = weights / jnp.sum(weights, axis=1, keepdims=True)
            probs_t[h] = probs.T.astype(BF16)
            mixed = jnp.dot(probs.astype(BF16), value_head, preferred_element_type=F32)
            mixed_gain[:, h * HD : (h + 1) * HD] = mixed / stabilize(mixed)


def attend(length, queries, keys, values):
    seq_len, width = queries.shape
    shapes = (
        jax.ShapeDtypeStruct((width // HD, seq_len, seq_len), BF16),
        jax.ShapeDtypeStruct((seq_len, width), F32),
        jax.ShapeDtypeStruct(values.shape, F32),
    )
    call = kernel_call(
        attention_kernel, shapes, [SMEM, VMEM, VMEM, VMEM], flops=10**8, nbytes=3 * 10**6
    )
    return call(length, queries, keys, values)


def head_step(back_mixed, probs_t, mixed_gain, value_gain, found):
    heads = probs_t.shape[0]
    kv_heads = value_gain.shape[1] // HD
    group_size = heads // kv_heads
    for g in range(kv_heads):
        total = jnp.zeros((probs_t.shape[1], HD), F32)
        for h in range(g * group_size, (g + 1) * group_size):
            at = slice(h * HD, (h + 1) * HD)
            sens_mixed = (mixed_gain[:, at] * back_mixed[:, at]).astype(BF16)
            total += jnp.dot(probs_t[h], sens_mixed, preferred_element_type=F32)
        at = slice(g * HD, (g + 1) * HD)
        found[:, at] = (value_gain[:, at] * total).astype(BF16)


def sum_heads_kernel(count, product, *refs):
    backs, (probs_t, mixed_gain, value_gain, found, total) = refs[:count], refs[count:]
    back_mixed = product[...]
    for back in backs:
        back_mixed += back[...].astype(F32)
    total[...] = back_mixed
    head_step(total, probs_t, mixed_gain, value_gain, found)


def sum_heads(product, backs, probs_t, mixed_gain, value_gain):
    call = kernel_call(
        functools.partial(sum_heads_kernel, len(backs)),
        jax.ShapeDtypeStruct(value_gain.shape, BF16),
        [VMEM] * (4 + len(backs)),
        [pltpu.VMEM(product.shape, F32)],
        flops=5 * 10**7,
        nbytes=3 * 10**6,
    )
    return call(product, *backs, probs_t, mixed_gain, value_gain)


def product_kernel(use_mine, mine, theirs, block, own, *backs):
    seq_len = own.shape[0]

    def multiply(operand):
        product = by_columns(operand[...], block[...])
        own[...] = product[:seq_len]
        for k, back in enumerate(backs):
            back[...] = product[(k + 1) * seq_len : (k + 2) * seq_len].astype(BF16)

    @pl.when(use_mine[0] == 1)
    def _():
        multiply(mine)

    @pl.when(use_mine[0] == 0)
    def _():
        multiply(theirs)


def spread_products(use_mine, mine, theirs, block, seq_len):
    count = mine.shape[0] // seq_len
    width = block.shape[0]
    shapes = (jax.ShapeDtypeStruct((seq_len, width), F32),) + tuple(
        jax.ShapeDtypeStruct((seq_len, width), BF16) for _ in range(count - 1)
    )
    call = kernel_call(
        product_kernel, shapes, [SMEM, VMEM, VMEM, VMEM], flops=10**9, nbytes=5 * 10**6, limit=32
    )
    return call(use_mine, mine, theirs, block)


def sensitivity_kernel(length, inputs, branch, *refs):
    current, sens = refs if len(refs) == 2 else (None, refs[0])
    inputs_f = inputs[...].astype(F32)
    branch_f = branch[...].astype(F32)
    totals = inputs_f + branch_f
    if current is None:
        row = lax.broadcasted_iota(jnp.int32, totals.shape, 0)
        entering = jnp.where(row < length[0], totals, 0.0).astype(BF16).astype(F32)
    else:
        entering = current[...].astype(F32)
    sens[...] = (branch_f * (entering / stabilize(totals)) / stabilize(branch_f)).astype(BF16)


def sensitivity(length, inputs, branch, *current):
    call = kernel_call(
        sensitivity_kernel,
        jax.ShapeDtypeStruct(inputs.shape, BF16),
        [SMEM] + [VMEM] * (2 + len(current)),
        flops=10**7,
        nbytes=10**6,
    )
    return call(length, inputs, branch, *current)


def outgoing_kernel(place, inputs, branch, sens_own, sens_other, value_rows, outgoing):
    core, length = place[0], place[1]
    width = sens_own.shape[1]
    inputs_f = inputs[...].astype(F32)
    totals = inputs_f + branch[...].astype(F32)
    row = lax.broadcasted_iota(jnp.int32, totals.shape, 0)
    entering = jnp.where(row < length, totals, 0.0).astype(BF16).astype(F32)
    own = value_rows[:, pl.ds(pl.multiple_of(core * width, 128), width)]
    other = value_rows[:, pl.ds(pl.multiple_of((1 - core) * width, 128), width)]
    back_inputs = by_columns(sens_own[...], own) + by_columns(sens_other[...], other)
    kept = inputs_f * (entering / stabilize(totals))
    outgoing[...] = (kept + inputs_f * back_inputs).astype(BF16)


def last_outgoing(place, inputs, branch, sens_own, sens_other, value_rows):
    call = kernel_call(
        outgoing_kernel,
        jax.ShapeDtypeStruct(inputs.shape, BF16),
        [SMEM] + [VMEM] * 5,
        flops=2 * 10**8,
        nbytes=2 * 10**6,
    )
    return call(place, inputs, branch, sens_own, sens_other, value_rows)


def pair_attention_kernel(place, kept, got, probs_out, gain_t, value_gain, values):
    seq_len = kept.shape[0] - 8
    width = kept.shape[1] - 2 * HD
    heads = width // HD
    row = lax.broadcasted_iota(jnp.int32, (seq_len, seq_len), 0)
    column = lax.broadcasted_iota(jnp.int32, (seq_len, seq_len), 1)

    @pl.when(place[3] == 1)
    def _():
        for half, b in ((kept, place[4]), (got, 1 - place[4])):
            tokens = pl.ds(pl.multiple_of(b * seq_len, 128), seq_len)
            length = jnp.max(half[seq_len:, :HD].astype(F32), axis=0, keepdims=True)
            allowed = (column <= row) & (column.astype(F32) < length)
            value_head = half[:seq_len, width + HD :]
            value_f = value_head.astype(F32)
            values[tokens] = value_f
            value_gain[tokens] = value_f / stabilize(value_f)
            stacked = [half[:seq_len, h * HD : (h + 1) * HD] for h in range(heads)]
            scores = by_columns(
                jnp.concatenate(stacked, 0), half[:seq_len, width : width + HD]
            ) / math.sqrt(HD)
            scores = jnp.where(jnp.concatenate([allowed] * heads, 0), scores, -1000000000.0)
            weights = jnp.exp(scores - jnp.max(scores, axis=1, keepdims=True))
            probs = (weights / jnp.sum(weights, axis=1, keepdims=True)).astype(BF16)
            mixed = jnp.dot(probs, value_head, preferred_element_type=F32)
            gain = mixed / stabilize(mixed)
            for h in range(heads):
                at = slice(h * seq_len, (h + 1) * seq_len)
                probs_out[b, h] = probs[at]
                gain_t[h * HD : (h + 1) * HD, tokens] = gain[at].T


def pair_attend(place, kept, got):
    seq_len, width = kept.shape[0] - 8, kept.shape[1] - 2 * HD
    shapes = (
        jax.ShapeDtypeStruct((2, width // HD, seq_len, seq_len), BF16),
        jax.ShapeDtypeStruct((width, 2 * seq_len), F32),
        jax.ShapeDtypeStruct((2 * seq_len, HD), F32),
        jax.ShapeDtypeStruct((2 * seq_len, HD), F32),
    )
    return kernel_call(
        pair_attention_kernel, shapes, [SMEM, VMEM, VMEM], flops=10**8, nbytes=3 * 10**6
    )(place, kept, got)


def main_kernel(count, place, *refs):
    sens, out_block, (before, kept_sum, probs, gain_t, value_gain, values) = refs[:4], refs[4], refs[5:11]
    own_pieces, other_pieces = refs[11 : 11 + count], refs[11 + count : 11 + 2 * count]
    found, halves, total = refs[11 + 2 * count :]
    pos, core, group, active, side = [place[i] for i in range(5)]
    seq_len, half_width = sens[0].shape
    width = out_block.shape[1]
    per_core = half_width // width
    quarter = own_pieces[0].shape[0]

    @pl.when(active == 0)
    def _():
        found[...] = before[...]

    @pl.when(active == 1)
    def _():
        for j, half in ((0, core), (1, 1 - core)):
            for i, sequence in ((0, side), (1, 1 - side)):
                rows = pl.ds(pl.multiple_of(sequence * seq_len, 128), seq_len)
                halves[half, rows, :] = sens[2 * j + i][...]

        def part(k):
            owner = lax.rem(pos - k + count + 1, count + 1)
            start = pl.multiple_of(lax.rem(owner, per_core) * width, 128)
            return halves[owner // per_core, :, pl.ds(start, width)]

        rows = pl.ds(pl.multiple_of(side * 2 * quarter, 16), 2 * quarter)
        total[...] = by_columns(out_block[rows, :], part(0))
        for k in range(count):
            operand = part(k + 1)
            for at, piece in ((group, own_pieces[k]), (1 - group, other_pieces[k])):
                rows = pl.ds(pl.multiple_of(at * quarter, 8), quarter)
                total[rows, :] += by_columns(piece[...], operand)
        heats = []
        for b in range(2):
            tokens = slice(b * seq_len, (b + 1) * seq_len)
            back_values = jnp.zeros((HD, seq_len), F32)
            for h in range(probs.shape[1]):
                at = slice(h * HD, (h + 1) * HD)
                sens_mixed = (gain_t[at, tokens] * total[at, tokens]).astype(BF16)
                back_values += jnp.dot(sens_mixed, probs[b, h], preferred_element_type=F32)
            sens_values = (value_gain[tokens] * back_values.T).astype(BF16)
            found[tokens] = sens_values
            heats.append(by_token(sens_values.astype(F32) * values[tokens]))
        mine = jnp.where(side == 0, heats[0], heats[1]) + kept_sum[...]
        found[2 * seq_len :] = heat_rows_of(mine, jnp.where(side == 0, heats[1], heats[0]))


def by_token(array):
    groups = [array[:, at : at + 128] for at in range(0, array.shape[1], 128)]
    return jnp.sum(sum(groups).T, axis=0, keepdims=True)


def heat_rows_of(mine, theirs):
    rows = []
    for heat in (mine, theirs):
        high = heat.astype(BF16).astype(F32)
        rows += [high, heat - high]
    rows.append(jnp.zeros((12, mine.shape[1]), F32))
    return jnp.concatenate(rows, 0).astype(BF16)


def pack_kernel(place, found, got, values, kept_sum, packed):
    side = place[4]
    seq_len = found.shape[0]

    @pl.when(place[3] == 1)
    def _():
        mine, theirs = (
            jnp.where(side == 0, array[:, :HD], array[:, HD:]) for array in (found, got)
        )
        packed[:seq_len] = jnp.where(side == 0, mine, theirs)
        packed[seq_len : 2 * seq_len] = jnp.where(side == 0, theirs, mine)
        heat = by_token(found[...].astype(F32) * values[...]) + kept_sum[...]
        packed[2 * seq_len :] = heat_rows_of(heat, jnp.zeros_like(heat))


def pack_last(place, found, got, values, kept_sum):
    seq_len = found.shape[0]
    shape = jax.ShapeDtypeStruct((2 * seq_len + 16, HD), BF16)
    return kernel_call(pack_kernel, shape, [SMEM] + [VMEM] * 4, nbytes=10**6)(
        place, found, got, values, kept_sum
    )


def main_step(place, sens, out_block, quarters, before, kept_sum, rest):
    count = len(quarters[0])
    seq_len, half_width = sens[0].shape
    operands = [*sens, out_block, before, kept_sum, *rest, *quarters[0], *quarters[1]]
    call = kernel_call(
        functools.partial(main_kernel, count),
        jax.ShapeDtypeStruct(before.shape, BF16),
        [SMEM] + [VMEM] * len(operands),
        [pltpu.VMEM((2, 2 * seq_len, half_width), BF16), pltpu.VMEM(rest[1].shape, F32)],
        flops=10**9,
        nbytes=6 * 10**6,
        limit=32,
    )
    return call(place, *operands)


def main_plain(place, sens, out_block, quarters, before, kept_sum, rest):
    pos, core, group, active, side = [place[i] for i in range(5)]
    seq_len = sens[0].shape[0]
    width = out_block.shape[1]
    mine, theirs = (ordered(side == 0, sens[2 * j], sens[2 * j + 1], 0) for j in range(2))
    sens_full = ordered(core == 0, mine, theirs, 1)
    count = len(quarters[0])
    quarter = quarters[0][0].shape[0]
    totals = [0.0, 0.0]
    for k in range(count + 1):
        operand = part_of(sens_full, lax.rem(pos - k + count + 1, count + 1), width, 1)
        for half in range(2):
            if k:
                piece = quarters[half][k - 1]
            else:
                at = 2 * side + (group if half == 0 else 1 - group)
                piece = part_of(out_block, at, quarter, 0)
            totals[half] += by_columns(piece, operand)
    total = ordered(group == 0, totals[0], totals[1], 0)
    probs, gain_t, value_gain, values = rest
    sens_mixed = (gain_t * total).astype(BF16).reshape(-1, HD, 2, seq_len)
    back_values = jnp.einsum("hdbt,bhts->bsd", sens_mixed, probs, preferred_element_type=F32)
    found = (value_gain * back_values.reshape(2 * seq_len, HD)).astype(BF16)
    heats = jnp.sum((found.astype(F32) * values).reshape(2, 1, seq_len, HD), axis=3)
    mine = jnp.where(side == 0, heats[0], heats[1]) + kept_sum
    rows = heat_rows_of(mine, jnp.where(side == 0, heats[1], heats[0]))
    return jnp.where(active == 1, jnp.concatenate([found, rows], 0), before)


def turn_kernel(place, *refs):
    *pieces, turned = refs
    count = len(pieces)
    for k, piece in enumerate(pieces):
        rows = piece.shape[0]
        at = pl.multiple_of(lax.rem(place[0] - k + count, count) * rows, 128)
        turned[:, pl.ds(at, rows)] = piece[...].astype(F32).T.astype(BF16)


def turned_side_by_side(place, pieces):
    rows, width = pieces[0].shape
    shape = jax.ShapeDtypeStruct((width, rows * len(pieces)), BF16)
    specs = [SMEM] + [VMEM] * len(pieces)
    return kernel_call(turn_kernel, shape, specs, nbytes=10**6)(place, *pieces)


def heat_of(own, other, place, count):
    partner = lax.rem(2 * place[4] - 1 + count, count)
    size = own[0].shape[0]
    heat = 0.0
    for source in (own, [other[k * size : (k + 1) * size] for k in range(count)]):
        rows = [source[k][size - 16 :].astype(F32) for k in range(count)]
        heat += rows[0][0:1] + rows[0][1:2]
        for k in {1 % count, count - 1}:
            heat += jnp.where(partner == k, rows[k][2:3] + rows[k][3:4], 0.0)
    return heat / DW


def relevance_kernel(count, place, inputs_t, value_rows, *refs):
    own, (other, relevance, heat) = refs[:count], refs[count:]
    pos, core = place[0], place[1]
    size = own[0].shape[0]
    rows = size - 16
    relevance[...] = jnp.zeros_like(relevance)
    for k in range(count):
        source = lax.rem(pos - k + count, count)
        tokens = inputs_t[:, pl.ds(pl.multiple_of(source // 2 * rows, 128), rows)]
        for c, sens in ((core, own[k][:rows]), (1 - core, other[k * size : k * size + rows])):
            head = 2 * c + lax.rem(source, 2)
            at = pl.ds(pl.multiple_of(head * HD, 128), HD)
            relevance[:, at] += jnp.dot(tokens, sens, preferred_element_type=F32)
    rows = relevance.shape[0]
    value_block = value_rows[pl.ds(pl.multiple_of(pos * rows, 16), rows), :]
    relevance[...] *= value_block.astype(F32)
    heat[...] = heat_of(own, other, place, count)


def relevance_step(place, inputs_t, value_rows, own, other):
    shapes = (
        jax.ShapeDtypeStruct((inputs_t.shape[0], value_rows.shape[1]), F32),
        jax.ShapeDtypeStruct((1, (own[0].shape[0] - 16) // 2), F32),
    )
    call = kernel_call(
        functools.partial(relevance_kernel, len(own)),
        shapes,
        [SMEM] + [VMEM] * (3 + len(own)),
        flops=2 * 10**8,
        nbytes=2 * 10**6,
    )
    return call(place, inputs_t, value_rows, *own, other)


def relevance_plain(place, inputs_t, value_rows, own, other):
    pos, core = place[0], place[1]
    count, size = len(own), own[0].shape[0]
    rows = size - 16
    seq_len = rows // 2
    heat = heat_of(own, other, place, count)
    other = [other[k * size : k * size + rows] for k in range(count)]
    own = [piece[:rows] for piece in own]
    even = lax.rem(pos, 2) == 0
    by_core = []
    for sens in (own, other):
        same = jnp.concatenate([sens[k] for k in range(0, count, 2)], 0)
        cross = jnp.concatenate(
            [jnp.where(even, sens[(k - 1) % count], sens[k + 1]) for k in range(0, count, 2)], 0
        )
        by_core.append(ordered(even, same, cross, 1))
    inputs = inputs_t.reshape(-1, count, seq_len)
    tokens = []
    for k in range(0, count, 2):
        tokens.append(jnp.where(even, inputs[:, k], inputs[:, k + 1]))
        tokens.append(jnp.where(even, inputs[:, (k - 1) % count], inputs[:, k]))
    all_sens = ordered(core == 0, by_core[0], by_core[1], 1)
    summed = jnp.dot(jnp.concatenate(tokens, 1), all_sens, preferred_element_type=F32)
    return part_of(value_rows, pos, inputs_t.shape[0], 0).astype(F32) * summed, heat


def moved(shard, axes, target):
    sizes = [lax.axis_size(axis) for axis in axes]
    places = list(itertools.product(*[range(size) for size in sizes]))
    index = {place: i for i, place in enumerate(places)}
    pairs = [(index[place], index[target(*place)]) for place in places if target(*place) is not None]
    return lax.ppermute(shard, axes, pairs)


def along_dp(shard, by):
    peers = lax.axis_size("dp")
    return moved(shard, ("dp",), lambda i: ((i + by) % peers,)) if by else shard


def other_core(shard):
    return moved(shard, ("mp",), lambda c: (1 - c,))


def from_next_section(shard):
    return moved(shard, ("section",), lambda s: (s - 1,) if s > 0 else None)


def ordered(first_is_mine, mine, theirs, axis):
    return jnp.concatenate(
        [jnp.where(first_is_mine, mine, theirs), jnp.where(first_is_mine, theirs, mine)], axis
    )


def part_of(array, index, width, axis):
    return lax.dynamic_slice_in_dim(array, index * width, width, axis)


def once(array, *others):
    return lax.optimization_barrier((array,) + others)[0]


def early_move(shard, axes, target):
    last = lax.axis_size("section") - 1
    at = axes.index("section")
    return moved(shard, axes, lambda *place: target(*place) if place[at] < last else None)


def early_pair(shard):
    return early_move(shard, ("dp", "section"), lambda i, s: (i ^ 1, s))


def early_core(shard):
    return early_move(shard, ("section", "mp"), lambda s, c: (s, 1 - c))


def spread_product(sens_branch, out_block):
    axes = ("dp", "section", "mp")
    peers, cores = lax.axis_size("dp"), lax.axis_size("mp")
    last = lax.axis_size("section") - 1
    pos, core = lax.axis_index("dp"), lax.axis_index("mp")
    seq_len = sens_branch.shape[0]
    width = out_block.shape[1]
    per_core = peers // cores
    arrived = []
    for k in range(peers):
        to = lax.rem(pos + k, peers)
        part = part_of(sens_branch, lax.rem(to, per_core), width, 1)
        if k:
            part = moved(
                part,
                axes,
                lambda i, s, c: ((i + k) % peers, s, c)
                if s == last and c == (i + k) % peers // per_core
                else None,
            )
        arrived.append(part)
    mine = jnp.concatenate(arrived, 0)
    theirs = moved(
        mine,
        axes,
        lambda i, s, c: (i, s, 1 - c) if s == last and c == i // per_core else None,
    )
    if width % 128 == 0:
        use_mine = (core == pos // per_core).astype(jnp.int32)[None]
        own, *sent = spread_products(use_mine, mine, theirs, out_block, seq_len)
    else:
        product = by_columns(jnp.where(core == pos // per_core, mine, theirs), out_block)
        own, *sent = jnp.split(product, peers, axis=0)
    backs = [
        moved(
            sent[k - 1].astype(BF16),
            axes,
            lambda i, s, c: ((i - k) % peers, s, c) if s == last else None,
        )
        for k in range(1, peers)
    ]
    return own, backs


def on_device(hidden_in, attn_out, queries, keys, value_weight, out_weight, lengths):
    inputs = hidden_in[0, 0]
    branch = attn_out[0, 0]
    query_rows = queries[0, 0]
    key_rows = keys[0, 0]
    value_rows = value_weight[0]
    out_block = out_weight[0]
    seq_len, half_width = inputs.shape
    kv_width = key_rows.shape[1]
    head_width = query_rows.shape[1] // 2
    quarter = head_width // 2
    sections = lax.axis_size("section")
    section_pos = lax.axis_index("section")
    group_pos = lax.axis_index("groups")
    peers = lax.axis_size("dp")
    dp_pos = lax.axis_index("dp")
    core_pos = lax.axis_index("mp")
    block_rows = half_width // peers
    side = lax.rem(dp_pos, 2)
    even = side == 0
    is_last = section_pos == sections - 1
    in_tiles = out_block.shape[1] % 128 == 0 and peers <= 8

    def place(active):
        flags = [dp_pos, core_pos, group_pos, active, side]
        return jnp.stack([jnp.asarray(flag, jnp.int32) for flag in flags])

    def core_exchange(mine, take):
        return moved(
            mine, ("section", "mp"), lambda s, c: (s, 1 - c) if take(s == sections - 1) else None
        )

    def values_of(take):
        value_part = jnp.dot(inputs, value_rows, preferred_element_type=F32)
        part_mine = part_of(value_part, core_pos, kv_width, 1)
        part_other = part_of(value_part, 1 - core_pos, kv_width, 1)
        return part_mine + core_exchange(part_other.astype(BF16), take).astype(F32)

    where_last = jnp.stack([core_pos, lengths[0]])

    def last_section():
        values_f = values_of(lambda last: last)
        rest = attend(lengths, query_rows, key_rows, values_f)
        sens_branch = sensitivity(lengths, inputs, branch)
        own, backs = spread_product(sens_branch, out_block)
        leaves, tree = jax.tree.flatten(early_shapes[-1])
        filler = lengths[0].astype(BF16)
        unused = [jnp.full(leaf.shape, filler + k, BF16) for k, leaf in enumerate(leaves)]
        own, *unused = lax.optimization_barrier((own, *unused))
        if peers > 8:
            for back in backs:
                own = own + back.astype(F32)
            backs = []
        found = sum_heads(own, backs, *rest)
        other = core_exchange(found, lambda last: last)
        outgoing = last_outgoing(where_last, inputs, branch, found, other, value_rows)
        return values_f, found, outgoing, jax.tree.unflatten(tree, unused)

    def early_section():
        own_quarters = []
        for k in range(1, peers):
            rows = part_of(out_block, 2 * lax.rem(dp_pos + k, 2) + group_pos, quarter, 0)
            own_quarters.append(
                early_move(rows, ("dp", "section"), lambda i, s: ((i + k) % peers, s))
            )
        other_quarters = [
            early_move(rows, ("groups", "section"), lambda g, s: (1 - g, s))
            for rows in own_quarters
        ]
        values_f = values_of(lambda last: not last)

        def half_of(which):
            parts = [
                part_of(query_rows, which, head_width, 1),
                part_of(key_rows, which, HD, 1),
                part_of(values_f, which, HD, 1).astype(BF16),
            ]
            packed = jnp.concatenate(parts, 1)
            mark = jnp.full((8, packed.shape[1]), lengths[0].astype(BF16))
            return jnp.concatenate([packed, mark], 0)

        found = jnp.full((seq_len, kv_width), lengths[0].astype(BF16))
        outgoing = jnp.full((seq_len, half_width), lengths[0].astype(BF16))
        kept_half, sent_half, found, outgoing, *_ = lax.optimization_barrier(
            (half_of(side), half_of(1 - side), found, outgoing, *own_quarters)
            + (other_quarters[0], other_quarters[-1])
        )
        halves = (kept_half, early_pair(sent_half))
        return values_f, found, outgoing, (own_quarters, other_quarters, halves)

    early_shapes = jax.eval_shape(early_section)
    values_f, found, outgoing, prepared = lax.cond(is_last, last_section, early_section)
    own_quarters, other_quarters, (kept_half, got_half) = prepared
    arrived = from_next_section(outgoing)

    rows = once(inputs, outgoing)
    pieces = [
        along_dp(part_of(rows, lax.rem(dp_pos + k, peers), block_rows, 1), k) for k in range(peers)
    ]
    sens_mine = sensitivity(lengths, inputs, branch, arrived)
    sens_partner = early_pair(sens_mine)

    kept_half, got_half, found, arrived, *pieces = lax.optimization_barrier(
        (kept_half, got_half, found, arrived, *pieces, sens_mine)
    )[:-1]
    rest = pair_attend(place(~is_last), kept_half, got_half)
    if in_tiles:
        inputs_t = turned_side_by_side(place(0), pieces)
    else:
        inputs_t = jnp.concatenate(pieces, 0).T

    totals = inputs.astype(F32) + branch.astype(F32)
    valid_rows = (lax.iota(jnp.int32, seq_len) < lengths[0]).astype(F32)
    current = (totals * valid_rows[:, None]).astype(BF16)

    def kept_of(entering):
        return inputs.astype(F32) * (entering.astype(F32) / stabilize(totals))

    got = moved(found, ("dp", "section"), lambda i, s: (i ^ 1, s) if s == sections - 1 else None)
    last_kept = jnp.sum(kept_of(current), axis=1)[None]
    sens_values = pack_last(place(is_last), found, got, values_f, last_kept)

    for turn in range(1, sections):
        active = section_pos == sections - 1 - turn
        current = jnp.where(active, arrived, current)
        kept_sum = jnp.sum(kept_of(arrived), axis=1)[None]
        if turn > 1:
            sens_mine = sensitivity(lengths, inputs, branch, arrived)
            sens_partner = early_pair(sens_mine)
        else:
            sens_partner, *ready = lax.optimization_barrier(
                (sens_partner, sens_values, kept_sum, inputs_t, *rest)
            )
            sens_values, kept_sum, inputs_t, *rest = ready
        sens = [sens_mine, sens_partner, early_core(sens_mine), early_core(sens_partner)]
        step = main_step if in_tiles else main_plain
        sens_values = step(
            place(active),
            sens,
            out_block,
            (own_quarters, other_quarters),
            sens_values,
            kept_sum,
            rest,
        )
        if turn + 1 < sections:
            mine_now, theirs_now = (part_of(sens_values, w, seq_len, 0) for w in (side, 1 - side))
            found_now = ordered(even, mine_now, early_pair(theirs_now), 1)
            sens_all = ordered(core_pos == 0, found_now, early_core(found_now), 1)
            back_inputs = by_columns(sens_all, value_rows)
            outgoing = kept_of(current) + inputs.astype(F32) * back_inputs
            arrived = from_next_section(outgoing.astype(BF16))

    own_sens = [along_dp(sens_values, k) for k in range(peers)]
    other_sens = other_core(jnp.concatenate(own_sens, 0))
    step = relevance_step if in_tiles else relevance_plain
    relevance_rows, heat_rows = step(place(0), inputs_t, value_rows, own_sens, other_sens)
    return (heat_rows[None], relevance_rows[None])


def solution(mesh):
    placed = (
        P("section", ("groups", "dp"), None, "mp"),
        P("section", ("groups", "dp"), None, "mp"),
        P("section", ("groups", "dp"), None, "mp"),
        P("section", ("groups", "dp"), None, "mp"),
        P("section", "mp", None),
        P("section", "mp", "dp"),
        P(("groups", "dp")),
    )
    return jax.shard_map(
        on_device,
        mesh=mesh,
        in_specs=placed,
        out_specs=(
            P("section", ("groups", "dp"), None),
            P(("groups", "section"), ("mp", "dp"), None),
        ),
        check_vma=False,
    )
```

time: 119 us -> 107 us (0.90)
  other arithmetic: 8.64 us -> 1.36 us
  local copies, waits for them, and re-layouts: 8.78 us -> 6.25 us
  starting transfers between devices: 45.6 us -> 43.7 us
    select_n x4 -> x0, other arithmetic: 4.99 us -> none  [the longest x2 3.83 us: start_gather(): jnp.where((pos == 1) | (pos == 2), *both)]
    split x2 -> x0, local copies, waits for them, and re-layouts: 3.59 us -> none  [start_gather(): return ([pair, pair_swapped, second, jnp.split(near, cut)], *others[-2:])]
    ppermute x22 -> x20, starting transfers between devices: 45.6 us -> 43.7 us  [moved(): return lax.ppermute(shard, axes, pairs)]
    add x1, other arithmetic: 1.58 us -> 0.02 us  [values_of(): return part_mine + core_exchange(part_other.astype(BF16), take).astype(F32)]
    pallas_call x4 -> x5, Pallas kernels: 10.2 us -> 9.61 us  [the longest x1 4.03 us: main_step(): return call(place, *operands)]
    ppermute x22 -> x20, waiting for transfers between devices: 42.1 us -> 41.9 us  [moved(): return lax.ppermute(shard, axes, pairs)]
    dynamic_slice x3 -> x4, local copies, waits for them, and re-layouts: 3.68 us -> 3.74 us  [part_of(): return lax.dynamic_slice_in_dim(array, index * width, width, axis)]
  transfers between devices with their start and end apart: 22 -> 20, of which waited for: 10 -> 11; matrix products, arithmetic and copies ran while one was open for 8% -> 4% of each run, Pallas kernels for 4% -> 5%
where the time goes in v6:
time: 107 us
  starting transfers between devices  43.7 us (41%)
  waiting for transfers between devices  41.9 us (39%)
  Pallas kernels  11.1 us (10%)
  local copies, waits for them, and re-layouts  6.25 us (6%)
  between operations  1.49 us (1%)
  other arithmetic  1.36 us (1%)
    ppermute x20, starting transfers between devices, moved(): return lax.ppermute(shard, axes, pairs)  43.7 us
    ppermute x20, waiting for transfers between devices, moved(): return lax.ppermute(shard, axes, pairs)  41.9 us
    pallas_call x1, Pallas kernels, main_step(): return call(place, *operands)  4.03 us
    dynamic_slice x4, local copies, waits for them, and re-layouts, part_of(): return lax.dynamic_slice_in_dim(array, index * width, width, axis)  3.74 us
  transfers between devices with their start and end apart: 20, of which 11 were waited for; matrix products, arithmetic and copies ran while one was open for 4% of the time, Pallas kernels for 5%

profile of v6, /device:TPU:0, one launch (start us, length us, event | category | flops | bytes accessed | tf_op | source)
XLA Modules:
  0.0 106.8 jit_solution(5414032174980595145)
XLA Ops:
  1.4 61.3 %conditional.1 = (f32[128,256]{1,0:T(8,128)S(1)}, bf16[128,256]{1,0:T(8,128)(2,1)}, bf16[128,1280]{1,0:T(8,128)(2,1)}, bf16[320,640]{1,0:T(8,128)(2,1)}, bf16[32...) conditional(s32[]{:T(128)} %convert_element_type.64, ...), branch_computations={%region_0.0_spmd, %region_1.2_spmd} | conditional | flops 1530459136 | bytes 55613120 | solution.py:642
  1.4 2.4 %constant_dynamic-slice_fusion = (bf16[320,640]{1,0:T(8,128)(2,1)}, bf16[320,640]{1,0:T(8,128)(2,1)S(1)}, bf16[320,640]{1,0:T(8,128)(2,1)}) fusion(bf16[1280,640]{1,0:T(8,128)(2,1)} %get-tuple-element.45, s32[]{:T(128)S(6)} %select_n.56, s32[]{:T(128)S(6)} %select_n.55, s32[]{:T(128)S(6)} %select_n.54), kind=kLoop, calls=%fused_computation.15 | loop fusion | bytes 2457612 | tf_op jit(solution)/shard_map/cond/branch_0_fun/dynamic_slice | solution.py:486
  3.7 5.1 %collective-permute-start.1 = (bf16[320,640]{1,0:T(8,128)(2,1)}, bf16[320,640]{1,0:T(8,128)(2,1)S(1)}, u32[]{:S(2)}, u32[]{:S(2)}) collective-permute-start(bf16[320,640]{1,0:T(8,128)(2,1)} %get-tuple-element.151), channel_id=1, source_target_pairs={{0,4},{4,8},{8,12},{12,0},{1,5},{5,9},{9,13},{13,1},{16,20},{20,24... | collective-permute-start | bytes 1228808 | tf_op jit(solution)/shard_map/cond/branch_0_fun/ppermute | solution.py:463
  8.8 3.9 %collective-permute-start.3 = (bf16[320,640]{1,0:T(8,128)(2,1)}, bf16[320,640]{1,0:T(8,128)(2,1)}, u32[]{:S(2)}, u32[]{:S(2)}) collective-permute-start(bf16[320,640]{1,0:T(8,128)(2,1)} %get-tuple-element.149), channel_id=1, source_target_pairs={{0,12},{4,0},{8,4},{12,8},{1,13},{5,1},{9,5},{13,9},{16,28},{20,16... | collective-permute-start | bytes 1228808 | tf_op jit(solution)/shard_map/cond/branch_0_fun/ppermute | solution.py:463
  12.8 0.3 fusion.12
  13.2 1.9 %collective-permute-start = (bf16[128,256]{1,0:T(8,128)(2,1)S(1)}, bf16[128,256]{1,0:T(8,128)(2,1)S(1)}, u32[]{:S(2)}, u32[]{:S(2)}) collective-permute-start(bf16[128,256]{1,0:T(8,128)(2,1)S(1)} %dynamic-slice_convert_fusion), channel_id=1, source_target_pairs={{0,1},{1,0},{4,5},{5,4},{8,9},{9,8},{12,13},{13,12},{16,17},{17,16... | collective-permute-start | bytes 196616 | tf_op jit(solution)/shard_map/cond/branch_0_fun/ppermute | solution.py:463
  15.1 2.9 %collective-permute-start.2 = (bf16[320,640]{1,0:T(8,128)(2,1)S(1)}, bf16[320,640]{1,0:T(8,128)(2,1)}, u32[]{:S(2)}, u32[]{:S(2)}) collective-permute-start(bf16[320,640]{1,0:T(8,128)(2,1)S(1)} %get-tuple-element.150), channel_id=1, source_target_pairs={{0,8},{4,12},{8,0},{12,4},{1,9},{5,13},{9,1},{13,5},{16,24},{20,28... | collective-permute-start | bytes 1228808 | tf_op jit(solution)/shard_map/cond/branch_0_fun/ppermute | solution.py:463
  18.8 2.6 %collective-permute-done.1 = bf16[320,640]{1,0:T(8,128)(2,1)S(1)} collective-permute-done((bf16[320,640]{1,0:T(8,128)(2,1)}, bf16[320,640]{1,0:T(8,128)(2,1)S(1)}, u32[]{:S(2)}, u32[]{:S(2)}) %collective-permute-start.1) | collective-permute-done | bytes 409632 | tf_op jit(solution)/shard_map/cond/branch_0_fun/ppermute | solution.py:463
  21.4 3.7 %collective-permute-start.4 = (bf16[320,640]{1,0:T(8,128)(2,1)S(1)}, bf16[320,640]{1,0:T(8,128)(2,1)}, u32[]{:S(2)}, u32[]{:S(2)}) collective-permute-start(bf16[320,640]{1,0:T(8,128)(2,1)S(1)} %collective-permute-done.1), channel_id=1, source_target_pairs={{0,16},{16,0},{1,17},{17,1},{4,20},{20,4},{5,21},{21,5},{8,24},{24... | collective-permute-start | bytes 1228808 | tf_op jit(solution)/shard_map/cond/branch_0_fun/ppermute | solution.py:463
  25.0 4.3 %collective-permute-done.3 = bf16[320,640]{1,0:T(8,128)(2,1)} collective-permute-done((bf16[320,640]{1,0:T(8,128)(2,1)}, bf16[320,640]{1,0:T(8,128)(2,1)}, u32[]{:S(2)}, u32[]{:S(2)}) %collective-permute-start.3) | collective-permute-done | bytes 409632 | tf_op jit(solution)/shard_map/cond/branch_0_fun/ppermute | solution.py:463
  29.4 3.4 %collective-permute-start.5 = (bf16[320,640]{1,0:T(8,128)(2,1)}, bf16[320,640]{1,0:T(8,128)(2,1)}, u32[]{:S(2)}, u32[]{:S(2)}) collective-permute-start(bf16[320,640]{1,0:T(8,128)(2,1)} %collective-permute-done.3), channel_id=1, source_target_pairs={{0,16},{16,0},{1,17},{17,1},{4,20},{20,4},{5,21},{21,5},{8,24},{24... | collective-permute-start | bytes 1228808 | tf_op jit(solution)/shard_map/cond/branch_0_fun/ppermute | solution.py:463
  32.8 14.1 %collective-permute-done.2 = bf16[320,640]{1,0:T(8,128)(2,1)} collective-permute-done((bf16[320,640]{1,0:T(8,128)(2,1)S(1)}, bf16[320,640]{1,0:T(8,128)(2,1)}, u32[]{:S(2)}, u32[]{:S(2)}) %collective-permute-start.2) | collective-permute-done | bytes 409632 | tf_op jit(solution)/shard_map/cond/branch_0_fun/ppermute | solution.py:463
  46.9 3.4 %collective-permute-start.6 = (bf16[320,640]{1,0:T(8,128)(2,1)}, bf16[320,640]{1,0:T(8,128)(2,1)}, u32[]{:S(2)}, u32[]{:S(2)}) collective-permute-start(bf16[320,640]{1,0:T(8,128)(2,1)} %collective-permute-done.2), channel_id=1, source_target_pairs={{0,16},{16,0},{1,17},{17,1},{4,20},{20,4},{5,21},{21,5},{8,24},{24... | collective-permute-start | bytes 1228808 | tf_op jit(solution)/shard_map/cond/branch_0_fun/ppermute | solution.py:463
  50.4 0.8 fusion.7
  51.1 0.6 broadcast_in_dim.26
  51.8 0.8 broadcast_in_dim.27
  52.5 1.9 %collective-permute-start.7 = (bf16[136,896]{1,0:T(8,128)(2,1)S(1)}, bf16[136,896]{1,0:T(8,128)(2,1)S(1)}, u32[]{:S(2)}, u32[]{:S(2)}) collective-permute-start(bf16[136,896]{1,0:T(8,128)(2,1)S(1)} %get-tuple-element.51), channel_id=1, source_target_pairs={{0,4},{4,0},{8,12},{12,8},{1,5},{5,1},{9,13},{13,9},{16,20},{20,16... | collective-permute-start | bytes 731144 | tf_op jit(solution)/shard_map/cond/branch_0_fun/ppermute | solution.py:463
  54.5 6.1 %collective-permute-done.6 = bf16[320,640]{1,0:T(8,128)(2,1)} collective-permute-done((bf16[320,640]{1,0:T(8,128)(2,1)}, bf16[320,640]{1,0:T(8,128)(2,1)}, u32[]{:S(2)}, u32[]{:S(2)}) %collective-permute-start.6) | collective-permute-done | bytes 409632 | tf_op jit(solution)/shard_map/cond/branch_0_fun/ppermute | solution.py:463
  60.5 1.5 %collective-permute-done.7 = bf16[136,896]{1,0:T(8,128)(2,1)S(1)} collective-permute-done((bf16[136,896]{1,0:T(8,128)(2,1)S(1)}, bf16[136,896]{1,0:T(8,128)(2,1)S(1)}, u32[]{:S(2)}, u32[]{:S(2)}) %collective-permute-start.7) | collective-permute-done | bytes 243744 | tf_op jit(solution)/shard_map/cond/branch_0_fun/ppermute | solution.py:463
  62.0 0.7 copy-done.19
  62.7 1.4 %collective-permute-start.17 = (bf16[128,1280]{1,0:T(8,128)(2,1)}, bf16[128,1280]{1,0:T(8,128)(2,1)S(1)}, u32[]{:S(2)}, u32[]{:S(2)}) collective-permute-start(bf16[128,1280]{1,0:T(8,128)(2,1)} %get-tuple-element.113), channel_id=1, source_target_pairs={{2,0},{3,1},{6,4},{7,5},{10,8},{11,9},{14,12},{15,13},{18,16},{19,... | collective-permute-start | bytes 983048 | tf_op jit(solution)/shard_map/ppermute | solution.py:463
  64.1 1.3 %constant_dynamic-slice_fusion.11 = (bf16[128,320]{1,0:T(8,128)(2,1)S(1)}, bf16[128,320]{1,0:T(8,128)(2,1)S(1)}, bf16[128,320]{1,0:T(8,128)(2,1)S(1)}, bf16[128,320]{1,0:T(8,128)(2,1)S(1)}) fusion(bf16[128,1280]{1,0:T(8,128)(2,1)} %bitcast.37, s32[]{:T(128)S(6)} %select_n.72, s32[]{:T(128)S(6)} %select_n.71, s32[]{:T(128)S(6)} %select_n.70, s32[]{:T(128)S(6)} %select_n.69), kind=kLoop, calls=%fused_computation.38 | loop fusion | bytes 655376 | tf_op jit(solution)/shard_map/dynamic_slice | solution.py:486
  65.4 0.3 collective-permute-start.19
  65.8 2.5 %collective-permute-start.20 = (bf16[128,320]{1,0:T(8,128)(2,1)S(1)}, bf16[128,320]{1,0:T(8,128)(2,1)S(1)}, u32[]{:S(2)}, u32[]{:S(2)}) collective-permute-start(bf16[128,320]{1,0:T(8,128)(2,1)S(1)} %get-tuple-element.165), channel_id=1, source_target_pairs={{0,8},{4,12},{8,0},{12,4},{1,9},{5,13},{9,1},{13,5},{2,10},{6,14},... | collective-permute-start | bytes 245768 | tf_op jit(solution)/shard_map/ppermute | solution.py:463
  68.3 2.8 %collective-permute-start.21 = (bf16[128,320]{1,0:T(8,128)(2,1)S(1)}, bf16[128,320]{1,0:T(8,128)(2,1)S(1)}, u32[]{:S(2)}, u32[]{:S(2)}) collective-permute-start(bf16[128,320]{1,0:T(8,128)(2,1)S(1)} %get-tuple-element.164), channel_id=1, source_target_pairs={{0,12},{4,0},{8,4},{12,8},{1,13},{5,1},{9,5},{13,9},{2,14},{6,2},{... | collective-permute-start | bytes 245768 | tf_op jit(solution)/shard_map/ppermute | solution.py:463
  71.1 3.3 %collective-permute-done.17.refs_0_ = bf16[128,1280]{1,0:T(8,128)(2,1)S(1)} collective-permute-done((bf16[128,1280]{1,0:T(8,128)(2,1)}, bf16[128,1280]{1,0:T(8,128)(2,1)S(1)}, u32[]{:S(2)}, u32[]{:S(2)}) %collective-permute-start.17) | collective-permute-done | bytes 327712 | tf_op jit(solution)/shard_map/ppermute | solution.py:463
  74.5 1.4 %shard_map.86.refs_0_ = bf16[128,1280]{1,0:T(8,128)(2,1)S(1)} custom-call(s32[1]{0:T(128)} %copy.31.length, bf16[128,1280]{1,0:T(8,128)(2,1)} %bitcast.38, bf16[128,1280]{1,0:T(8,128)(2,1)} %bitcast.40, bf16[128,1280]{1,0:T(8,128)(2,1)S(1)} %collective-permute-done.17.refs_0_), custom_call_target="tpu_custom_call" | custom-call | flops 10000000 | bytes 1000000 | tf_op jit(solution)/shard_map/pallas_call | solution.py:167
  75.9 1.9 %collective-permute-start.18 = (bf16[128,1280]{1,0:T(8,128)(2,1)S(1)}, bf16[128,1280]{1,0:T(8,128)(2,1)S(1)}, u32[]{:S(2)}, u32[]{:S(2)}) collective-permute-start(bf16[128,1280]{1,0:T(8,128)(2,1)S(1)} %shard_map.86.refs_0_), channel_id=1, source_target_pairs={{0,4},{4,0},{8,12},{12,8},{1,5},{5,1},{9,13},{13,9},{16,20},{20,16... | collective-permute-start | bytes 983048 | tf_op jit(solution)/shard_map/ppermute | solution.py:463
  77.9 0.1 stack.64.place
  77.9 0.1 stack.67.place
  78.1 1.9 %collective-permute-start.23 = (bf16[128,1280]{1,0:T(8,128)(2,1)S(1)}, bf16[128,1280]{1,0:T(8,128)(2,1)S(1)}, u32[]{:S(2)}, u32[]{:S(2)}) collective-permute-start(bf16[128,1280]{1,0:T(8,128)(2,1)S(1)} %shard_map.86.refs_0_), channel_id=1, source_target_pairs={{0,1},{1,0},{4,5},{5,4},{8,9},{9,8},{12,13},{13,12},{16,17},{17,16... | collective-permute-start | bytes 983048 | tf_op jit(solution)/shard_map/ppermute | solution.py:463
  80.1 0.7 collective-permute-start.22
  80.8 0.5 fusion.11
  81.2 0.7 shard_map.88.inputs_t
  82.0 2.0 %shard_map.89 = (bf16[2,5,128,128]{3,2,1,0:T(8,128)(2,1)S(1)}, f32[640,256]{1,0:T(8,128)S(1)}, f32[256,128]{1,0:T(8,128)S(1)}, f32[256,128]{1,0:T(8,128)S(1)}) custom-call(s32[5]{0:T(128)S(1)} %stack.70.place, bf16[136,896]{1,0:T(8,128)(2,1)} %get-tuple-element.125.kept, bf16[136,896]{1,0:T(8,128)(2,1)S(1)} %copy-done.20), custom_call_target="tpu_custom_call" | custom-call | flops 100000000 | bytes 3000000 | tf_op jit(solution)/shard_map/pallas_call | solution.py:235
  84.0 0.9 shard_map.87.refs_5_
  84.8 1.7 %collective-permute-done.18.refs_1_ = bf16[128,1280]{1,0:T(8,128)(2,1)S(1)} collective-permute-done((bf16[128,1280]{1,0:T(8,128)(2,1)S(1)}, bf16[128,1280]{1,0:T(8,128)(2,1)S(1)}, u32[]{:S(2)}, u32[]{:S(2)}) %collective-permute-start.18) | collective-permute-done | bytes 327712 | tf_op jit(solution)/shard_map/ppermute | solution.py:463
  86.5 1.9 %collective-permute-start.24 = (bf16[128,1280]{1,0:T(8,128)(2,1)S(1)}, bf16[128,1280]{1,0:T(8,128)(2,1)S(1)}, u32[]{:S(2)}, u32[]{:S(2)}) collective-permute-start(bf16[128,1280]{1,0:T(8,128)(2,1)S(1)} %collective-permute-done.18.refs_1_), channel_id=1, source_target_pairs={{0,1},{1,0},{4,5},{5,4},{8,9},{9,8},{12,13},{13,12},{16,17},{17,16... | collective-permute-start | bytes 983048 | tf_op jit(solution)/shard_map/ppermute | solution.py:463
  88.4 0.1 stack.73.place
  88.5 1.5 %collective-permute-done.24.refs_3_ = bf16[128,1280]{1,0:T(8,128)(2,1)S(1)} collective-permute-done((bf16[128,1280]{1,0:T(8,128)(2,1)S(1)}, bf16[128,1280]{1,0:T(8,128)(2,1)S(1)}, u32[]{:S(2)}, u32[]{:S(2)}) %collective-permute-start.24) | collective-permute-done | bytes 327712 | tf_op jit(solution)/shard_map/ppermute | solution.py:463
  90.0 4.0 %shard_map.90.refs_0_ = bf16[272,128]{1,0:T(8,128)(2,1)S(1)} custom-call(s32[5]{0:T(128)S(1)} %stack.73.place, bf16[128,1280]{1,0:T(8,128)(2,1)S(1)} %shard_map.86.refs_0_, bf16[128,1280]{1,0:T(8,128)(2,1)S(1)} %collective-permute-done.18.refs_1_, bf16[128,1280]{1,0:T(8,128)(2,1)S(1)} %collective-permute-done.23.refs_2_, ...), custom_call_target="tpu_custom_call" | custom-call | flops 1000000000 | bytes 6000000 | tf_op jit(solution)/shard_map/pallas_call | solution.py:338
  94.0 0.6 collective-permute-start.25
  94.6 1.2 %collective-permute-start.26 = (bf16[272,128]{1,0:T(8,128)(2,1)S(1)}, bf16[272,128]{1,0:T(8,128)(2,1)S(1)}, u32[]{:S(2)}, u32[]{:S(2)}) collective-permute-start(bf16[272,128]{1,0:T(8,128)(2,1)S(1)} %shard_map.90.refs_0_), channel_id=1, source_target_pairs={{0,8},{4,12},{8,0},{12,4},{1,9},{5,13},{9,1},{13,5},{2,10},{6,14},... | collective-permute-start | bytes 208904 | tf_op jit(solution)/shard_map/ppermute | solution.py:463
  95.8 2.1 %collective-permute-start.27 = (bf16[272,128]{1,0:T(8,128)(2,1)S(1)}, bf16[272,128]{1,0:T(8,128)(2,1)S(1)}, u32[]{:S(2)}, u32[]{:S(2)}) collective-permute-start(bf16[272,128]{1,0:T(8,128)(2,1)S(1)} %shard_map.90.refs_0_), channel_id=1, source_target_pairs={{0,12},{4,0},{8,4},{12,8},{1,13},{5,1},{9,5},{13,9},{2,14},{6,2},{... | collective-permute-start | bytes 208904 | tf_op jit(solution)/shard_map/ppermute | solution.py:463
  97.9 3.0 %collective-permute-done.25.refs_1_ = bf16[272,128]{1,0:T(8,128)(2,1)S(1)} collective-permute-done((bf16[272,128]{1,0:T(8,128)(2,1)S(1)}, bf16[272,128]{1,0:T(8,128)(2,1)S(1)}, u32[]{:S(2)}, u32[]{:S(2)}) %collective-permute-start.25) | collective-permute-done | bytes 69664 | tf_op jit(solution)/shard_map/ppermute | solution.py:463
  101.0 2.2 %collective-permute-done.26.refs_2_ = bf16[272,128]{1,0:T(8,128)(2,1)S(1)} collective-permute-done((bf16[272,128]{1,0:T(8,128)(2,1)S(1)}, bf16[272,128]{1,0:T(8,128)(2,1)S(1)}, u32[]{:S(2)}, u32[]{:S(2)}) %collective-permute-start.26) | collective-permute-done | bytes 69664 | tf_op jit(solution)/shard_map/ppermute | solution.py:463
  103.3 1.5 %collective-permute-done.28.refs_4_ = bf16[1088,128]{1,0:T(8,128)(2,1)S(1)} collective-permute-done((bf16[1088,128]{1,0:T(8,128)(2,1)S(1)}, bf16[1088,128]{1,0:T(8,128)(2,1)S(1)}, u32[]{:S(2)}, u32[]{:S(2)}) %collective-permute-start.28) | collective-permute-done | bytes 278560 | tf_op jit(solution)/shard_map/ppermute | solution.py:463
  104.8 2.0 %shard_map.91 = (f32[320,512]{1,0:T(8,128)}, f32[1,128]{1,0:T(1,128)}) custom-call(s32[5]{0:T(128)S(1)} %stack.64.place, bf16[320,512]{1,0:T(8,128)(2,1)S(1)} %shard_map.88.inputs_t, bf16[1280,512]{1,0:T(8,128)(2,1)S(1)} %bitcast.34, bf16[272,128]{1,0:T(8,128)(2,1)S(1)} %shard_map.90.refs_0_, bf16[272,128]{1,0:T(8,128)(2,1)S(1)} %collective-permute-done.25.refs_1_, ...), custom_call_target="tpu_custom_call" | custom-call | flops 200000000 | bytes 2000000 | tf_op jit(solution)/shard_map/pallas_call | solution.py:429
  (38 shorter events, 0.4 us)
Async XLA Ops:
  1.4 11.4 %copy-start.1 = (bf16[1280,512]{1,0:T(8,128)(2,1)S(1)}, bf16[1280,512]{1,0:T(8,128)(2,1)}, u32[]{:S(2)}) copy-start(bf16[1280,512]{1,0:T(8,128)(2,1)} %get-tuple-element.39) | copy-start | bytes 3932164 | tf_op jit(solution)/shard_map/cond
  1.4 11.4 %copy-start.5 = (bf16[128,1280]{1,0:T(8,128)(2,1)S(1)}, bf16[128,1280]{1,0:T(8,128)(2,1)}, u32[]{:S(2)}) copy-start(bf16[128,1280]{1,0:T(8,128)(2,1)} %get-tuple-element.38) | copy-start | bytes 983044 | tf_op jit(solution)/shard_map/cond
  3.7 14.9 %copy-start.13 = (bf16[128,1280]{1,0:T(8,128)(2,1)S(1)}, bf16[128,1280]{1,0:T(8,128)(2,1)}, u32[]{:S(2)}) copy-start(bf16[128,1280]{1,0:T(8,128)(2,1)} %get-tuple-element.41) | copy-start | bytes 983044 | tf_op jit(solution)/shard_map/cond
  3.7 17.6 %collective-permute-start.1 = (bf16[320,640]{1,0:T(8,128)(2,1)}, bf16[320,640]{1,0:T(8,128)(2,1)S(1)}, u32[]{:S(2)}, u32[]{:S(2)}) collective-permute-start(bf16[320,640]{1,0:T(8,128)(2,1)} %get-tuple-element.151), channel_id=1, source_target_pairs={{0,4},{4,8},{8,12},{12,0},{1,5},{5,9},{9,13},{13,1},{16,20},{20,24... | collective-permute-start | bytes 1228808 | tf_op jit(solution)/shard_map/cond/branch_0_fun/ppermute | solution.py:463
  8.8 20.6 %collective-permute-start.3 = (bf16[320,640]{1,0:T(8,128)(2,1)}, bf16[320,640]{1,0:T(8,128)(2,1)}, u32[]{:S(2)}, u32[]{:S(2)}) collective-permute-start(bf16[320,640]{1,0:T(8,128)(2,1)} %get-tuple-element.149), channel_id=1, source_target_pairs={{0,12},{4,0},{8,4},{12,8},{1,13},{5,1},{9,5},{13,9},{16,28},{20,16... | collective-permute-start | bytes 1228808 | tf_op jit(solution)/shard_map/cond/branch_0_fun/ppermute | solution.py:463
  12.8 6.0 %copy-start.17 = (bf16[128,256]{1,0:T(8,128)(2,1)S(1)}, bf16[128,256]{1,0:T(8,128)(2,1)}, u32[]{:S(2)}) copy-start(bf16[128,256]{1,0:T(8,128)(2,1)} %get-tuple-element.43) | copy-start | bytes 196612 | tf_op jit(solution)/shard_map/cond
  13.2 19.6 %collective-permute-start = (bf16[128,256]{1,0:T(8,128)(2,1)S(1)}, bf16[128,256]{1,0:T(8,128)(2,1)S(1)}, u32[]{:S(2)}, u32[]{:S(2)}) collective-permute-start(bf16[128,256]{1,0:T(8,128)(2,1)S(1)} %dynamic-slice_convert_fusion), channel_id=1, source_target_pairs={{0,1},{1,0},{4,5},{5,4},{8,9},{9,8},{12,13},{13,12},{16,17},{17,16... | collective-permute-start | bytes 196616 | tf_op jit(solution)/shard_map/cond/branch_0_fun/ppermute | solution.py:463
  15.1 31.8 %collective-permute-start.2 = (bf16[320,640]{1,0:T(8,128)(2,1)S(1)}, bf16[320,640]{1,0:T(8,128)(2,1)}, u32[]{:S(2)}, u32[]{:S(2)}) collective-permute-start(bf16[320,640]{1,0:T(8,128)(2,1)S(1)} %get-tuple-element.150), channel_id=1, source_target_pairs={{0,8},{4,12},{8,0},{12,4},{1,9},{5,13},{9,1},{13,5},{16,24},{20,28... | collective-permute-start | bytes 1228808 | tf_op jit(solution)/shard_map/cond/branch_0_fun/ppermute | solution.py:463
  21.4 40.6 %copy-start.16 = (bf16[320,640]{1,0:T(8,128)(2,1)}, bf16[320,640]{1,0:T(8,128)(2,1)S(1)}, u32[]{:S(2)}) copy-start(bf16[320,640]{1,0:T(8,128)(2,1)S(1)} %collective-permute-done.1) | copy-start | bytes 1228804 | tf_op jit(solution)/shard_map/cond
  21.4 29.8 %collective-permute-start.4 = (bf16[320,640]{1,0:T(8,128)(2,1)S(1)}, bf16[320,640]{1,0:T(8,128)(2,1)}, u32[]{:S(2)}, u32[]{:S(2)}) collective-permute-start(bf16[320,640]{1,0:T(8,128)(2,1)S(1)} %collective-permute-done.1), channel_id=1, source_target_pairs={{0,16},{16,0},{1,17},{17,1},{4,20},{20,4},{5,21},{21,5},{8,24},{24... | collective-permute-start | bytes 1228808 | tf_op jit(solution)/shard_map/cond/branch_0_fun/ppermute | solution.py:463
  29.4 21.8 %collective-permute-start.5 = (bf16[320,640]{1,0:T(8,128)(2,1)}, bf16[320,640]{1,0:T(8,128)(2,1)}, u32[]{:S(2)}, u32[]{:S(2)}) collective-permute-start(bf16[320,640]{1,0:T(8,128)(2,1)} %collective-permute-done.3), channel_id=1, source_target_pairs={{0,16},{16,0},{1,17},{17,1},{4,20},{20,4},{5,21},{21,5},{8,24},{24... | collective-permute-start | bytes 1228808 | tf_op jit(solution)/shard_map/cond/branch_0_fun/ppermute | solution.py:463
  46.9 13.6 %collective-permute-start.6 = (bf16[320,640]{1,0:T(8,128)(2,1)}, bf16[320,640]{1,0:T(8,128)(2,1)}, u32[]{:S(2)}, u32[]{:S(2)}) collective-permute-start(bf16[320,640]{1,0:T(8,128)(2,1)} %collective-permute-done.2), channel_id=1, source_target_pairs={{0,16},{16,0},{1,17},{17,1},{4,20},{20,4},{5,21},{21,5},{8,24},{24... | collective-permute-start | bytes 1228808 | tf_op jit(solution)/shard_map/cond/branch_0_fun/ppermute | solution.py:463
  52.5 9.4 %collective-permute-start.7 = (bf16[136,896]{1,0:T(8,128)(2,1)S(1)}, bf16[136,896]{1,0:T(8,128)(2,1)S(1)}, u32[]{:S(2)}, u32[]{:S(2)}) collective-permute-start(bf16[136,896]{1,0:T(8,128)(2,1)S(1)} %get-tuple-element.51), channel_id=1, source_target_pairs={{0,4},{4,0},{8,12},{12,8},{1,5},{5,1},{9,13},{13,9},{16,20},{20,16... | collective-permute-start | bytes 731144 | tf_op jit(solution)/shard_map/cond/branch_0_fun/ppermute | solution.py:463
  62.0 0.7 copy-start.19
  62.7 18.0 %copy-start.4 = (bf16[1,1,128,1280]{3,2,1,0:T(8,128)(2,1)S(1)}, bf16[1,1,128,1280]{3,2,1,0:T(8,128)(2,1)}, u32[]{:S(2)}) copy-start(bf16[1,1,128,1280]{3,2,1,0:T(8,128)(2,1)} %param.9) | copy-start | bytes 983044
  62.7 18.1 %copy-start.8 = (bf16[1,1,128,1280]{3,2,1,0:T(8,128)(2,1)S(1)}, bf16[1,1,128,1280]{3,2,1,0:T(8,128)(2,1)}, u32[]{:S(2)}) copy-start(bf16[1,1,128,1280]{3,2,1,0:T(8,128)(2,1)} %param.10) | copy-start | bytes 983044
  62.7 11.8 %collective-permute-start.17 = (bf16[128,1280]{1,0:T(8,128)(2,1)}, bf16[128,1280]{1,0:T(8,128)(2,1)S(1)}, u32[]{:S(2)}, u32[]{:S(2)}) collective-permute-start(bf16[128,1280]{1,0:T(8,128)(2,1)} %get-tuple-element.113), channel_id=1, source_target_pairs={{2,0},{3,1},{6,4},{7,5},{10,8},{11,9},{14,12},{15,13},{18,16},{19,... | collective-permute-start | bytes 983048 | tf_op jit(solution)/shard_map/ppermute | solution.py:463
  65.4 14.6 %collective-permute-start.19 = (bf16[128,320]{1,0:T(8,128)(2,1)S(1)}, bf16[128,320]{1,0:T(8,128)(2,1)S(1)}, u32[]{:S(2)}, u32[]{:S(2)}) collective-permute-start(bf16[128,320]{1,0:T(8,128)(2,1)S(1)} %get-tuple-element.166), channel_id=1, source_target_pairs={{0,4},{4,8},{8,12},{12,0},{1,5},{5,9},{9,13},{13,1},{2,6},{6,10},{... | collective-permute-start | bytes 245768 | tf_op jit(solution)/shard_map/ppermute | solution.py:463
  65.8 14.2 %collective-permute-start.20 = (bf16[128,320]{1,0:T(8,128)(2,1)S(1)}, bf16[128,320]{1,0:T(8,128)(2,1)S(1)}, u32[]{:S(2)}, u32[]{:S(2)}) collective-permute-start(bf16[128,320]{1,0:T(8,128)(2,1)S(1)} %get-tuple-element.165), channel_id=1, source_target_pairs={{0,8},{4,12},{8,0},{12,4},{1,9},{5,13},{9,1},{13,5},{2,10},{6,14},... | collective-permute-start | bytes 245768 | tf_op jit(solution)/shard_map/ppermute | solution.py:463
  68.3 13.7 %copy-start.20 = (bf16[136,896]{1,0:T(8,128)(2,1)S(1)}, bf16[136,896]{1,0:T(8,128)(2,1)}, u32[]{:S(2)}) copy-start(bf16[136,896]{1,0:T(8,128)(2,1)} %get-tuple-element.126.got) | copy-start | bytes 731140
  68.3 11.8 %collective-permute-start.21 = (bf16[128,320]{1,0:T(8,128)(2,1)S(1)}, bf16[128,320]{1,0:T(8,128)(2,1)S(1)}, u32[]{:S(2)}, u32[]{:S(2)}) collective-permute-start(bf16[128,320]{1,0:T(8,128)(2,1)S(1)} %get-tuple-element.164), channel_id=1, source_target_pairs={{0,12},{4,0},{8,4},{12,8},{1,13},{5,1},{9,5},{13,9},{2,14},{6,2},{... | collective-permute-start | bytes 245768 | tf_op jit(solution)/shard_map/ppermute | solution.py:463
  75.9 10.6 %collective-permute-start.18 = (bf16[128,1280]{1,0:T(8,128)(2,1)S(1)}, bf16[128,1280]{1,0:T(8,128)(2,1)S(1)}, u32[]{:S(2)}, u32[]{:S(2)}) collective-permute-start(bf16[128,1280]{1,0:T(8,128)(2,1)S(1)} %shard_map.86.refs_0_), channel_id=1, source_target_pairs={{0,4},{4,0},{8,12},{12,8},{1,5},{5,1},{9,13},{13,9},{16,20},{20,16... | collective-permute-start | bytes 983048 | tf_op jit(solution)/shard_map/ppermute | solution.py:463
  78.1 10.4 %collective-permute-start.23 = (bf16[128,1280]{1,0:T(8,128)(2,1)S(1)}, bf16[128,1280]{1,0:T(8,128)(2,1)S(1)}, u32[]{:S(2)}, u32[]{:S(2)}) collective-permute-start(bf16[128,1280]{1,0:T(8,128)(2,1)S(1)} %shard_map.86.refs_0_), channel_id=1, source_target_pairs={{0,1},{1,0},{4,5},{5,4},{8,9},{9,8},{12,13},{13,12},{16,17},{17,16... | collective-permute-start | bytes 983048 | tf_op jit(solution)/shard_map/ppermute | solution.py:463
  80.1 3.9 %collective-permute-start.22 = (bf16[128,256]{1,0:T(8,128)(2,1)}, bf16[128,256]{1,0:T(8,128)(2,1)S(1)}, u32[]{:S(2)}, u32[]{:S(2)}) collective-permute-start(bf16[128,256]{1,0:T(8,128)(2,1)} %get-tuple-element.118.found), channel_id=1, source_target_pairs={{2,6},{6,2},{10,14},{14,10},{3,7},{7,3},{11,15},{15,11},{18,22},{2... | collective-permute-start | bytes 196616 | tf_op jit(solution)/shard_map/ppermute | solution.py:463
  86.5 3.5 %collective-permute-start.24 = (bf16[128,1280]{1,0:T(8,128)(2,1)S(1)}, bf16[128,1280]{1,0:T(8,128)(2,1)S(1)}, u32[]{:S(2)}, u32[]{:S(2)}) collective-permute-start(bf16[128,1280]{1,0:T(8,128)(2,1)S(1)} %collective-permute-done.18.refs_1_), channel_id=1, source_target_pairs={{0,1},{1,0},{4,5},{5,4},{8,9},{9,8},{12,13},{13,12},{16,17},{17,16... | collective-permute-start | bytes 983048 | tf_op jit(solution)/shard_map/ppermute | solution.py:463
  90.0 14.8 %copy-start = (bf16[1,1280,512]{2,1,0:T(8,128)(2,1)S(1)}, bf16[1,1280,512]{2,1,0:T(8,128)(2,1)}, u32[]{:S(2)}) copy-start(bf16[1,1280,512]{2,1,0:T(8,128)(2,1)} %param.13) | copy-start | bytes 3932164
  94.0 6.9 %collective-permute-start.25 = (bf16[272,128]{1,0:T(8,128)(2,1)S(1)}, bf16[272,128]{1,0:T(8,128)(2,1)S(1)}, u32[]{:S(2)}, u32[]{:S(2)}) collective-permute-start(bf16[272,128]{1,0:T(8,128)(2,1)S(1)} %shard_map.90.refs_0_), channel_id=1, source_target_pairs={{0,4},{4,8},{8,12},{12,0},{1,5},{5,9},{9,13},{13,1},{2,6},{6,10},{... | collective-permute-start | bytes 208904 | tf_op jit(solution)/shard_map/ppermute | solution.py:463
  94.6 8.6 %collective-permute-start.26 = (bf16[272,128]{1,0:T(8,128)(2,1)S(1)}, bf16[272,128]{1,0:T(8,128)(2,1)S(1)}, u32[]{:S(2)}, u32[]{:S(2)}) collective-permute-start(bf16[272,128]{1,0:T(8,128)(2,1)S(1)} %shard_map.90.refs_0_), channel_id=1, source_target_pairs={{0,8},{4,12},{8,0},{12,4},{1,9},{5,13},{9,1},{13,5},{2,10},{6,14},... | collective-permute-start | bytes 208904 | tf_op jit(solution)/shard_map/ppermute | solution.py:463
  95.8 7.3 %collective-permute-start.27 = (bf16[272,128]{1,0:T(8,128)(2,1)S(1)}, bf16[272,128]{1,0:T(8,128)(2,1)S(1)}, u32[]{:S(2)}, u32[]{:S(2)}) collective-permute-start(bf16[272,128]{1,0:T(8,128)(2,1)S(1)} %shard_map.90.refs_0_), channel_id=1, source_target_pairs={{0,12},{4,0},{8,4},{12,8},{1,13},{5,1},{9,5},{13,9},{2,14},{6,2},{... | collective-permute-start | bytes 208904 | tf_op jit(solution)/shard_map/ppermute | solution.py:463
  103.2 1.6 %collective-permute-start.28 = (bf16[1088,128]{1,0:T(8,128)(2,1)S(1)}, bf16[1088,128]{1,0:T(8,128)(2,1)S(1)}, u32[]{:S(2)}, u32[]{:S(2)}) collective-permute-start(bf16[1088,128]{1,0:T(8,128)(2,1)S(1)} %pad_maximum_fusion.1), channel_id=1, source_target_pairs={{0,1},{1,0},{2,3},{3,2},{4,5},{5,4},{6,7},{7,6},{8,9},{9,8},{10,11... | collective-permute-start | bytes 835592 | tf_op jit(solution)/shard_map/ppermute | solution.py:463

commit v7 on v6

--- a/solution.py
+++ b/solution.py
@@ -73,7 +73,7 @@
         jax.ShapeDtypeStruct(values.shape, F32),
     )
     call = kernel_call(
-        attention_kernel, shapes, [SMEM, VMEM, VMEM, VMEM], flops=10**8, nbytes=3 * 10**6
+        attention_kernel, shapes, [SMEM, VMEM, VMEM, VMEM], flops=10**5, nbytes=10**4
     )
     return call(length, queries, keys, values)
 
@@ -167,6 +167,39 @@
     return call(length, inputs, branch, *current)
 
 
+def gain_kernel(inputs, branch, gain):
+    branch_f = branch[...].astype(F32)
+    totals = inputs[...].astype(F32) + branch_f
+    gain[...] = (branch_f / stabilize(totals) / stabilize(branch_f)).astype(BF16)
+
+
+def branch_gain(inputs, branch):
+    shape = jax.ShapeDtypeStruct(inputs.shape, BF16)
+    return kernel_call(gain_kernel, shape, [VMEM, VMEM], flops=10**7, nbytes=10**6)(inputs, branch)
+
+
+def pair_sensitivity_kernel(inputs, branch, gain, current, partner, sens, kept_sum):
+    seq_len = inputs.shape[0]
+    inputs_f = inputs[...].astype(F32)
+    branch_f = branch[...].astype(F32)
+    sens_total = current[...].astype(F32) / stabilize(inputs_f + branch_f)
+    sens[:seq_len] = (branch_f * sens_total / stabilize(branch_f)).astype(BF16)
+    sens[seq_len:] = (partner[...].astype(F32) * gain[...].astype(F32)).astype(BF16)
+    kept_sum[...] = by_token(inputs_f * sens_total)
+
+
+def pair_sensitivity(inputs, branch, gain, current, partner):
+    seq_len, width = inputs.shape
+    shapes = (
+        jax.ShapeDtypeStruct((2 * seq_len, width), BF16),
+        jax.ShapeDtypeStruct((1, seq_len), F32),
+    )
+    call = kernel_call(
+        pair_sensitivity_kernel, shapes, [VMEM] * 5, flops=10**7, nbytes=2 * 10**6
+    )
+    return call(inputs, branch, gain, current, partner)
+
+
 def outgoing_kernel(place, inputs, branch, sens_own, sens_other, value_rows, outgoing):
     core, length = place[0], place[1]
     width = sens_own.shape[1]
@@ -205,7 +238,7 @@
             tokens = pl.ds(pl.multiple_of(b * seq_len, 128), seq_len)
             length = jnp.max(half[seq_len:, :HD].astype(F32), axis=0, keepdims=True)
             allowed = (column <= row) & (column.astype(F32) < length)
-            value_head = half[:seq_len, width + HD :]
+            value_head = half[:seq_len, width + HD : width + 2 * HD]
             value_f = value_head.astype(F32)
             values[tokens] = value_f
             value_gain[tokens] = value_f / stabilize(value_f)
@@ -238,11 +271,11 @@
 
 
 def main_kernel(count, place, *refs):
-    sens, out_block, (before, kept_sum, probs, gain_t, value_gain, values) = refs[:4], refs[4], refs[5:11]
-    own_pieces, other_pieces = refs[11 : 11 + count], refs[11 + count : 11 + 2 * count]
-    found, halves, total = refs[11 + 2 * count :]
+    sens, out_block, (before, kept_sum, probs, gain_t, value_gain, values) = refs[:2], refs[2], refs[3:9]
+    own_pieces, other_pieces = refs[9 : 9 + count], refs[9 + count : 9 + 2 * count]
+    found, halves, total = refs[9 + 2 * count :]
     pos, core, group, active, side = [place[i] for i in range(5)]
-    seq_len, half_width = sens[0].shape
+    seq_len, half_width = sens[0].shape[0] // 2, sens[0].shape[1]
     width = out_block.shape[1]
     per_core = half_width // width
     quarter = own_pieces[0].shape[0]
@@ -256,7 +289,7 @@
         for j, half in ((0, core), (1, 1 - core)):
             for i, sequence in ((0, side), (1, 1 - side)):
                 rows = pl.ds(pl.multiple_of(sequence * seq_len, 128), seq_len)
-                halves[half, rows, :] = sens[2 * j + i][...]
+                halves[half, rows, :] = sens[j][i * seq_len : (i + 1) * seq_len]
 
         def part(k):
             owner = lax.rem(pos - k + count + 1, count + 1)
@@ -324,7 +357,7 @@
 
 def main_step(place, sens, out_block, quarters, before, kept_sum, rest):
     count = len(quarters[0])
-    seq_len, half_width = sens[0].shape
+    seq_len, half_width = sens[0].shape[0] // 2, sens[0].shape[1]
     operands = [*sens, out_block, before, kept_sum, *rest, *quarters[0], *quarters[1]]
     call = kernel_call(
         functools.partial(main_kernel, count),
@@ -340,9 +373,9 @@
 
 def main_plain(place, sens, out_block, quarters, before, kept_sum, rest):
     pos, core, group, active, side = [place[i] for i in range(5)]
-    seq_len = sens[0].shape[0]
+    seq_len = sens[0].shape[0] // 2
     width = out_block.shape[1]
-    mine, theirs = (ordered(side == 0, sens[2 * j], sens[2 * j + 1], 0) for j in range(2))
+    mine, theirs = (ordered(side == 0, half[:seq_len], half[seq_len:], 0) for half in sens)
     sens_full = ordered(core == 0, mine, theirs, 1)
     count = len(quarters[0])
     quarter = quarters[0][0].shape[0]
@@ -396,21 +429,20 @@
 
 
 def relevance_kernel(count, place, inputs_t, value_rows, *refs):
-    own, (other, relevance, heat) = refs[:count], refs[count:]
+    own, (other, relevance, heat, sens) = refs[:count], refs[count:]
     pos, core = place[0], place[1]
     size = own[0].shape[0]
     rows = size - 16
-    relevance[...] = jnp.zeros_like(relevance)
     for k in range(count):
         source = lax.rem(pos - k + count, count)
-        tokens = inputs_t[:, pl.ds(pl.multiple_of(source // 2 * rows, 128), rows)]
-        for c, sens in ((core, own[k][:rows]), (1 - core, other[k * size : k * size + rows])):
+        tokens = pl.ds(pl.multiple_of(source // 2 * rows, 128), rows)
+        for c, piece in ((core, own[k][:rows]), (1 - core, other[k * size : k * size + rows])):
             head = 2 * c + lax.rem(source, 2)
-            at = pl.ds(pl.multiple_of(head * HD, 128), HD)
-            relevance[:, at] += jnp.dot(tokens, sens, preferred_element_type=F32)
+            sens[tokens, pl.ds(pl.multiple_of(head * HD, 128), HD)] = piece
     rows = relevance.shape[0]
     value_block = value_rows[pl.ds(pl.multiple_of(pos * rows, 16), rows), :]
-    relevance[...] *= value_block.astype(F32)
+    summed = jnp.dot(inputs_t[...], sens[...], preferred_element_type=F32)
+    relevance[...] = value_block.astype(F32) * summed
     heat[...] = heat_of(own, other, place, count)
 
 
@@ -423,6 +455,7 @@
         functools.partial(relevance_kernel, len(own)),
         shapes,
         [SMEM] + [VMEM] * (3 + len(own)),
+        [pltpu.VMEM((inputs_t.shape[1], value_rows.shape[1]), BF16)],
         flops=2 * 10**8,
         nbytes=2 * 10**6,
     )
@@ -472,8 +505,10 @@
     return moved(shard, ("mp",), lambda c: (1 - c,))
 
 
-def from_next_section(shard):
-    return moved(shard, ("section",), lambda s: (s - 1,) if s > 0 else None)
+def from_next_section(shard, flip_pair=0):
+    return moved(
+        shard, ("dp", "section"), lambda i, s: (i ^ flip_pair, s - 1) if s > 0 else None
+    )
 
 
 def ordered(first_is_mine, mine, theirs, axis):
@@ -580,23 +615,22 @@
             mine, ("section", "mp"), lambda s, c: (s, 1 - c) if take(s == sections - 1) else None
         )
 
-    def values_of(take):
-        value_part = jnp.dot(inputs, value_rows, preferred_element_type=F32)
+    def values_of(take, rows):
+        value_part = jnp.dot(rows, value_rows, preferred_element_type=F32)
         part_mine = part_of(value_part, core_pos, kv_width, 1)
         part_other = part_of(value_part, 1 - core_pos, kv_width, 1)
         return part_mine + core_exchange(part_other.astype(BF16), take).astype(F32)
 
-    where_last = jnp.stack([core_pos, lengths[0]])
-
     def last_section():
-        values_f = values_of(lambda last: last)
-        rest = attend(lengths, query_rows, key_rows, values_f)
         sens_branch = sensitivity(lengths, inputs, branch)
         own, backs = spread_product(sens_branch, out_block)
+        values_f = values_of(lambda last: last, once(inputs, own))
+        rest = attend(lengths, query_rows, key_rows, values_f)
         leaves, tree = jax.tree.flatten(early_shapes[-1])
         filler = lengths[0].astype(BF16)
         unused = [jnp.full(leaf.shape, filler + k, BF16) for k, leaf in enumerate(leaves)]
-        own, *unused = lax.optimization_barrier((own, *unused))
+        where_last = jnp.stack([core_pos, lengths[0]])
+        own, where_last, *unused = lax.optimization_barrier((own, where_last, *unused))
         if peers > 8:
             for back in backs:
                 own = own + back.astype(F32)
@@ -617,7 +651,7 @@
             early_move(rows, ("groups", "section"), lambda g, s: (1 - g, s))
             for rows in own_quarters
         ]
-        values_f = values_of(lambda last: not last)
+        values_f = values_of(lambda last: not last, inputs)
 
         def half_of(which):
             parts = [
@@ -631,28 +665,27 @@
 
         found = jnp.full((seq_len, kv_width), lengths[0].astype(BF16))
         outgoing = jnp.full((seq_len, half_width), lengths[0].astype(BF16))
-        kept_half, sent_half, found, outgoing, *_ = lax.optimization_barrier(
-            (half_of(side), half_of(1 - side), found, outgoing, *own_quarters)
-            + (other_quarters[0], other_quarters[-1])
+        partner_gain = early_pair(branch_gain(inputs, branch))
+        sent_half = half_of(1 - side)
+        sent_half = once(sent_half, *own_quarters, other_quarters[0], other_quarters[-1])
+        got_half = early_pair(sent_half)
+        kept_half, found, outgoing = half_of(side), *lax.optimization_barrier((found, outgoing, values_f))[:2]
+        return values_f, found, outgoing, (
+            own_quarters,
+            other_quarters,
+            (kept_half, got_half, partner_gain),
         )
-        halves = (kept_half, early_pair(sent_half))
-        return values_f, found, outgoing, (own_quarters, other_quarters, halves)
 
     early_shapes = jax.eval_shape(early_section)
     values_f, found, outgoing, prepared = lax.cond(is_last, last_section, early_section)
-    own_quarters, other_quarters, (kept_half, got_half) = prepared
+    own_quarters, other_quarters, (kept_half, got_half, partner_gain) = prepared
     arrived = from_next_section(outgoing)
+    partner_arrived = from_next_section(outgoing, 1)
 
     rows = once(inputs, outgoing)
     pieces = [
         along_dp(part_of(rows, lax.rem(dp_pos + k, peers), block_rows, 1), k) for k in range(peers)
     ]
-    sens_mine = sensitivity(lengths, inputs, branch, arrived)
-    sens_partner = early_pair(sens_mine)
-
-    kept_half, got_half, found, arrived, *pieces = lax.optimization_barrier(
-        (kept_half, got_half, found, arrived, *pieces, sens_mine)
-    )[:-1]
     rest = pair_attend(place(~is_last), kept_half, got_half)
     if in_tiles:
         inputs_t = turned_side_by_side(place(0), pieces)
@@ -673,16 +706,14 @@
     for turn in range(1, sections):
         active = section_pos == sections - 1 - turn
         current = jnp.where(active, arrived, current)
-        kept_sum = jnp.sum(kept_of(arrived), axis=1)[None]
-        if turn > 1:
-            sens_mine = sensitivity(lengths, inputs, branch, arrived)
-            sens_partner = early_pair(sens_mine)
-        else:
-            sens_partner, *ready = lax.optimization_barrier(
-                (sens_partner, sens_values, kept_sum, inputs_t, *rest)
+        if turn == 1:
+            arrived, partner_arrived, sens_values, inputs_t, *rest = lax.optimization_barrier(
+                (arrived, partner_arrived, sens_values, inputs_t, *rest)
             )
-            sens_values, kept_sum, inputs_t, *rest = ready
-        sens = [sens_mine, sens_partner, early_core(sens_mine), early_core(sens_partner)]
+        sens_own, kept_sum = pair_sensitivity(
+            inputs, branch, partner_gain, arrived, partner_arrived
+        )
+        sens = [sens_own, early_core(sens_own)]
         step = main_step if in_tiles else main_plain
         sens_values = step(
             place(active),
@@ -700,6 +731,7 @@
             back_inputs = by_columns(sens_all, value_rows)
             outgoing = kept_of(current) + inputs.astype(F32) * back_inputs
             arrived = from_next_section(outgoing.astype(BF16))
+            partner_arrived = from_next_section(outgoing.astype(BF16), 1)
 
     own_sens = [along_dp(sens_values, k) for k in range(peers)]
     other_sens = other_core(jnp.concatenate(own_sens, 0))

time: 107 us -> 107 us (level)
  waiting for transfers between devices: 41.9 us -> 32.9 us
  starting transfers between devices: 43.7 us -> 51 us
    ppermute x20, waiting for transfers between devices: 41.9 us -> 32.9 us  [moved(): return lax.ppermute(shard, axes, pairs)]
    ppermute x20, starting transfers between devices: 43.7 us -> 51 us  [moved(): return lax.ppermute(shard, axes, pairs)]
    pallas_call x1 -> x2, Pallas kernels: 1.45 us -> 2.17 us  [the longest x1 1.83 us: pair_sensitivity(): return call(inputs, branch, gain, current, partner)]
  transfers between devices with their start and end apart: 20 -> 20, of which waited for: 11 -> 9; matrix products, arithmetic and copies ran while one was open for 4% -> 5% of each run, Pallas kernels for 5% -> 3%
where the time goes in v7:
time: 107 us; the launch traced here: 106 us
  starting transfers between devices  51 us (48%)
  waiting for transfers between devices  32.9 us (31%)
  Pallas kernels  11.2 us (10%)
  local copies, waits for them, and re-layouts  6.97 us (7%)
  between operations  1.46 us (1%)
  other arithmetic  1.43 us (1%)
    ppermute x20, starting transfers between devices, moved(): return lax.ppermute(shard, axes, pairs)  51 us
    ppermute x20, waiting for transfers between devices, moved(): return lax.ppermute(shard, axes, pairs)  32.9 us
    dynamic_slice x4, local copies, waits for them, and re-layouts, part_of(): return lax.dynamic_slice_in_dim(array, index * width, width, axis)  4.5 us
    pallas_call x1, Pallas kernels, main_step(): return call(place, *operands)  4.03 us
  transfers between devices with their start and end apart: 20, of which 9 were waited for; matrix products, arithmetic and copies ran while one was open for 5% of the time, Pallas kernels for 3%

profile of v7, /device:TPU:0, one launch (start us, length us, event | category | flops | bytes accessed | tf_op | source)
XLA Modules:
  0.0 106.3 jit_solution(18215535484771922937)
XLA Ops:
  0.7 60.3 %conditional.1 = (f32[128,256]{1,0:T(8,128)S(1)}, bf16[128,256]{1,0:T(8,128)(2,1)}, bf16[128,1280]{1,0:T(8,128)(2,1)}, bf16[320,640]{1,0:T(8,128)(2,1)}, bf16[32...) conditional(s32[]{:T(128)} %convert_element_type.60, ...), branch_computations={%region_0.0_spmd, %region_1.2_spmd} | conditional | flops 1430559104 | bytes 38794944 | solution.py:680
  0.7 2.4 %constant_dynamic-slice_fusion.4 = (bf16[320,640]{1,0:T(8,128)(2,1)}, bf16[320,640]{1,0:T(8,128)(2,1)}, bf16[320,640]{1,0:T(8,128)(2,1)}) fusion(bf16[1280,640]{1,0:T(8,128)(2,1)} %get-tuple-element.44, s32[]{:T(128)S(6)} %select_n.51, s32[]{:T(128)S(6)} %select_n.50, s32[]{:T(128)S(6)} %select_n.49), kind=kLoop, calls=%fused_computation.19 | loop fusion | bytes 2457612 | tf_op jit(solution)/shard_map/cond/branch_0_fun/dynamic_slice | solution.py:521
  3.2 5.1 %collective-permute-start.1 = (bf16[320,640]{1,0:T(8,128)(2,1)}, bf16[320,640]{1,0:T(8,128)(2,1)}, u32[]{:S(2)}, u32[]{:S(2)}) collective-permute-start(bf16[320,640]{1,0:T(8,128)(2,1)} %get-tuple-element.141), channel_id=1, source_target_pairs={{0,4},{4,8},{8,12},{12,0},{1,5},{5,9},{9,13},{13,1},{16,20},{20,24... | collective-permute-start | bytes 1228808 | tf_op jit(solution)/shard_map/cond/branch_0_fun/ppermute | solution.py:496
  8.2 3.9 %collective-permute-start.3 = (bf16[320,640]{1,0:T(8,128)(2,1)}, bf16[320,640]{1,0:T(8,128)(2,1)}, u32[]{:S(2)}, u32[]{:S(2)}) collective-permute-start(bf16[320,640]{1,0:T(8,128)(2,1)} %get-tuple-element.139), channel_id=1, source_target_pairs={{0,12},{4,0},{8,4},{12,8},{1,13},{5,1},{9,5},{13,9},{16,28},{20,16... | collective-permute-start | bytes 1228808 | tf_op jit(solution)/shard_map/cond/branch_0_fun/ppermute | solution.py:496
  12.2 2.9 %collective-permute-start.2 = (bf16[320,640]{1,0:T(8,128)(2,1)}, bf16[320,640]{1,0:T(8,128)(2,1)}, u32[]{:S(2)}, u32[]{:S(2)}) collective-permute-start(bf16[320,640]{1,0:T(8,128)(2,1)} %get-tuple-element.140), channel_id=1, source_target_pairs={{0,8},{4,12},{8,0},{12,4},{1,9},{5,13},{9,1},{13,5},{16,24},{20,28... | collective-permute-start | bytes 1228808 | tf_op jit(solution)/shard_map/cond/branch_0_fun/ppermute | solution.py:496
  15.1 0.3 fusion.12
  15.5 1.9 %collective-permute-start = (bf16[128,256]{1,0:T(8,128)(2,1)S(1)}, bf16[128,256]{1,0:T(8,128)(2,1)S(1)}, u32[]{:S(2)}, u32[]{:S(2)}) collective-permute-start(bf16[128,256]{1,0:T(8,128)(2,1)S(1)} %dynamic-slice_convert_fusion), channel_id=1, source_target_pairs={{0,1},{1,0},{4,5},{5,4},{8,9},{9,8},{12,13},{13,12},{16,17},{17,16... | collective-permute-start | bytes 196616 | tf_op jit(solution)/shard_map/cond/branch_0_fun/ppermute | solution.py:496
  17.4 0.3 branch_0_fun.1
  17.8 3.5 %collective-permute-start.8 = (bf16[128,1280]{1,0:T(8,128)(2,1)S(1)}, bf16[128,1280]{1,0:T(8,128)(2,1)}, u32[]{:S(2)}, u32[]{:S(2)}) collective-permute-start(bf16[128,1280]{1,0:T(8,128)(2,1)S(1)} %branch_0_fun.1), channel_id=1, source_target_pairs={{0,4},{4,0},{8,12},{12,8},{1,5},{5,1},{9,13},{13,9},{16,20},{20,16... | collective-permute-start | bytes 983048 | tf_op jit(solution)/shard_map/cond/branch_0_fun/ppermute | solution.py:496
  22.1 3.4 %collective-permute-start.4 = (bf16[320,640]{1,0:T(8,128)(2,1)}, bf16[320,640]{1,0:T(8,128)(2,1)}, u32[]{:S(2)}, u32[]{:S(2)}) collective-permute-start(bf16[320,640]{1,0:T(8,128)(2,1)} %collective-permute-done.1), channel_id=1, source_target_pairs={{0,16},{16,0},{1,17},{17,1},{4,20},{20,4},{5,21},{21,5},{8,24},{24... | collective-permute-start | bytes 1228808 | tf_op jit(solution)/shard_map/cond/branch_0_fun/ppermute | solution.py:496
  25.5 3.4 %collective-permute-done.3 = bf16[320,640]{1,0:T(8,128)(2,1)} collective-permute-done((bf16[320,640]{1,0:T(8,128)(2,1)}, bf16[320,640]{1,0:T(8,128)(2,1)}, u32[]{:S(2)}, u32[]{:S(2)}) %collective-permute-start.3) | collective-permute-done | bytes 409632 | tf_op jit(solution)/shard_map/cond/branch_0_fun/ppermute | solution.py:496
  28.9 3.4 %collective-permute-start.6 = (bf16[320,640]{1,0:T(8,128)(2,1)}, bf16[320,640]{1,0:T(8,128)(2,1)}, u32[]{:S(2)}, u32[]{:S(2)}) collective-permute-start(bf16[320,640]{1,0:T(8,128)(2,1)} %collective-permute-done.3), channel_id=1, source_target_pairs={{0,16},{16,0},{1,17},{17,1},{4,20},{20,4},{5,21},{21,5},{8,24},{24... | collective-permute-start | bytes 1228808 | tf_op jit(solution)/shard_map/cond/branch_0_fun/ppermute | solution.py:496
  32.3 14.0 %collective-permute-done.2 = bf16[320,640]{1,0:T(8,128)(2,1)} collective-permute-done((bf16[320,640]{1,0:T(8,128)(2,1)}, bf16[320,640]{1,0:T(8,128)(2,1)}, u32[]{:S(2)}, u32[]{:S(2)}) %collective-permute-start.2) | collective-permute-done | bytes 409632 | tf_op jit(solution)/shard_map/cond/branch_0_fun/ppermute | solution.py:496
  46.3 3.4 %collective-permute-start.5 = (bf16[320,640]{1,0:T(8,128)(2,1)}, bf16[320,640]{1,0:T(8,128)(2,1)}, u32[]{:S(2)}, u32[]{:S(2)}) collective-permute-start(bf16[320,640]{1,0:T(8,128)(2,1)} %collective-permute-done.2), channel_id=1, source_target_pairs={{0,16},{16,0},{1,17},{17,1},{4,20},{20,4},{5,21},{21,5},{8,24},{24... | collective-permute-start | bytes 1228808 | tf_op jit(solution)/shard_map/cond/branch_0_fun/ppermute | solution.py:496
  49.8 6.3 %collective-permute-start.7 = (bf16[136,896]{1,0:T(8,128)(2,1)S(1)}, bf16[136,896]{1,0:T(8,128)(2,1)S(1)}, u32[]{:S(2)}, u32[]{:S(2)}) collective-permute-start(bf16[136,896]{1,0:T(8,128)(2,1)S(1)} %fusion.9), channel_id=1, source_target_pairs={{0,4},{4,0},{8,12},{12,8},{1,5},{5,1},{9,13},{13,9},{16,20},{20,16... | collective-permute-start | bytes 731144 | tf_op jit(solution)/shard_map/cond/branch_0_fun/ppermute | solution.py:496
  56.2 0.7 broadcast_in_dim.28
  56.9 0.6 broadcast_in_dim.14
  57.6 2.3 %collective-permute-done.5 = bf16[320,640]{1,0:T(8,128)(2,1)} collective-permute-done((bf16[320,640]{1,0:T(8,128)(2,1)}, bf16[320,640]{1,0:T(8,128)(2,1)}, u32[]{:S(2)}, u32[]{:S(2)}) %collective-permute-start.5) | collective-permute-done | bytes 409632 | tf_op jit(solution)/shard_map/cond/branch_0_fun/ppermute | solution.py:496
  59.9 0.4 collective-permute-done.7
  60.3 0.7 copy-done.14
  61.0 1.4 %collective-permute-start.18 = (bf16[128,1280]{1,0:T(8,128)(2,1)}, bf16[128,1280]{1,0:T(8,128)(2,1)S(1)}, u32[]{:S(2)}, u32[]{:S(2)}) collective-permute-start(bf16[128,1280]{1,0:T(8,128)(2,1)} %get-tuple-element.110), channel_id=1, source_target_pairs={{2,0},{6,4},{10,8},{14,12},{3,1},{7,5},{11,9},{15,13},{18,16},{22,... | collective-permute-start | bytes 983048 | tf_op jit(solution)/shard_map/ppermute | solution.py:496
  62.4 1.3 %collective-permute-start.19 = (bf16[128,1280]{1,0:T(8,128)(2,1)}, bf16[128,1280]{1,0:T(8,128)(2,1)S(1)}, u32[]{:S(2)}, u32[]{:S(2)}) collective-permute-start(bf16[128,1280]{1,0:T(8,128)(2,1)} %get-tuple-element.110), channel_id=1, source_target_pairs={{2,4},{6,0},{10,12},{14,8},{3,5},{7,1},{11,13},{15,9},{18,20},{22,... | collective-permute-start | bytes 983048 | tf_op jit(solution)/shard_map/ppermute | solution.py:496
  63.7 2.0 %constant_dynamic-slice_fusion.11 = (bf16[128,320]{1,0:T(8,128)(2,1)}, bf16[128,320]{1,0:T(8,128)(2,1)}, bf16[128,320]{1,0:T(8,128)(2,1)}, bf16[128,320]{1,0:T(8,128)(2,1)S(1)}) fusion(bf16[128,1280]{1,0:T(8,128)(2,1)} %bitcast.31, s32[]{:T(128)S(6)} %select_n.72, s32[]{:T(128)S(6)} %select_n.71, s32[]{:T(128)S(6)} %select_n.70, s32[]{:T(128)S(6)} %select_n.69), kind=kLoop, calls=%fused_computation.37 | loop fusion | bytes 655376 | tf_op jit(solution)/shard_map/dynamic_slice | solution.py:521
  65.7 2.0 %collective-permute-start.21 = (bf16[128,320]{1,0:T(8,128)(2,1)}, bf16[128,320]{1,0:T(8,128)(2,1)S(1)}, u32[]{:S(2)}, u32[]{:S(2)}) collective-permute-start(bf16[128,320]{1,0:T(8,128)(2,1)} %get-tuple-element.154), channel_id=1, source_target_pairs={{0,4},{4,8},{8,12},{12,0},{1,5},{5,9},{9,13},{13,1},{2,6},{6,10},{... | collective-permute-start | bytes 245768 | tf_op jit(solution)/shard_map/ppermute | solution.py:496
  67.8 2.9 %collective-permute-start.22 = (bf16[128,320]{1,0:T(8,128)(2,1)}, bf16[128,320]{1,0:T(8,128)(2,1)S(1)}, u32[]{:S(2)}, u32[]{:S(2)}) collective-permute-start(bf16[128,320]{1,0:T(8,128)(2,1)} %get-tuple-element.153), channel_id=1, source_target_pairs={{0,8},{4,12},{8,0},{12,4},{1,9},{5,13},{9,1},{13,5},{2,10},{6,14},... | collective-permute-start | bytes 245768 | tf_op jit(solution)/shard_map/ppermute | solution.py:496
  70.7 0.7 collective-permute-start.20
  72.0 3.0 %collective-permute-start.23 = (bf16[128,320]{1,0:T(8,128)(2,1)}, bf16[128,320]{1,0:T(8,128)(2,1)S(1)}, u32[]{:S(2)}, u32[]{:S(2)}) collective-permute-start(bf16[128,320]{1,0:T(8,128)(2,1)} %get-tuple-element.152), channel_id=1, source_target_pairs={{0,12},{4,0},{8,4},{12,8},{1,13},{5,1},{9,5},{13,9},{2,14},{6,2},{... | collective-permute-start | bytes 245768 | tf_op jit(solution)/shard_map/ppermute | solution.py:496
  75.0 1.3 %fusion.10 = f32[128]{0:T(128)S(1)} fusion(f32[128]{0:T(128)S(1)} %compare_convert_fusion, bf16[1,1,128,1280]{3,2,1,0:T(8,128)(2,1)} %param.10, bf16[1,1,128,1280]{3,2,1,0:T(8,128)(2,1)S(1)} %copy-done), kind=kLoop, calls=%fused_computation.32 | loop fusion | flops 2129792 | bytes 656384 | tf_op jit(solution)/shard_map/reduce_sum | solution.py:703
  76.3 0.1 stack.71.place
  76.4 0.1 stack.66.place
  76.5 0.1 stack.68.place
  76.6 1.6 %shard_map.88 = (bf16[2,5,128,128]{3,2,1,0:T(8,128)(2,1)S(1)}, f32[640,256]{1,0:T(8,128)S(1)}, f32[256,128]{1,0:T(8,128)S(1)}, f32[256,128]{1,0:T(8,128)S(1)}) custom-call(s32[5]{0:T(128)S(1)} %stack.71.place, bf16[136,896]{1,0:T(8,128)(2,1)S(1)} %get-tuple-element.114.kept, bf16[136,896]{1,0:T(8,128)(2,1)S(1)} %copy-done.15), custom_call_target="tpu_custom_call" | custom-call | flops 100000000 | bytes 3000000 | tf_op jit(solution)/shard_map/pallas_call | solution.py:268
  78.1 0.9 shard_map.86.refs_3_
  79.0 0.7 shard_map.87.inputs_t
  79.8 4.0 %collective-permute-done.18.current = bf16[128,1280]{1,0:T(8,128)(2,1)S(1)} collective-permute-done((bf16[128,1280]{1,0:T(8,128)(2,1)}, bf16[128,1280]{1,0:T(8,128)(2,1)S(1)}, u32[]{:S(2)}, u32[]{:S(2)}) %collective-permute-start.18) | collective-permute-done | bytes 327712 | tf_op jit(solution)/shard_map/ppermute | solution.py:496
  83.8 1.8 %shard_map.89 = (bf16[256,1280]{1,0:T(8,128)(2,1)S(1)}, f32[1,128]{1,0:T(1,128)S(1)}) custom-call(bf16[128,1280]{1,0:T(8,128)(2,1)S(1)} %bitcast.32, bf16[128,1280]{1,0:T(8,128)(2,1)} %bitcast.38, bf16[128,1280]{1,0:T(8,128)(2,1)} %get-tuple-element.121.gain, bf16[128,1280]{1,0:T(8,128)(2,1)S(1)} %collective-permute-done.18.current, ...), custom_call_target="tpu_custom_call" | custom-call | flops 10000000 | bytes 2000000 | tf_op jit(solution)/shard_map/pallas_call | solution.py:200
  85.6 1.9 %collective-permute-start.24 = (bf16[256,1280]{1,0:T(8,128)(2,1)S(1)}, bf16[256,1280]{1,0:T(8,128)(2,1)S(1)}, u32[]{:S(2)}, u32[]{:S(2)}) collective-permute-start(bf16[256,1280]{1,0:T(8,128)(2,1)S(1)} %get-tuple-element.124.refs_0_), channel_id=1, source_target_pairs={{0,1},{1,0},{4,5},{5,4},{8,9},{9,8},{12,13},{13,12},{16,17},{17,16... | collective-permute-start | bytes 1966088 | tf_op jit(solution)/shard_map/ppermute | solution.py:496
  87.6 0.1 stack.74.place
  87.6 2.0 %collective-permute-done.24.refs_1_ = bf16[256,1280]{1,0:T(8,128)(2,1)S(1)} collective-permute-done((bf16[256,1280]{1,0:T(8,128)(2,1)S(1)}, bf16[256,1280]{1,0:T(8,128)(2,1)S(1)}, u32[]{:S(2)}, u32[]{:S(2)}) %collective-permute-start.24) | collective-permute-done | bytes 655392 | tf_op jit(solution)/shard_map/ppermute | solution.py:496
  89.6 4.0 %shard_map.90.refs_0_ = bf16[272,128]{1,0:T(8,128)(2,1)S(1)} custom-call(s32[5]{0:T(128)S(1)} %stack.74.place, bf16[256,1280]{1,0:T(8,128)(2,1)S(1)} %get-tuple-element.124.refs_0_, bf16[256,1280]{1,0:T(8,128)(2,1)S(1)} %collective-permute-done.24.refs_1_, bf16[1280,640]{1,0:T(8,128)(2,1)} %bitcast.41, bf16[272,128]{1,0:T(8,128)(2,1)S(1)} %shard_map.86.refs_3_, ...), custom_call_target="tpu_custom_call" | custom-call | flops 1000000000 | bytes 6000000 | tf_op jit(solution)/shard_map/pallas_call | solution.py:371
  93.7 1.1 %collective-permute-start.25 = (bf16[272,128]{1,0:T(8,128)(2,1)S(1)}, bf16[272,128]{1,0:T(8,128)(2,1)S(1)}, u32[]{:S(2)}, u32[]{:S(2)}) collective-permute-start(bf16[272,128]{1,0:T(8,128)(2,1)S(1)} %shard_map.90.refs_0_), channel_id=1, source_target_pairs={{0,4},{4,8},{8,12},{12,0},{1,5},{5,9},{9,13},{13,1},{2,6},{6,10},{... | collective-permute-start | bytes 208904 | tf_op jit(solution)/shard_map/ppermute | solution.py:496
  94.7 0.3 collective-permute-start.26
  95.0 2.5 %collective-permute-start.27 = (bf16[272,128]{1,0:T(8,128)(2,1)S(1)}, bf16[272,128]{1,0:T(8,128)(2,1)S(1)}, u32[]{:S(2)}, u32[]{:S(2)}) collective-permute-start(bf16[272,128]{1,0:T(8,128)(2,1)S(1)} %shard_map.90.refs_0_), channel_id=1, source_target_pairs={{0,12},{4,0},{8,4},{12,8},{1,13},{5,1},{9,5},{13,9},{2,14},{6,2},{... | collective-permute-start | bytes 208904 | tf_op jit(solution)/shard_map/ppermute | solution.py:496
  97.5 3.0 %collective-permute-done.25.refs_1_ = bf16[272,128]{1,0:T(8,128)(2,1)S(1)} collective-permute-done((bf16[272,128]{1,0:T(8,128)(2,1)S(1)}, bf16[272,128]{1,0:T(8,128)(2,1)S(1)}, u32[]{:S(2)}, u32[]{:S(2)}) %collective-permute-start.25) | collective-permute-done | bytes 69664 | tf_op jit(solution)/shard_map/ppermute | solution.py:496
  100.6 2.2 %collective-permute-done.26.refs_2_ = bf16[272,128]{1,0:T(8,128)(2,1)S(1)} collective-permute-done((bf16[272,128]{1,0:T(8,128)(2,1)S(1)}, bf16[272,128]{1,0:T(8,128)(2,1)S(1)}, u32[]{:S(2)}, u32[]{:S(2)}) %collective-permute-start.26) | collective-permute-done | bytes 69664 | tf_op jit(solution)/shard_map/ppermute | solution.py:496
  102.8 0.1 collective-permute-start.28
  102.9 1.5 %collective-permute-done.28.refs_4_ = bf16[1088,128]{1,0:T(8,128)(2,1)S(1)} collective-permute-done((bf16[1088,128]{1,0:T(8,128)(2,1)S(1)}, bf16[1088,128]{1,0:T(8,128)(2,1)S(1)}, u32[]{:S(2)}, u32[]{:S(2)}) %collective-permute-start.28) | collective-permute-done | bytes 278560 | tf_op jit(solution)/shard_map/ppermute | solution.py:496
  104.5 1.8 %shard_map.91 = (f32[320,512]{1,0:T(8,128)}, f32[1,128]{1,0:T(1,128)}) custom-call(s32[5]{0:T(128)S(1)} %stack.66.place, bf16[320,512]{1,0:T(8,128)(2,1)S(1)} %shard_map.87.inputs_t, bf16[1280,512]{1,0:T(8,128)(2,1)S(1)} %bitcast.35, bf16[272,128]{1,0:T(8,128)(2,1)S(1)} %shard_map.90.refs_0_, bf16[272,128]{1,0:T(8,128)(2,1)S(1)} %collective-permute-done.25.refs_1_, ...), custom_call_target="tpu_custom_call" | custom-call | flops 200000000 | bytes 2000000 | tf_op jit(solution)/shard_map/pallas_call | solution.py:462
  (37 shorter events, 0.3 us)
Async XLA Ops:
  0.6 74.3 %copy-start = (bf16[1,1,128,1280]{3,2,1,0:T(8,128)(2,1)S(1)}, bf16[1,1,128,1280]{3,2,1,0:T(8,128)(2,1)}, u32[]{:S(2)}) copy-start(bf16[1,1,128,1280]{3,2,1,0:T(8,128)(2,1)} %param.9) | copy-start | bytes 983044
  0.7 14.4 %copy-start.1 = (bf16[128,1280]{1,0:T(8,128)(2,1)S(1)}, bf16[128,1280]{1,0:T(8,128)(2,1)}, u32[]{:S(2)}) copy-start(bf16[128,1280]{1,0:T(8,128)(2,1)} %get-tuple-element.38.inputs) | copy-start | bytes 983044 | tf_op jit(solution)/shard_map/cond
  0.7 14.4 %copy-start.4 = (bf16[1280,512]{1,0:T(8,128)(2,1)S(1)}, bf16[1280,512]{1,0:T(8,128)(2,1)}, u32[]{:S(2)}) copy-start(bf16[1280,512]{1,0:T(8,128)(2,1)} %get-tuple-element.39) | copy-start | bytes 3932164 | tf_op jit(solution)/shard_map/cond
  3.1 14.3 %copy-start.6 = (bf16[128,1280]{1,0:T(8,128)(2,1)S(1)}, bf16[128,1280]{1,0:T(8,128)(2,1)}, u32[]{:S(2)}) copy-start(bf16[128,1280]{1,0:T(8,128)(2,1)} %get-tuple-element.51.branch) | copy-start | bytes 983044 | tf_op jit(solution)/shard_map/cond
  3.2 18.9 %collective-permute-start.1 = (bf16[320,640]{1,0:T(8,128)(2,1)}, bf16[320,640]{1,0:T(8,128)(2,1)}, u32[]{:S(2)}, u32[]{:S(2)}) collective-permute-start(bf16[320,640]{1,0:T(8,128)(2,1)} %get-tuple-element.141), channel_id=1, source_target_pairs={{0,4},{4,8},{8,12},{12,0},{1,5},{5,9},{9,13},{13,1},{16,20},{20,24... | collective-permute-start | bytes 1228808 | tf_op jit(solution)/shard_map/cond/branch_0_fun/ppermute | solution.py:496
  8.2 20.7 %collective-permute-start.3 = (bf16[320,640]{1,0:T(8,128)(2,1)}, bf16[320,640]{1,0:T(8,128)(2,1)}, u32[]{:S(2)}, u32[]{:S(2)}) collective-permute-start(bf16[320,640]{1,0:T(8,128)(2,1)} %get-tuple-element.139), channel_id=1, source_target_pairs={{0,12},{4,0},{8,4},{12,8},{1,13},{5,1},{9,5},{13,9},{16,28},{20,16... | collective-permute-start | bytes 1228808 | tf_op jit(solution)/shard_map/cond/branch_0_fun/ppermute | solution.py:496
  12.2 34.2 %collective-permute-start.2 = (bf16[320,640]{1,0:T(8,128)(2,1)}, bf16[320,640]{1,0:T(8,128)(2,1)}, u32[]{:S(2)}, u32[]{:S(2)}) collective-permute-start(bf16[320,640]{1,0:T(8,128)(2,1)} %get-tuple-element.140), channel_id=1, source_target_pairs={{0,8},{4,12},{8,0},{12,4},{1,9},{5,13},{9,1},{13,5},{16,24},{20,28... | collective-permute-start | bytes 1228808 | tf_op jit(solution)/shard_map/cond/branch_0_fun/ppermute | solution.py:496
  15.1 6.8 %copy-start.10 = (bf16[128,1280]{1,0:T(8,128)(2,1)S(1)}, bf16[128,1280]{1,0:T(8,128)(2,1)}, u32[]{:S(2)}) copy-start(bf16[128,1280]{1,0:T(8,128)(2,1)} %get-tuple-element.47) | copy-start | bytes 983044 | tf_op jit(solution)/shard_map/cond
  15.5 6.6 %copy-start.12 = (bf16[128,256]{1,0:T(8,128)(2,1)S(1)}, bf16[128,256]{1,0:T(8,128)(2,1)}, u32[]{:S(2)}) copy-start(bf16[128,256]{1,0:T(8,128)(2,1)} %get-tuple-element.49) | copy-start | bytes 196612 | tf_op jit(solution)/shard_map/cond
  15.5 16.8 %collective-permute-start = (bf16[128,256]{1,0:T(8,128)(2,1)S(1)}, bf16[128,256]{1,0:T(8,128)(2,1)S(1)}, u32[]{:S(2)}, u32[]{:S(2)}) collective-permute-start(bf16[128,256]{1,0:T(8,128)(2,1)S(1)} %dynamic-slice_convert_fusion), channel_id=1, source_target_pairs={{0,1},{1,0},{4,5},{5,4},{8,9},{9,8},{12,13},{13,12},{16,17},{17,16... | collective-permute-start | bytes 196616 | tf_op jit(solution)/shard_map/cond/branch_0_fun/ppermute | solution.py:496
  17.8 39.8 %collective-permute-start.8 = (bf16[128,1280]{1,0:T(8,128)(2,1)S(1)}, bf16[128,1280]{1,0:T(8,128)(2,1)}, u32[]{:S(2)}, u32[]{:S(2)}) collective-permute-start(bf16[128,1280]{1,0:T(8,128)(2,1)S(1)} %branch_0_fun.1), channel_id=1, source_target_pairs={{0,4},{4,0},{8,12},{12,8},{1,5},{5,1},{9,13},{13,9},{16,20},{20,16... | collective-permute-start | bytes 983048 | tf_op jit(solution)/shard_map/cond/branch_0_fun/ppermute | solution.py:496
  22.1 27.8 %collective-permute-start.4 = (bf16[320,640]{1,0:T(8,128)(2,1)}, bf16[320,640]{1,0:T(8,128)(2,1)}, u32[]{:S(2)}, u32[]{:S(2)}) collective-permute-start(bf16[320,640]{1,0:T(8,128)(2,1)} %collective-permute-done.1), channel_id=1, source_target_pairs={{0,16},{16,0},{1,17},{17,1},{4,20},{20,4},{5,21},{21,5},{8,24},{24... | collective-permute-start | bytes 1228808 | tf_op jit(solution)/shard_map/cond/branch_0_fun/ppermute | solution.py:496
  28.9 21.0 %collective-permute-start.6 = (bf16[320,640]{1,0:T(8,128)(2,1)}, bf16[320,640]{1,0:T(8,128)(2,1)}, u32[]{:S(2)}, u32[]{:S(2)}) collective-permute-start(bf16[320,640]{1,0:T(8,128)(2,1)} %collective-permute-done.3), channel_id=1, source_target_pairs={{0,16},{16,0},{1,17},{17,1},{4,20},{20,4},{5,21},{21,5},{8,24},{24... | collective-permute-start | bytes 1228808 | tf_op jit(solution)/shard_map/cond/branch_0_fun/ppermute | solution.py:496
  46.3 13.6 %collective-permute-start.5 = (bf16[320,640]{1,0:T(8,128)(2,1)}, bf16[320,640]{1,0:T(8,128)(2,1)}, u32[]{:S(2)}, u32[]{:S(2)}) collective-permute-start(bf16[320,640]{1,0:T(8,128)(2,1)} %collective-permute-done.2), channel_id=1, source_target_pairs={{0,16},{16,0},{1,17},{17,1},{4,20},{20,4},{5,21},{21,5},{8,24},{24... | collective-permute-start | bytes 1228808 | tf_op jit(solution)/shard_map/cond/branch_0_fun/ppermute | solution.py:496
  49.8 10.5 %collective-permute-start.7 = (bf16[136,896]{1,0:T(8,128)(2,1)S(1)}, bf16[136,896]{1,0:T(8,128)(2,1)S(1)}, u32[]{:S(2)}, u32[]{:S(2)}) collective-permute-start(bf16[136,896]{1,0:T(8,128)(2,1)S(1)} %fusion.9), channel_id=1, source_target_pairs={{0,4},{4,0},{8,12},{12,8},{1,5},{5,1},{9,13},{13,9},{16,20},{20,16... | collective-permute-start | bytes 731144 | tf_op jit(solution)/shard_map/cond/branch_0_fun/ppermute | solution.py:496
  60.3 0.7 copy-start.14
  61.0 15.6 %copy-start.15 = (bf16[136,896]{1,0:T(8,128)(2,1)S(1)}, bf16[136,896]{1,0:T(8,128)(2,1)}, u32[]{:S(2)}) copy-start(bf16[136,896]{1,0:T(8,128)(2,1)} %get-tuple-element.115.got) | copy-start | bytes 731140
  61.0 22.8 %collective-permute-start.18 = (bf16[128,1280]{1,0:T(8,128)(2,1)}, bf16[128,1280]{1,0:T(8,128)(2,1)S(1)}, u32[]{:S(2)}, u32[]{:S(2)}) collective-permute-start(bf16[128,1280]{1,0:T(8,128)(2,1)} %get-tuple-element.110), channel_id=1, source_target_pairs={{2,0},{6,4},{10,8},{14,12},{3,1},{7,5},{11,9},{15,13},{18,16},{22,... | collective-permute-start | bytes 983048 | tf_op jit(solution)/shard_map/ppermute | solution.py:496
  62.4 21.4 %collective-permute-start.19 = (bf16[128,1280]{1,0:T(8,128)(2,1)}, bf16[128,1280]{1,0:T(8,128)(2,1)S(1)}, u32[]{:S(2)}, u32[]{:S(2)}) collective-permute-start(bf16[128,1280]{1,0:T(8,128)(2,1)} %get-tuple-element.110), channel_id=1, source_target_pairs={{2,4},{6,0},{10,12},{14,8},{3,5},{7,1},{11,13},{15,9},{18,20},{22,... | collective-permute-start | bytes 983048 | tf_op jit(solution)/shard_map/ppermute | solution.py:496
  65.7 13.3 %collective-permute-start.21 = (bf16[128,320]{1,0:T(8,128)(2,1)}, bf16[128,320]{1,0:T(8,128)(2,1)S(1)}, u32[]{:S(2)}, u32[]{:S(2)}) collective-permute-start(bf16[128,320]{1,0:T(8,128)(2,1)} %get-tuple-element.154), channel_id=1, source_target_pairs={{0,4},{4,8},{8,12},{12,0},{1,5},{5,9},{9,13},{13,1},{2,6},{6,10},{... | collective-permute-start | bytes 245768 | tf_op jit(solution)/shard_map/ppermute | solution.py:496
  67.8 11.3 %collective-permute-start.22 = (bf16[128,320]{1,0:T(8,128)(2,1)}, bf16[128,320]{1,0:T(8,128)(2,1)S(1)}, u32[]{:S(2)}, u32[]{:S(2)}) collective-permute-start(bf16[128,320]{1,0:T(8,128)(2,1)} %get-tuple-element.153), channel_id=1, source_target_pairs={{0,8},{4,12},{8,0},{12,4},{1,9},{5,13},{9,1},{13,5},{2,10},{6,14},... | collective-permute-start | bytes 245768 | tf_op jit(solution)/shard_map/ppermute | solution.py:496
  70.7 1.3 %collective-permute-start.20 = (bf16[128,256]{1,0:T(8,128)(2,1)}, bf16[128,256]{1,0:T(8,128)(2,1)S(1)}, u32[]{:S(2)}, u32[]{:S(2)}) collective-permute-start(bf16[128,256]{1,0:T(8,128)(2,1)} %get-tuple-element.111.found), channel_id=1, source_target_pairs={{2,6},{6,2},{10,14},{14,10},{3,7},{7,3},{11,15},{15,11},{18,22},{2... | collective-permute-start | bytes 196616 | tf_op jit(solution)/shard_map/ppermute | solution.py:496
  72.0 7.0 %collective-permute-start.23 = (bf16[128,320]{1,0:T(8,128)(2,1)}, bf16[128,320]{1,0:T(8,128)(2,1)S(1)}, u32[]{:S(2)}, u32[]{:S(2)}) collective-permute-start(bf16[128,320]{1,0:T(8,128)(2,1)} %get-tuple-element.152), channel_id=1, source_target_pairs={{0,12},{4,0},{8,4},{12,8},{1,13},{5,1},{9,5},{13,9},{2,14},{6,2},{... | collective-permute-start | bytes 245768 | tf_op jit(solution)/shard_map/ppermute | solution.py:496
  85.6 4.0 %collective-permute-start.24 = (bf16[256,1280]{1,0:T(8,128)(2,1)S(1)}, bf16[256,1280]{1,0:T(8,128)(2,1)S(1)}, u32[]{:S(2)}, u32[]{:S(2)}) collective-permute-start(bf16[256,1280]{1,0:T(8,128)(2,1)S(1)} %get-tuple-element.124.refs_0_), channel_id=1, source_target_pairs={{0,1},{1,0},{4,5},{5,4},{8,9},{9,8},{12,13},{13,12},{16,17},{17,16... | collective-permute-start | bytes 1966088 | tf_op jit(solution)/shard_map/ppermute | solution.py:496
  89.6 14.8 %copy-start.3 = (bf16[1,1280,512]{2,1,0:T(8,128)(2,1)S(1)}, bf16[1,1280,512]{2,1,0:T(8,128)(2,1)}, u32[]{:S(2)}) copy-start(bf16[1,1280,512]{2,1,0:T(8,128)(2,1)} %param.13) | copy-start | bytes 3932164
  93.7 6.9 %collective-permute-start.25 = (bf16[272,128]{1,0:T(8,128)(2,1)S(1)}, bf16[272,128]{1,0:T(8,128)(2,1)S(1)}, u32[]{:S(2)}, u32[]{:S(2)}) collective-permute-start(bf16[272,128]{1,0:T(8,128)(2,1)S(1)} %shard_map.90.refs_0_), channel_id=1, source_target_pairs={{0,4},{4,8},{8,12},{12,0},{1,5},{5,9},{9,13},{13,1},{2,6},{6,10},{... | collective-permute-start | bytes 208904 | tf_op jit(solution)/shard_map/ppermute | solution.py:496
  94.7 8.1 %collective-permute-start.26 = (bf16[272,128]{1,0:T(8,128)(2,1)S(1)}, bf16[272,128]{1,0:T(8,128)(2,1)S(1)}, u32[]{:S(2)}, u32[]{:S(2)}) collective-permute-start(bf16[272,128]{1,0:T(8,128)(2,1)S(1)} %shard_map.90.refs_0_), channel_id=1, source_target_pairs={{0,8},{4,12},{8,0},{12,4},{1,9},{5,13},{9,1},{13,5},{2,10},{6,14},... | collective-permute-start | bytes 208904 | tf_op jit(solution)/shard_map/ppermute | solution.py:496
  95.0 7.8 %collective-permute-start.27 = (bf16[272,128]{1,0:T(8,128)(2,1)S(1)}, bf16[272,128]{1,0:T(8,128)(2,1)S(1)}, u32[]{:S(2)}, u32[]{:S(2)}) collective-permute-start(bf16[272,128]{1,0:T(8,128)(2,1)S(1)} %shard_map.90.refs_0_), channel_id=1, source_target_pairs={{0,12},{4,0},{8,4},{12,8},{1,13},{5,1},{9,5},{13,9},{2,14},{6,2},{... | collective-permute-start | bytes 208904 | tf_op jit(solution)/shard_map/ppermute | solution.py:496
  102.8 1.6 %collective-permute-start.28 = (bf16[1088,128]{1,0:T(8,128)(2,1)S(1)}, bf16[1088,128]{1,0:T(8,128)(2,1)S(1)}, u32[]{:S(2)}, u32[]{:S(2)}) collective-permute-start(bf16[1088,128]{1,0:T(8,128)(2,1)S(1)} %pad_maximum_fusion.1), channel_id=1, source_target_pairs={{0,1},{1,0},{2,3},{3,2},{4,5},{5,4},{6,7},{7,6},{8,9},{9,8},{10,11... | collective-permute-start | bytes 835592 | tf_op jit(solution)/shard_map/ppermute | solution.py:496

commit v8 on v7

--- a/solution.py
+++ b/solution.py
@@ -419,12 +419,14 @@
 def heat_of(own, other, place, count):
     partner = lax.rem(2 * place[4] - 1 + count, count)
     size = own[0].shape[0]
-    heat = 0.0
+    sums = []
     for source in (own, [other[k * size : (k + 1) * size] for k in range(count)]):
         rows = [source[k][size - 16 :].astype(F32) for k in range(count)]
-        heat += rows[0][0:1] + rows[0][1:2]
-        for k in {1 % count, count - 1}:
+        heat = rows[0][0:1] + rows[0][1:2]
+        for k in sorted({1 % count, count - 1}):
             heat += jnp.where(partner == k, rows[k][2:3] + rows[k][3:4], 0.0)
+        sums.append(heat)
+    heat = sums[0] + sums[1]
     return heat / DW
 
 

time: 107 us -> 107 us (level)
  no operation moved by 1% of the time
where the time goes in v8:
time: 107 us; the launch traced here: 106 us
  starting transfers between devices  51 us (48%)
  waiting for transfers between devices  32.9 us (31%)
  Pallas kernels  11.2 us (10%)
  local copies, waits for them, and re-layouts  6.97 us (7%)
  between operations  1.46 us (1%)
  other arithmetic  1.43 us (1%)
    ppermute x20, starting transfers between devices, moved(): return lax.ppermute(shard, axes, pairs)  51 us
    ppermute x20, waiting for transfers between devices, moved(): return lax.ppermute(shard, axes, pairs)  32.9 us
    dynamic_slice x4, local copies, waits for them, and re-layouts, part_of(): return lax.dynamic_slice_in_dim(array, index * width, width, axis)  4.5 us
    pallas_call x1, Pallas kernels, main_step(): return call(place, *operands)  4.03 us
  transfers between devices with their start and end apart: 20, of which 9 were waited for; matrix products, arithmetic and copies ran while one was open for 5% of the time, Pallas kernels for 3%

profile of v8, /device:TPU:0, one launch (start us, length us, event | category | flops | bytes accessed | tf_op | source)
XLA Modules:
  0.0 106.3 jit_solution(13977057307888430415)
XLA Ops:
  0.7 60.3 %conditional.1 = (f32[128,256]{1,0:T(8,128)S(1)}, bf16[128,256]{1,0:T(8,128)(2,1)}, bf16[128,1280]{1,0:T(8,128)(2,1)}, bf16[320,640]{1,0:T(8,128)(2,1)}, bf16[32...) conditional(s32[]{:T(128)} %convert_element_type.60, ...), branch_computations={%region_0.0_spmd, %region_1.2_spmd} | conditional | flops 1430559104 | bytes 38794944 | solution.py:682
  0.7 2.4 %constant_dynamic-slice_fusion.4 = (bf16[320,640]{1,0:T(8,128)(2,1)}, bf16[320,640]{1,0:T(8,128)(2,1)}, bf16[320,640]{1,0:T(8,128)(2,1)}) fusion(bf16[1280,640]{1,0:T(8,128)(2,1)} %get-tuple-element.44, s32[]{:T(128)S(6)} %select_n.51, s32[]{:T(128)S(6)} %select_n.50, s32[]{:T(128)S(6)} %select_n.49), kind=kLoop, calls=%fused_computation.19 | loop fusion | bytes 2457612 | tf_op jit(solution)/shard_map/cond/branch_0_fun/dynamic_slice | solution.py:523
  3.2 5.1 %collective-permute-start.1 = (bf16[320,640]{1,0:T(8,128)(2,1)}, bf16[320,640]{1,0:T(8,128)(2,1)}, u32[]{:S(2)}, u32[]{:S(2)}) collective-permute-start(bf16[320,640]{1,0:T(8,128)(2,1)} %get-tuple-element.141), channel_id=1, source_target_pairs={{0,4},{4,8},{8,12},{12,0},{1,5},{5,9},{9,13},{13,1},{16,20},{20,24... | collective-permute-start | bytes 1228808 | tf_op jit(solution)/shard_map/cond/branch_0_fun/ppermute | solution.py:498
  8.2 3.9 %collective-permute-start.3 = (bf16[320,640]{1,0:T(8,128)(2,1)}, bf16[320,640]{1,0:T(8,128)(2,1)}, u32[]{:S(2)}, u32[]{:S(2)}) collective-permute-start(bf16[320,640]{1,0:T(8,128)(2,1)} %get-tuple-element.139), channel_id=1, source_target_pairs={{0,12},{4,0},{8,4},{12,8},{1,13},{5,1},{9,5},{13,9},{16,28},{20,16... | collective-permute-start | bytes 1228808 | tf_op jit(solution)/shard_map/cond/branch_0_fun/ppermute | solution.py:498
  12.2 2.9 %collective-permute-start.2 = (bf16[320,640]{1,0:T(8,128)(2,1)}, bf16[320,640]{1,0:T(8,128)(2,1)}, u32[]{:S(2)}, u32[]{:S(2)}) collective-permute-start(bf16[320,640]{1,0:T(8,128)(2,1)} %get-tuple-element.140), channel_id=1, source_target_pairs={{0,8},{4,12},{8,0},{12,4},{1,9},{5,13},{9,1},{13,5},{16,24},{20,28... | collective-permute-start | bytes 1228808 | tf_op jit(solution)/shard_map/cond/branch_0_fun/ppermute | solution.py:498
  15.1 0.3 fusion.12
  15.5 1.9 %collective-permute-start = (bf16[128,256]{1,0:T(8,128)(2,1)S(1)}, bf16[128,256]{1,0:T(8,128)(2,1)S(1)}, u32[]{:S(2)}, u32[]{:S(2)}) collective-permute-start(bf16[128,256]{1,0:T(8,128)(2,1)S(1)} %dynamic-slice_convert_fusion), channel_id=1, source_target_pairs={{0,1},{1,0},{4,5},{5,4},{8,9},{9,8},{12,13},{13,12},{16,17},{17,16... | collective-permute-start | bytes 196616 | tf_op jit(solution)/shard_map/cond/branch_0_fun/ppermute | solution.py:498
  17.4 0.3 branch_0_fun.1
  17.8 3.5 %collective-permute-start.8 = (bf16[128,1280]{1,0:T(8,128)(2,1)S(1)}, bf16[128,1280]{1,0:T(8,128)(2,1)}, u32[]{:S(2)}, u32[]{:S(2)}) collective-permute-start(bf16[128,1280]{1,0:T(8,128)(2,1)S(1)} %branch_0_fun.1), channel_id=1, source_target_pairs={{0,4},{4,0},{8,12},{12,8},{1,5},{5,1},{9,13},{13,9},{16,20},{20,16... | collective-permute-start | bytes 983048 | tf_op jit(solution)/shard_map/cond/branch_0_fun/ppermute | solution.py:498
  22.1 3.4 %collective-permute-start.4 = (bf16[320,640]{1,0:T(8,128)(2,1)}, bf16[320,640]{1,0:T(8,128)(2,1)}, u32[]{:S(2)}, u32[]{:S(2)}) collective-permute-start(bf16[320,640]{1,0:T(8,128)(2,1)} %collective-permute-done.1), channel_id=1, source_target_pairs={{0,16},{16,0},{1,17},{17,1},{4,20},{20,4},{5,21},{21,5},{8,24},{24... | collective-permute-start | bytes 1228808 | tf_op jit(solution)/shard_map/cond/branch_0_fun/ppermute | solution.py:498
  25.5 3.4 %collective-permute-done.3 = bf16[320,640]{1,0:T(8,128)(2,1)} collective-permute-done((bf16[320,640]{1,0:T(8,128)(2,1)}, bf16[320,640]{1,0:T(8,128)(2,1)}, u32[]{:S(2)}, u32[]{:S(2)}) %collective-permute-start.3) | collective-permute-done | bytes 409632 | tf_op jit(solution)/shard_map/cond/branch_0_fun/ppermute | solution.py:498
  28.9 3.4 %collective-permute-start.6 = (bf16[320,640]{1,0:T(8,128)(2,1)}, bf16[320,640]{1,0:T(8,128)(2,1)}, u32[]{:S(2)}, u32[]{:S(2)}) collective-permute-start(bf16[320,640]{1,0:T(8,128)(2,1)} %collective-permute-done.3), channel_id=1, source_target_pairs={{0,16},{16,0},{1,17},{17,1},{4,20},{20,4},{5,21},{21,5},{8,24},{24... | collective-permute-start | bytes 1228808 | tf_op jit(solution)/shard_map/cond/branch_0_fun/ppermute | solution.py:498
  32.3 14.0 %collective-permute-done.2 = bf16[320,640]{1,0:T(8,128)(2,1)} collective-permute-done((bf16[320,640]{1,0:T(8,128)(2,1)}, bf16[320,640]{1,0:T(8,128)(2,1)}, u32[]{:S(2)}, u32[]{:S(2)}) %collective-permute-start.2) | collective-permute-done | bytes 409632 | tf_op jit(solution)/shard_map/cond/branch_0_fun/ppermute | solution.py:498
  46.3 3.4 %collective-permute-start.5 = (bf16[320,640]{1,0:T(8,128)(2,1)}, bf16[320,640]{1,0:T(8,128)(2,1)}, u32[]{:S(2)}, u32[]{:S(2)}) collective-permute-start(bf16[320,640]{1,0:T(8,128)(2,1)} %collective-permute-done.2), channel_id=1, source_target_pairs={{0,16},{16,0},{1,17},{17,1},{4,20},{20,4},{5,21},{21,5},{8,24},{24... | collective-permute-start | bytes 1228808 | tf_op jit(solution)/shard_map/cond/branch_0_fun/ppermute | solution.py:498
  49.8 6.3 %collective-permute-start.7 = (bf16[136,896]{1,0:T(8,128)(2,1)S(1)}, bf16[136,896]{1,0:T(8,128)(2,1)S(1)}, u32[]{:S(2)}, u32[]{:S(2)}) collective-permute-start(bf16[136,896]{1,0:T(8,128)(2,1)S(1)} %fusion.9), channel_id=1, source_target_pairs={{0,4},{4,0},{8,12},{12,8},{1,5},{5,1},{9,13},{13,9},{16,20},{20,16... | collective-permute-start | bytes 731144 | tf_op jit(solution)/shard_map/cond/branch_0_fun/ppermute | solution.py:498
  56.2 0.7 broadcast_in_dim.28
  56.9 0.6 broadcast_in_dim.14
  57.6 2.3 %collective-permute-done.5 = bf16[320,640]{1,0:T(8,128)(2,1)} collective-permute-done((bf16[320,640]{1,0:T(8,128)(2,1)}, bf16[320,640]{1,0:T(8,128)(2,1)}, u32[]{:S(2)}, u32[]{:S(2)}) %collective-permute-start.5) | collective-permute-done | bytes 409632 | tf_op jit(solution)/shard_map/cond/branch_0_fun/ppermute | solution.py:498
  59.9 0.4 collective-permute-done.7
  60.3 0.7 copy-done.14
  61.0 1.4 %collective-permute-start.18 = (bf16[128,1280]{1,0:T(8,128)(2,1)}, bf16[128,1280]{1,0:T(8,128)(2,1)S(1)}, u32[]{:S(2)}, u32[]{:S(2)}) collective-permute-start(bf16[128,1280]{1,0:T(8,128)(2,1)} %get-tuple-element.110), channel_id=1, source_target_pairs={{2,0},{6,4},{10,8},{14,12},{3,1},{7,5},{11,9},{15,13},{18,16},{22,... | collective-permute-start | bytes 983048 | tf_op jit(solution)/shard_map/ppermute | solution.py:498
  62.4 1.3 %collective-permute-start.19 = (bf16[128,1280]{1,0:T(8,128)(2,1)}, bf16[128,1280]{1,0:T(8,128)(2,1)S(1)}, u32[]{:S(2)}, u32[]{:S(2)}) collective-permute-start(bf16[128,1280]{1,0:T(8,128)(2,1)} %get-tuple-element.110), channel_id=1, source_target_pairs={{2,4},{6,0},{10,12},{14,8},{3,5},{7,1},{11,13},{15,9},{18,20},{22,... | collective-permute-start | bytes 983048 | tf_op jit(solution)/shard_map/ppermute | solution.py:498
  63.7 2.0 %constant_dynamic-slice_fusion.11 = (bf16[128,320]{1,0:T(8,128)(2,1)}, bf16[128,320]{1,0:T(8,128)(2,1)}, bf16[128,320]{1,0:T(8,128)(2,1)}, bf16[128,320]{1,0:T(8,128)(2,1)S(1)}) fusion(bf16[128,1280]{1,0:T(8,128)(2,1)} %bitcast.31, s32[]{:T(128)S(6)} %select_n.72, s32[]{:T(128)S(6)} %select_n.71, s32[]{:T(128)S(6)} %select_n.70, s32[]{:T(128)S(6)} %select_n.69), kind=kLoop, calls=%fused_computation.37 | loop fusion | bytes 655376 | tf_op jit(solution)/shard_map/dynamic_slice | solution.py:523
  65.7 2.0 %collective-permute-start.21 = (bf16[128,320]{1,0:T(8,128)(2,1)}, bf16[128,320]{1,0:T(8,128)(2,1)S(1)}, u32[]{:S(2)}, u32[]{:S(2)}) collective-permute-start(bf16[128,320]{1,0:T(8,128)(2,1)} %get-tuple-element.154), channel_id=1, source_target_pairs={{0,4},{4,8},{8,12},{12,0},{1,5},{5,9},{9,13},{13,1},{2,6},{6,10},{... | collective-permute-start | bytes 245768 | tf_op jit(solution)/shard_map/ppermute | solution.py:498
  67.8 2.9 %collective-permute-start.22 = (bf16[128,320]{1,0:T(8,128)(2,1)}, bf16[128,320]{1,0:T(8,128)(2,1)S(1)}, u32[]{:S(2)}, u32[]{:S(2)}) collective-permute-start(bf16[128,320]{1,0:T(8,128)(2,1)} %get-tuple-element.153), channel_id=1, source_target_pairs={{0,8},{4,12},{8,0},{12,4},{1,9},{5,13},{9,1},{13,5},{2,10},{6,14},... | collective-permute-start | bytes 245768 | tf_op jit(solution)/shard_map/ppermute | solution.py:498
  70.7 0.7 collective-permute-start.20
  72.0 3.0 %collective-permute-start.23 = (bf16[128,320]{1,0:T(8,128)(2,1)}, bf16[128,320]{1,0:T(8,128)(2,1)S(1)}, u32[]{:S(2)}, u32[]{:S(2)}) collective-permute-start(bf16[128,320]{1,0:T(8,128)(2,1)} %get-tuple-element.152), channel_id=1, source_target_pairs={{0,12},{4,0},{8,4},{12,8},{1,13},{5,1},{9,5},{13,9},{2,14},{6,2},{... | collective-permute-start | bytes 245768 | tf_op jit(solution)/shard_map/ppermute | solution.py:498
  75.0 1.3 %fusion.10 = f32[128]{0:T(128)S(1)} fusion(f32[128]{0:T(128)S(1)} %compare_convert_fusion, bf16[1,1,128,1280]{3,2,1,0:T(8,128)(2,1)} %param.10, bf16[1,1,128,1280]{3,2,1,0:T(8,128)(2,1)S(1)} %copy-done), kind=kLoop, calls=%fused_computation.32 | loop fusion | flops 2129792 | bytes 656384 | tf_op jit(solution)/shard_map/reduce_sum | solution.py:705
  76.3 0.1 stack.71.place
  76.4 0.1 stack.66.place
  76.5 0.1 stack.68.place
  76.6 1.6 %shard_map.88 = (bf16[2,5,128,128]{3,2,1,0:T(8,128)(2,1)S(1)}, f32[640,256]{1,0:T(8,128)S(1)}, f32[256,128]{1,0:T(8,128)S(1)}, f32[256,128]{1,0:T(8,128)S(1)}) custom-call(s32[5]{0:T(128)S(1)} %stack.71.place, bf16[136,896]{1,0:T(8,128)(2,1)S(1)} %get-tuple-element.114.kept, bf16[136,896]{1,0:T(8,128)(2,1)S(1)} %copy-done.15), custom_call_target="tpu_custom_call" | custom-call | flops 100000000 | bytes 3000000 | tf_op jit(solution)/shard_map/pallas_call | solution.py:268
  78.1 0.9 shard_map.86.refs_3_
  79.0 0.7 shard_map.87.inputs_t
  79.8 4.0 %collective-permute-done.18.current = bf16[128,1280]{1,0:T(8,128)(2,1)S(1)} collective-permute-done((bf16[128,1280]{1,0:T(8,128)(2,1)}, bf16[128,1280]{1,0:T(8,128)(2,1)S(1)}, u32[]{:S(2)}, u32[]{:S(2)}) %collective-permute-start.18) | collective-permute-done | bytes 327712 | tf_op jit(solution)/shard_map/ppermute | solution.py:498
  83.8 1.8 %shard_map.89 = (bf16[256,1280]{1,0:T(8,128)(2,1)S(1)}, f32[1,128]{1,0:T(1,128)S(1)}) custom-call(bf16[128,1280]{1,0:T(8,128)(2,1)S(1)} %bitcast.32, bf16[128,1280]{1,0:T(8,128)(2,1)} %bitcast.38, bf16[128,1280]{1,0:T(8,128)(2,1)} %get-tuple-element.121.gain, bf16[128,1280]{1,0:T(8,128)(2,1)S(1)} %collective-permute-done.18.current, ...), custom_call_target="tpu_custom_call" | custom-call | flops 10000000 | bytes 2000000 | tf_op jit(solution)/shard_map/pallas_call | solution.py:200
  85.6 1.9 %collective-permute-start.24 = (bf16[256,1280]{1,0:T(8,128)(2,1)S(1)}, bf16[256,1280]{1,0:T(8,128)(2,1)S(1)}, u32[]{:S(2)}, u32[]{:S(2)}) collective-permute-start(bf16[256,1280]{1,0:T(8,128)(2,1)S(1)} %get-tuple-element.124.refs_0_), channel_id=1, source_target_pairs={{0,1},{1,0},{4,5},{5,4},{8,9},{9,8},{12,13},{13,12},{16,17},{17,16... | collective-permute-start | bytes 1966088 | tf_op jit(solution)/shard_map/ppermute | solution.py:498
  87.6 0.1 stack.74.place
  87.6 2.0 %collective-permute-done.24.refs_1_ = bf16[256,1280]{1,0:T(8,128)(2,1)S(1)} collective-permute-done((bf16[256,1280]{1,0:T(8,128)(2,1)S(1)}, bf16[256,1280]{1,0:T(8,128)(2,1)S(1)}, u32[]{:S(2)}, u32[]{:S(2)}) %collective-permute-start.24) | collective-permute-done | bytes 655392 | tf_op jit(solution)/shard_map/ppermute | solution.py:498
  89.6 4.0 %shard_map.90.refs_0_ = bf16[272,128]{1,0:T(8,128)(2,1)S(1)} custom-call(s32[5]{0:T(128)S(1)} %stack.74.place, bf16[256,1280]{1,0:T(8,128)(2,1)S(1)} %get-tuple-element.124.refs_0_, bf16[256,1280]{1,0:T(8,128)(2,1)S(1)} %collective-permute-done.24.refs_1_, bf16[1280,640]{1,0:T(8,128)(2,1)} %bitcast.41, bf16[272,128]{1,0:T(8,128)(2,1)S(1)} %shard_map.86.refs_3_, ...), custom_call_target="tpu_custom_call" | custom-call | flops 1000000000 | bytes 6000000 | tf_op jit(solution)/shard_map/pallas_call | solution.py:371
  93.7 1.1 %collective-permute-start.25 = (bf16[272,128]{1,0:T(8,128)(2,1)S(1)}, bf16[272,128]{1,0:T(8,128)(2,1)S(1)}, u32[]{:S(2)}, u32[]{:S(2)}) collective-permute-start(bf16[272,128]{1,0:T(8,128)(2,1)S(1)} %shard_map.90.refs_0_), channel_id=1, source_target_pairs={{0,4},{4,8},{8,12},{12,0},{1,5},{5,9},{9,13},{13,1},{2,6},{6,10},{... | collective-permute-start | bytes 208904 | tf_op jit(solution)/shard_map/ppermute | solution.py:498
  94.7 0.3 collective-permute-start.26
  95.0 2.5 %collective-permute-start.27 = (bf16[272,128]{1,0:T(8,128)(2,1)S(1)}, bf16[272,128]{1,0:T(8,128)(2,1)S(1)}, u32[]{:S(2)}, u32[]{:S(2)}) collective-permute-start(bf16[272,128]{1,0:T(8,128)(2,1)S(1)} %shard_map.90.refs_0_), channel_id=1, source_target_pairs={{0,12},{4,0},{8,4},{12,8},{1,13},{5,1},{9,5},{13,9},{2,14},{6,2},{... | collective-permute-start | bytes 208904 | tf_op jit(solution)/shard_map/ppermute | solution.py:498
  97.5 3.0 %collective-permute-done.25.refs_1_ = bf16[272,128]{1,0:T(8,128)(2,1)S(1)} collective-permute-done((bf16[272,128]{1,0:T(8,128)(2,1)S(1)}, bf16[272,128]{1,0:T(8,128)(2,1)S(1)}, u32[]{:S(2)}, u32[]{:S(2)}) %collective-permute-start.25) | collective-permute-done | bytes 69664 | tf_op jit(solution)/shard_map/ppermute | solution.py:498
  100.6 2.2 %collective-permute-done.26.refs_2_ = bf16[272,128]{1,0:T(8,128)(2,1)S(1)} collective-permute-done((bf16[272,128]{1,0:T(8,128)(2,1)S(1)}, bf16[272,128]{1,0:T(8,128)(2,1)S(1)}, u32[]{:S(2)}, u32[]{:S(2)}) %collective-permute-start.26) | collective-permute-done | bytes 69664 | tf_op jit(solution)/shard_map/ppermute | solution.py:498
  102.8 0.1 collective-permute-start.28
  102.9 1.5 %collective-permute-done.28.refs_4_ = bf16[1088,128]{1,0:T(8,128)(2,1)S(1)} collective-permute-done((bf16[1088,128]{1,0:T(8,128)(2,1)S(1)}, bf16[1088,128]{1,0:T(8,128)(2,1)S(1)}, u32[]{:S(2)}, u32[]{:S(2)}) %collective-permute-start.28) | collective-permute-done | bytes 278560 | tf_op jit(solution)/shard_map/ppermute | solution.py:498
  104.5 1.8 %shard_map.91 = (f32[320,512]{1,0:T(8,128)}, f32[1,128]{1,0:T(1,128)}) custom-call(s32[5]{0:T(128)S(1)} %stack.66.place, bf16[320,512]{1,0:T(8,128)(2,1)S(1)} %shard_map.87.inputs_t, bf16[1280,512]{1,0:T(8,128)(2,1)S(1)} %bitcast.35, bf16[272,128]{1,0:T(8,128)(2,1)S(1)} %shard_map.90.refs_0_, bf16[272,128]{1,0:T(8,128)(2,1)S(1)} %collective-permute-done.25.refs_1_, ...), custom_call_target="tpu_custom_call" | custom-call | flops 200000000 | bytes 2000000 | tf_op jit(solution)/shard_map/pallas_call | solution.py:464
  (37 shorter events, 0.3 us)
Async XLA Ops:
  0.6 74.3 %copy-start = (bf16[1,1,128,1280]{3,2,1,0:T(8,128)(2,1)S(1)}, bf16[1,1,128,1280]{3,2,1,0:T(8,128)(2,1)}, u32[]{:S(2)}) copy-start(bf16[1,1,128,1280]{3,2,1,0:T(8,128)(2,1)} %param.9) | copy-start | bytes 983044
  0.7 14.4 %copy-start.1 = (bf16[128,1280]{1,0:T(8,128)(2,1)S(1)}, bf16[128,1280]{1,0:T(8,128)(2,1)}, u32[]{:S(2)}) copy-start(bf16[128,1280]{1,0:T(8,128)(2,1)} %get-tuple-element.38.inputs) | copy-start | bytes 983044 | tf_op jit(solution)/shard_map/cond
  0.7 14.4 %copy-start.4 = (bf16[1280,512]{1,0:T(8,128)(2,1)S(1)}, bf16[1280,512]{1,0:T(8,128)(2,1)}, u32[]{:S(2)}) copy-start(bf16[1280,512]{1,0:T(8,128)(2,1)} %get-tuple-element.39) | copy-start | bytes 3932164 | tf_op jit(solution)/shard_map/cond
  3.1 14.3 %copy-start.6 = (bf16[128,1280]{1,0:T(8,128)(2,1)S(1)}, bf16[128,1280]{1,0:T(8,128)(2,1)}, u32[]{:S(2)}) copy-start(bf16[128,1280]{1,0:T(8,128)(2,1)} %get-tuple-element.51.branch) | copy-start | bytes 983044 | tf_op jit(solution)/shard_map/cond
  3.2 18.9 %collective-permute-start.1 = (bf16[320,640]{1,0:T(8,128)(2,1)}, bf16[320,640]{1,0:T(8,128)(2,1)}, u32[]{:S(2)}, u32[]{:S(2)}) collective-permute-start(bf16[320,640]{1,0:T(8,128)(2,1)} %get-tuple-element.141), channel_id=1, source_target_pairs={{0,4},{4,8},{8,12},{12,0},{1,5},{5,9},{9,13},{13,1},{16,20},{20,24... | collective-permute-start | bytes 1228808 | tf_op jit(solution)/shard_map/cond/branch_0_fun/ppermute | solution.py:498
  8.2 20.7 %collective-permute-start.3 = (bf16[320,640]{1,0:T(8,128)(2,1)}, bf16[320,640]{1,0:T(8,128)(2,1)}, u32[]{:S(2)}, u32[]{:S(2)}) collective-permute-start(bf16[320,640]{1,0:T(8,128)(2,1)} %get-tuple-element.139), channel_id=1, source_target_pairs={{0,12},{4,0},{8,4},{12,8},{1,13},{5,1},{9,5},{13,9},{16,28},{20,16... | collective-permute-start | bytes 1228808 | tf_op jit(solution)/shard_map/cond/branch_0_fun/ppermute | solution.py:498
  12.2 34.2 %collective-permute-start.2 = (bf16[320,640]{1,0:T(8,128)(2,1)}, bf16[320,640]{1,0:T(8,128)(2,1)}, u32[]{:S(2)}, u32[]{:S(2)}) collective-permute-start(bf16[320,640]{1,0:T(8,128)(2,1)} %get-tuple-element.140), channel_id=1, source_target_pairs={{0,8},{4,12},{8,0},{12,4},{1,9},{5,13},{9,1},{13,5},{16,24},{20,28... | collective-permute-start | bytes 1228808 | tf_op jit(solution)/shard_map/cond/branch_0_fun/ppermute | solution.py:498
  15.1 6.8 %copy-start.10 = (bf16[128,1280]{1,0:T(8,128)(2,1)S(1)}, bf16[128,1280]{1,0:T(8,128)(2,1)}, u32[]{:S(2)}) copy-start(bf16[128,1280]{1,0:T(8,128)(2,1)} %get-tuple-element.47) | copy-start | bytes 983044 | tf_op jit(solution)/shard_map/cond
  15.5 6.6 %copy-start.12 = (bf16[128,256]{1,0:T(8,128)(2,1)S(1)}, bf16[128,256]{1,0:T(8,128)(2,1)}, u32[]{:S(2)}) copy-start(bf16[128,256]{1,0:T(8,128)(2,1)} %get-tuple-element.49) | copy-start | bytes 196612 | tf_op jit(solution)/shard_map/cond
  15.5 16.8 %collective-permute-start = (bf16[128,256]{1,0:T(8,128)(2,1)S(1)}, bf16[128,256]{1,0:T(8,128)(2,1)S(1)}, u32[]{:S(2)}, u32[]{:S(2)}) collective-permute-start(bf16[128,256]{1,0:T(8,128)(2,1)S(1)} %dynamic-slice_convert_fusion), channel_id=1, source_target_pairs={{0,1},{1,0},{4,5},{5,4},{8,9},{9,8},{12,13},{13,12},{16,17},{17,16... | collective-permute-start | bytes 196616 | tf_op jit(solution)/shard_map/cond/branch_0_fun/ppermute | solution.py:498
  17.8 39.8 %collective-permute-start.8 = (bf16[128,1280]{1,0:T(8,128)(2,1)S(1)}, bf16[128,1280]{1,0:T(8,128)(2,1)}, u32[]{:S(2)}, u32[]{:S(2)}) collective-permute-start(bf16[128,1280]{1,0:T(8,128)(2,1)S(1)} %branch_0_fun.1), channel_id=1, source_target_pairs={{0,4},{4,0},{8,12},{12,8},{1,5},{5,1},{9,13},{13,9},{16,20},{20,16... | collective-permute-start | bytes 983048 | tf_op jit(solution)/shard_map/cond/branch_0_fun/ppermute | solution.py:498
  22.1 27.8 %collective-permute-start.4 = (bf16[320,640]{1,0:T(8,128)(2,1)}, bf16[320,640]{1,0:T(8,128)(2,1)}, u32[]{:S(2)}, u32[]{:S(2)}) collective-permute-start(bf16[320,640]{1,0:T(8,128)(2,1)} %collective-permute-done.1), channel_id=1, source_target_pairs={{0,16},{16,0},{1,17},{17,1},{4,20},{20,4},{5,21},{21,5},{8,24},{24... | collective-permute-start | bytes 1228808 | tf_op jit(solution)/shard_map/cond/branch_0_fun/ppermute | solution.py:498
  28.9 21.0 %collective-permute-start.6 = (bf16[320,640]{1,0:T(8,128)(2,1)}, bf16[320,640]{1,0:T(8,128)(2,1)}, u32[]{:S(2)}, u32[]{:S(2)}) collective-permute-start(bf16[320,640]{1,0:T(8,128)(2,1)} %collective-permute-done.3), channel_id=1, source_target_pairs={{0,16},{16,0},{1,17},{17,1},{4,20},{20,4},{5,21},{21,5},{8,24},{24... | collective-permute-start | bytes 1228808 | tf_op jit(solution)/shard_map/cond/branch_0_fun/ppermute | solution.py:498
  46.3 13.6 %collective-permute-start.5 = (bf16[320,640]{1,0:T(8,128)(2,1)}, bf16[320,640]{1,0:T(8,128)(2,1)}, u32[]{:S(2)}, u32[]{:S(2)}) collective-permute-start(bf16[320,640]{1,0:T(8,128)(2,1)} %collective-permute-done.2), channel_id=1, source_target_pairs={{0,16},{16,0},{1,17},{17,1},{4,20},{20,4},{5,21},{21,5},{8,24},{24... | collective-permute-start | bytes 1228808 | tf_op jit(solution)/shard_map/cond/branch_0_fun/ppermute | solution.py:498
  49.8 10.5 %collective-permute-start.7 = (bf16[136,896]{1,0:T(8,128)(2,1)S(1)}, bf16[136,896]{1,0:T(8,128)(2,1)S(1)}, u32[]{:S(2)}, u32[]{:S(2)}) collective-permute-start(bf16[136,896]{1,0:T(8,128)(2,1)S(1)} %fusion.9), channel_id=1, source_target_pairs={{0,4},{4,0},{8,12},{12,8},{1,5},{5,1},{9,13},{13,9},{16,20},{20,16... | collective-permute-start | bytes 731144 | tf_op jit(solution)/shard_map/cond/branch_0_fun/ppermute | solution.py:498
  60.3 0.7 copy-start.14
  61.0 15.6 %copy-start.15 = (bf16[136,896]{1,0:T(8,128)(2,1)S(1)}, bf16[136,896]{1,0:T(8,128)(2,1)}, u32[]{:S(2)}) copy-start(bf16[136,896]{1,0:T(8,128)(2,1)} %get-tuple-element.115.got) | copy-start | bytes 731140
  61.0 22.8 %collective-permute-start.18 = (bf16[128,1280]{1,0:T(8,128)(2,1)}, bf16[128,1280]{1,0:T(8,128)(2,1)S(1)}, u32[]{:S(2)}, u32[]{:S(2)}) collective-permute-start(bf16[128,1280]{1,0:T(8,128)(2,1)} %get-tuple-element.110), channel_id=1, source_target_pairs={{2,0},{6,4},{10,8},{14,12},{3,1},{7,5},{11,9},{15,13},{18,16},{22,... | collective-permute-start | bytes 983048 | tf_op jit(solution)/shard_map/ppermute | solution.py:498
  62.4 21.4 %collective-permute-start.19 = (bf16[128,1280]{1,0:T(8,128)(2,1)}, bf16[128,1280]{1,0:T(8,128)(2,1)S(1)}, u32[]{:S(2)}, u32[]{:S(2)}) collective-permute-start(bf16[128,1280]{1,0:T(8,128)(2,1)} %get-tuple-element.110), channel_id=1, source_target_pairs={{2,4},{6,0},{10,12},{14,8},{3,5},{7,1},{11,13},{15,9},{18,20},{22,... | collective-permute-start | bytes 983048 | tf_op jit(solution)/shard_map/ppermute | solution.py:498
  65.7 13.3 %collective-permute-start.21 = (bf16[128,320]{1,0:T(8,128)(2,1)}, bf16[128,320]{1,0:T(8,128)(2,1)S(1)}, u32[]{:S(2)}, u32[]{:S(2)}) collective-permute-start(bf16[128,320]{1,0:T(8,128)(2,1)} %get-tuple-element.154), channel_id=1, source_target_pairs={{0,4},{4,8},{8,12},{12,0},{1,5},{5,9},{9,13},{13,1},{2,6},{6,10},{... | collective-permute-start | bytes 245768 | tf_op jit(solution)/shard_map/ppermute | solution.py:498
  67.8 11.3 %collective-permute-start.22 = (bf16[128,320]{1,0:T(8,128)(2,1)}, bf16[128,320]{1,0:T(8,128)(2,1)S(1)}, u32[]{:S(2)}, u32[]{:S(2)}) collective-permute-start(bf16[128,320]{1,0:T(8,128)(2,1)} %get-tuple-element.153), channel_id=1, source_target_pairs={{0,8},{4,12},{8,0},{12,4},{1,9},{5,13},{9,1},{13,5},{2,10},{6,14},... | collective-permute-start | bytes 245768 | tf_op jit(solution)/shard_map/ppermute | solution.py:498
  70.7 1.3 %collective-permute-start.20 = (bf16[128,256]{1,0:T(8,128)(2,1)}, bf16[128,256]{1,0:T(8,128)(2,1)S(1)}, u32[]{:S(2)}, u32[]{:S(2)}) collective-permute-start(bf16[128,256]{1,0:T(8,128)(2,1)} %get-tuple-element.111.found), channel_id=1, source_target_pairs={{2,6},{6,2},{10,14},{14,10},{3,7},{7,3},{11,15},{15,11},{18,22},{2... | collective-permute-start | bytes 196616 | tf_op jit(solution)/shard_map/ppermute | solution.py:498
  72.0 7.0 %collective-permute-start.23 = (bf16[128,320]{1,0:T(8,128)(2,1)}, bf16[128,320]{1,0:T(8,128)(2,1)S(1)}, u32[]{:S(2)}, u32[]{:S(2)}) collective-permute-start(bf16[128,320]{1,0:T(8,128)(2,1)} %get-tuple-element.152), channel_id=1, source_target_pairs={{0,12},{4,0},{8,4},{12,8},{1,13},{5,1},{9,5},{13,9},{2,14},{6,2},{... | collective-permute-start | bytes 245768 | tf_op jit(solution)/shard_map/ppermute | solution.py:498
  85.6 4.0 %collective-permute-start.24 = (bf16[256,1280]{1,0:T(8,128)(2,1)S(1)}, bf16[256,1280]{1,0:T(8,128)(2,1)S(1)}, u32[]{:S(2)}, u32[]{:S(2)}) collective-permute-start(bf16[256,1280]{1,0:T(8,128)(2,1)S(1)} %get-tuple-element.124.refs_0_), channel_id=1, source_target_pairs={{0,1},{1,0},{4,5},{5,4},{8,9},{9,8},{12,13},{13,12},{16,17},{17,16... | collective-permute-start | bytes 1966088 | tf_op jit(solution)/shard_map/ppermute | solution.py:498
  89.6 14.8 %copy-start.3 = (bf16[1,1280,512]{2,1,0:T(8,128)(2,1)S(1)}, bf16[1,1280,512]{2,1,0:T(8,128)(2,1)}, u32[]{:S(2)}) copy-start(bf16[1,1280,512]{2,1,0:T(8,128)(2,1)} %param.13) | copy-start | bytes 3932164
  93.7 6.9 %collective-permute-start.25 = (bf16[272,128]{1,0:T(8,128)(2,1)S(1)}, bf16[272,128]{1,0:T(8,128)(2,1)S(1)}, u32[]{:S(2)}, u32[]{:S(2)}) collective-permute-start(bf16[272,128]{1,0:T(8,128)(2,1)S(1)} %shard_map.90.refs_0_), channel_id=1, source_target_pairs={{0,4},{4,8},{8,12},{12,0},{1,5},{5,9},{9,13},{13,1},{2,6},{6,10},{... | collective-permute-start | bytes 208904 | tf_op jit(solution)/shard_map/ppermute | solution.py:498
  94.7 8.1 %collective-permute-start.26 = (bf16[272,128]{1,0:T(8,128)(2,1)S(1)}, bf16[272,128]{1,0:T(8,128)(2,1)S(1)}, u32[]{:S(2)}, u32[]{:S(2)}) collective-permute-start(bf16[272,128]{1,0:T(8,128)(2,1)S(1)} %shard_map.90.refs_0_), channel_id=1, source_target_pairs={{0,8},{4,12},{8,0},{12,4},{1,9},{5,13},{9,1},{13,5},{2,10},{6,14},... | collective-permute-start | bytes 208904 | tf_op jit(solution)/shard_map/ppermute | solution.py:498
  95.0 7.8 %collective-permute-start.27 = (bf16[272,128]{1,0:T(8,128)(2,1)S(1)}, bf16[272,128]{1,0:T(8,128)(2,1)S(1)}, u32[]{:S(2)}, u32[]{:S(2)}) collective-permute-start(bf16[272,128]{1,0:T(8,128)(2,1)S(1)} %shard_map.90.refs_0_), channel_id=1, source_target_pairs={{0,12},{4,0},{8,4},{12,8},{1,13},{5,1},{9,5},{13,9},{2,14},{6,2},{... | collective-permute-start | bytes 208904 | tf_op jit(solution)/shard_map/ppermute | solution.py:498
  102.8 1.6 %collective-permute-start.28 = (bf16[1088,128]{1,0:T(8,128)(2,1)S(1)}, bf16[1088,128]{1,0:T(8,128)(2,1)S(1)}, u32[]{:S(2)}, u32[]{:S(2)}) collective-permute-start(bf16[1088,128]{1,0:T(8,128)(2,1)S(1)} %pad_maximum_fusion.1), channel_id=1, source_target_pairs={{0,1},{1,0},{2,3},{3,2},{4,5},{5,4},{6,7},{7,6},{8,9},{9,8},{10,11... | collective-permute-start | bytes 835592 | tf_op jit(solution)/shard_map/ppermute | solution.py:498

commit v9 on v8

--- a/solution.py
+++ b/solution.py
@@ -178,26 +178,32 @@
     return kernel_call(gain_kernel, shape, [VMEM, VMEM], flops=10**7, nbytes=10**6)(inputs, branch)
 
 
-def pair_sensitivity_kernel(inputs, branch, gain, current, partner, sens, kept_sum):
-    seq_len = inputs.shape[0]
+def pair_sensitivity_kernel(own_gain, gain, current, partner, sens):
+    seq_len = current.shape[0]
+    sens[:seq_len] = (current[...].astype(F32) * own_gain[...].astype(F32)).astype(BF16)
+    sens[seq_len:] = (partner[...].astype(F32) * gain[...].astype(F32)).astype(BF16)
+
+
+def pair_sensitivity(own_gain, gain, current, partner):
+    seq_len, width = current.shape
+    shape = jax.ShapeDtypeStruct((2 * seq_len, width), BF16)
+    call = kernel_call(
+        pair_sensitivity_kernel, shape, [VMEM] * 4, flops=10**7, nbytes=2 * 10**6
+    )
+    return call(own_gain, gain, current, partner)
+
+
+def kept_kernel(inputs, branch, current, kept_sum):
     inputs_f = inputs[...].astype(F32)
-    branch_f = branch[...].astype(F32)
-    sens_total = current[...].astype(F32) / stabilize(inputs_f + branch_f)
-    sens[:seq_len] = (branch_f * sens_total / stabilize(branch_f)).astype(BF16)
-    sens[seq_len:] = (partner[...].astype(F32) * gain[...].astype(F32)).astype(BF16)
-    kept_sum[...] = by_token(inputs_f * sens_total)
-
-
-def pair_sensitivity(inputs, branch, gain, current, partner):
-    seq_len, width = inputs.shape
-    shapes = (
-        jax.ShapeDtypeStruct((2 * seq_len, width), BF16),
-        jax.ShapeDtypeStruct((1, seq_len), F32),
-    )
-    call = kernel_call(
-        pair_sensitivity_kernel, shapes, [VMEM] * 5, flops=10**7, nbytes=2 * 10**6
-    )
-    return call(inputs, branch, gain, current, partner)
+    totals = inputs_f + branch[...].astype(F32)
+    kept_sum[...] = by_token(inputs_f * (current[...].astype(F32) / stabilize(totals)))
+
+
+def sum_of_kept(inputs, branch, current):
+    shape = jax.ShapeDtypeStruct((1, inputs.shape[0]), F32)
+    return kernel_call(kept_kernel, shape, [VMEM] * 3, flops=10**5, nbytes=10**4)(
+        inputs, branch, current
+    )
 
 
 def outgoing_kernel(place, inputs, branch, sens_own, sens_other, value_rows, outgoing):
@@ -689,6 +695,7 @@
         along_dp(part_of(rows, lax.rem(dp_pos + k, peers), block_rows, 1), k) for k in range(peers)
     ]
     rest = pair_attend(place(~is_last), kept_half, got_half)
+    own_gain = branch_gain(inputs, branch)
     if in_tiles:
         inputs_t = turned_side_by_side(place(0), pieces)
     else:
@@ -709,12 +716,11 @@
         active = section_pos == sections - 1 - turn
         current = jnp.where(active, arrived, current)
         if turn == 1:
-            arrived, partner_arrived, sens_values, inputs_t, *rest = lax.optimization_barrier(
-                (arrived, partner_arrived, sens_values, inputs_t, *rest)
+            arrived, partner_arrived, inputs_t, own_gain, *rest = lax.optimization_barrier(
+                (arrived, partner_arrived, inputs_t, own_gain, *rest)
             )
-        sens_own, kept_sum = pair_sensitivity(
-            inputs, branch, partner_gain, arrived, partner_arrived
-        )
+        sens_own = pair_sensitivity(own_gain, partner_gain, arrived, partner_arrived)
+        kept_sum = sum_of_kept(inputs, branch, arrived)
         sens = [sens_own, early_core(sens_own)]
         step = main_step if in_tiles else main_plain
         sens_values = step(

time: 107 us -> 107 us (level)
  Pallas kernels: 11.2 us -> 12.7 us
    pallas_call x1 -> x2, Pallas kernels: 0.34 us -> 1.65 us  [branch_gain(): kernel_call(gain_kernel, shape, [VMEM, VMEM], flops=10 ** 7, nbytes=10 ** 6)]
  transfers between devices with their start and end apart: 20 -> 20, of which waited for: 9 -> 8; matrix products, arithmetic and copies ran while one was open for 5% -> 4% of each run, Pallas kernels for 3% -> 7%
where the time goes in v9:
time: 107 us; the launch traced here: 106 us
  starting transfers between devices  50.8 us (47%)
  waiting for transfers between devices  32.8 us (31%)
  Pallas kernels  12.7 us (12%)
  local copies, waits for them, and re-layouts  6.27 us (6%)
  between operations  1.59 us (1%)
    ppermute x20, starting transfers between devices, moved(): return lax.ppermute(shard, axes, pairs)  50.8 us
    ppermute x20, waiting for transfers between devices, moved(): return lax.ppermute(shard, axes, pairs)  32.8 us
    dynamic_slice x4, local copies, waits for them, and re-layouts, part_of(): return lax.dynamic_slice_in_dim(array, index * width, width, axis)  4.42 us
    pallas_call x1, Pallas kernels, main_step(): return call(place, *operands)  3.67 us
  transfers between devices with their start and end apart: 20, of which 8 were waited for; matrix products, arithmetic and copies ran while one was open for 4% of the time, Pallas kernels for 7%

profile of v9, /device:TPU:0, one launch (start us, length us, event | category | flops | bytes accessed | tf_op | source)
XLA Modules:
  0.0 105.8 jit_solution(2224414586689849718)
XLA Ops:
  0.7 59.5 %conditional.1 = (f32[128,256]{1,0:T(8,128)S(1)}, bf16[128,256]{1,0:T(8,128)(2,1)}, bf16[128,1280]{1,0:T(8,128)(2,1)}, bf16[320,640]{1,0:T(8,128)(2,1)}, bf16[32...) conditional(s32[]{:T(128)} %convert_element_type.60, ...), branch_computations={%region_0.0_spmd, %region_1.2_spmd} | conditional | flops 1430559104 | bytes 45348568 | solution.py:688
  0.7 2.4 %constant_dynamic-slice_fusion.4 = (bf16[320,640]{1,0:T(8,128)(2,1)}, bf16[320,640]{1,0:T(8,128)(2,1)}, bf16[320,640]{1,0:T(8,128)(2,1)}) fusion(bf16[1280,640]{1,0:T(8,128)(2,1)} %get-tuple-element.44, s32[]{:T(128)S(6)} %select_n.51, s32[]{:T(128)S(6)} %select_n.50, s32[]{:T(128)S(6)} %select_n.49), kind=kLoop, calls=%fused_computation.19 | loop fusion | bytes 2457612 | tf_op jit(solution)/shard_map/cond/branch_0_fun/dynamic_slice | solution.py:529
  3.1 5.1 %collective-permute-start.1 = (bf16[320,640]{1,0:T(8,128)(2,1)}, bf16[320,640]{1,0:T(8,128)(2,1)}, u32[]{:S(2)}, u32[]{:S(2)}) collective-permute-start(bf16[320,640]{1,0:T(8,128)(2,1)} %get-tuple-element.137), channel_id=1, source_target_pairs={{0,4},{4,8},{8,12},{12,0},{1,5},{5,9},{9,13},{13,1},{16,20},{20,24... | collective-permute-start | bytes 1228808 | tf_op jit(solution)/shard_map/cond/branch_0_fun/ppermute | solution.py:504
  8.2 3.9 %collective-permute-start.3 = (bf16[320,640]{1,0:T(8,128)(2,1)}, bf16[320,640]{1,0:T(8,128)(2,1)}, u32[]{:S(2)}, u32[]{:S(2)}) collective-permute-start(bf16[320,640]{1,0:T(8,128)(2,1)} %get-tuple-element.135), channel_id=1, source_target_pairs={{0,12},{4,0},{8,4},{12,8},{1,13},{5,1},{9,5},{13,9},{16,28},{20,16... | collective-permute-start | bytes 1228808 | tf_op jit(solution)/shard_map/cond/branch_0_fun/ppermute | solution.py:504
  12.2 2.9 %collective-permute-start.2 = (bf16[320,640]{1,0:T(8,128)(2,1)}, bf16[320,640]{1,0:T(8,128)(2,1)}, u32[]{:S(2)}, u32[]{:S(2)}) collective-permute-start(bf16[320,640]{1,0:T(8,128)(2,1)} %get-tuple-element.136), channel_id=1, source_target_pairs={{0,8},{4,12},{8,0},{12,4},{1,9},{5,13},{9,1},{13,5},{16,24},{20,28... | collective-permute-start | bytes 1228808 | tf_op jit(solution)/shard_map/cond/branch_0_fun/ppermute | solution.py:504
  15.1 0.3 fusion.12
  15.5 1.9 %collective-permute-start = (bf16[128,256]{1,0:T(8,128)(2,1)S(1)}, bf16[128,256]{1,0:T(8,128)(2,1)S(1)}, u32[]{:S(2)}, u32[]{:S(2)}) collective-permute-start(bf16[128,256]{1,0:T(8,128)(2,1)S(1)} %dynamic-slice_convert_fusion), channel_id=1, source_target_pairs={{0,1},{1,0},{4,5},{5,4},{8,9},{9,8},{12,13},{13,12},{16,17},{17,16... | collective-permute-start | bytes 196616 | tf_op jit(solution)/shard_map/cond/branch_0_fun/ppermute | solution.py:504
  17.4 0.3 branch_0_fun.1
  17.8 3.5 %collective-permute-start.8 = (bf16[128,1280]{1,0:T(8,128)(2,1)S(1)}, bf16[128,1280]{1,0:T(8,128)(2,1)S(1)}, u32[]{:S(2)}, u32[]{:S(2)}) collective-permute-start(bf16[128,1280]{1,0:T(8,128)(2,1)S(1)} %branch_0_fun.1), channel_id=1, source_target_pairs={{0,4},{4,0},{8,12},{12,8},{1,5},{5,1},{9,13},{13,9},{16,20},{20,16... | collective-permute-start | bytes 983048 | tf_op jit(solution)/shard_map/cond/branch_0_fun/ppermute | solution.py:504
  22.1 3.4 %collective-permute-start.4 = (bf16[320,640]{1,0:T(8,128)(2,1)}, bf16[320,640]{1,0:T(8,128)(2,1)S(1)}, u32[]{:S(2)}, u32[]{:S(2)}) collective-permute-start(bf16[320,640]{1,0:T(8,128)(2,1)} %collective-permute-done.1), channel_id=1, source_target_pairs={{0,16},{16,0},{1,17},{17,1},{4,20},{20,4},{5,21},{21,5},{8,24},{24... | collective-permute-start | bytes 1228808 | tf_op jit(solution)/shard_map/cond/branch_0_fun/ppermute | solution.py:504
  25.5 3.4 %collective-permute-done.3 = bf16[320,640]{1,0:T(8,128)(2,1)} collective-permute-done((bf16[320,640]{1,0:T(8,128)(2,1)}, bf16[320,640]{1,0:T(8,128)(2,1)}, u32[]{:S(2)}, u32[]{:S(2)}) %collective-permute-start.3) | collective-permute-done | bytes 409632 | tf_op jit(solution)/shard_map/cond/branch_0_fun/ppermute | solution.py:504
  28.9 3.4 %collective-permute-start.6 = (bf16[320,640]{1,0:T(8,128)(2,1)}, bf16[320,640]{1,0:T(8,128)(2,1)S(1)}, u32[]{:S(2)}, u32[]{:S(2)}) collective-permute-start(bf16[320,640]{1,0:T(8,128)(2,1)} %collective-permute-done.3), channel_id=1, source_target_pairs={{0,16},{16,0},{1,17},{17,1},{4,20},{20,4},{5,21},{21,5},{8,24},{24... | collective-permute-start | bytes 1228808 | tf_op jit(solution)/shard_map/cond/branch_0_fun/ppermute | solution.py:504
  32.3 14.0 %collective-permute-done.2 = bf16[320,640]{1,0:T(8,128)(2,1)} collective-permute-done((bf16[320,640]{1,0:T(8,128)(2,1)}, bf16[320,640]{1,0:T(8,128)(2,1)}, u32[]{:S(2)}, u32[]{:S(2)}) %collective-permute-start.2) | collective-permute-done | bytes 409632 | tf_op jit(solution)/shard_map/cond/branch_0_fun/ppermute | solution.py:504
  46.3 3.4 %collective-permute-start.5 = (bf16[320,640]{1,0:T(8,128)(2,1)}, bf16[320,640]{1,0:T(8,128)(2,1)S(1)}, u32[]{:S(2)}, u32[]{:S(2)}) collective-permute-start(bf16[320,640]{1,0:T(8,128)(2,1)} %collective-permute-done.2), channel_id=1, source_target_pairs={{0,16},{16,0},{1,17},{17,1},{4,20},{20,4},{5,21},{21,5},{8,24},{24... | collective-permute-start | bytes 1228808 | tf_op jit(solution)/shard_map/cond/branch_0_fun/ppermute | solution.py:504
  49.8 6.2 %collective-permute-start.7 = (bf16[136,896]{1,0:T(8,128)(2,1)S(1)}, bf16[136,896]{1,0:T(8,128)(2,1)S(1)}, u32[]{:S(2)}, u32[]{:S(2)}) collective-permute-start(bf16[136,896]{1,0:T(8,128)(2,1)S(1)} %fusion.9), channel_id=1, source_target_pairs={{0,4},{4,0},{8,12},{12,8},{1,5},{5,1},{9,13},{13,9},{16,20},{20,16... | collective-permute-start | bytes 731144 | tf_op jit(solution)/shard_map/cond/branch_0_fun/ppermute | solution.py:504
  56.1 0.7 broadcast_in_dim.28
  56.8 0.6 broadcast_in_dim.14
  57.5 2.3 %collective-permute-done.5 = bf16[320,640]{1,0:T(8,128)(2,1)S(1)} collective-permute-done((bf16[320,640]{1,0:T(8,128)(2,1)}, bf16[320,640]{1,0:T(8,128)(2,1)S(1)}, u32[]{:S(2)}, u32[]{:S(2)}) %collective-permute-start.5) | collective-permute-done | bytes 409632 | tf_op jit(solution)/shard_map/cond/branch_0_fun/ppermute | solution.py:504
  59.8 0.4 collective-permute-done.7
  60.2 1.3 %collective-permute-start.18 = (bf16[128,1280]{1,0:T(8,128)(2,1)}, bf16[128,1280]{1,0:T(8,128)(2,1)S(1)}, u32[]{:S(2)}, u32[]{:S(2)}) collective-permute-start(bf16[128,1280]{1,0:T(8,128)(2,1)} %get-tuple-element.108), channel_id=1, source_target_pairs={{2,0},{6,4},{10,8},{14,12},{3,1},{7,5},{11,9},{15,13},{18,16},{22,... | collective-permute-start | bytes 983048 | tf_op jit(solution)/shard_map/ppermute | solution.py:504
  61.5 1.3 %collective-permute-start.19 = (bf16[128,1280]{1,0:T(8,128)(2,1)}, bf16[128,1280]{1,0:T(8,128)(2,1)S(1)}, u32[]{:S(2)}, u32[]{:S(2)}) collective-permute-start(bf16[128,1280]{1,0:T(8,128)(2,1)} %get-tuple-element.108), channel_id=1, source_target_pairs={{2,4},{6,0},{10,12},{14,8},{3,5},{7,1},{11,13},{15,9},{18,20},{22,... | collective-permute-start | bytes 983048 | tf_op jit(solution)/shard_map/ppermute | solution.py:504
  62.9 1.9 %constant_dynamic-slice_fusion.11 = (bf16[128,320]{1,0:T(8,128)(2,1)S(1)}, bf16[128,320]{1,0:T(8,128)(2,1)S(1)}, bf16[128,320]{1,0:T(8,128)(2,1)}, bf16[128,320]{1,0:T(8,128)(2,1)S(1)}) fusion(bf16[128,1280]{1,0:T(8,128)(2,1)} %bitcast.31, s32[]{:T(128)S(6)} %select_n.71, s32[]{:T(128)S(6)} %select_n.70, s32[]{:T(128)S(6)} %select_n.69, s32[]{:T(128)S(6)} %select_n.68), kind=kLoop, calls=%fused_computation.37 | loop fusion | bytes 655376 | tf_op jit(solution)/shard_map/dynamic_slice | solution.py:529
  64.8 2.0 %collective-permute-start.20 = (bf16[128,320]{1,0:T(8,128)(2,1)}, bf16[128,320]{1,0:T(8,128)(2,1)S(1)}, u32[]{:S(2)}, u32[]{:S(2)}) collective-permute-start(bf16[128,320]{1,0:T(8,128)(2,1)} %get-tuple-element.150), channel_id=1, source_target_pairs={{0,4},{4,8},{8,12},{12,0},{1,5},{5,9},{9,13},{13,1},{2,6},{6,10},{... | collective-permute-start | bytes 245768 | tf_op jit(solution)/shard_map/ppermute | solution.py:504
  66.8 3.0 %collective-permute-start.21 = (bf16[128,320]{1,0:T(8,128)(2,1)S(1)}, bf16[128,320]{1,0:T(8,128)(2,1)S(1)}, u32[]{:S(2)}, u32[]{:S(2)}) collective-permute-start(bf16[128,320]{1,0:T(8,128)(2,1)S(1)} %get-tuple-element.149), channel_id=1, source_target_pairs={{0,8},{4,12},{8,0},{12,4},{1,9},{5,13},{9,1},{13,5},{2,10},{6,14},... | collective-permute-start | bytes 245768 | tf_op jit(solution)/shard_map/ppermute | solution.py:504
  69.8 2.9 %collective-permute-start.22 = (bf16[128,320]{1,0:T(8,128)(2,1)S(1)}, bf16[128,320]{1,0:T(8,128)(2,1)S(1)}, u32[]{:S(2)}, u32[]{:S(2)}) collective-permute-start(bf16[128,320]{1,0:T(8,128)(2,1)S(1)} %get-tuple-element.148), channel_id=1, source_target_pairs={{0,12},{4,0},{8,4},{12,8},{1,13},{5,1},{9,5},{13,9},{2,14},{6,2},{... | collective-permute-start | bytes 245768 | tf_op jit(solution)/shard_map/ppermute | solution.py:504
  72.7 0.1 stack.69.place
  72.7 0.1 stack.66.place
  72.8 1.3 %shard_map.87.own_gain = bf16[128,1280]{1,0:T(8,128)(2,1)S(1)} custom-call(bf16[128,1280]{1,0:T(8,128)(2,1)S(1)} %bitcast.33, bf16[128,1280]{1,0:T(8,128)(2,1)} %bitcast.39), custom_call_target="tpu_custom_call" | custom-call | flops 10000000 | bytes 1000000 | tf_op jit(solution)/shard_map/pallas_call | solution.py:178
  74.2 2.1 %shard_map.88 = (bf16[2,5,128,128]{3,2,1,0:T(8,128)(2,1)S(1)}, f32[640,256]{1,0:T(8,128)S(1)}, f32[256,128]{1,0:T(8,128)S(1)}, f32[256,128]{1,0:T(8,128)S(1)}) custom-call(s32[5]{0:T(128)S(1)} %stack.69.place, bf16[136,896]{1,0:T(8,128)(2,1)} %copy-done.16, bf16[136,896]{1,0:T(8,128)(2,1)} %copy-done.27), custom_call_target="tpu_custom_call" | custom-call | flops 100000000 | bytes 3000000 | tf_op jit(solution)/shard_map/pallas_call | solution.py:274
  76.3 0.7 shard_map.86.inputs_t
  77.1 5.5 %collective-permute-done.18.current = bf16[128,1280]{1,0:T(8,128)(2,1)S(1)} collective-permute-done((bf16[128,1280]{1,0:T(8,128)(2,1)}, bf16[128,1280]{1,0:T(8,128)(2,1)S(1)}, u32[]{:S(2)}, u32[]{:S(2)}) %collective-permute-start.18) | collective-permute-done | bytes 327712 | tf_op jit(solution)/shard_map/ppermute | solution.py:504
  82.5 0.2 shard_map.89.refs_0_
  82.7 1.9 %collective-permute-start.23 = (bf16[256,1280]{1,0:T(8,128)(2,1)S(1)}, bf16[256,1280]{1,0:T(8,128)(2,1)S(1)}, u32[]{:S(2)}, u32[]{:S(2)}) collective-permute-start(bf16[256,1280]{1,0:T(8,128)(2,1)S(1)} %shard_map.89.refs_0_), channel_id=1, source_target_pairs={{0,1},{1,0},{4,5},{5,4},{8,9},{9,8},{12,13},{13,12},{16,17},{17,16... | collective-permute-start | bytes 1966088 | tf_op jit(solution)/shard_map/ppermute | solution.py:504
  84.6 0.7 collective-permute-start.24
  86.0 0.4 fusion.10
  86.3 0.1 stack.74.place
  86.4 0.1 stack.72.place
  86.5 1.1 shard_map.90.refs_3_
  87.6 1.5 %shard_map.91.refs_4_ = f32[1,128]{1,0:T(1,128)S(1)} custom-call(bf16[128,1280]{1,0:T(8,128)(2,1)} %bitcast.32, bf16[128,1280]{1,0:T(8,128)(2,1)} %bitcast.40, bf16[128,1280]{1,0:T(8,128)(2,1)S(1)} %collective-permute-done.18.current), custom_call_target="tpu_custom_call" | custom-call | flops 100000 | bytes 10000 | tf_op jit(solution)/shard_map/pallas_call | solution.py:204
  89.1 3.7 %shard_map.92.refs_0_ = bf16[272,128]{1,0:T(8,128)(2,1)S(1)} custom-call(s32[5]{0:T(128)S(1)} %stack.72.place, bf16[256,1280]{1,0:T(8,128)(2,1)S(1)} %shard_map.89.refs_0_, bf16[256,1280]{1,0:T(8,128)(2,1)S(1)} %collective-permute-done.23.refs_1_, bf16[1280,640]{1,0:T(8,128)(2,1)} %bitcast.43, bf16[272,128]{1,0:T(8,128)(2,1)S(1)} %shard_map.90.refs_3_, ...), custom_call_target="tpu_custom_call" | custom-call | flops 1000000000 | bytes 6000000 | tf_op jit(solution)/shard_map/pallas_call | solution.py:377
  92.8 1.1 %collective-permute-start.25 = (bf16[272,128]{1,0:T(8,128)(2,1)S(1)}, bf16[272,128]{1,0:T(8,128)(2,1)S(1)}, u32[]{:S(2)}, u32[]{:S(2)}) collective-permute-start(bf16[272,128]{1,0:T(8,128)(2,1)S(1)} %shard_map.92.refs_0_), channel_id=1, source_target_pairs={{0,4},{4,8},{8,12},{12,0},{1,5},{5,9},{9,13},{13,1},{2,6},{6,10},{... | collective-permute-start | bytes 208904 | tf_op jit(solution)/shard_map/ppermute | solution.py:504
  93.9 0.3 collective-permute-start.26
  94.2 2.5 %collective-permute-start.27 = (bf16[272,128]{1,0:T(8,128)(2,1)S(1)}, bf16[272,128]{1,0:T(8,128)(2,1)S(1)}, u32[]{:S(2)}, u32[]{:S(2)}) collective-permute-start(bf16[272,128]{1,0:T(8,128)(2,1)S(1)} %shard_map.92.refs_0_), channel_id=1, source_target_pairs={{0,12},{4,0},{8,4},{12,8},{1,13},{5,1},{9,5},{13,9},{2,14},{6,2},{... | collective-permute-start | bytes 208904 | tf_op jit(solution)/shard_map/ppermute | solution.py:504
  96.7 3.0 %collective-permute-done.25.refs_1_ = bf16[272,128]{1,0:T(8,128)(2,1)S(1)} collective-permute-done((bf16[272,128]{1,0:T(8,128)(2,1)S(1)}, bf16[272,128]{1,0:T(8,128)(2,1)S(1)}, u32[]{:S(2)}, u32[]{:S(2)}) %collective-permute-start.25) | collective-permute-done | bytes 69664 | tf_op jit(solution)/shard_map/ppermute | solution.py:504
  99.8 2.6 %collective-permute-done.26.refs_2_ = bf16[272,128]{1,0:T(8,128)(2,1)S(1)} collective-permute-done((bf16[272,128]{1,0:T(8,128)(2,1)S(1)}, bf16[272,128]{1,0:T(8,128)(2,1)S(1)}, u32[]{:S(2)}, u32[]{:S(2)}) %collective-permute-start.26) | collective-permute-done | bytes 69664 | tf_op jit(solution)/shard_map/ppermute | solution.py:504
  102.4 0.1 collective-permute-start.28
  102.4 1.5 %collective-permute-done.28.refs_4_ = bf16[1088,128]{1,0:T(8,128)(2,1)S(1)} collective-permute-done((bf16[1088,128]{1,0:T(8,128)(2,1)S(1)}, bf16[1088,128]{1,0:T(8,128)(2,1)S(1)}, u32[]{:S(2)}, u32[]{:S(2)}) %collective-permute-start.28) | collective-permute-done | bytes 278560 | tf_op jit(solution)/shard_map/ppermute | solution.py:504
  104.0 1.8 %shard_map.93 = (f32[320,512]{1,0:T(8,128)}, f32[1,128]{1,0:T(1,128)}) custom-call(s32[5]{0:T(128)S(1)} %stack.66.place, bf16[320,512]{1,0:T(8,128)(2,1)S(1)} %shard_map.86.inputs_t, bf16[1280,512]{1,0:T(8,128)(2,1)S(1)} %bitcast.36, bf16[272,128]{1,0:T(8,128)(2,1)S(1)} %shard_map.92.refs_0_, bf16[272,128]{1,0:T(8,128)(2,1)S(1)} %collective-permute-done.25.refs_1_, ...), custom_call_target="tpu_custom_call" | custom-call | flops 200000000 | bytes 2000000 | tf_op jit(solution)/shard_map/pallas_call | solution.py:470
  (61 shorter events, 0.3 us)
Async XLA Ops:
  0.6 72.2 %copy-start = (bf16[1,1,128,1280]{3,2,1,0:T(8,128)(2,1)S(1)}, bf16[1,1,128,1280]{3,2,1,0:T(8,128)(2,1)}, u32[]{:S(2)}) copy-start(bf16[1,1,128,1280]{3,2,1,0:T(8,128)(2,1)} %param.9) | copy-start | bytes 983044
  0.7 14.4 %copy-start.2 = (bf16[128,1280]{1,0:T(8,128)(2,1)S(1)}, bf16[128,1280]{1,0:T(8,128)(2,1)}, u32[]{:S(2)}) copy-start(bf16[128,1280]{1,0:T(8,128)(2,1)} %get-tuple-element.38.inputs) | copy-start | bytes 983044 | tf_op jit(solution)/shard_map/cond
  0.7 14.4 %copy-start.5 = (bf16[1280,512]{1,0:T(8,128)(2,1)S(1)}, bf16[1280,512]{1,0:T(8,128)(2,1)}, u32[]{:S(2)}) copy-start(bf16[1280,512]{1,0:T(8,128)(2,1)} %get-tuple-element.39) | copy-start | bytes 3932164 | tf_op jit(solution)/shard_map/cond
  3.1 14.3 %copy-start.8 = (bf16[128,1280]{1,0:T(8,128)(2,1)S(1)}, bf16[128,1280]{1,0:T(8,128)(2,1)}, u32[]{:S(2)}) copy-start(bf16[128,1280]{1,0:T(8,128)(2,1)} %get-tuple-element.51.branch) | copy-start | bytes 983044 | tf_op jit(solution)/shard_map/cond
  3.1 18.9 %collective-permute-start.1 = (bf16[320,640]{1,0:T(8,128)(2,1)}, bf16[320,640]{1,0:T(8,128)(2,1)}, u32[]{:S(2)}, u32[]{:S(2)}) collective-permute-start(bf16[320,640]{1,0:T(8,128)(2,1)} %get-tuple-element.137), channel_id=1, source_target_pairs={{0,4},{4,8},{8,12},{12,0},{1,5},{5,9},{9,13},{13,1},{16,20},{20,24... | collective-permute-start | bytes 1228808 | tf_op jit(solution)/shard_map/cond/branch_0_fun/ppermute | solution.py:504
  8.2 20.7 %collective-permute-start.3 = (bf16[320,640]{1,0:T(8,128)(2,1)}, bf16[320,640]{1,0:T(8,128)(2,1)}, u32[]{:S(2)}, u32[]{:S(2)}) collective-permute-start(bf16[320,640]{1,0:T(8,128)(2,1)} %get-tuple-element.135), channel_id=1, source_target_pairs={{0,12},{4,0},{8,4},{12,8},{1,13},{5,1},{9,5},{13,9},{16,28},{20,16... | collective-permute-start | bytes 1228808 | tf_op jit(solution)/shard_map/cond/branch_0_fun/ppermute | solution.py:504
  12.2 34.2 %collective-permute-start.2 = (bf16[320,640]{1,0:T(8,128)(2,1)}, bf16[320,640]{1,0:T(8,128)(2,1)}, u32[]{:S(2)}, u32[]{:S(2)}) collective-permute-start(bf16[320,640]{1,0:T(8,128)(2,1)} %get-tuple-element.136), channel_id=1, source_target_pairs={{0,8},{4,12},{8,0},{12,4},{1,9},{5,13},{9,1},{13,5},{16,24},{20,28... | collective-permute-start | bytes 1228808 | tf_op jit(solution)/shard_map/cond/branch_0_fun/ppermute | solution.py:504
  15.1 6.8 %copy-start.14 = (bf16[128,1280]{1,0:T(8,128)(2,1)S(1)}, bf16[128,1280]{1,0:T(8,128)(2,1)}, u32[]{:S(2)}) copy-start(bf16[128,1280]{1,0:T(8,128)(2,1)} %get-tuple-element.47) | copy-start | bytes 983044 | tf_op jit(solution)/shard_map/cond
  15.5 6.6 %copy-start.25 = (bf16[128,256]{1,0:T(8,128)(2,1)S(1)}, bf16[128,256]{1,0:T(8,128)(2,1)}, u32[]{:S(2)}) copy-start(bf16[128,256]{1,0:T(8,128)(2,1)} %get-tuple-element.49) | copy-start | bytes 196612 | tf_op jit(solution)/shard_map/cond
  15.5 16.8 %collective-permute-start = (bf16[128,256]{1,0:T(8,128)(2,1)S(1)}, bf16[128,256]{1,0:T(8,128)(2,1)S(1)}, u32[]{:S(2)}, u32[]{:S(2)}) collective-permute-start(bf16[128,256]{1,0:T(8,128)(2,1)S(1)} %dynamic-slice_convert_fusion), channel_id=1, source_target_pairs={{0,1},{1,0},{4,5},{5,4},{8,9},{9,8},{12,13},{13,12},{16,17},{17,16... | collective-permute-start | bytes 196616 | tf_op jit(solution)/shard_map/cond/branch_0_fun/ppermute | solution.py:504
  17.8 39.7 %collective-permute-start.8 = (bf16[128,1280]{1,0:T(8,128)(2,1)S(1)}, bf16[128,1280]{1,0:T(8,128)(2,1)S(1)}, u32[]{:S(2)}, u32[]{:S(2)}) collective-permute-start(bf16[128,1280]{1,0:T(8,128)(2,1)S(1)} %branch_0_fun.1), channel_id=1, source_target_pairs={{0,4},{4,0},{8,12},{12,8},{1,5},{5,1},{9,13},{13,9},{16,20},{20,16... | collective-permute-start | bytes 983048 | tf_op jit(solution)/shard_map/cond/branch_0_fun/ppermute | solution.py:504
  22.1 27.8 %collective-permute-start.4 = (bf16[320,640]{1,0:T(8,128)(2,1)}, bf16[320,640]{1,0:T(8,128)(2,1)S(1)}, u32[]{:S(2)}, u32[]{:S(2)}) collective-permute-start(bf16[320,640]{1,0:T(8,128)(2,1)} %collective-permute-done.1), channel_id=1, source_target_pairs={{0,16},{16,0},{1,17},{17,1},{4,20},{20,4},{5,21},{21,5},{8,24},{24... | collective-permute-start | bytes 1228808 | tf_op jit(solution)/shard_map/cond/branch_0_fun/ppermute | solution.py:504
  28.9 21.0 %collective-permute-start.6 = (bf16[320,640]{1,0:T(8,128)(2,1)}, bf16[320,640]{1,0:T(8,128)(2,1)S(1)}, u32[]{:S(2)}, u32[]{:S(2)}) collective-permute-start(bf16[320,640]{1,0:T(8,128)(2,1)} %collective-permute-done.3), channel_id=1, source_target_pairs={{0,16},{16,0},{1,17},{17,1},{4,20},{20,4},{5,21},{21,5},{8,24},{24... | collective-permute-start | bytes 1228808 | tf_op jit(solution)/shard_map/cond/branch_0_fun/ppermute | solution.py:504
  46.3 13.5 %collective-permute-start.5 = (bf16[320,640]{1,0:T(8,128)(2,1)}, bf16[320,640]{1,0:T(8,128)(2,1)S(1)}, u32[]{:S(2)}, u32[]{:S(2)}) collective-permute-start(bf16[320,640]{1,0:T(8,128)(2,1)} %collective-permute-done.2), channel_id=1, source_target_pairs={{0,16},{16,0},{1,17},{17,1},{4,20},{20,4},{5,21},{21,5},{8,24},{24... | collective-permute-start | bytes 1228808 | tf_op jit(solution)/shard_map/cond/branch_0_fun/ppermute | solution.py:504
  49.8 10.4 %collective-permute-start.7 = (bf16[136,896]{1,0:T(8,128)(2,1)S(1)}, bf16[136,896]{1,0:T(8,128)(2,1)S(1)}, u32[]{:S(2)}, u32[]{:S(2)}) collective-permute-start(bf16[136,896]{1,0:T(8,128)(2,1)S(1)} %fusion.9), channel_id=1, source_target_pairs={{0,4},{4,0},{8,12},{12,8},{1,5},{5,1},{9,13},{13,9},{16,20},{20,16... | collective-permute-start | bytes 731144 | tf_op jit(solution)/shard_map/cond/branch_0_fun/ppermute | solution.py:504
  57.5 2.7 %copy-start.23 = (bf16[128,1280]{1,0:T(8,128)(2,1)}, bf16[128,1280]{1,0:T(8,128)(2,1)S(1)}, u32[]{:S(2)}) copy-start(bf16[128,1280]{1,0:T(8,128)(2,1)S(1)} %collective-permute-done.8) | copy-start | bytes 983044 | tf_op jit(solution)/shard_map/cond
  60.2 2.7 %copy-start.21 = (bf16[320,640]{1,0:T(8,128)(2,1)}, bf16[320,640]{1,0:T(8,128)(2,1)S(1)}, u32[]{:S(2)}) copy-start(bf16[320,640]{1,0:T(8,128)(2,1)S(1)} %get-tuple-element.131.refs_13_) | copy-start | bytes 1228804
  60.2 6.6 %copy-start.27 = (bf16[136,896]{1,0:T(8,128)(2,1)}, bf16[136,896]{1,0:T(8,128)(2,1)S(1)}, u32[]{:S(2)}) copy-start(bf16[136,896]{1,0:T(8,128)(2,1)S(1)} %get-tuple-element.111.got) | copy-start | bytes 731140
  60.2 12.5 %copy-start.16 = (bf16[136,896]{1,0:T(8,128)(2,1)}, bf16[136,896]{1,0:T(8,128)(2,1)S(1)}, u32[]{:S(2)}) copy-start(bf16[136,896]{1,0:T(8,128)(2,1)S(1)} %get-tuple-element.110.kept) | copy-start | bytes 731140
  60.2 13.9 %copy-start.17 = (bf16[320,640]{1,0:T(8,128)(2,1)}, bf16[320,640]{1,0:T(8,128)(2,1)S(1)}, u32[]{:S(2)}) copy-start(bf16[320,640]{1,0:T(8,128)(2,1)S(1)} %get-tuple-element.130.refs_12_) | copy-start | bytes 1228804
  60.2 13.9 %copy-start.19 = (bf16[320,640]{1,0:T(8,128)(2,1)}, bf16[320,640]{1,0:T(8,128)(2,1)S(1)}, u32[]{:S(2)}) copy-start(bf16[320,640]{1,0:T(8,128)(2,1)S(1)} %get-tuple-element.132.refs_14_) | copy-start | bytes 1228804
  60.2 16.8 %copy-start.13 = (f32[128,256]{1,0:T(8,128)}, f32[128,256]{1,0:T(8,128)S(1)}, u32[]{:S(2)}) copy-start(f32[128,256]{1,0:T(8,128)S(1)} %get-tuple-element.122.values) | copy-start | bytes 393220
  60.2 22.3 %collective-permute-start.18 = (bf16[128,1280]{1,0:T(8,128)(2,1)}, bf16[128,1280]{1,0:T(8,128)(2,1)S(1)}, u32[]{:S(2)}, u32[]{:S(2)}) collective-permute-start(bf16[128,1280]{1,0:T(8,128)(2,1)} %get-tuple-element.108), channel_id=1, source_target_pairs={{2,0},{6,4},{10,8},{14,12},{3,1},{7,5},{11,9},{15,13},{18,16},{22,... | collective-permute-start | bytes 983048 | tf_op jit(solution)/shard_map/ppermute | solution.py:504
  61.5 21.0 %collective-permute-start.19 = (bf16[128,1280]{1,0:T(8,128)(2,1)}, bf16[128,1280]{1,0:T(8,128)(2,1)S(1)}, u32[]{:S(2)}, u32[]{:S(2)}) collective-permute-start(bf16[128,1280]{1,0:T(8,128)(2,1)} %get-tuple-element.108), channel_id=1, source_target_pairs={{2,4},{6,0},{10,12},{14,8},{3,5},{7,1},{11,13},{15,9},{18,20},{22,... | collective-permute-start | bytes 983048 | tf_op jit(solution)/shard_map/ppermute | solution.py:504
  64.8 17.7 %copy-start.24 = (bf16[128,1280]{1,0:T(8,128)(2,1)S(1)}, bf16[128,1280]{1,0:T(8,128)(2,1)}, u32[]{:S(2)}) copy-start(bf16[128,1280]{1,0:T(8,128)(2,1)} %get-tuple-element.118.gain) | copy-start | bytes 983044
  64.8 11.5 %collective-permute-start.20 = (bf16[128,320]{1,0:T(8,128)(2,1)}, bf16[128,320]{1,0:T(8,128)(2,1)S(1)}, u32[]{:S(2)}, u32[]{:S(2)}) collective-permute-start(bf16[128,320]{1,0:T(8,128)(2,1)} %get-tuple-element.150), channel_id=1, source_target_pairs={{0,4},{4,8},{8,12},{12,0},{1,5},{5,9},{9,13},{13,1},{2,6},{6,10},{... | collective-permute-start | bytes 245768 | tf_op jit(solution)/shard_map/ppermute | solution.py:504
  66.8 9.5 %collective-permute-start.21 = (bf16[128,320]{1,0:T(8,128)(2,1)S(1)}, bf16[128,320]{1,0:T(8,128)(2,1)S(1)}, u32[]{:S(2)}, u32[]{:S(2)}) collective-permute-start(bf16[128,320]{1,0:T(8,128)(2,1)S(1)} %get-tuple-element.149), channel_id=1, source_target_pairs={{0,8},{4,12},{8,0},{12,4},{1,9},{5,13},{9,1},{13,5},{2,10},{6,14},... | collective-permute-start | bytes 245768 | tf_op jit(solution)/shard_map/ppermute | solution.py:504
  69.8 6.5 %collective-permute-start.22 = (bf16[128,320]{1,0:T(8,128)(2,1)S(1)}, bf16[128,320]{1,0:T(8,128)(2,1)S(1)}, u32[]{:S(2)}, u32[]{:S(2)}) collective-permute-start(bf16[128,320]{1,0:T(8,128)(2,1)S(1)} %get-tuple-element.148), channel_id=1, source_target_pairs={{0,12},{4,0},{8,4},{12,8},{1,13},{5,1},{9,5},{13,9},{2,14},{6,2},{... | collective-permute-start | bytes 245768 | tf_op jit(solution)/shard_map/ppermute | solution.py:504
  76.3 9.7 %copy-start.1 = (bf16[1,1,128,1280]{3,2,1,0:T(8,128)(2,1)S(1)}, bf16[1,1,128,1280]{3,2,1,0:T(8,128)(2,1)}, u32[]{:S(2)}) copy-start(bf16[1,1,128,1280]{3,2,1,0:T(8,128)(2,1)} %param.9) | copy-start | bytes 983044
  76.3 9.6 %copy-start.7 = (bf16[1,1,128,1280]{3,2,1,0:T(8,128)(2,1)S(1)}, bf16[1,1,128,1280]{3,2,1,0:T(8,128)(2,1)}, u32[]{:S(2)}) copy-start(bf16[1,1,128,1280]{3,2,1,0:T(8,128)(2,1)} %param.10) | copy-start | bytes 983044
  82.7 6.4 %collective-permute-start.23 = (bf16[256,1280]{1,0:T(8,128)(2,1)S(1)}, bf16[256,1280]{1,0:T(8,128)(2,1)S(1)}, u32[]{:S(2)}, u32[]{:S(2)}) collective-permute-start(bf16[256,1280]{1,0:T(8,128)(2,1)S(1)} %shard_map.89.refs_0_), channel_id=1, source_target_pairs={{0,1},{1,0},{4,5},{5,4},{8,9},{9,8},{12,13},{13,12},{16,17},{17,16... | collective-permute-start | bytes 1966088 | tf_op jit(solution)/shard_map/ppermute | solution.py:504
  84.6 1.9 %collective-permute-start.24 = (bf16[128,256]{1,0:T(8,128)(2,1)}, bf16[128,256]{1,0:T(8,128)(2,1)S(1)}, u32[]{:S(2)}, u32[]{:S(2)}) collective-permute-start(bf16[128,256]{1,0:T(8,128)(2,1)} %get-tuple-element.121.found), channel_id=1, source_target_pairs={{2,6},{6,2},{10,14},{14,10},{3,7},{7,3},{11,15},{15,11},{18,22},{2... | collective-permute-start | bytes 196616 | tf_op jit(solution)/shard_map/ppermute | solution.py:504
  86.5 2.6 %copy-start.18 = (bf16[320,640]{1,0:T(8,128)(2,1)S(1)}, bf16[320,640]{1,0:T(8,128)(2,1)}, u32[]{:S(2)}) copy-start(bf16[320,640]{1,0:T(8,128)(2,1)} %copy-done.17) | copy-start | bytes 1228804
  86.5 2.6 %copy-start.20 = (bf16[320,640]{1,0:T(8,128)(2,1)S(1)}, bf16[320,640]{1,0:T(8,128)(2,1)}, u32[]{:S(2)}) copy-start(bf16[320,640]{1,0:T(8,128)(2,1)} %copy-done.19) | copy-start | bytes 1228804
  86.5 2.6 %copy-start.22 = (bf16[320,640]{1,0:T(8,128)(2,1)S(1)}, bf16[320,640]{1,0:T(8,128)(2,1)}, u32[]{:S(2)}) copy-start(bf16[320,640]{1,0:T(8,128)(2,1)} %copy-done.21) | copy-start | bytes 1228804
  89.1 14.9 %copy-start.4 = (bf16[1,1280,512]{2,1,0:T(8,128)(2,1)S(1)}, bf16[1,1280,512]{2,1,0:T(8,128)(2,1)}, u32[]{:S(2)}) copy-start(bf16[1,1280,512]{2,1,0:T(8,128)(2,1)} %param.13) | copy-start | bytes 3932164
  92.8 6.9 %collective-permute-start.25 = (bf16[272,128]{1,0:T(8,128)(2,1)S(1)}, bf16[272,128]{1,0:T(8,128)(2,1)S(1)}, u32[]{:S(2)}, u32[]{:S(2)}) collective-permute-start(bf16[272,128]{1,0:T(8,128)(2,1)S(1)} %shard_map.92.refs_0_), channel_id=1, source_target_pairs={{0,4},{4,8},{8,12},{12,0},{1,5},{5,9},{9,13},{13,1},{2,6},{6,10},{... | collective-permute-start | bytes 208904 | tf_op jit(solution)/shard_map/ppermute | solution.py:504
  93.9 8.4 %collective-permute-start.26 = (bf16[272,128]{1,0:T(8,128)(2,1)S(1)}, bf16[272,128]{1,0:T(8,128)(2,1)S(1)}, u32[]{:S(2)}, u32[]{:S(2)}) collective-permute-start(bf16[272,128]{1,0:T(8,128)(2,1)S(1)} %shard_map.92.refs_0_), channel_id=1, source_target_pairs={{0,8},{4,12},{8,0},{12,4},{1,9},{5,13},{9,1},{13,5},{2,10},{6,14},... | collective-permute-start | bytes 208904 | tf_op jit(solution)/shard_map/ppermute | solution.py:504
  94.2 8.1 %collective-permute-start.27 = (bf16[272,128]{1,0:T(8,128)(2,1)S(1)}, bf16[272,128]{1,0:T(8,128)(2,1)S(1)}, u32[]{:S(2)}, u32[]{:S(2)}) collective-permute-start(bf16[272,128]{1,0:T(8,128)(2,1)S(1)} %shard_map.92.refs_0_), channel_id=1, source_target_pairs={{0,12},{4,0},{8,4},{12,8},{1,13},{5,1},{9,5},{13,9},{2,14},{6,2},{... | collective-permute-start | bytes 208904 | tf_op jit(solution)/shard_map/ppermute | solution.py:504
  102.4 1.6 %collective-permute-start.28 = (bf16[1088,128]{1,0:T(8,128)(2,1)S(1)}, bf16[1088,128]{1,0:T(8,128)(2,1)S(1)}, u32[]{:S(2)}, u32[]{:S(2)}) collective-permute-start(bf16[1088,128]{1,0:T(8,128)(2,1)S(1)} %pad_maximum_fusion.1), channel_id=1, source_target_pairs={{0,1},{1,0},{2,3},{3,2},{4,5},{5,4},{6,7},{7,6},{8,9},{9,8},{10,11... | collective-permute-start | bytes 835592 | tf_op jit(solution)/shard_map/ppermute | solution.py:504

commit v10 on v9

--- a/solution.py
+++ b/solution.py
@@ -302,8 +302,7 @@
             start = pl.multiple_of(lax.rem(owner, per_core) * width, 128)
             return halves[owner // per_core, :, pl.ds(start, width)]
 
-        rows = pl.ds(pl.multiple_of(side * 2 * quarter, 16), 2 * quarter)
-        total[...] = by_columns(out_block[rows, :], part(0))
+        total[...] = by_columns(out_block[...], part(0))
         for k in range(count):
             operand = part(k + 1)
             for at, piece in ((group, own_pieces[k]), (1 - group, other_pieces[k])):
@@ -392,8 +391,7 @@
             if k:
                 piece = quarters[half][k - 1]
             else:
-                at = 2 * side + (group if half == 0 else 1 - group)
-                piece = part_of(out_block, at, quarter, 0)
+                piece = part_of(out_block, group if half == 0 else 1 - group, quarter, 0)
             totals[half] += by_columns(piece, operand)
     total = ordered(group == 0, totals[0], totals[1], 0)
     probs, gain_t, value_gain, values = rest
@@ -696,6 +694,7 @@
     ]
     rest = pair_attend(place(~is_last), kept_half, got_half)
     own_gain = branch_gain(inputs, branch)
+    own_block = part_of(out_block, side, head_width, 0)
     if in_tiles:
         inputs_t = turned_side_by_side(place(0), pieces)
     else:
@@ -716,8 +715,8 @@
         active = section_pos == sections - 1 - turn
         current = jnp.where(active, arrived, current)
         if turn == 1:
-            arrived, partner_arrived, inputs_t, own_gain, *rest = lax.optimization_barrier(
-                (arrived, partner_arrived, inputs_t, own_gain, *rest)
+            arrived, partner_arrived, inputs_t, own_gain, own_block, *rest = lax.optimization_barrier(
+                (arrived, partner_arrived, inputs_t, own_gain, own_block, *rest)
             )
         sens_own = pair_sensitivity(own_gain, partner_gain, arrived, partner_arrived)
         kept_sum = sum_of_kept(inputs, branch, arrived)
@@ -726,7 +725,7 @@
         sens_values = step(
             place(active),
             sens,
-            out_block,
+            own_block,
             (own_quarters, other_quarters),
             sens_values,
             kept_sum,

time: 107 us -> 110 us (1.028)
  local copies, waits for them, and re-layouts: 6.27 us -> 9.44 us
  starting transfers between devices: 50.8 us -> 49.2 us
    unnamed x28 -> x30, local copies, waits for them, and re-layouts: 0.07 us -> 1.61 us
    ppermute x20, starting transfers between devices: 50.8 us -> 49.2 us  [moved(): return lax.ppermute(shard, axes, pairs)]
    dynamic_slice x4 -> x5, local copies, waits for them, and re-layouts: 4.42 us -> 5.9 us  [part_of(): return lax.dynamic_slice_in_dim(array, index * width, width, axis)]
  transfers between devices with their start and end apart: 20 -> 20, of which waited for: 8 -> 8; matrix products, arithmetic and copies ran while one was open for 4% -> 6% of each run, Pallas kernels for 7% -> 6%
where the time goes in v10:
time: 110 us; the launch traced here: 109 us
  starting transfers between devices  49.2 us (45%)
  waiting for transfers between devices  32.6 us (30%)
  Pallas kernels  13.3 us (12%)
  local copies, waits for them, and re-layouts  9.44 us (9%)
  between operations  1.59 us (1%)
  other arithmetic  1.11 us (1%)
    ppermute x20, starting transfers between devices, moved(): return lax.ppermute(shard, axes, pairs)  49.2 us
    ppermute x20, waiting for transfers between devices, moved(): return lax.ppermute(shard, axes, pairs)  32.6 us
    dynamic_slice x5, local copies, waits for them, and re-layouts, part_of(): return lax.dynamic_slice_in_dim(array, index * width, width, axis)  5.9 us
    pallas_call x1, Pallas kernels, main_step(): return call(place, *operands)  3.41 us
  transfers between devices with their start and end apart: 20, of which 8 were waited for; matrix products, arithmetic and copies ran while one was open for 6% of the time, Pallas kernels for 6%

profile of v10, /device:TPU:0, one launch (start us, length us, event | category | flops | bytes accessed | tf_op | source)
XLA Modules:
  0.0 108.5 jit_solution(7418817586126711073)
XLA Ops:
  0.7 59.6 %conditional.1 = (f32[128,256]{1,0:T(8,128)}, bf16[128,256]{1,0:T(8,128)(2,1)}, bf16[128,1280]{1,0:T(8,128)(2,1)S(1)}, bf16[320,640]{1,0:T(8,128)(2,1)S(1)}, bf1...) conditional(s32[]{:T(128)} %convert_element_type.60, ...), branch_computations={%region_0.0_spmd, %region_1.2_spmd} | conditional | flops 1430559104 | bytes 37746312 | solution.py:686
  0.7 2.5 %constant_dynamic-slice_fusion.4 = (bf16[320,640]{1,0:T(8,128)(2,1)}, bf16[320,640]{1,0:T(8,128)(2,1)}, bf16[320,640]{1,0:T(8,128)(2,1)}) fusion(bf16[1280,640]{1,0:T(8,128)(2,1)} %get-tuple-element.44, s32[]{:T(128)S(6)} %select_n.53, s32[]{:T(128)S(6)} %select_n.52, s32[]{:T(128)S(6)} %select_n.51), kind=kLoop, calls=%fused_computation.19 | loop fusion | bytes 2457612 | tf_op jit(solution)/shard_map/cond/branch_0_fun/dynamic_slice | solution.py:527
  3.2 5.1 %collective-permute-start.1 = (bf16[320,640]{1,0:T(8,128)(2,1)}, bf16[320,640]{1,0:T(8,128)(2,1)S(1)}, u32[]{:S(2)}, u32[]{:S(2)}) collective-permute-start(bf16[320,640]{1,0:T(8,128)(2,1)} %get-tuple-element.139), channel_id=1, source_target_pairs={{0,4},{4,8},{8,12},{12,0},{1,5},{5,9},{9,13},{13,1},{16,20},{20,24... | collective-permute-start | bytes 1228808 | tf_op jit(solution)/shard_map/cond/branch_0_fun/ppermute | solution.py:502
  8.2 3.9 %collective-permute-start.3 = (bf16[320,640]{1,0:T(8,128)(2,1)}, bf16[320,640]{1,0:T(8,128)(2,1)}, u32[]{:S(2)}, u32[]{:S(2)}) collective-permute-start(bf16[320,640]{1,0:T(8,128)(2,1)} %get-tuple-element.137), channel_id=1, source_target_pairs={{0,12},{4,0},{8,4},{12,8},{1,13},{5,1},{9,5},{13,9},{16,28},{20,16... | collective-permute-start | bytes 1228808 | tf_op jit(solution)/shard_map/cond/branch_0_fun/ppermute | solution.py:502
  12.2 2.9 %collective-permute-start.2 = (bf16[320,640]{1,0:T(8,128)(2,1)}, bf16[320,640]{1,0:T(8,128)(2,1)}, u32[]{:S(2)}, u32[]{:S(2)}) collective-permute-start(bf16[320,640]{1,0:T(8,128)(2,1)} %get-tuple-element.138), channel_id=1, source_target_pairs={{0,8},{4,12},{8,0},{12,4},{1,9},{5,13},{9,1},{13,5},{16,24},{20,28... | collective-permute-start | bytes 1228808 | tf_op jit(solution)/shard_map/cond/branch_0_fun/ppermute | solution.py:502
  15.1 0.3 fusion.12
  15.5 1.9 %collective-permute-start = (bf16[128,256]{1,0:T(8,128)(2,1)S(1)}, bf16[128,256]{1,0:T(8,128)(2,1)S(1)}, u32[]{:S(2)}, u32[]{:S(2)}) collective-permute-start(bf16[128,256]{1,0:T(8,128)(2,1)S(1)} %dynamic-slice_convert_fusion), channel_id=1, source_target_pairs={{0,1},{1,0},{4,5},{5,4},{8,9},{9,8},{12,13},{13,12},{16,17},{17,16... | collective-permute-start | bytes 196616 | tf_op jit(solution)/shard_map/cond/branch_0_fun/ppermute | solution.py:502
  17.5 0.3 branch_0_fun.1
  17.8 3.5 %collective-permute-start.8 = (bf16[128,1280]{1,0:T(8,128)(2,1)S(1)}, bf16[128,1280]{1,0:T(8,128)(2,1)}, u32[]{:S(2)}, u32[]{:S(2)}) collective-permute-start(bf16[128,1280]{1,0:T(8,128)(2,1)S(1)} %branch_0_fun.1), channel_id=1, source_target_pairs={{0,4},{4,0},{8,12},{12,8},{1,5},{5,1},{9,13},{13,9},{16,20},{20,16... | collective-permute-start | bytes 983048 | tf_op jit(solution)/shard_map/cond/branch_0_fun/ppermute | solution.py:502
  22.1 3.4 %collective-permute-start.4 = (bf16[320,640]{1,0:T(8,128)(2,1)S(1)}, bf16[320,640]{1,0:T(8,128)(2,1)}, u32[]{:S(2)}, u32[]{:S(2)}) collective-permute-start(bf16[320,640]{1,0:T(8,128)(2,1)S(1)} %collective-permute-done.1), channel_id=1, source_target_pairs={{0,16},{16,0},{1,17},{17,1},{4,20},{20,4},{5,21},{21,5},{8,24},{24... | collective-permute-start | bytes 1228808 | tf_op jit(solution)/shard_map/cond/branch_0_fun/ppermute | solution.py:502
  25.5 3.4 %collective-permute-done.3 = bf16[320,640]{1,0:T(8,128)(2,1)} collective-permute-done((bf16[320,640]{1,0:T(8,128)(2,1)}, bf16[320,640]{1,0:T(8,128)(2,1)}, u32[]{:S(2)}, u32[]{:S(2)}) %collective-permute-start.3) | collective-permute-done | bytes 409632 | tf_op jit(solution)/shard_map/cond/branch_0_fun/ppermute | solution.py:502
  28.9 3.4 %collective-permute-start.6 = (bf16[320,640]{1,0:T(8,128)(2,1)}, bf16[320,640]{1,0:T(8,128)(2,1)}, u32[]{:S(2)}, u32[]{:S(2)}) collective-permute-start(bf16[320,640]{1,0:T(8,128)(2,1)} %collective-permute-done.3), channel_id=1, source_target_pairs={{0,16},{16,0},{1,17},{17,1},{4,20},{20,4},{5,21},{21,5},{8,24},{24... | collective-permute-start | bytes 1228808 | tf_op jit(solution)/shard_map/cond/branch_0_fun/ppermute | solution.py:502
  32.3 0.7 convert_add_fusion
  33.0 13.4 %collective-permute-done.2 = bf16[320,640]{1,0:T(8,128)(2,1)} collective-permute-done((bf16[320,640]{1,0:T(8,128)(2,1)}, bf16[320,640]{1,0:T(8,128)(2,1)}, u32[]{:S(2)}, u32[]{:S(2)}) %collective-permute-start.2) | collective-permute-done | bytes 409632 | tf_op jit(solution)/shard_map/cond/branch_0_fun/ppermute | solution.py:502
  46.4 3.4 %collective-permute-start.5 = (bf16[320,640]{1,0:T(8,128)(2,1)}, bf16[320,640]{1,0:T(8,128)(2,1)}, u32[]{:S(2)}, u32[]{:S(2)}) collective-permute-start(bf16[320,640]{1,0:T(8,128)(2,1)} %collective-permute-done.2), channel_id=1, source_target_pairs={{0,16},{16,0},{1,17},{17,1},{4,20},{20,4},{5,21},{21,5},{8,24},{24... | collective-permute-start | bytes 1228808 | tf_op jit(solution)/shard_map/cond/branch_0_fun/ppermute | solution.py:502
  49.8 0.9 dynamic-slice_convert_fusion.1
  50.7 5.0 %collective-permute-start.7 = (bf16[136,896]{1,0:T(8,128)(2,1)S(1)}, bf16[136,896]{1,0:T(8,128)(2,1)}, u32[]{:S(2)}, u32[]{:S(2)}) collective-permute-start(bf16[136,896]{1,0:T(8,128)(2,1)S(1)} %fusion.9), channel_id=1, source_target_pairs={{0,4},{4,0},{8,12},{12,8},{1,5},{5,1},{9,13},{13,9},{16,20},{20,16... | collective-permute-start | bytes 731144 | tf_op jit(solution)/shard_map/cond/branch_0_fun/ppermute | solution.py:502
  55.8 0.6 broadcast_in_dim.14
  56.5 3.5 %collective-permute-done.5 = bf16[320,640]{1,0:T(8,128)(2,1)} collective-permute-done((bf16[320,640]{1,0:T(8,128)(2,1)}, bf16[320,640]{1,0:T(8,128)(2,1)}, u32[]{:S(2)}, u32[]{:S(2)}) %collective-permute-start.5) | collective-permute-done | bytes 409632 | tf_op jit(solution)/shard_map/cond/branch_0_fun/ppermute | solution.py:502
  59.9 0.3 collective-permute-done.7
  60.3 0.7 copy-done.22
  61.0 0.7 copy-done.18
  61.7 0.1 copy-done.20
  61.8 1.3 %collective-permute-start.18 = (bf16[128,1280]{1,0:T(8,128)(2,1)}, bf16[128,1280]{1,0:T(8,128)(2,1)S(1)}, u32[]{:S(2)}, u32[]{:S(2)}) collective-permute-start(bf16[128,1280]{1,0:T(8,128)(2,1)} %copy-done.22), channel_id=1, source_target_pairs={{2,0},{6,4},{10,8},{14,12},{3,1},{7,5},{11,9},{15,13},{18,16},{22,... | collective-permute-start | bytes 983048 | tf_op jit(solution)/shard_map/ppermute | solution.py:502
  63.1 1.4 %collective-permute-start.19 = (bf16[128,1280]{1,0:T(8,128)(2,1)}, bf16[128,1280]{1,0:T(8,128)(2,1)S(1)}, u32[]{:S(2)}, u32[]{:S(2)}) collective-permute-start(bf16[128,1280]{1,0:T(8,128)(2,1)} %copy-done.22), channel_id=1, source_target_pairs={{2,4},{6,0},{10,12},{14,8},{3,5},{7,1},{11,13},{15,9},{18,20},{22,... | collective-permute-start | bytes 983048 | tf_op jit(solution)/shard_map/ppermute | solution.py:502
  64.6 2.0 %constant_dynamic-slice_fusion.11 = (bf16[128,320]{1,0:T(8,128)(2,1)S(1)}, bf16[128,320]{1,0:T(8,128)(2,1)}, bf16[128,320]{1,0:T(8,128)(2,1)}, bf16[128,320]{1,0:T(8,128)(2,1)S(1)}) fusion(bf16[128,1280]{1,0:T(8,128)(2,1)} %bitcast.33, s32[]{:T(128)S(6)} %select_n.74, s32[]{:T(128)S(6)} %select_n.73, s32[]{:T(128)S(6)} %select_n.72, s32[]{:T(128)S(6)} %select_n.71), kind=kLoop, calls=%fused_computation.38 | loop fusion | bytes 655376 | tf_op jit(solution)/shard_map/dynamic_slice | solution.py:527
  66.6 1.7 %collective-permute-start.20 = (bf16[128,320]{1,0:T(8,128)(2,1)}, bf16[128,320]{1,0:T(8,128)(2,1)S(1)}, u32[]{:S(2)}, u32[]{:S(2)}) collective-permute-start(bf16[128,320]{1,0:T(8,128)(2,1)} %get-tuple-element.152), channel_id=1, source_target_pairs={{0,4},{4,8},{8,12},{12,0},{1,5},{5,9},{9,13},{13,1},{2,6},{6,10},{... | collective-permute-start | bytes 245768 | tf_op jit(solution)/shard_map/ppermute | solution.py:502
  68.3 2.7 %collective-permute-start.21 = (bf16[128,320]{1,0:T(8,128)(2,1)}, bf16[128,320]{1,0:T(8,128)(2,1)S(1)}, u32[]{:S(2)}, u32[]{:S(2)}) collective-permute-start(bf16[128,320]{1,0:T(8,128)(2,1)} %get-tuple-element.151), channel_id=1, source_target_pairs={{0,8},{4,12},{8,0},{12,4},{1,9},{5,13},{9,1},{13,5},{2,10},{6,14},... | collective-permute-start | bytes 245768 | tf_op jit(solution)/shard_map/ppermute | solution.py:502
  71.0 2.9 %collective-permute-start.22 = (bf16[128,320]{1,0:T(8,128)(2,1)S(1)}, bf16[128,320]{1,0:T(8,128)(2,1)S(1)}, u32[]{:S(2)}, u32[]{:S(2)}) collective-permute-start(bf16[128,320]{1,0:T(8,128)(2,1)S(1)} %get-tuple-element.150), channel_id=1, source_target_pairs={{0,12},{4,0},{8,4},{12,8},{1,13},{5,1},{9,5},{13,9},{2,14},{6,2},{... | collective-permute-start | bytes 245768 | tf_op jit(solution)/shard_map/ppermute | solution.py:502
  74.1 1.3 %shard_map.87.own_gain = bf16[128,1280]{1,0:T(8,128)(2,1)S(1)} custom-call(bf16[128,1280]{1,0:T(8,128)(2,1)S(1)} %bitcast.35, bf16[128,1280]{1,0:T(8,128)(2,1)} %bitcast.41), custom_call_target="tpu_custom_call" | custom-call | flops 10000000 | bytes 1000000 | tf_op jit(solution)/shard_map/pallas_call | solution.py:178
  75.4 2.0 %shard_map.88 = (bf16[2,5,128,128]{3,2,1,0:T(8,128)(2,1)S(1)}, f32[640,256]{1,0:T(8,128)S(1)}, f32[256,128]{1,0:T(8,128)S(1)}, f32[256,128]{1,0:T(8,128)S(1)}) custom-call(s32[5]{0:T(128)S(1)} %stack.69.place, bf16[136,896]{1,0:T(8,128)(2,1)S(1)} %copy-done.19, bf16[136,896]{1,0:T(8,128)(2,1)} %get-tuple-element.112.got), custom_call_target="tpu_custom_call" | custom-call | flops 100000000 | bytes 3000000 | tf_op jit(solution)/shard_map/pallas_call | solution.py:274
  77.4 1.4 %dynamic-slice_bitcast_fusion.refs_2_ = bf16[640,640]{1,0:T(8,128)(2,1)S(1)} fusion(bf16[1,1280,640]{2,1,0:T(8,128)(2,1)} %param.14, s32[]{:T(128)S(6)} %select_n.75), kind=kLoop, calls=%fused_computation.30 | loop fusion | bytes 1638404 | tf_op jit(solution)/shard_map/dynamic_slice | solution.py:527
  78.9 0.7 shard_map.86.inputs_t
  79.6 4.8 %collective-permute-done.18.current = bf16[128,1280]{1,0:T(8,128)(2,1)S(1)} collective-permute-done((bf16[128,1280]{1,0:T(8,128)(2,1)}, bf16[128,1280]{1,0:T(8,128)(2,1)S(1)}, u32[]{:S(2)}, u32[]{:S(2)}) %collective-permute-start.18) | collective-permute-done | bytes 327712 | tf_op jit(solution)/shard_map/ppermute | solution.py:502
  84.5 1.1 %shard_map.89.refs_0_ = bf16[256,1280]{1,0:T(8,128)(2,1)S(1)} custom-call(bf16[128,1280]{1,0:T(8,128)(2,1)S(1)} %shard_map.87.own_gain, bf16[128,1280]{1,0:T(8,128)(2,1)} %get-tuple-element.119.gain, bf16[128,1280]{1,0:T(8,128)(2,1)S(1)} %collective-permute-done.18.current, bf16[128,1280]{1,0:T(8,128)(2,1)S(1)} %collective-permute-done.19.partner), custom_call_target="tpu_custom_call" | custom-call | flops 10000000 | bytes 2000000 | tf_op jit(solution)/shard_map/pallas_call | solution.py:193
  85.6 1.9 %collective-permute-start.23 = (bf16[256,1280]{1,0:T(8,128)(2,1)S(1)}, bf16[256,1280]{1,0:T(8,128)(2,1)S(1)}, u32[]{:S(2)}, u32[]{:S(2)}) collective-permute-start(bf16[256,1280]{1,0:T(8,128)(2,1)S(1)} %shard_map.89.refs_0_), channel_id=1, source_target_pairs={{0,1},{1,0},{4,5},{5,4},{8,9},{9,8},{12,13},{13,12},{16,17},{17,16... | collective-permute-start | bytes 1966088 | tf_op jit(solution)/shard_map/ppermute | solution.py:502
  87.6 0.7 collective-permute-start.24
  88.9 0.4 fusion.10
  89.5 1.0 shard_map.90.refs_3_
  90.5 1.5 %shard_map.91.refs_4_ = f32[1,128]{1,0:T(1,128)S(1)} custom-call(bf16[128,1280]{1,0:T(8,128)(2,1)} %bitcast.34, bf16[128,1280]{1,0:T(8,128)(2,1)} %bitcast.42, bf16[128,1280]{1,0:T(8,128)(2,1)S(1)} %collective-permute-done.18.current), custom_call_target="tpu_custom_call" | custom-call | flops 100000 | bytes 10000 | tf_op jit(solution)/shard_map/pallas_call | solution.py:204
  92.1 3.4 %shard_map.92.refs_0_ = bf16[272,128]{1,0:T(8,128)(2,1)S(1)} custom-call(s32[5]{0:T(128)S(1)} %stack.72.place, bf16[256,1280]{1,0:T(8,128)(2,1)S(1)} %shard_map.89.refs_0_, bf16[256,1280]{1,0:T(8,128)(2,1)S(1)} %collective-permute-done.23.refs_1_, bf16[640,640]{1,0:T(8,128)(2,1)S(1)} %dynamic-slice_bitcast_fusion.refs_2_, ...), custom_call_target="tpu_custom_call" | custom-call | flops 1000000000 | bytes 6000000 | tf_op jit(solution)/shard_map/pallas_call | solution.py:376
  95.5 1.1 %collective-permute-start.25 = (bf16[272,128]{1,0:T(8,128)(2,1)S(1)}, bf16[272,128]{1,0:T(8,128)(2,1)S(1)}, u32[]{:S(2)}, u32[]{:S(2)}) collective-permute-start(bf16[272,128]{1,0:T(8,128)(2,1)S(1)} %shard_map.92.refs_0_), channel_id=1, source_target_pairs={{0,4},{4,8},{8,12},{12,0},{1,5},{5,9},{9,13},{13,1},{2,6},{6,10},{... | collective-permute-start | bytes 208904 | tf_op jit(solution)/shard_map/ppermute | solution.py:502
  96.6 0.4 collective-permute-start.26
  97.0 2.4 %collective-permute-start.27 = (bf16[272,128]{1,0:T(8,128)(2,1)S(1)}, bf16[272,128]{1,0:T(8,128)(2,1)S(1)}, u32[]{:S(2)}, u32[]{:S(2)}) collective-permute-start(bf16[272,128]{1,0:T(8,128)(2,1)S(1)} %shard_map.92.refs_0_), channel_id=1, source_target_pairs={{0,12},{4,0},{8,4},{12,8},{1,13},{5,1},{9,5},{13,9},{2,14},{6,2},{... | collective-permute-start | bytes 208904 | tf_op jit(solution)/shard_map/ppermute | solution.py:502
  99.4 3.0 %collective-permute-done.25.refs_1_ = bf16[272,128]{1,0:T(8,128)(2,1)S(1)} collective-permute-done((bf16[272,128]{1,0:T(8,128)(2,1)S(1)}, bf16[272,128]{1,0:T(8,128)(2,1)S(1)}, u32[]{:S(2)}, u32[]{:S(2)}) %collective-permute-start.25) | collective-permute-done | bytes 69664 | tf_op jit(solution)/shard_map/ppermute | solution.py:502
  102.5 2.6 %collective-permute-done.26.refs_2_ = bf16[272,128]{1,0:T(8,128)(2,1)S(1)} collective-permute-done((bf16[272,128]{1,0:T(8,128)(2,1)S(1)}, bf16[272,128]{1,0:T(8,128)(2,1)S(1)}, u32[]{:S(2)}, u32[]{:S(2)}) %collective-permute-start.26) | collective-permute-done | bytes 69664 | tf_op jit(solution)/shard_map/ppermute | solution.py:502
  105.1 1.5 %collective-permute-done.28.refs_4_ = bf16[1088,128]{1,0:T(8,128)(2,1)S(1)} collective-permute-done((bf16[1088,128]{1,0:T(8,128)(2,1)S(1)}, bf16[1088,128]{1,0:T(8,128)(2,1)S(1)}, u32[]{:S(2)}, u32[]{:S(2)}) %collective-permute-start.28) | collective-permute-done | bytes 278560 | tf_op jit(solution)/shard_map/ppermute | solution.py:502
  106.7 1.8 %shard_map.93 = (f32[320,512]{1,0:T(8,128)}, f32[1,128]{1,0:T(1,128)}) custom-call(s32[5]{0:T(128)S(1)} %stack.66.place, bf16[320,512]{1,0:T(8,128)(2,1)S(1)} %shard_map.86.inputs_t, bf16[1280,512]{1,0:T(8,128)(2,1)S(1)} %bitcast.38, bf16[272,128]{1,0:T(8,128)(2,1)S(1)} %shard_map.92.refs_0_, bf16[272,128]{1,0:T(8,128)(2,1)S(1)} %collective-permute-done.25.refs_1_, ...), custom_call_target="tpu_custom_call" | custom-call | flops 200000000 | bytes 2000000 | tf_op jit(solution)/shard_map/pallas_call | solution.py:468
  (62 shorter events, 0.7 us)
Async XLA Ops:
  0.6 73.5 %copy-start.6 = (bf16[1,1,128,1280]{3,2,1,0:T(8,128)(2,1)S(1)}, bf16[1,1,128,1280]{3,2,1,0:T(8,128)(2,1)}, u32[]{:S(2)}) copy-start(bf16[1,1,128,1280]{3,2,1,0:T(8,128)(2,1)} %param.9) | copy-start | bytes 983044
  0.7 14.4 %copy-start.8 = (bf16[128,1280]{1,0:T(8,128)(2,1)S(1)}, bf16[128,1280]{1,0:T(8,128)(2,1)}, u32[]{:S(2)}) copy-start(bf16[128,1280]{1,0:T(8,128)(2,1)} %get-tuple-element.38.inputs) | copy-start | bytes 983044 | tf_op jit(solution)/shard_map/cond
  0.7 14.4 %copy-start.11 = (bf16[1280,512]{1,0:T(8,128)(2,1)S(1)}, bf16[1280,512]{1,0:T(8,128)(2,1)}, u32[]{:S(2)}) copy-start(bf16[1280,512]{1,0:T(8,128)(2,1)} %get-tuple-element.39) | copy-start | bytes 3932164 | tf_op jit(solution)/shard_map/cond
  3.2 14.3 %copy-start.14 = (bf16[128,1280]{1,0:T(8,128)(2,1)S(1)}, bf16[128,1280]{1,0:T(8,128)(2,1)}, u32[]{:S(2)}) copy-start(bf16[128,1280]{1,0:T(8,128)(2,1)} %get-tuple-element.51.branch) | copy-start | bytes 983044 | tf_op jit(solution)/shard_map/cond
  3.2 18.9 %collective-permute-start.1 = (bf16[320,640]{1,0:T(8,128)(2,1)}, bf16[320,640]{1,0:T(8,128)(2,1)S(1)}, u32[]{:S(2)}, u32[]{:S(2)}) collective-permute-start(bf16[320,640]{1,0:T(8,128)(2,1)} %get-tuple-element.139), channel_id=1, source_target_pairs={{0,4},{4,8},{8,12},{12,0},{1,5},{5,9},{9,13},{13,1},{16,20},{20,24... | collective-permute-start | bytes 1228808 | tf_op jit(solution)/shard_map/cond/branch_0_fun/ppermute | solution.py:502
  8.2 20.7 %collective-permute-start.3 = (bf16[320,640]{1,0:T(8,128)(2,1)}, bf16[320,640]{1,0:T(8,128)(2,1)}, u32[]{:S(2)}, u32[]{:S(2)}) collective-permute-start(bf16[320,640]{1,0:T(8,128)(2,1)} %get-tuple-element.137), channel_id=1, source_target_pairs={{0,12},{4,0},{8,4},{12,8},{1,13},{5,1},{9,5},{13,9},{16,28},{20,16... | collective-permute-start | bytes 1228808 | tf_op jit(solution)/shard_map/cond/branch_0_fun/ppermute | solution.py:502
  12.2 34.2 %collective-permute-start.2 = (bf16[320,640]{1,0:T(8,128)(2,1)}, bf16[320,640]{1,0:T(8,128)(2,1)}, u32[]{:S(2)}, u32[]{:S(2)}) collective-permute-start(bf16[320,640]{1,0:T(8,128)(2,1)} %get-tuple-element.138), channel_id=1, source_target_pairs={{0,8},{4,12},{8,0},{12,4},{1,9},{5,13},{9,1},{13,5},{16,24},{20,28... | collective-permute-start | bytes 1228808 | tf_op jit(solution)/shard_map/cond/branch_0_fun/ppermute | solution.py:502
  15.1 6.8 %copy-start.16 = (bf16[128,1280]{1,0:T(8,128)(2,1)S(1)}, bf16[128,1280]{1,0:T(8,128)(2,1)}, u32[]{:S(2)}) copy-start(bf16[128,1280]{1,0:T(8,128)(2,1)} %get-tuple-element.47) | copy-start | bytes 983044 | tf_op jit(solution)/shard_map/cond
  15.5 6.5 %copy-start.23 = (bf16[128,256]{1,0:T(8,128)(2,1)S(1)}, bf16[128,256]{1,0:T(8,128)(2,1)}, u32[]{:S(2)}) copy-start(bf16[128,256]{1,0:T(8,128)(2,1)} %get-tuple-element.49) | copy-start | bytes 196612 | tf_op jit(solution)/shard_map/cond
  15.5 16.8 %collective-permute-start = (bf16[128,256]{1,0:T(8,128)(2,1)S(1)}, bf16[128,256]{1,0:T(8,128)(2,1)S(1)}, u32[]{:S(2)}, u32[]{:S(2)}) collective-permute-start(bf16[128,256]{1,0:T(8,128)(2,1)S(1)} %dynamic-slice_convert_fusion), channel_id=1, source_target_pairs={{0,1},{1,0},{4,5},{5,4},{8,9},{9,8},{12,13},{13,12},{16,17},{17,16... | collective-permute-start | bytes 196616 | tf_op jit(solution)/shard_map/cond/branch_0_fun/ppermute | solution.py:502
  17.8 38.7 %collective-permute-start.8 = (bf16[128,1280]{1,0:T(8,128)(2,1)S(1)}, bf16[128,1280]{1,0:T(8,128)(2,1)}, u32[]{:S(2)}, u32[]{:S(2)}) collective-permute-start(bf16[128,1280]{1,0:T(8,128)(2,1)S(1)} %branch_0_fun.1), channel_id=1, source_target_pairs={{0,4},{4,0},{8,12},{12,8},{1,5},{5,1},{9,13},{13,9},{16,20},{20,16... | collective-permute-start | bytes 983048 | tf_op jit(solution)/shard_map/cond/branch_0_fun/ppermute | solution.py:502
  22.1 28.6 %collective-permute-start.4 = (bf16[320,640]{1,0:T(8,128)(2,1)S(1)}, bf16[320,640]{1,0:T(8,128)(2,1)}, u32[]{:S(2)}, u32[]{:S(2)}) collective-permute-start(bf16[320,640]{1,0:T(8,128)(2,1)S(1)} %collective-permute-done.1), channel_id=1, source_target_pairs={{0,16},{16,0},{1,17},{17,1},{4,20},{20,4},{5,21},{21,5},{8,24},{24... | collective-permute-start | bytes 1228808 | tf_op jit(solution)/shard_map/cond/branch_0_fun/ppermute | solution.py:502
  28.9 21.8 %collective-permute-start.6 = (bf16[320,640]{1,0:T(8,128)(2,1)}, bf16[320,640]{1,0:T(8,128)(2,1)}, u32[]{:S(2)}, u32[]{:S(2)}) collective-permute-start(bf16[320,640]{1,0:T(8,128)(2,1)} %collective-permute-done.3), channel_id=1, source_target_pairs={{0,16},{16,0},{1,17},{17,1},{4,20},{20,4},{5,21},{21,5},{8,24},{24... | collective-permute-start | bytes 1228808 | tf_op jit(solution)/shard_map/cond/branch_0_fun/ppermute | solution.py:502
  46.4 13.6 %collective-permute-start.5 = (bf16[320,640]{1,0:T(8,128)(2,1)}, bf16[320,640]{1,0:T(8,128)(2,1)}, u32[]{:S(2)}, u32[]{:S(2)}) collective-permute-start(bf16[320,640]{1,0:T(8,128)(2,1)} %collective-permute-done.2), channel_id=1, source_target_pairs={{0,16},{16,0},{1,17},{17,1},{4,20},{20,4},{5,21},{21,5},{8,24},{24... | collective-permute-start | bytes 1228808 | tf_op jit(solution)/shard_map/cond/branch_0_fun/ppermute | solution.py:502
  50.7 9.6 %collective-permute-start.7 = (bf16[136,896]{1,0:T(8,128)(2,1)S(1)}, bf16[136,896]{1,0:T(8,128)(2,1)}, u32[]{:S(2)}, u32[]{:S(2)}) collective-permute-start(bf16[136,896]{1,0:T(8,128)(2,1)S(1)} %fusion.9), channel_id=1, source_target_pairs={{0,4},{4,0},{8,12},{12,8},{1,5},{5,1},{9,13},{13,9},{16,20},{20,16... | collective-permute-start | bytes 731144 | tf_op jit(solution)/shard_map/cond/branch_0_fun/ppermute | solution.py:502
  60.3 0.7 copy-start.22
  61.0 0.7 copy-start.18
  61.0 0.8 copy-start.20
  61.8 22.7 %collective-permute-start.18 = (bf16[128,1280]{1,0:T(8,128)(2,1)}, bf16[128,1280]{1,0:T(8,128)(2,1)S(1)}, u32[]{:S(2)}, u32[]{:S(2)}) collective-permute-start(bf16[128,1280]{1,0:T(8,128)(2,1)} %copy-done.22), channel_id=1, source_target_pairs={{2,0},{6,4},{10,8},{14,12},{3,1},{7,5},{11,9},{15,13},{18,16},{22,... | collective-permute-start | bytes 983048 | tf_op jit(solution)/shard_map/ppermute | solution.py:502
  63.1 12.3 %copy-start.19 = (bf16[136,896]{1,0:T(8,128)(2,1)S(1)}, bf16[136,896]{1,0:T(8,128)(2,1)}, u32[]{:S(2)}) copy-start(bf16[136,896]{1,0:T(8,128)(2,1)} %copy-done.18) | copy-start | bytes 731140
  63.1 21.4 %collective-permute-start.19 = (bf16[128,1280]{1,0:T(8,128)(2,1)}, bf16[128,1280]{1,0:T(8,128)(2,1)S(1)}, u32[]{:S(2)}, u32[]{:S(2)}) collective-permute-start(bf16[128,1280]{1,0:T(8,128)(2,1)} %copy-done.22), channel_id=1, source_target_pairs={{2,4},{6,0},{10,12},{14,8},{3,5},{7,1},{11,13},{15,9},{18,20},{22,... | collective-permute-start | bytes 983048 | tf_op jit(solution)/shard_map/ppermute | solution.py:502
  66.6 12.3 %collective-permute-start.20 = (bf16[128,320]{1,0:T(8,128)(2,1)}, bf16[128,320]{1,0:T(8,128)(2,1)S(1)}, u32[]{:S(2)}, u32[]{:S(2)}) collective-permute-start(bf16[128,320]{1,0:T(8,128)(2,1)} %get-tuple-element.152), channel_id=1, source_target_pairs={{0,4},{4,8},{8,12},{12,0},{1,5},{5,9},{9,13},{13,1},{2,6},{6,10},{... | collective-permute-start | bytes 245768 | tf_op jit(solution)/shard_map/ppermute | solution.py:502
  68.3 10.6 %collective-permute-start.21 = (bf16[128,320]{1,0:T(8,128)(2,1)}, bf16[128,320]{1,0:T(8,128)(2,1)S(1)}, u32[]{:S(2)}, u32[]{:S(2)}) collective-permute-start(bf16[128,320]{1,0:T(8,128)(2,1)} %get-tuple-element.151), channel_id=1, source_target_pairs={{0,8},{4,12},{8,0},{12,4},{1,9},{5,13},{9,1},{13,5},{2,10},{6,14},... | collective-permute-start | bytes 245768 | tf_op jit(solution)/shard_map/ppermute | solution.py:502
  71.0 7.9 %collective-permute-start.22 = (bf16[128,320]{1,0:T(8,128)(2,1)S(1)}, bf16[128,320]{1,0:T(8,128)(2,1)S(1)}, u32[]{:S(2)}, u32[]{:S(2)}) collective-permute-start(bf16[128,320]{1,0:T(8,128)(2,1)S(1)} %get-tuple-element.150), channel_id=1, source_target_pairs={{0,12},{4,0},{8,4},{12,8},{1,13},{5,1},{9,5},{13,9},{2,14},{6,2},{... | collective-permute-start | bytes 245768 | tf_op jit(solution)/shard_map/ppermute | solution.py:502
  77.4 1.5 %copy-start.4 = (f32[256,128]{1,0:T(8,128)}, f32[256,128]{1,0:T(8,128)S(1)}, u32[]{:S(2)}) copy-start(f32[256,128]{1,0:T(8,128)S(1)} %get-tuple-element.128.refs_8_) | copy-start | bytes 393220
  77.4 7.1 %copy-start = (bf16[2,5,128,128]{3,2,1,0:T(8,128)(2,1)}, bf16[2,5,128,128]{3,2,1,0:T(8,128)(2,1)S(1)}, u32[]{:S(2)}) copy-start(bf16[2,5,128,128]{3,2,1,0:T(8,128)(2,1)S(1)} %get-tuple-element.125.refs_5_) | copy-start | bytes 983044
  77.4 7.1 %copy-start.2 = (f32[256,128]{1,0:T(8,128)}, f32[256,128]{1,0:T(8,128)S(1)}, u32[]{:S(2)}) copy-start(f32[256,128]{1,0:T(8,128)S(1)} %get-tuple-element.127.refs_7_) | copy-start | bytes 393220
  78.9 10.0 %copy-start.7 = (bf16[1,1,128,1280]{3,2,1,0:T(8,128)(2,1)S(1)}, bf16[1,1,128,1280]{3,2,1,0:T(8,128)(2,1)}, u32[]{:S(2)}) copy-start(bf16[1,1,128,1280]{3,2,1,0:T(8,128)(2,1)} %param.9) | copy-start | bytes 983044
  78.9 10.0 %copy-start.13 = (bf16[1,1,128,1280]{3,2,1,0:T(8,128)(2,1)S(1)}, bf16[1,1,128,1280]{3,2,1,0:T(8,128)(2,1)}, u32[]{:S(2)}) copy-start(bf16[1,1,128,1280]{3,2,1,0:T(8,128)(2,1)} %param.10) | copy-start | bytes 983044
  85.6 6.4 %collective-permute-start.23 = (bf16[256,1280]{1,0:T(8,128)(2,1)S(1)}, bf16[256,1280]{1,0:T(8,128)(2,1)S(1)}, u32[]{:S(2)}, u32[]{:S(2)}) collective-permute-start(bf16[256,1280]{1,0:T(8,128)(2,1)S(1)} %shard_map.89.refs_0_), channel_id=1, source_target_pairs={{0,1},{1,0},{4,5},{5,4},{8,9},{9,8},{12,13},{13,12},{16,17},{17,16... | collective-permute-start | bytes 1966088 | tf_op jit(solution)/shard_map/ppermute | solution.py:502
  87.6 1.9 %collective-permute-start.24 = (bf16[128,256]{1,0:T(8,128)(2,1)}, bf16[128,256]{1,0:T(8,128)(2,1)S(1)}, u32[]{:S(2)}, u32[]{:S(2)}) collective-permute-start(bf16[128,256]{1,0:T(8,128)(2,1)} %get-tuple-element.123.found), channel_id=1, source_target_pairs={{2,6},{6,2},{10,14},{14,10},{3,7},{7,3},{11,15},{15,11},{18,22},{2... | collective-permute-start | bytes 196616 | tf_op jit(solution)/shard_map/ppermute | solution.py:502
  89.5 2.6 %copy-start.1 = (bf16[2,5,128,128]{3,2,1,0:T(8,128)(2,1)S(1)}, bf16[2,5,128,128]{3,2,1,0:T(8,128)(2,1)}, u32[]{:S(2)}) copy-start(bf16[2,5,128,128]{3,2,1,0:T(8,128)(2,1)} %copy-done) | copy-start | bytes 983044
  89.5 2.6 %copy-start.3 = (f32[256,128]{1,0:T(8,128)S(1)}, f32[256,128]{1,0:T(8,128)}, u32[]{:S(2)}) copy-start(f32[256,128]{1,0:T(8,128)} %copy-done.2) | copy-start | bytes 393220
  89.5 2.6 %copy-start.5 = (f32[256,128]{1,0:T(8,128)S(1)}, f32[256,128]{1,0:T(8,128)}, u32[]{:S(2)}) copy-start(f32[256,128]{1,0:T(8,128)} %copy-done.4) | copy-start | bytes 393220
  89.5 2.6 %copy-start.21 = (bf16[320,640]{1,0:T(8,128)(2,1)S(1)}, bf16[320,640]{1,0:T(8,128)(2,1)}, u32[]{:S(2)}) copy-start(bf16[320,640]{1,0:T(8,128)(2,1)} %copy-done.20) | copy-start | bytes 1228804
  92.1 14.6 %copy-start.10 = (bf16[1,1280,512]{2,1,0:T(8,128)(2,1)S(1)}, bf16[1,1280,512]{2,1,0:T(8,128)(2,1)}, u32[]{:S(2)}) copy-start(bf16[1,1280,512]{2,1,0:T(8,128)(2,1)} %param.13) | copy-start | bytes 3932164
  95.5 6.9 %collective-permute-start.25 = (bf16[272,128]{1,0:T(8,128)(2,1)S(1)}, bf16[272,128]{1,0:T(8,128)(2,1)S(1)}, u32[]{:S(2)}, u32[]{:S(2)}) collective-permute-start(bf16[272,128]{1,0:T(8,128)(2,1)S(1)} %shard_map.92.refs_0_), channel_id=1, source_target_pairs={{0,4},{4,8},{8,12},{12,0},{1,5},{5,9},{9,13},{13,1},{2,6},{6,10},{... | collective-permute-start | bytes 208904 | tf_op jit(solution)/shard_map/ppermute | solution.py:502
  96.6 8.4 %collective-permute-start.26 = (bf16[272,128]{1,0:T(8,128)(2,1)S(1)}, bf16[272,128]{1,0:T(8,128)(2,1)S(1)}, u32[]{:S(2)}, u32[]{:S(2)}) collective-permute-start(bf16[272,128]{1,0:T(8,128)(2,1)S(1)} %shard_map.92.refs_0_), channel_id=1, source_target_pairs={{0,8},{4,12},{8,0},{12,4},{1,9},{5,13},{9,1},{13,5},{2,10},{6,14},... | collective-permute-start | bytes 208904 | tf_op jit(solution)/shard_map/ppermute | solution.py:502
  97.0 8.0 %collective-permute-start.27 = (bf16[272,128]{1,0:T(8,128)(2,1)S(1)}, bf16[272,128]{1,0:T(8,128)(2,1)S(1)}, u32[]{:S(2)}, u32[]{:S(2)}) collective-permute-start(bf16[272,128]{1,0:T(8,128)(2,1)S(1)} %shard_map.92.refs_0_), channel_id=1, source_target_pairs={{0,12},{4,0},{8,4},{12,8},{1,13},{5,1},{9,5},{13,9},{2,14},{6,2},{... | collective-permute-start | bytes 208904 | tf_op jit(solution)/shard_map/ppermute | solution.py:502
  105.1 1.6 %collective-permute-start.28 = (bf16[1088,128]{1,0:T(8,128)(2,1)S(1)}, bf16[1088,128]{1,0:T(8,128)(2,1)S(1)}, u32[]{:S(2)}, u32[]{:S(2)}) collective-permute-start(bf16[1088,128]{1,0:T(8,128)(2,1)S(1)} %pad_maximum_fusion.1), channel_id=1, source_target_pairs={{0,1},{1,0},{2,3},{3,2},{4,5},{5,4},{6,7},{7,6},{8,9},{9,8},{10,11... | collective-permute-start | bytes 835592 | tf_op jit(solution)/shard_map/ppermute | solution.py:502
